TPU v7x, 32 devices: a whole 2x2x4 slice. The times are simulated.
32 devices in a mesh: grp: 2 (over y), wide: 16 (over z, x, core), narrow: 1.
Axes of the slice: x: 2, y: 2, z: 4, core: 2. Of those that a mesh axis runs over, the one named last changes fastest.
Arguments:
- dissim: float32 [1, 768, 384], P(None, ('grp', 'wide'), 'narrow'), parts along dimension 1, may hold values from 0.5 to 9.5
- classes: int32 [1, 768, 384], P(None, ('grp', 'wide'), 'narrow'), parts along dimension 1, may hold values from 0 to 3
- coords: float32 [16, 1, 768], P(None, 'narrow', ('grp', 'wide')), parts along dimension 2, may hold values from -3 to 3
Outputs:
- final_coords: float32 [16, 1, 768], P(None, 'narrow', ('grp', 'wide')), parts along dimension 2
- stress: float32 [6], P('grp'), parts along dimension 0
There are 2 independent parts, one for each index of `grp`. A program takes and returns all parts, laid end to end along the dimension named above; each array names one. Nothing has to cross between parts.
All inputs are finite; a program needn't handle non-finite values.
Results may differ from a plain program's by a relative error of at most 0.0003.
Values sent between devices are 32-bit elements; how exact they have to be, the bound alone decides.
No kernel may reach another device: no remote copies, remote signals or barrier semaphores. Data moves between devices by JAX's collectives and lax.ppermute only.
A program may use at most 64 MiB of HBM per device.

v0:
```python
import jax
import jax.numpy as jnp
from jax import lax
from jax.sharding import PartitionSpec as P

ITERS = 3


def class_weight(class_codes):
    return jnp.where(
        class_codes == 3,
        1.0,
        jnp.where(class_codes == 2, 0.5, jnp.where(class_codes == 1, 0.25, 0.0)),
    ).astype(jnp.float32)


def body(dissim, classes, coords):
    halves = dissim.shape[0]
    per_dev = dissim.shape[1]
    columns = dissim.shape[2]
    coord_dims = coords.shape[0]
    row_count = halves * per_dev
    dis_tile = dissim.reshape(row_count, columns)
    weight = class_weight(classes.reshape(row_count, columns))
    denom_local = jnp.sum(weight * dis_tile * dis_tile)
    half_index = lax.axis_index("narrow")
    denom_total = lax.psum(denom_local, ("wide", "narrow"))
    positions = coords
    numbers = []
    for sweep in range(ITERS):
        row_points = lax.all_gather(positions, "narrow", axis=1, tiled=True)
        row_x = row_points.reshape(coord_dims, row_count)
        row_sq = jnp.sum(row_x * row_x, axis=0)
        fold_column_x = lax.dynamic_index_in_dim(
            lax.all_gather(row_points, "wide", axis=2, tiled=True), half_index, 1, keepdims=False
        )
        inner_prod = lax.dot_general(
            row_x,
            fold_column_x,
            (((0,), (0,)), ((), ())),
            precision=lax.Precision.HIGHEST,
            preferred_element_type=jnp.float32,
        )
        col_sq = jnp.sum(fold_column_x * fold_column_x, axis=0)
        distance = jnp.sqrt(row_sq[:, None] + col_sq[None, :] - 2.0 * inner_prod + 1.0)
        ratios = weight * dis_tile / distance
        pull_term = lax.dot_general(
            weight - ratios,
            fold_column_x,
            (((1,), (1,)), ((), ())),
            precision=lax.Precision.HIGHEST,
            preferred_element_type=jnp.float32,
        )
        misfit = dis_tile - distance
        pull_sums = pull_term.reshape(halves, per_dev, coord_dims).transpose(0, 2, 1)
        weight_sum, ratio_sum, pull_share = (
            lax.psum_scatter(
                jnp.sum(weight, axis=1).reshape(halves, per_dev),
                "narrow",
                scatter_dimension=0,
                tiled=True,
            ),
            lax.psum_scatter(
                jnp.sum(ratios, axis=1).reshape(halves, per_dev),
                "narrow",
                scatter_dimension=0,
                tiled=True,
            ),
            lax.psum_scatter(pull_sums, "narrow", scatter_dimension=0, tiled=True),
        )
        own_coords = positions[:, 0, :]
        updated = (own_coords * (1.0 + ratio_sum[0]) + pull_share[0]) / (1.0 + weight_sum[0])
        positions = updated[:, None, :]
        numbers.append(
            lax.psum(jnp.sum(weight * misfit * misfit), ("wide", "narrow")) / denom_total
        )
    stress = jnp.stack(numbers)
    return (positions, stress)


def solution(mesh):
    return jax.shard_map(
        body,
        mesh=mesh,
        in_specs=(
            P(None, ("grp", "wide"), "narrow"),
            P(None, ("grp", "wide"), "narrow"),
            P(None, "narrow", ("grp", "wide")),
        ),
        out_specs=(P(None, "narrow", ("grp", "wide")), P("grp")),
        check_vma=False,
    )
```

profile of v0, /device:TPU:0, one launch (start us, length us, event | category | flops | bytes accessed | tf_op | source)
XLA Modules:
  0.0 104.3 jit_solution(16599617905876419756)
XLA Ops:
  0.6 0.7 multiply_reduce_fusion.3
  1.3 0.0 copy-start.2
  1.3 0.9 fusion.26
  2.3 0.0 copy-done.2
  2.3 0.1 copy.7
  2.3 23.6 %all_gather.12 = f32[16,1,384]{0,1,2:T(1,128)S(1)} all-gather(f32[16,1,24]{0,1,2:T(1,128)S(1)} %copy.7), channel_id=1, replica_groups=mesh['grp'=2,'wide'=16,'narrow'=1] {'wide'}, dimensions={2}, use_global_device_ids=true | all-gather | bytes 26112 | tf_op jit(solution)/shard_map/all_gather | solution.py:35
  25.9 0.0 copy-start
  25.9 0.1 multiply_reduce_fusion.2
  26.1 0.6 copy-done
  26.7 0.0 copy-done.1
  26.7 1.0 %fusion.15 = (f32[]{:T(128)}, f32[24]{0:T(128)S(1)}, f32[]{:T(128)}, f32[24,384]{1,0:T(8,128)S(1)}) fusion(f32[1,24,384]{2,1,0:T(8,128)S(1)} %copy-done.1, s32[1,24,384]{2,1,0:T(8,128)S(1)} %copy-done, f32[16,24]{1,0:T(8,128)S(1)} %bitcast.139, f32[16,384]{0,1:T(8,128)S(1)} %bitcast.136, f32[384]{0:T(512)S(1)} %multiply_reduce_fusion.2, ...), kind=kOutput, calls=%fused_computation.27 | convolution fusion | flops 1944550 | bytes 138440 | tf_op jit(solution)/shard_map/dot_general | solution.py:37
  27.8 0.5 fusion.25
  28.2 0.1 copy.9
  28.3 18.0 %all_gather.13 = f32[16,1,384]{0,1,2:T(1,128)S(1)} all-gather(f32[16,1,24]{0,1,2:T(1,128)S(1)} %copy.9), channel_id=1, replica_groups=mesh['grp'=2,'wide'=16,'narrow'=1] {'wide'}, dimensions={2}, use_global_device_ids=true | all-gather | bytes 26112 | tf_op jit(solution)/shard_map/all_gather | solution.py:35
  46.3 0.1 multiply_reduce_fusion.1
  46.4 1.0 fusion.16
  47.4 0.5 fusion.23
  47.9 0.1 copy.10
  48.0 19.3 %all_gather.14 = f32[16,1,384]{0,1,2:T(1,128)S(1)} all-gather(f32[16,1,24]{0,1,2:T(1,128)S(1)} %copy.10), channel_id=1, replica_groups=mesh['grp'=2,'wide'=16,'narrow'=1] {'wide'}, dimensions={2}, use_global_device_ids=true | all-gather | bytes 26112 | tf_op jit(solution)/shard_map/all_gather | solution.py:35
  67.2 0.1 multiply_reduce_fusion
  67.4 1.0 fusion.17
  68.4 1.1 %fusion.14 = f32[16,1,24]{2,0,1:T(8,128)} fusion(f32[16,384]{0,1:T(8,128)S(1)} %bitcast.134, f32[24,384]{1,0:T(8,128)S(1)} %get-tuple-element.23, f32[16,1,24]{2,0,1:T(8,128)S(1)} %get-tuple-element.22, f32[24]{0:T(128)S(1)} %broadcast_add_fusion, f32[24]{0:T(128)S(1)} %broadcast_add_fusion.2, f32[1,24,384]{2,1,0:T(8,128)S(1)} %copy-done.1, ...), kind=kOutput, calls=%fused_computation.20 | convolution fusion | flops 1853568 | bytes 138432 | tf_op jit(solution)/shard_map/dot_general | solution.py:47
  69.4 30.5 %all-reduce = (f32[]{:T(128)}, f32[]{:T(128)}, f32[]{:T(128)}, f32[]{:T(128)}) all-reduce(f32[]{:T(128)} %get-tuple-element.10, f32[]{:T(128)} %get-tuple-element.12, f32[]{:T(128)} %get-tuple-element.8, f32[]{:T(128)} %get-tuple-element.6), channel_id=1, replica_groups=mesh['grp'=2,'wide'=16,'narrow'=1] {'wide','narrow'}, use_global_device_ids=true, to_apply=%region_17.18 | all-reduce | flops 4 | bytes 32 | tf_op jit(solution)/shard_map/psum | solution.py:75
  103.7 0.6 pad_maximum_fusion
  (5 shorter events, 0.0 us)
Async XLA Ops:
  1.3 0.9 copy-start.2
  25.9 0.8 copy-start
  25.9 0.8 copy-start.1
where the time goes:
time: 105 us; the launch traced here: 104 us
  blocking collectives  91.3 us (87%)
  matrix products  5.06 us (5%)
  between operations  4.42 us (4%)
  other arithmetic  2.64 us (3%)
    all_gather x3, blocking collectives, body(): lax.all_gather(row_points, 'wide', axis=2, tiled=True)  60.8 us
    psum x1, blocking collectives, body(): lax.psum(jnp.sum(weight * misfit * misfit), ('wide', 'narrow'))  30.5 us
    dot_general x3, matrix products, body(): lax.dot_general(row_x, fold_column_x, (((0,), (0,)), ((), ())), precision...  3.07 us

commit v1 on v0

--- a/solution.py
+++ b/solution.py
@@ -1,9 +1,15 @@
+import functools
+
 import jax
 import jax.numpy as jnp
 from jax import lax
+from jax.experimental import pallas as pl
+from jax.experimental.pallas import tpu as pltpu
 from jax.sharding import PartitionSpec as P
 
 ITERS = 3
+REPLICATED_BYTES = 1 << 22
+HIGHEST = lax.Precision.HIGHEST
 
 
 def class_weight(class_codes):
@@ -14,7 +20,73 @@
     ).astype(jnp.float32)
 
 
-def body(dissim, classes, coords):
+def group_kernel(per_dev, dis_ref, cls_ref, x_ref, out_ref, stress_ref, w_ref, wd_ref):
+    weight = class_weight(cls_ref[...])
+    dis = dis_ref[...]
+    weighted = weight * dis
+    w_ref[...] = weight
+    wd_ref[...] = weighted
+    denom = jnp.sum(weighted * dis)
+    x = x_ref[...]
+    ones = jnp.ones((8, x.shape[1]), jnp.float32)
+    nt = (((1,), (1,)), ((), ()))
+    dot = functools.partial(
+        lax.dot_general, dimension_numbers=nt, precision=HIGHEST, preferred_element_type=jnp.float32
+    )
+    weight_sum = dot(ones, weight)[0:1]
+    for sweep in range(ITERS):
+        xt = x.T
+        col_sq = jnp.sum(x * x, axis=0, keepdims=True)
+        row_sq = jnp.sum(xt * xt, axis=1, keepdims=True)
+        inner = jnp.dot(xt, x, precision=HIGHEST, preferred_element_type=jnp.float32)
+        distance = jnp.sqrt(row_sq + col_sq - 2.0 * inner + 1.0)
+        ratios = wd_ref[...] / distance
+        misfit = dis_ref[...] - distance
+        stress_ref[sweep] = jnp.sum(w_ref[...] * misfit * misfit) / denom
+        pull = dot(x, w_ref[...] - ratios)
+        ratio_sum = dot(ones, ratios)[0:1]
+        x = (x * (1.0 + ratio_sum) + pull) / (1.0 + weight_sum)
+    mine = lax.axis_index("wide") * per_dev
+    points = x.shape[1]
+    pick = lax.broadcasted_iota(jnp.int32, (points, per_dev), 0) == mine + lax.broadcasted_iota(
+        jnp.int32, (points, per_dev), 1
+    )
+    out_ref[...] = jnp.dot(
+        x, pick.astype(jnp.float32), precision=HIGHEST, preferred_element_type=jnp.float32
+    )
+
+
+def replicated_body(dissim, classes, coords):
+    coord_dims, _, per_dev = coords.shape
+    columns = dissim.shape[2]
+    dis = lax.all_gather(dissim[0], "wide", axis=0, tiled=True)
+    cls = lax.all_gather(classes[0], "wide", axis=0, tiled=True)
+    x = lax.all_gather(coords[:, 0, :].T, "wide", axis=0, tiled=True).T
+    vmem = pl.BlockSpec(memory_space=pltpu.VMEM)
+    final, stress = pl.pallas_call(
+        functools.partial(group_kernel, per_dev),
+        out_shape=(
+            jax.ShapeDtypeStruct((coord_dims, per_dev), jnp.float32),
+            jax.ShapeDtypeStruct((ITERS,), jnp.float32),
+        ),
+        in_specs=[vmem, vmem, vmem],
+        out_specs=(vmem, pl.BlockSpec(memory_space=pltpu.SMEM)),
+        scratch_shapes=[
+            pltpu.VMEM((columns, columns), jnp.float32),
+            pltpu.VMEM((columns, columns), jnp.float32),
+        ],
+        compiler_params=pltpu.CompilerParams(vmem_limit_bytes=32 << 20),
+        cost_estimate=pl.CostEstimate(
+            flops=ITERS * 24 * columns * columns * coord_dims,
+            bytes_accessed=8 * columns * columns,
+            transcendentals=ITERS * columns * columns,
+        ),
+        name="group_smacof",
+    )(dis, cls, x)
+    return (final[:, None, :], stress)
+
+
+def distributed_body(dissim, classes, coords):
     halves = dissim.shape[0]
     per_dev = dissim.shape[1]
     columns = dissim.shape[2]
@@ -79,6 +151,11 @@
 
 
 def solution(mesh):
+    def body(dissim, classes, coords):
+        group_bytes = 8 * dissim.size * mesh.shape["wide"]
+        small = mesh.shape["narrow"] == 1 and group_bytes <= REPLICATED_BYTES
+        return (replicated_body if small else distributed_body)(dissim, classes, coords)
+
     return jax.shard_map(
         body,
         mesh=mesh,

time: 105 us -> 72.9 us (0.69)
  blocking collectives: 91.3 us -> 63.3 us
  Pallas kernels: 0 us -> 7.95 us
  matrix products: 5.06 us -> 0 us
  between operations: 4.42 us -> 0.64 us
  other arithmetic: 2.64 us -> 0 us
    psum x1 -> x0, blocking collectives: 30.5 us -> none  [body(): lax.psum(jnp.sum(weight * misfit * misfit), ('wide', 'narrow'))]
    pallas_call x0 -> x1, Pallas kernels: none -> 7.95 us  [replicated_body(): pl.pallas_call(functools.partial(group_kernel, per_dev), out_shape=(jax.S...]
    dot_general x6 -> x0, matrix products: 5.06 us -> none  [the longest x3 3.07 us: body(): lax.dot_general(row_x, fold_column_x, (((0,), (0,)), ((), ())), precision...]
    all_gather x3, blocking collectives: 60.8 us -> 63.3 us  [the longest x1 23.7 us: replicated_body(): x = lax.all_gather(coords[:, 0, :].T, 'wide', axis=0, tiled=True).T]
    reduce_sum x5 -> x0, other arithmetic: 2.03 us -> none  [the longest x1 0.9 us: body(): jnp.sum(weight, axis=1).reshape(halves, per_dev)]
where the time goes in v1:
time: 72.9 us; the launch traced here: 72.7 us
  blocking collectives  63.3 us (87%)
  Pallas kernels  7.95 us (11%)
  local copies, waits for them, and re-layouts  0.81 us (1%)
    all_gather x1, blocking collectives, replicated_body(): x = lax.all_gather(coords[:, 0, :].T, 'wide', axis=0, tiled=True).T  23.7 us
    all_gather x1, blocking collectives, replicated_body(): cls = lax.all_gather(classes[0], 'wide', axis=0, tiled=True)  20.4 us
    all_gather x1, blocking collectives, replicated_body(): dis = lax.all_gather(dissim[0], 'wide', axis=0, tiled=True)  19.2 us
    pallas_call x1, Pallas kernels, replicated_body(): pl.pallas_call(functools.partial(group_kernel, per_dev), out_shape=(jax.S...  7.95 us

profile of v1, /device:TPU:0, one launch (start us, length us, event | category | flops | bytes accessed | tf_op | source)
XLA Modules:
  0.0 72.7 jit_solution(2729217134321953639)
XLA Ops:
  0.6 23.7 %all-gather.2 = f32[16,24,16]{1,2,0:T(8,128)S(1)} all-gather(f32[1,24,16]{1,2,0:T(8,128)} %bitcast.16), channel_id=1, replica_groups=mesh['grp'=2,'wide'=16,'narrow'=1] {'wide'}, dimensions={0}, use_global_device_ids=true | all-gather | bytes 26112 | tf_op jit(solution)/shard_map/all_gather | solution.py:64
  24.3 0.0 copy-start
  24.4 0.1 reshape.7
  24.5 0.6 copy-done
  25.1 0.0 copy-start.1
  25.1 19.2 %all-gather = f32[1,384,384]{2,1,0:T(8,128)S(1)} all-gather(f32[1,24,384]{2,1,0:T(8,128)S(1)} %copy-done), channel_id=2, replica_groups=mesh['grp'=2,'wide'=16,'narrow'=1] {'wide'}, dimensions={1}, use_global_device_ids=true | all-gather | bytes 626688 | tf_op jit(solution)/shard_map/all_gather | solution.py:62
  44.3 0.0 copy-done.1
  44.3 20.4 %all-gather.1 = s32[1,384,384]{2,1,0:T(8,128)S(1)} all-gather(s32[1,24,384]{2,1,0:T(8,128)S(1)} %copy-done.1), channel_id=3, replica_groups=mesh['grp'=2,'wide'=16,'narrow'=1] {'wide'}, dimensions={1}, use_global_device_ids=true | all-gather | bytes 626688 | tf_op jit(solution)/shard_map/all_gather | solution.py:63
  64.7 7.9 %group_smacof.1 = (f32[16,24]{1,0:T(8,128)}, f32[3]{0:T(128)}) custom-call(f32[384,384]{1,0:T(8,128)S(1)} %bitcast.13, s32[384,384]{1,0:T(8,128)S(1)} %bitcast.14, f32[16,384]{1,0:T(8,128)S(1)} %bitcast.15), custom_call_target="tpu_custom_call" | custom-call | flops 169869312 | bytes 1179648 | tf_op jit(solution)/shard_map/group_smacof/pallas_call | solution.py:66
  (1 shorter events, 0.0 us)
Async XLA Ops:
  24.3 0.8 %copy-start = (f32[1,24,384]{2,1,0:T(8,128)S(1)}, f32[1,24,384]{2,1,0:T(8,128)}, u32[]{:S(2)}) copy-start(f32[1,24,384]{2,1,0:T(8,128)} %param.3) | copy-start | bytes 110596
  25.1 19.2 %copy-start.1 = (s32[1,24,384]{2,1,0:T(8,128)S(1)}, s32[1,24,384]{2,1,0:T(8,128)}, u32[]{:S(2)}) copy-start(s32[1,24,384]{2,1,0:T(8,128)} %param.4) | copy-start | bytes 110596

commit v2 on v0

--- a/solution.py
+++ b/solution.py
@@ -1,9 +1,15 @@
+import functools
+
 import jax
 import jax.numpy as jnp
 from jax import lax
+from jax.experimental import pallas as pl
+from jax.experimental.pallas import tpu as pltpu
 from jax.sharding import PartitionSpec as P
 
 ITERS = 3
+REPLICATED_BYTES = 1 << 22
+LANES = 128
 
 
 def class_weight(class_codes):
@@ -14,7 +20,106 @@
     ).astype(jnp.float32)
 
 
-def body(dissim, classes, coords):
+def split_bf16(value, terms):
+    parts = []
+    for _ in range(terms):
+        part = value.astype(jnp.bfloat16)
+        parts.append(part)
+        value = value - part.astype(jnp.float32)
+    return parts
+
+
+def pack_kernel(dis_ref, cls_ref, x_ref, out_ref):
+    columns = dis_ref.shape[1]
+    coord_dims, per_dev = x_ref.shape
+    out_ref[:, :columns] = dis_ref[...]
+    out_ref[:, columns : 2 * columns] = class_weight(cls_ref[...])
+    padded = jnp.concatenate(
+        [x_ref[...], jnp.zeros((LANES - coord_dims, per_dev), jnp.float32)], axis=0
+    )
+    out_ref[:, 2 * columns :] = padded.T
+
+
+def group_kernel(per_dev, coord_dims, data_ref, out_ref, stress_ref, wd_ref):
+    points = data_ref.shape[0]
+    dis = data_ref[:, :points]
+    weight = data_ref[:, points : 2 * points]
+    weighted = weight * dis
+    wd_ref[...] = weighted
+    denom = jnp.sum(weighted * dis)
+    x = data_ref[:, 2 * points :].T[:coord_dims]
+    nt = (((1,), (1,)), ((), ()))
+    tn = (((0,), (0,)), ((), ()))
+    dot = functools.partial(lax.dot_general, preferred_element_type=jnp.float32)
+    ones = jnp.ones((coord_dims, points), jnp.bfloat16)
+    one = jnp.ones((3, points), jnp.float32)
+    pad = jnp.zeros((coord_dims - 6, points), jnp.float32)
+    scale = 1.0 / (1.0 + dot(weight.astype(jnp.bfloat16), ones, nt).T[0:1])
+    for sweep in range(ITERS):
+        hi, mid, lo = split_bf16(x, 3)
+        norm = jnp.sum(x * x, axis=0, keepdims=True)
+        row_norm = [p.astype(jnp.float32) for p in split_bf16(norm, 3)]
+        col_norm = [p.astype(jnp.float32) for p in split_bf16(norm + 1.0, 3)]
+        left_norm = jnp.concatenate([*row_norm, one, pad], axis=0).astype(jnp.bfloat16)
+        right_norm = jnp.concatenate([one, *col_norm, pad], axis=0).astype(jnp.bfloat16)
+        left = jnp.concatenate(
+            [-2.0 * hi, -2.0 * hi, -2.0 * hi, -2.0 * mid, -2.0 * mid, -2.0 * lo, left_norm], axis=0
+        )
+        right = jnp.concatenate([hi, mid, lo, hi, mid, hi, right_norm], axis=0)
+        square = dot(left, right, tn)
+        inverse = lax.rsqrt(square)
+        weight = data_ref[:, points : 2 * points]
+        misfit = data_ref[:, :points] - square * inverse
+        stress_ref[sweep] = jnp.sum(weight * misfit * misfit) / denom
+        pull_hi, pull_lo = split_bf16(weight - wd_ref[...] * inverse, 2)
+        sides = jnp.concatenate([hi, mid, ones], axis=0)
+        sums = (dot(pull_hi, sides, nt) + dot(pull_lo, sides, nt)).T
+        pull = sums[:coord_dims] + sums[coord_dims : 2 * coord_dims]
+        x = x + (pull - x * sums[2 * coord_dims : 2 * coord_dims + 1]) * scale
+    mine = lax.axis_index("wide") * per_dev
+    shape = (points, per_dev)
+    pick = lax.broadcasted_iota(jnp.int32, shape, 0) == mine + lax.broadcasted_iota(
+        jnp.int32, shape, 1
+    )
+    pick = pick.astype(jnp.float32).astype(jnp.bfloat16)
+    out_ref[...] = sum(dot(p, pick, (((1,), (0,)), ((), ()))) for p in split_bf16(x, 3))
+
+
+def replicated_body(dissim, classes, coords):
+    coord_dims, _, per_dev = coords.shape
+    points = dissim.shape[2]
+    vmem = pl.BlockSpec(memory_space=pltpu.VMEM)
+    params = pltpu.CompilerParams(vmem_limit_bytes=32 << 20)
+    packed = pl.pallas_call(
+        pack_kernel,
+        out_shape=jax.ShapeDtypeStruct((per_dev, 2 * points + LANES), jnp.float32),
+        in_specs=[vmem, vmem, vmem],
+        out_specs=vmem,
+        compiler_params=params,
+        name="pack_rows",
+    )(dissim[0], classes[0], coords[:, 0, :])
+    data = lax.all_gather(packed, "wide", axis=0, tiled=True)
+    final, stress = pl.pallas_call(
+        functools.partial(group_kernel, per_dev, coord_dims),
+        out_shape=(
+            jax.ShapeDtypeStruct((coord_dims, per_dev), jnp.float32),
+            jax.ShapeDtypeStruct((ITERS,), jnp.float32),
+        ),
+        in_specs=[vmem],
+        out_specs=(vmem, pl.BlockSpec(memory_space=pltpu.SMEM)),
+        scratch_shapes=[pltpu.VMEM((points, points), jnp.float32)],
+        compiler_params=params,
+        cost_estimate=pl.CostEstimate(
+            flops=ITERS * 24 * points * points * coord_dims,
+            bytes_accessed=8 * points * points,
+            transcendentals=ITERS * points * points,
+        ),
+        name="group_smacof",
+    )(data)
+    return (final[:, None, :], stress)
+
+
+def distributed_body(dissim, classes, coords):
     halves = dissim.shape[0]
     per_dev = dissim.shape[1]
     columns = dissim.shape[2]
@@ -79,6 +184,11 @@
 
 
 def solution(mesh):
+    def body(dissim, classes, coords):
+        group_bytes = 8 * dissim.size * mesh.shape["wide"]
+        small = mesh.shape["narrow"] == 1 and group_bytes <= REPLICATED_BYTES
+        return (replicated_body if small else distributed_body)(dissim, classes, coords)
+
     return jax.shard_map(
         body,
         mesh=mesh,

time: 105 us -> 63.4 us (0.60)
  blocking collectives: 91.3 us -> 0 us
  waiting for transfers between devices: 0 us -> 41.9 us
  between operations: 4.42 us -> 14.1 us
  matrix products: 5.06 us -> 0 us
  Pallas kernels: 0 us -> 3.46 us
  local copies, waits for them, and re-layouts: 0.86 us -> 3.56 us
  other arithmetic: 2.64 us -> 0 us
    all_gather x3 -> x0, blocking collectives: 60.8 us -> none  [body(): lax.all_gather(row_points, 'wide', axis=2, tiled=True)]
    all_gather x0 -> x1, waiting for transfers between devices: none -> 41.9 us  [replicated_body(): data = lax.all_gather(packed, 'wide', axis=0, tiled=True)]
    psum x1 -> x0, blocking collectives: 30.5 us -> none  [body(): lax.psum(jnp.sum(weight * misfit * misfit), ('wide', 'narrow'))]
    dot_general x6 -> x0, matrix products: 5.06 us -> none  [the longest x3 3.07 us: body(): lax.dot_general(row_x, fold_column_x, (((0,), (0,)), ((), ())), precision...]
    pallas_call x0 -> x2, Pallas kernels: none -> 3.46 us  [the longest x1 2.76 us: replicated_body(): pl.pallas_call(functools.partial(group_kernel, per_dev, coord_dims), out_...]
    unnamed x7 -> x8, local copies, waits for them, and re-layouts: 0.72 us -> 3.56 us
    reduce_sum x5 -> x0, other arithmetic: 2.03 us -> none  [the longest x1 0.9 us: body(): jnp.sum(weight, axis=1).reshape(halves, per_dev)]
  transfers between devices with their start and end apart: 0 -> 1, of which waited for: 0 -> 1; matrix products, arithmetic and copies ran while one was open for 0% -> 0% of each run, Pallas kernels for 0% -> 0%
where the time goes in v2:
time: 63.4 us; the launch traced here: 63 us
  waiting for transfers between devices  41.9 us (66%)
  between operations  14.1 us (22%)
  local copies, waits for them, and re-layouts  3.56 us (6%)
  Pallas kernels  3.46 us (5%)
    all_gather x1, waiting for transfers between devices, replicated_body(): data = lax.all_gather(packed, 'wide', axis=0, tiled=True)  41.9 us
    unnamed x8, local copies, waits for them, and re-layouts  3.56 us
    pallas_call x1, Pallas kernels, replicated_body(): pl.pallas_call(functools.partial(group_kernel, per_dev, coord_dims), out_...  2.76 us
  transfers between devices with their start and end apart: 1, of which 1 were waited for; matrix products, arithmetic and copies ran while one was open for 0% of the time, Pallas kernels for 0%

profile of v2, /device:TPU:0, one launch (start us, length us, event | category | flops | bytes accessed | tf_op | source)
XLA Modules:
  0.0 63.0 jit_solution(1542429318987102782)
XLA Ops:
  7.2 0.0 all-gather.2.cloned.1.call-start
  7.2 0.0 copy-start.1
  7.2 0.8 %copy-done.1 = f32[1,24,384]{2,1,0:T(8,128)S(1)} copy-done((f32[1,24,384]{2,1,0:T(8,128)S(1)}, f32[1,24,384]{2,1,0:T(8,128)}, u32[]{:S(2)}) %copy-start.1) | copy-done | bytes 36888
  8.0 0.0 copy-start.2
  8.0 0.8 %copy-done.2 = s32[1,24,384]{2,1,0:T(8,128)S(1)} copy-done((s32[1,24,384]{2,1,0:T(8,128)S(1)}, s32[1,24,384]{2,1,0:T(8,128)}, u32[]{:S(2)}) %copy-start.2) | copy-done | bytes 36888
  8.7 0.0 copy-start.3
  8.8 0.7 %copy-done.3 = f32[16,1,24]{2,1,0:T(1,128)S(1)} copy-done((f32[16,1,24]{2,1,0:T(1,128)S(1)}, f32[16,1,24]{2,1,0:T(1,128)}, u32[]{:S(2)}) %copy-start.3) | copy-done | bytes 1560
  9.4 0.7 %pack_rows.1 = f32[24,896]{1,0:T(8,128)} custom-call(f32[24,384]{1,0:T(8,128)S(1)} %bitcast.6, s32[24,384]{1,0:T(8,128)S(1)} %bitcast.7, f32[16,24]{1,0:T(8,128)S(1)} %bitcast.8), custom_call_target="tpu_custom_call" | custom-call | tf_op jit(solution)/shard_map/pack_rows/pallas_call | solution.py:93
  10.1 0.0 all-gather.2.cloned.1.call-update
  10.2 41.9 %all-gather.2.cloned.1.call-done.data_ref = f32[384,896]{1,0:T(8,128)} async-done(((f32[24,896]{1,0:T(8,128)}), f32[384,896]{1,0:T(8,128)}) %all-gather.2.cloned.1.call-update) | async-done | bytes 1376272 | tf_op jit(solution)/shard_map/all_gather | solution.py:101
  52.1 0.0 copy-start
  52.1 1.3 %copy-done = f32[384,896]{1,0:T(8,128)S(1)} copy-done((f32[384,896]{1,0:T(8,128)S(1)}, f32[384,896]{1,0:T(8,128)}, u32[]{:S(2)}) %copy-start) | copy-done | bytes 1376280
  53.4 2.8 %group_smacof.1 = (f32[16,24]{1,0:T(8,128)}, f32[3]{0:T(128)}) custom-call(f32[384,896]{1,0:T(8,128)S(1)} %copy-done), custom_call_target="tpu_custom_call" | custom-call | flops 169869312 | bytes 1179648 | tf_op jit(solution)/shard_map/group_smacof/pallas_call | solution.py:102
Async XLA Ops:
  7.2 44.9 %all-gather.2.cloned.1.call-start = ((), (), s32[]{:S(2)}) async-start(), calls=%async_computation | async-start | bytes 1462272 | tf_op jit(solution)/shard_map/all_gather | solution.py:101
  7.2 0.8 %copy-start.1 = (f32[1,24,384]{2,1,0:T(8,128)S(1)}, f32[1,24,384]{2,1,0:T(8,128)}, u32[]{:S(2)}) copy-start(f32[1,24,384]{2,1,0:T(8,128)} %param.3) | copy-start | bytes 110596
  8.0 0.8 %copy-start.2 = (s32[1,24,384]{2,1,0:T(8,128)S(1)}, s32[1,24,384]{2,1,0:T(8,128)}, u32[]{:S(2)}) copy-start(s32[1,24,384]{2,1,0:T(8,128)} %param.4) | copy-start | bytes 110596
  8.7 0.7 %copy-start.3 = (f32[16,1,24]{2,1,0:T(1,128)S(1)}, f32[16,1,24]{2,1,0:T(1,128)}, u32[]{:S(2)}) copy-start(f32[16,1,24]{2,1,0:T(1,128)} %param.5) | copy-start | bytes 4612
  52.1 1.3 %copy-start = (f32[384,896]{1,0:T(8,128)S(1)}, f32[384,896]{1,0:T(8,128)}, u32[]{:S(2)}) copy-start(f32[384,896]{1,0:T(8,128)} %all-gather.2.cloned.1.call-done.data_ref) | copy-start | bytes 4128772
Sparse Core Ops, SparseCore 0:
  10.3 41.7 all-gather.1

commit v3 on v2

--- a/solution.py
+++ b/solution.py
@@ -29,19 +29,31 @@
     return parts
 
 
-def pack_kernel(dis_ref, cls_ref, x_ref, out_ref):
-    columns = dis_ref.shape[1]
+def pack_kernel(dis_hbm, cls_hbm, x_hbm, out_ref, cls_ref, x_ref, sems):
+    columns = cls_ref.shape[1]
+    copies = [
+        pltpu.make_async_copy(dis_hbm, out_ref.at[:, :columns], sems.at[0]),
+        pltpu.make_async_copy(cls_hbm, cls_ref, sems.at[1]),
+        pltpu.make_async_copy(x_hbm, x_ref, sems.at[2]),
+    ]
+    for copy in copies:
+        copy.start()
+    for copy in copies:
+        copy.wait()
+    out_ref[:, columns : 2 * columns] = class_weight(cls_ref[...])
     coord_dims, per_dev = x_ref.shape
-    out_ref[:, :columns] = dis_ref[...]
-    out_ref[:, columns : 2 * columns] = class_weight(cls_ref[...])
     padded = jnp.concatenate(
         [x_ref[...], jnp.zeros((LANES - coord_dims, per_dev), jnp.float32)], axis=0
     )
     out_ref[:, 2 * columns :] = padded.T
 
 
-def group_kernel(per_dev, coord_dims, data_ref, out_ref, stress_ref, wd_ref):
+def group_kernel(per_dev, coord_dims, offsets, slots_ref, out_ref, stress_ref, data_ref, wd_ref):
     points = data_ref.shape[0]
+    me = lax.axis_index("wide")
+    for slot, offset in enumerate(offsets):
+        rows = pl.ds(pl.multiple_of((me ^ offset) * per_dev, 8), per_dev)
+        data_ref[rows, :] = slots_ref[slot * per_dev : (slot + 1) * per_dev, :]
     dis = data_ref[:, :points]
     weight = data_ref[:, points : 2 * points]
     weighted = weight * dis
@@ -76,7 +88,7 @@
         sums = (dot(pull_hi, sides, nt) + dot(pull_lo, sides, nt)).T
         pull = sums[:coord_dims] + sums[coord_dims : 2 * coord_dims]
         x = x + (pull - x * sums[2 * coord_dims : 2 * coord_dims + 1]) * scale
-    mine = lax.axis_index("wide") * per_dev
+    mine = me * per_dev
     shape = (points, per_dev)
     pick = lax.broadcasted_iota(jnp.int32, shape, 0) == mine + lax.broadcasted_iota(
         jnp.int32, shape, 1
@@ -85,29 +97,49 @@
     out_ref[...] = sum(dot(p, pick, (((1,), (0,)), ((), ()))) for p in split_bf16(x, 3))
 
 
+def exchange(block, devices):
+    held, offsets = block, [0]
+    distance = devices // 2
+    while distance:
+        other = lax.ppermute(held, "wide", [(i, i ^ distance) for i in range(devices)])
+        held = jnp.concatenate([held, other], axis=0)
+        offsets += [offset ^ distance for offset in offsets]
+        distance //= 2
+    return held, offsets
+
+
 def replicated_body(dissim, classes, coords):
     coord_dims, _, per_dev = coords.shape
     points = dissim.shape[2]
     vmem = pl.BlockSpec(memory_space=pltpu.VMEM)
+    hbm = pl.BlockSpec(memory_space=pl.ANY)
     params = pltpu.CompilerParams(vmem_limit_bytes=32 << 20)
     packed = pl.pallas_call(
         pack_kernel,
         out_shape=jax.ShapeDtypeStruct((per_dev, 2 * points + LANES), jnp.float32),
-        in_specs=[vmem, vmem, vmem],
+        in_specs=[hbm, hbm, hbm],
         out_specs=vmem,
+        scratch_shapes=[
+            pltpu.VMEM((per_dev, points), jnp.int32),
+            pltpu.VMEM((coord_dims, per_dev), jnp.float32),
+            pltpu.SemaphoreType.DMA((3,)),
+        ],
         compiler_params=params,
         name="pack_rows",
     )(dissim[0], classes[0], coords[:, 0, :])
-    data = lax.all_gather(packed, "wide", axis=0, tiled=True)
+    data, offsets = exchange(packed, points // per_dev)
     final, stress = pl.pallas_call(
-        functools.partial(group_kernel, per_dev, coord_dims),
+        functools.partial(group_kernel, per_dev, coord_dims, offsets),
         out_shape=(
             jax.ShapeDtypeStruct((coord_dims, per_dev), jnp.float32),
             jax.ShapeDtypeStruct((ITERS,), jnp.float32),
         ),
         in_specs=[vmem],
         out_specs=(vmem, pl.BlockSpec(memory_space=pltpu.SMEM)),
-        scratch_shapes=[pltpu.VMEM((points, points), jnp.float32)],
+        scratch_shapes=[
+            pltpu.VMEM((points, 2 * points + LANES), jnp.float32),
+            pltpu.VMEM((points, points), jnp.float32),
+        ],
         compiler_params=params,
         cost_estimate=pl.CostEstimate(
             flops=ITERS * 24 * points * points * coord_dims,
@@ -186,7 +218,9 @@
 def solution(mesh):
     def body(dissim, classes, coords):
         group_bytes = 8 * dissim.size * mesh.shape["wide"]
-        small = mesh.shape["narrow"] == 1 and group_bytes <= REPLICATED_BYTES
+        devices = mesh.shape["wide"]
+        whole = mesh.shape["narrow"] == 1 and group_bytes <= REPLICATED_BYTES
+        small = whole and devices & (devices - 1) == 0 and dissim.shape[1] % 8 == 0
         return (replicated_body if small else distributed_body)(dissim, classes, coords)
 
     return jax.shard_map(

time: 63.4 us -> 31.3 us (0.49)
  the two profiles are of different devices: /device:TPU:0 before, /device:TPU:21 now
where the time goes in v3:
time: 31.3 us; the launch traced here: 31 us
  waiting for transfers between devices  17.3 us (55%)
  starting transfers between devices  7.54 us (24%)
  Pallas kernels  3.03 us (10%)
  local copies, waits for them, and re-layouts  2.32 us (7%)
  between operations  0.68 us (2%)
    ppermute x4, waiting for transfers between devices, exchange(): lax.ppermute(held, 'wide', [(i, i ^ distance) for i in range(devices)])  17.3 us
    ppermute x4, starting transfers between devices, exchange(): lax.ppermute(held, 'wide', [(i, i ^ distance) for i in range(devices)])  7.54 us
    pallas_call x1, Pallas kernels, replicated_body(): pl.pallas_call(functools.partial(group_kernel, per_dev, coord_dims, offse...  2.88 us
    unnamed x10, local copies, waits for them, and re-layouts  2.28 us
  transfers between devices with their start and end apart: 4, of which 4 were waited for; matrix products, arithmetic and copies ran while one was open for 0% of the time, Pallas kernels for 0%

profile of v3, /device:TPU:21, one launch (start us, length us, event | category | flops | bytes accessed | tf_op | source)
XLA Modules:
  0.0 31.0 jit_solution(8642832071414790430)
XLA Ops:
  0.6 0.0 copy-start
  0.6 0.8 %copy-done = f32[1,24,384]{2,1,0:T(8,128)S(1)} copy-done((f32[1,24,384]{2,1,0:T(8,128)S(1)}, f32[1,24,384]{2,1,0:T(8,128)}, u32[]{:S(2)}) %copy-start) | copy-done | bytes 36888
  1.4 0.0 copy-start.1
  1.4 0.8 %copy-done.1 = s32[1,24,384]{2,1,0:T(8,128)S(1)} copy-done((s32[1,24,384]{2,1,0:T(8,128)S(1)}, s32[1,24,384]{2,1,0:T(8,128)}, u32[]{:S(2)}) %copy-start.1) | copy-done | bytes 36888
  2.2 0.0 copy-start.2
  2.2 0.7 %copy-done.2 = f32[16,1,24]{2,1,0:T(1,128)S(1)} copy-done((f32[16,1,24]{2,1,0:T(1,128)S(1)}, f32[16,1,24]{2,1,0:T(1,128)}, u32[]{:S(2)}) %copy-start.2) | copy-done | bytes 1560
  2.9 0.2 pack_rows.1
  3.0 0.1 collective-permute-start
  3.1 4.3 %collective-permute-done = f32[24,896]{1,0:T(8,128)S(1)} collective-permute-done((f32[24,896]{1,0:T(8,128)S(1)}, f32[24,896]{1,0:T(8,128)S(1)}, u32[]{:S(2)}, u32[]{:S(2)}) %collective-permute-start) | collective-permute-done | bytes 86048 | tf_op jit(solution)/shard_map/ppermute | solution.py:104
  7.4 4.0 %collective-permute-start.1 = (f32[48,896]{1,0:T(8,128)S(1)}, f32[48,896]{1,0:T(8,128)S(1)}, u32[]{:S(2)}, u32[]{:S(2)}) collective-permute-start(f32[48,896]{1,0:T(8,128)S(1)} %pad_maximum_fusion.2), channel_id=1, source_target_pairs={{0,4},{1,5},{2,6},{3,7},{4,0},{5,1},{6,2},{7,3},{8,12},{9,13},{10,... | collective-permute-start | bytes 516104 | tf_op jit(solution)/shard_map/ppermute | solution.py:104
  11.4 4.2 %collective-permute-done.1 = f32[48,896]{1,0:T(8,128)S(1)} collective-permute-done((f32[48,896]{1,0:T(8,128)S(1)}, f32[48,896]{1,0:T(8,128)S(1)}, u32[]{:S(2)}, u32[]{:S(2)}) %collective-permute-start.1) | collective-permute-done | bytes 172064 | tf_op jit(solution)/shard_map/ppermute | solution.py:104
  15.6 1.3 %collective-permute-start.2 = (f32[96,896]{1,0:T(8,128)S(1)}, f32[96,896]{1,0:T(8,128)S(1)}, u32[]{:S(2)}, u32[]{:S(2)}) collective-permute-start(f32[96,896]{1,0:T(8,128)S(1)} %pad_maximum_fusion.1), channel_id=1, source_target_pairs={{0,2},{1,3},{2,0},{3,1},{4,6},{5,7},{6,4},{7,5},{8,10},{9,11},{10,... | collective-permute-start | bytes 1032200 | tf_op jit(solution)/shard_map/ppermute | solution.py:104
  16.9 7.2 %collective-permute-done.2 = f32[96,896]{1,0:T(8,128)S(1)} collective-permute-done((f32[96,896]{1,0:T(8,128)S(1)}, f32[96,896]{1,0:T(8,128)S(1)}, u32[]{:S(2)}, u32[]{:S(2)}) %collective-permute-start.2) | collective-permute-done | bytes 344096 | tf_op jit(solution)/shard_map/ppermute | solution.py:104
  24.1 0.1 pad_maximum_fusion
  24.2 2.1 %collective-permute-start.3 = (f32[192,896]{1,0:T(8,128)S(1)}, f32[192,896]{1,0:T(8,128)S(1)}, u32[]{:S(2)}, u32[]{:S(2)}) collective-permute-start(f32[192,896]{1,0:T(8,128)S(1)} %pad_maximum_fusion), channel_id=1, source_target_pairs={{0,1},{1,0},{2,3},{3,2},{4,5},{5,4},{6,7},{7,6},{8,9},{9,8},{10,11... | collective-permute-start | bytes 2064392 | tf_op jit(solution)/shard_map/ppermute | solution.py:104
  26.4 1.7 %collective-permute-done.3 = f32[192,896]{1,0:T(8,128)S(1)} collective-permute-done((f32[192,896]{1,0:T(8,128)S(1)}, f32[192,896]{1,0:T(8,128)S(1)}, u32[]{:S(2)}, u32[]{:S(2)}) %collective-permute-start.3) | collective-permute-done | bytes 688160 | tf_op jit(solution)/shard_map/ppermute | solution.py:104
  28.1 2.9 %group_smacof.1 = (f32[16,24]{1,0:T(8,128)}, f32[3]{0:T(128)}) custom-call(f32[384,896]{1,0:T(8,128)S(1)} %constant_dynamic-update-slice_fusion.slots_ref), custom_call_target="tpu_custom_call" | custom-call | flops 169869312 | bytes 1179648 | tf_op jit(solution)/shard_map/group_smacof/pallas_call | solution.py:131
  (7 shorter events, 0.1 us)
Async XLA Ops:
  0.6 0.8 %copy-start = (f32[1,24,384]{2,1,0:T(8,128)S(1)}, f32[1,24,384]{2,1,0:T(8,128)}, u32[]{:S(2)}) copy-start(f32[1,24,384]{2,1,0:T(8,128)} %param.3) | copy-start | bytes 110596
  1.4 0.8 %copy-start.1 = (s32[1,24,384]{2,1,0:T(8,128)S(1)}, s32[1,24,384]{2,1,0:T(8,128)}, u32[]{:S(2)}) copy-start(s32[1,24,384]{2,1,0:T(8,128)} %param.4) | copy-start | bytes 110596
  2.2 0.7 %copy-start.2 = (f32[16,1,24]{2,1,0:T(1,128)S(1)}, f32[16,1,24]{2,1,0:T(1,128)}, u32[]{:S(2)}) copy-start(f32[16,1,24]{2,1,0:T(1,128)} %param.5) | copy-start | bytes 4612
  3.0 4.4 %collective-permute-start = (f32[24,896]{1,0:T(8,128)S(1)}, f32[24,896]{1,0:T(8,128)S(1)}, u32[]{:S(2)}, u32[]{:S(2)}) collective-permute-start(f32[24,896]{1,0:T(8,128)S(1)} %pack_rows.1), channel_id=1, source_target_pairs={{0,8},{1,9},{2,10},{3,11},{4,12},{5,13},{6,14},{7,15},{8,0},{9,1},... | collective-permute-start | bytes 258056 | tf_op jit(solution)/shard_map/ppermute | solution.py:104
  7.4 8.2 %collective-permute-start.1 = (f32[48,896]{1,0:T(8,128)S(1)}, f32[48,896]{1,0:T(8,128)S(1)}, u32[]{:S(2)}, u32[]{:S(2)}) collective-permute-start(f32[48,896]{1,0:T(8,128)S(1)} %pad_maximum_fusion.2), channel_id=1, source_target_pairs={{0,4},{1,5},{2,6},{3,7},{4,0},{5,1},{6,2},{7,3},{8,12},{9,13},{10,... | collective-permute-start | bytes 516104 | tf_op jit(solution)/shard_map/ppermute | solution.py:104
  15.6 8.5 %collective-permute-start.2 = (f32[96,896]{1,0:T(8,128)S(1)}, f32[96,896]{1,0:T(8,128)S(1)}, u32[]{:S(2)}, u32[]{:S(2)}) collective-permute-start(f32[96,896]{1,0:T(8,128)S(1)} %pad_maximum_fusion.1), channel_id=1, source_target_pairs={{0,2},{1,3},{2,0},{3,1},{4,6},{5,7},{6,4},{7,5},{8,10},{9,11},{10,... | collective-permute-start | bytes 1032200 | tf_op jit(solution)/shard_map/ppermute | solution.py:104
  24.2 3.9 %collective-permute-start.3 = (f32[192,896]{1,0:T(8,128)S(1)}, f32[192,896]{1,0:T(8,128)S(1)}, u32[]{:S(2)}, u32[]{:S(2)}) collective-permute-start(f32[192,896]{1,0:T(8,128)S(1)} %pad_maximum_fusion), channel_id=1, source_target_pairs={{0,1},{1,0},{2,3},{3,2},{4,5},{5,4},{6,7},{7,6},{8,9},{9,8},{10,11... | collective-permute-start | bytes 2064392 | tf_op jit(solution)/shard_map/ppermute | solution.py:104

commit v4 on v0

--- a/solution.py
+++ b/solution.py
@@ -1,9 +1,14 @@
+import functools
+
 import jax
 import jax.numpy as jnp
 from jax import lax
+from jax.experimental import pallas as pl
+from jax.experimental.pallas import tpu as pltpu
 from jax.sharding import PartitionSpec as P
 
 ITERS = 3
+LANES = 128
 
 
 def class_weight(class_codes):
@@ -14,7 +19,166 @@
     ).astype(jnp.float32)
 
 
-def body(dissim, classes, coords):
+def split_bf16(value, terms):
+    parts = []
+    for _ in range(terms):
+        part = value.astype(jnp.bfloat16)
+        parts.append(part)
+        value = value - part.astype(jnp.float32)
+    return parts
+
+
+def as_tile(x):
+    half = x.shape[0] // 2
+    pad = jnp.zeros((half, LANES - 2 * x.shape[1]), jnp.float32)
+    return jnp.concatenate([x[:half], x[half:], pad], axis=1)
+
+
+def from_tiles(tiles_ref, per_dev):
+    tiles = [tiles_ref[i] for i in range(tiles_ref.shape[0])]
+    top = jnp.concatenate([t[:, :per_dev] for t in tiles], axis=1)
+    bottom = jnp.concatenate([t[:, per_dev : 2 * per_dev] for t in tiles], axis=1)
+    return jnp.concatenate([top, bottom], axis=0)
+
+
+def lane_sums(value):
+    rows = jnp.sum(value, axis=0, keepdims=True)
+    return sum(rows[:, i : i + LANES] for i in range(0, rows.shape[1], LANES))
+
+
+def start_kernel(x_ref, tiles_ref):
+    tiles_ref[...] = jnp.broadcast_to(as_tile(x_ref[...])[None], tiles_ref.shape)
+
+
+def sweep_kernel(last, dis_ref, cls_ref, x_ref, tiles_ref, sums_ref, out_ref, send_ref):
+    coord_dims, per_dev = x_ref.shape
+    points = dis_ref.shape[1]
+    nt = (((1,), (1,)), ((), ()))
+    tn = (((0,), (0,)), ((), ()))
+    dot = functools.partial(lax.dot_general, preferred_element_type=jnp.float32)
+    dis = dis_ref[...]
+    weight = class_weight(cls_ref[...])
+    weighted = weight * dis
+    own = x_ref[...]
+    x = from_tiles(tiles_ref, per_dev)
+    ones = jnp.ones((coord_dims, points), jnp.bfloat16)
+    own_hi, own_mid, own_lo = (-2.0 * p for p in split_bf16(own, 3))
+    hi, mid, lo = split_bf16(x, 3)
+    norm = jnp.sum(x * x, axis=0, keepdims=True)
+    own_norm = jnp.sum(own * own, axis=0, keepdims=True)
+    row_norm = [p.astype(jnp.float32) for p in split_bf16(own_norm, 3)]
+    col_norm = [p.astype(jnp.float32) for p in split_bf16(norm + 1.0, 3)]
+    left_norm = jnp.concatenate(
+        [
+            *row_norm,
+            jnp.ones((3, per_dev), jnp.float32),
+            jnp.zeros((coord_dims - 6, per_dev), jnp.float32),
+        ],
+        axis=0,
+    ).astype(jnp.bfloat16)
+    right_norm = jnp.concatenate(
+        [
+            jnp.ones((3, points), jnp.float32),
+            *col_norm,
+            jnp.zeros((coord_dims - 6, points), jnp.float32),
+        ],
+        axis=0,
+    ).astype(jnp.bfloat16)
+    left = jnp.concatenate(
+        [own_hi, own_hi, own_hi, own_mid, own_mid, own_lo, left_norm], axis=0
+    )
+    right = jnp.concatenate([hi, mid, lo, hi, mid, hi, right_norm], axis=0)
+    square = dot(left, right, tn)
+    inverse = lax.rsqrt(square)
+    misfit = dis - square * inverse
+    pulls = jnp.concatenate(
+        [*split_bf16(weight - weighted * inverse, 2), weight.astype(jnp.bfloat16)], axis=0
+    )
+    sides = jnp.concatenate([hi, mid, ones], axis=0)
+    sums = dot(pulls, sides, nt).T
+    weight_sum = sums[2 * coord_dims : 2 * coord_dims + 1, 2 * per_dev :]
+    sums = sums[:, :per_dev] + sums[:, per_dev : 2 * per_dev]
+    pull = sums[:coord_dims] + sums[coord_dims : 2 * coord_dims]
+    own = own + (pull - own * sums[2 * coord_dims : 2 * coord_dims + 1]) / (1.0 + weight_sum)
+    out_ref[...] = own
+    stress = lane_sums(weight * misfit * misfit)
+    if last:
+        rows = [sums_ref[0:1], sums_ref[1:2], stress, lane_sums(weighted * dis)]
+        pad = jnp.zeros((4, LANES), jnp.float32)
+        send = jnp.concatenate([*rows, pad], axis=0)
+    else:
+        send = as_tile(own)
+    send_ref[...] = jnp.broadcast_to(send[None], send_ref.shape)
+    return stress
+
+
+def early_kernel(dis_ref, cls_ref, x_ref, tiles_ref, stress_ref, out_ref, send_ref):
+    stress_ref[...] = sweep_kernel(
+        False, dis_ref, cls_ref, x_ref, tiles_ref, None, out_ref, send_ref
+    )
+
+
+def late_kernel(dis_ref, cls_ref, x_ref, tiles_ref, first_ref, second_ref, out_ref, send_ref):
+    sums = jnp.concatenate([first_ref[...], second_ref[...]], axis=0)
+    sweep_kernel(True, dis_ref, cls_ref, x_ref, tiles_ref, sums, out_ref, send_ref)
+
+
+def stress_kernel(tiles_ref, stress_ref):
+    total = tiles_ref[0]
+    for i in range(1, tiles_ref.shape[0]):
+        total = total + tiles_ref[i]
+    total = jnp.sum(total, axis=1, keepdims=True)
+    for sweep in range(ITERS):
+        stress_ref[sweep] = jnp.sum(total[sweep : sweep + 1] / total[ITERS : ITERS + 1])
+
+
+def small_body(dissim, classes, coords):
+    coord_dims, _, per_dev = coords.shape
+    points = dissim.shape[2]
+    devices = points // per_dev
+    vmem = pl.BlockSpec(memory_space=pltpu.VMEM)
+    call = functools.partial(
+        pl.pallas_call, compiler_params=pltpu.CompilerParams(vmem_limit_bytes=16 << 20)
+    )
+    tiles_shape = jax.ShapeDtypeStruct((devices, coord_dims // 2, LANES), jnp.float32)
+    x_shape = jax.ShapeDtypeStruct((coord_dims, per_dev), jnp.float32)
+    sums_shape = jax.ShapeDtypeStruct((1, LANES), jnp.float32)
+    dis, cls, x = dissim[0], classes[0], coords[:, 0, :]
+    swap = functools.partial(
+        lax.all_to_all, axis_name="wide", split_axis=0, concat_axis=0, tiled=True
+    )
+    tiles = swap(
+        call(start_kernel, out_shape=tiles_shape, in_specs=[vmem], out_specs=vmem, name="start")(x)
+    )
+    stresses = []
+    for sweep in range(ITERS - 1):
+        stress, x, tiles = call(
+            early_kernel,
+            out_shape=(sums_shape, x_shape, tiles_shape),
+            in_specs=[vmem] * 4,
+            out_specs=(vmem,) * 3,
+            name="sweep",
+        )(dis, cls, x, tiles)
+        tiles = swap(tiles)
+        stresses.append(stress)
+    x, tiles = call(
+        late_kernel,
+        out_shape=(x_shape, tiles_shape),
+        in_specs=[vmem] * 6,
+        out_specs=(vmem,) * 2,
+        name="last_sweep",
+    )(dis, cls, x, tiles, *stresses)
+    stress = call(
+        stress_kernel,
+        out_shape=jax.ShapeDtypeStruct((ITERS,), jnp.float32),
+        in_specs=[vmem],
+        out_specs=pl.BlockSpec(memory_space=pltpu.SMEM),
+        name="stress",
+    )(swap(tiles))
+    return (x[:, None, :], stress)
+
+
+def distributed_body(dissim, classes, coords):
     halves = dissim.shape[0]
     per_dev = dissim.shape[1]
     columns = dissim.shape[2]
@@ -79,6 +243,12 @@
 
 
 def solution(mesh):
+    def body(dissim, classes, coords):
+        coord_dims, halves, per_dev = coords.shape
+        small = halves == 1 and mesh.shape["narrow"] == 1 and coord_dims == 16
+        small = small and 2 * per_dev <= LANES and dissim.shape[2] % LANES == 0
+        return (small_body if small else distributed_body)(dissim, classes, coords)
+
     return jax.shard_map(
         body,
         mesh=mesh,

time: 105 us -> 47.3 us (0.45)
  blocking collectives: 91.3 us -> 42.6 us
  matrix products: 5.06 us -> 0 us
  between operations: 4.42 us -> 0.65 us
  Pallas kernels: 0 us -> 3.01 us
  other arithmetic: 2.64 us -> 0 us
    all_gather x3 -> x0, blocking collectives: 60.8 us -> none  [body(): lax.all_gather(row_points, 'wide', axis=2, tiled=True)]
    all_to_all x0 -> x4, blocking collectives: none -> 42.6 us  [the longest x2 19 us: small_body(): tiles = swap(tiles)]
    psum x1 -> x0, blocking collectives: 30.5 us -> none  [body(): lax.psum(jnp.sum(weight * misfit * misfit), ('wide', 'narrow'))]
    dot_general x6 -> x0, matrix products: 5.06 us -> none  [the longest x3 3.07 us: body(): lax.dot_general(row_x, fold_column_x, (((0,), (0,)), ((), ())), precision...]
    pallas_call x0 -> x5, Pallas kernels: none -> 3.01 us  [the longest x2 1.16 us: small_body(): call(early_kernel, out_shape=(sums_shape, x_shape, tiles_shape), in_specs...]
    reduce_sum x5 -> x0, other arithmetic: 2.03 us -> none  [the longest x1 0.9 us: body(): jnp.sum(weight, axis=1).reshape(halves, per_dev)]
where the time goes in v4:
time: 47.3 us; the launch traced here: 47 us
  blocking collectives  42.6 us (90%)
  Pallas kernels  3.01 us (6%)
  local copies, waits for them, and re-layouts  0.7 us (1%)
  between operations  0.65 us (1%)
    all_to_all x2, blocking collectives, small_body(): tiles = swap(tiles)  19 us
    all_to_all x1, blocking collectives, small_body(): swap(call(start_kernel, out_shape=tiles_shape, in_specs=[vmem], out_specs...  14.2 us
    all_to_all x1, blocking collectives, small_body(): swap(tiles)  9.47 us
    pallas_call x2, Pallas kernels, small_body(): call(early_kernel, out_shape=(sums_shape, x_shape, tiles_shape), in_specs...  1.16 us
    pallas_call x1, Pallas kernels, small_body(): call(late_kernel, out_shape=(x_shape, tiles_shape), in_specs=[vmem] * 6,...  1.12 us

profile of v4, /device:TPU:0, one launch (start us, length us, event | category | flops | bytes accessed | tf_op | source)
XLA Modules:
  0.0 47.0 jit_solution(15399682282927345833)
XLA Ops:
  0.6 0.0 copy-start.2
  0.6 0.7 %copy-done.2 = f32[16,1,24]{2,1,0:T(1,128)S(1)} copy-done((f32[16,1,24]{2,1,0:T(1,128)S(1)}, f32[16,1,24]{2,1,0:T(1,128)}, u32[]{:S(2)}) %copy-start.2) | copy-done | bytes 1560
  1.3 0.1 start.1
  1.4 0.0 copy-start
  1.4 0.0 copy-start.1
  1.4 14.2 %all_to_all.20.tiles_ref = f32[16,8,128]{2,1,0:T(8,128)S(1)} all-to-all(f32[16,8,128]{2,1,0:T(8,128)S(1)} %start.1), channel_id=1, replica_groups=mesh['grp'=2,'wide'=16,'narrow'=1] {'wide'}, dimensions={0} | all-to-all | bytes 131072 | tf_op jit(solution)/shard_map/all_to_all | solution.py:150
  15.6 0.0 copy-done
  15.6 0.0 copy-done.1
  15.6 0.6 %sweep.2 = (f32[1,128]{1,0:T(1,128)S(1)}, f32[16,24]{1,0:T(8,128)S(1)}, f32[16,8,128]{2,1,0:T(8,128)S(1)}) custom-call(f32[24,384]{1,0:T(8,128)S(1)} %bitcast.6, s32[24,384]{1,0:T(8,128)S(1)} %bitcast.9, f32[16,24]{1,0:T(8,128)S(1)} %bitcast.13, f32[16,8,128]{2,1,0:T(8,128)S(1)} %all_to_all.20.tiles_ref), custom_call_target="tpu_custom_call" | custom-call | tf_op jit(solution)/shard_map/sweep/pallas_call | solution.py:155
  16.2 9.5 %all_to_all.21.tiles_ref = f32[16,8,128]{2,1,0:T(8,128)S(1)} all-to-all(f32[16,8,128]{2,1,0:T(8,128)S(1)} %get-tuple-element.11), channel_id=1, replica_groups=mesh['grp'=2,'wide'=16,'narrow'=1] {'wide'}, dimensions={0} | all-to-all | bytes 131072 | tf_op jit(solution)/shard_map/all_to_all | solution.py:162
  25.7 0.6 %sweep.3 = (f32[1,128]{1,0:T(1,128)S(1)}, f32[16,24]{1,0:T(8,128)S(1)}, f32[16,8,128]{2,1,0:T(8,128)S(1)}) custom-call(f32[24,384]{1,0:T(8,128)S(1)} %bitcast.7, s32[24,384]{1,0:T(8,128)S(1)} %bitcast.10, f32[16,24]{1,0:T(8,128)S(1)} %get-tuple-element.10.x_ref, f32[16,8,128]{2,1,0:T(8,128)S(1)} %all_to_all.21.tiles_ref), custom_call_target="tpu_custom_call" | custom-call | tf_op jit(solution)/shard_map/sweep/pallas_call | solution.py:155
  26.2 9.5 %all_to_all.22.tiles_ref = f32[16,8,128]{2,1,0:T(8,128)S(1)} all-to-all(f32[16,8,128]{2,1,0:T(8,128)S(1)} %get-tuple-element.13), channel_id=1, replica_groups=mesh['grp'=2,'wide'=16,'narrow'=1] {'wide'}, dimensions={0} | all-to-all | bytes 131072 | tf_op jit(solution)/shard_map/all_to_all | solution.py:162
  35.7 1.1 %last_sweep.1 = (f32[16,24]{1,0:T(8,128)}, f32[16,8,128]{2,1,0:T(8,128)S(1)}) custom-call(f32[24,384]{1,0:T(8,128)S(1)} %bitcast.8, s32[24,384]{1,0:T(8,128)S(1)} %bitcast.11, f32[16,24]{1,0:T(8,128)S(1)} %get-tuple-element.12.x_ref, f32[16,8,128]{2,1,0:T(8,128)S(1)} %all_to_all.22.tiles_ref, f32[1,128]{1,0:T(1,128)S(1)} %get-tuple-element.14.first_ref, ...), custom_call_target="tpu_custom_call" | custom-call | tf_op jit(solution)/shard_map/last_sweep/pallas_call | solution.py:164
  36.9 9.5 %all_to_all.23.tiles_ref = f32[16,8,128]{2,1,0:T(8,128)S(1)} all-to-all(f32[16,8,128]{2,1,0:T(8,128)S(1)} %get-tuple-element.17), channel_id=1, replica_groups=mesh['grp'=2,'wide'=16,'narrow'=1] {'wide'}, dimensions={0} | all-to-all | bytes 131072 | tf_op jit(solution)/shard_map/all_to_all | solution.py:177
  46.3 0.7 %stress.1 = f32[3]{0:T(128)} custom-call(f32[16,8,128]{2,1,0:T(8,128)S(1)} %all_to_all.23.tiles_ref), custom_call_target="tpu_custom_call" | custom-call | tf_op jit(solution)/shard_map/stress/pallas_call | solution.py:171
Async XLA Ops:
  0.6 0.7 %copy-start.2 = (f32[16,1,24]{2,1,0:T(1,128)S(1)}, f32[16,1,24]{2,1,0:T(1,128)}, u32[]{:S(2)}) copy-start(f32[16,1,24]{2,1,0:T(1,128)} %param.5) | copy-start | bytes 4612
  1.4 14.2 %copy-start = (f32[1,24,384]{2,1,0:T(8,128)S(1)}, f32[1,24,384]{2,1,0:T(8,128)}, u32[]{:S(2)}) copy-start(f32[1,24,384]{2,1,0:T(8,128)} %param.3) | copy-start | bytes 110596
  1.4 14.2 %copy-start.1 = (s32[1,24,384]{2,1,0:T(8,128)S(1)}, s32[1,24,384]{2,1,0:T(8,128)}, u32[]{:S(2)}) copy-start(s32[1,24,384]{2,1,0:T(8,128)} %param.4) | copy-start | bytes 110596

commit v5 on v0

--- a/solution.py
+++ b/solution.py
@@ -1,9 +1,15 @@
+import functools
+
 import jax
 import jax.numpy as jnp
 from jax import lax
+from jax.experimental import pallas as pl
+from jax.experimental.pallas import tpu as pltpu
 from jax.sharding import PartitionSpec as P
 
 ITERS = 3
+LANES = 128
+MOST_PAIRS = 1 << 19
 
 
 def class_weight(class_codes):
@@ -14,7 +20,291 @@
     ).astype(jnp.float32)
 
 
-def body(dissim, classes, coords):
+def split_bf16(value, terms):
+    parts = []
+    for _ in range(terms):
+        part = value.astype(jnp.bfloat16)
+        parts.append(part)
+        value = value - part.astype(jnp.float32)
+    return parts
+
+
+SUBLANES = 8
+NT = (((1,), (1,)), ((), ()))
+TN = (((0,), (0,)), ((), ()))
+dot = functools.partial(lax.dot_general, preferred_element_type=jnp.float32)
+
+
+def lane_sums(value):
+    rows = jnp.sum(value, axis=0, keepdims=True)
+    return sum(rows[:, i : i + LANES] for i in range(0, rows.shape[1], LANES))
+
+
+def tile_spots(per_dev, points):
+    return [
+        (slice(row, row + SUBLANES), slice(column, column + LANES))
+        for row in range(0, per_dev, SUBLANES)
+        for column in range(0, points, LANES)
+    ]
+
+
+def pack_kernel(dis_hbm, cls_hbm, x_hbm, out_ref, dis_ref, cls_ref, x_ref, sems):
+    copies = [
+        pltpu.make_async_copy(src, dst, sems.at[i])
+        for i, (src, dst) in enumerate(
+            [(dis_hbm, dis_ref), (cls_hbm, cls_ref), (x_hbm, x_ref)]
+        )
+    ]
+    for copy in copies:
+        copy.start()
+    for copy in copies:
+        copy.wait()
+    spots = tile_spots(*dis_ref.shape)
+    for i, spot in enumerate(spots):
+        out_ref[i] = dis_ref[spot]
+        out_ref[len(spots) + i] = class_weight(cls_ref[spot])
+    half, per_dev = x_ref.shape[0] // 2, x_ref.shape[1]
+    pad = jnp.zeros((half, LANES - 2 * per_dev), jnp.float32)
+    out_ref[2 * len(spots)] = jnp.concatenate([x_ref[:half], x_ref[half:], pad], axis=1)
+
+
+def held_slots(offsets, own_ref, other_ref, tiles):
+    me = lax.axis_index("wide")
+    held = 2 * len(offsets)
+    for bit, ref in enumerate((own_ref, other_ref)):
+        for slot, offset in enumerate(offsets):
+            yield ref, slot * tiles, lax.rem(me ^ offset ^ bit, held)
+
+
+def coords_kernel(offsets, per_dev, own_ref, other_ref, x_ref, tile_ref):
+    tiles = own_ref.shape[0] // len(offsets)
+    for ref, base, place in held_slots(offsets, own_ref, other_ref, tiles):
+        tile_ref[place] = ref[base + tiles - 1]
+    blocks = [tile_ref[i] for i in range(tile_ref.shape[0])]
+    halves = [
+        jnp.concatenate([t[:, low : low + per_dev] for t in blocks], axis=1)
+        for low in (0, per_dev)
+    ]
+    x_ref[...] = jnp.concatenate(halves, axis=0)
+
+
+def rows_kernel(offsets, per_dev, own_ref, other_ref, dis_ref, weight_ref, scale_ref, denom_ref):
+    points = dis_ref.shape[1]
+    tiles = own_ref.shape[0] // len(offsets)
+    spots = tile_spots(per_dev, points)
+    for ref, base, place in held_slots(offsets, own_ref, other_ref, tiles):
+        for i, (rows, columns) in enumerate(spots):
+            start = pl.multiple_of(place * per_dev + rows.start, SUBLANES)
+            dis_ref[pl.ds(start, SUBLANES), columns] = ref[base + i]
+            weight_ref[pl.ds(start, SUBLANES), columns] = ref[base + len(spots) + i]
+    weight = weight_ref[...]
+    ones = jnp.ones((16, points), jnp.bfloat16)
+    scale_ref[...] = 1.0 / (1.0 + dot(weight.astype(jnp.bfloat16), ones, NT).T[0:1])
+    denom_ref[...] = lane_sums(weight * dis_ref[...] * dis_ref[...])
+
+
+def both_halves(own, other):
+    first = lax.axis_index("wide") < lax.axis_size("wide") // 2
+    low = jnp.where(first, own, other)
+    high = jnp.where(first, other, own)
+    return jnp.concatenate([low, high], axis=1)
+
+
+def side_norm(top, bottom, coord_dims):
+    pad = jnp.zeros((coord_dims - 6, top[0].shape[1]), jnp.float32)
+    rows = [p.astype(jnp.float32) for p in (*top, *bottom)]
+    return jnp.concatenate([*rows, pad], axis=0).astype(jnp.bfloat16)
+
+
+def squares(own, x):
+    coord_dims = x.shape[0]
+    own_hi, own_mid, own_lo = (-2.0 * p for p in split_bf16(own, 3))
+    hi, mid, lo = split_bf16(x, 3)
+    own_norm = split_bf16(jnp.sum(own * own, axis=0, keepdims=True), 3)
+    norm = split_bf16(jnp.sum(x * x, axis=0, keepdims=True) + 1.0, 3)
+    left_ones = [jnp.ones((3, own.shape[1]), jnp.bfloat16)]
+    right_ones = [jnp.ones((3, x.shape[1]), jnp.bfloat16)]
+    left = [own_hi, own_hi, own_hi, own_mid, own_mid, own_lo]
+    right = [hi, mid, lo, hi, mid, hi]
+    left = jnp.concatenate([*left, side_norm(own_norm, left_ones, coord_dims)], axis=0)
+    right = jnp.concatenate([*right, side_norm(right_ones, norm, coord_dims)], axis=0)
+    return dot(left, right, TN), hi, mid
+
+
+def moved(own, hi, mid, pull, scale):
+    coord_dims, count = own.shape
+    ones = jnp.ones((coord_dims, hi.shape[1]), jnp.bfloat16)
+    sides = jnp.concatenate([hi, mid, ones], axis=0)
+    sums = dot(jnp.concatenate(split_bf16(pull, 2), axis=0), sides, NT)
+    sums = (sums[:count] + sums[count:]).T
+    pulled = sums[:coord_dims] + sums[coord_dims : 2 * coord_dims]
+    return own + (pulled - own * sums[2 * coord_dims : 2 * coord_dims + 1]) * scale
+
+
+def sweep_kernel(dis_ref, weight_ref, scale_ref, own_ref, other_ref, x_ref, distance_ref):
+    own = own_ref[...]
+    square, hi, mid = squares(own, both_halves(own, other_ref[...]))
+    inverse = lax.rsqrt(square)
+    distance_ref[...] = square * inverse
+    weight = weight_ref[...]
+    x_ref[...] = moved(own, hi, mid, weight - weight * dis_ref[...] * inverse, scale_ref[...])
+
+
+def stress_rows(distance, dis_ref, weight_ref):
+    misfit = dis_ref[...] - distance
+    return lane_sums(weight_ref[...] * misfit * misfit)
+
+
+def stress_kernel(dis_ref, weight_ref, distance_ref, sums_ref):
+    sums_ref[...] = stress_rows(distance_ref[...], dis_ref, weight_ref)
+
+
+def last_kernel(dis_ref, weight_ref, own_ref, other_ref, first_ref, second_ref, denom_ref,
+                sums_ref, inverse_ref):
+    own = own_ref[...]
+    square, _, _ = squares(own, both_halves(own, other_ref[...]))
+    inverse = lax.rsqrt(square)
+    inverse_ref[...] = inverse
+    last = stress_rows(square * inverse, dis_ref, weight_ref)
+    pad = jnp.zeros((SUBLANES - 4, LANES), jnp.float32)
+    rows = [first_ref[...], second_ref[...], last, denom_ref[...], pad]
+    sums_ref[...] = jnp.concatenate(rows, axis=0)
+
+
+def final_kernel(per_dev, dis_ref, weight_ref, inverse_ref, scale_ref, own_ref, other_ref, x_ref):
+    own = own_ref[...]
+    blocks = own.shape[1] // per_dev
+    place = lax.rem(lax.axis_index("wide"), blocks)
+    hi, mid = split_bf16(both_halves(own, other_ref[...]), 2)
+    rows = pl.ds(pl.multiple_of(place * per_dev, SUBLANES), per_dev)
+    scaled = jnp.concatenate([own, jnp.broadcast_to(scale_ref[...], (SUBLANES, own.shape[1]))], axis=0)
+    mine = jnp.zeros((scaled.shape[0], per_dev), jnp.float32)
+    for i in range(blocks):
+        mine = jnp.where(place == i, scaled[:, i * per_dev : (i + 1) * per_dev], mine)
+    own, scale = mine[: own.shape[0]], mine[own.shape[0] : own.shape[0] + 1]
+    weight = weight_ref[rows, :]
+    pull = weight - weight * dis_ref[rows, :] * inverse_ref[rows, :]
+    x_ref[...] = moved(own, hi, mid, pull, scale)
+
+
+def total_kernel(own_ref, other_ref, stress_ref):
+    total = jnp.sum(own_ref[...] + other_ref[...], axis=1, keepdims=True)
+    for sweep in range(ITERS):
+        stress_ref[sweep] = jnp.sum(total[sweep : sweep + 1] / total[ITERS : ITERS + 1])
+
+
+def small_body(dissim, classes, coords):
+    coord_dims, _, per_dev = coords.shape
+    points = dissim.shape[2]
+    devices = points // per_dev
+    held = devices // 2
+    rows = held * per_dev
+    offsets = [0, *sorted(range(2, held, 2), key=lambda i: (i & (i - 1) != 0, -i))]
+    vmem = pl.BlockSpec(memory_space=pltpu.VMEM)
+    hbm = pl.BlockSpec(memory_space=pltpu.HBM)
+    f32 = functools.partial(jax.ShapeDtypeStruct, dtype=jnp.float32)
+
+    def call(kernel, name, outs, *args, spec=vmem, grant=16, out_spec=vmem, scratch=()):
+        return pl.pallas_call(
+            kernel,
+            out_shape=outs,
+            in_specs=[spec] * len(args),
+            out_specs=jax.tree.map(lambda _: out_spec, outs),
+            scratch_shapes=scratch,
+            compiler_params=pltpu.CompilerParams(vmem_limit_bytes=grant << 20),
+            cost_estimate=pl.CostEstimate(
+                flops=rows * points, bytes_accessed=4 * rows * points, transcendentals=rows * points
+            ),
+            name=name,
+        )(*args)
+
+    def swap(value, offset):
+        return lax.ppermute(value, "wide", [(i, i ^ offset) for i in range(devices)])
+
+    tiles = 2 * len(tile_spots(per_dev, points)) + 1
+    packed = call(
+        pack_kernel,
+        "pack",
+        f32((tiles, SUBLANES, LANES)),
+        dissim[0],
+        classes[0],
+        coords[:, 0, :],
+        spec=hbm,
+        grant=60,
+        scratch=[
+            pltpu.VMEM((per_dev, points), jnp.float32),
+            pltpu.VMEM((per_dev, points), jnp.int32),
+            pltpu.VMEM((coord_dims, per_dev), jnp.float32),
+            pltpu.SemaphoreType.DMA((3,)),
+        ],
+    )
+    mine = jnp.concatenate([packed, *(swap(packed, offset) for offset in offsets[1:])], axis=0)
+    theirs = swap(mine, 1)
+    own = call(
+        functools.partial(coords_kernel, offsets, per_dev),
+        "half_coords",
+        f32((coord_dims, rows)),
+        mine,
+        theirs,
+        scratch=[pltpu.VMEM((held, SUBLANES, LANES), jnp.float32)],
+    )
+    other = swap(own, held)
+    dis, weight, scale, denom = call(
+        functools.partial(rows_kernel, offsets, per_dev),
+        "half_rows",
+        (f32((rows, points)), f32((rows, points)), f32((1, rows)), f32((1, LANES))),
+        mine,
+        theirs,
+    )
+    sums = []
+    for _ in range(ITERS - 1):
+        own, distance = call(
+            sweep_kernel,
+            "sweep",
+            (f32((coord_dims, rows)), f32((rows, points))),
+            dis,
+            weight,
+            scale,
+            own,
+            other,
+        )
+        other = swap(own, held)
+        sums.append(call(stress_kernel, "stress_sum", f32((1, LANES)), dis, weight, distance))
+    sums, inverse = call(
+        last_kernel,
+        "last_stress",
+        (f32((SUBLANES, LANES)), f32((rows, points))),
+        dis,
+        weight,
+        own,
+        other,
+        *sums,
+        denom,
+    )
+    other_sums = swap(sums, held)
+    final = call(
+        functools.partial(final_kernel, per_dev),
+        "final",
+        f32((coord_dims, per_dev)),
+        dis,
+        weight,
+        inverse,
+        scale,
+        own,
+        other,
+    )
+    stress = call(
+        total_kernel,
+        "total",
+        f32((ITERS,)),
+        sums,
+        other_sums,
+        out_spec=pl.BlockSpec(memory_space=pltpu.SMEM),
+    )
+    return (final[:, None, :], stress)
+
+
+def distributed_body(dissim, classes, coords):
     halves = dissim.shape[0]
     per_dev = dissim.shape[1]
     columns = dissim.shape[2]
@@ -79,6 +369,15 @@
 
 
 def solution(mesh):
+    def body(dissim, classes, coords):
+        coord_dims, halves, per_dev = coords.shape
+        points, devices = dissim.shape[2], mesh.shape["wide"]
+        small = halves == 1 and mesh.shape["narrow"] == 1 and points * points <= MOST_PAIRS
+        small = small and coord_dims == 2 * SUBLANES and 2 * per_dev <= LANES
+        small = small and per_dev % SUBLANES == 0 and points % LANES == 0
+        small = small and devices >= 4 and devices & (devices - 1) == 0
+        return (small_body if small else distributed_body)(dissim, classes, coords)
+
     return jax.shard_map(
         body,
         mesh=mesh,

time: 105 us -> 34.9 us (0.33)
  blocking collectives: 91.3 us -> 0 us
  starting transfers between devices: 0 us -> 15.3 us
  waiting for transfers between devices: 0 us -> 12.4 us
  Pallas kernels: 0 us -> 5.33 us
  matrix products: 5.06 us -> 0 us
  between operations: 4.42 us -> 0.69 us
  other arithmetic: 2.64 us -> 0.91 us
    all_gather x3 -> x0, blocking collectives: 60.8 us -> none  [body(): lax.all_gather(row_points, 'wide', axis=2, tiled=True)]
    psum x1 -> x0, blocking collectives: 30.5 us -> none  [body(): lax.psum(jnp.sum(weight * misfit * misfit), ('wide', 'narrow'))]
    ppermute x0 -> x8, starting transfers between devices: none -> 15.3 us  [swap(): lax.ppermute(value, 'wide', [(i, i ^ offset) for i in range(devices)])]
    ppermute x0 -> x8, waiting for transfers between devices: none -> 12.4 us  [swap(): lax.ppermute(value, 'wide', [(i, i ^ offset) for i in range(devices)])]
    pallas_call x0 -> x10, Pallas kernels: none -> 5.33 us  [call(): pl.pallas_call(kernel, out_shape=outs, in_specs=[spec] * len(args), out_s...]
    dot_general x6 -> x0, matrix products: 5.06 us -> none  [the longest x3 3.07 us: body(): lax.dot_general(row_x, fold_column_x, (((0,), (0,)), ((), ())), precision...]
    reduce_sum x5 -> x0, other arithmetic: 2.03 us -> none  [the longest x1 0.9 us: body(): jnp.sum(weight, axis=1).reshape(halves, per_dev)]
  transfers between devices with their start and end apart: 0 -> 8, of which waited for: 0 -> 8; matrix products, arithmetic and copies ran while one was open for 0% -> 0% of each run, Pallas kernels for 0% -> 5%
where the time goes in v5:
time: 34.9 us; the launch traced here: 34.7 us
  starting transfers between devices  15.3 us (44%)
  waiting for transfers between devices  12.4 us (36%)
  Pallas kernels  5.33 us (15%)
  other arithmetic  0.91 us (3%)
  between operations  0.69 us (2%)
    ppermute x8, starting transfers between devices, swap(): lax.ppermute(value, 'wide', [(i, i ^ offset) for i in range(devices)])  15.3 us
    ppermute x8, waiting for transfers between devices, swap(): lax.ppermute(value, 'wide', [(i, i ^ offset) for i in range(devices)])  12.4 us
    pallas_call x10, Pallas kernels, call(): pl.pallas_call(kernel, out_shape=outs, in_specs=[spec] * len(args), out_s...  5.33 us
    concatenate x1, other arithmetic, small_body(): jnp.concatenate([packed, *(swap(packed, offset) for offset in offsets[1:]...  0.91 us
  transfers between devices with their start and end apart: 8, of which 8 were waited for; matrix products, arithmetic and copies ran while one was open for 0% of the time, Pallas kernels for 5%

profile of v5, /device:TPU:0, one launch (start us, length us, event | category | flops | bytes accessed | tf_op | source)
XLA Modules:
  0.0 34.7 jit_solution(1623651637494981201)
XLA Ops:
  0.6 1.5 %pack.1 = f32[19,8,128]{2,1,0:T(8,128)} custom-call(f32[24,384]{1,0:T(8,128)} %bitcast.6, s32[24,384]{1,0:T(8,128)} %bitcast.7, f32[16,24]{1,0:T(8,128)} %bitcast.9), custom_call_target="tpu_custom_call" | custom-call | flops 73728 | bytes 294912 | tf_op jit(solution)/shard_map/pack/pallas_call | solution.py:208
  2.2 4.0 %collective-permute-start.2 = (f32[19,8,128]{2,1,0:T(8,128)}, f32[19,8,128]{2,1,0:T(8,128)S(1)}, u32[]{:S(2)}, u32[]{:S(2)}) collective-permute-start(f32[19,8,128]{2,1,0:T(8,128)} %pack.1), channel_id=1, source_target_pairs={{0,6},{1,7},{2,4},{3,5},{4,2},{5,3},{6,0},{7,1},{8,14},{9,15},{10,... | collective-permute-start | bytes 233480 | tf_op jit(solution)/shard_map/ppermute | solution.py:222
  6.2 0.5 %collective-permute-start.1 = (f32[19,8,128]{2,1,0:T(8,128)}, f32[19,8,128]{2,1,0:T(8,128)S(1)}, u32[]{:S(2)}, u32[]{:S(2)}) collective-permute-start(f32[19,8,128]{2,1,0:T(8,128)} %pack.1), channel_id=1, source_target_pairs={{0,2},{1,3},{2,0},{3,1},{4,6},{5,7},{6,4},{7,5},{8,10},{9,11},{10,... | collective-permute-start | bytes 233480 | tf_op jit(solution)/shard_map/ppermute | solution.py:222
  6.7 0.1 collective-permute-start
  6.8 2.1 %collective-permute-done.2 = f32[19,8,128]{2,1,0:T(8,128)S(1)} collective-permute-done((f32[19,8,128]{2,1,0:T(8,128)}, f32[19,8,128]{2,1,0:T(8,128)S(1)}, u32[]{:S(2)}, u32[]{:S(2)}) %collective-permute-start.2) | collective-permute-done | bytes 77856 | tf_op jit(solution)/shard_map/ppermute | solution.py:222
  8.9 1.8 %collective-permute-done.1 = f32[19,8,128]{2,1,0:T(8,128)S(1)} collective-permute-done((f32[19,8,128]{2,1,0:T(8,128)}, f32[19,8,128]{2,1,0:T(8,128)S(1)}, u32[]{:S(2)}, u32[]{:S(2)}) %collective-permute-start.1) | collective-permute-done | bytes 77856 | tf_op jit(solution)/shard_map/ppermute | solution.py:222
  10.8 0.5 %collective-permute-done = f32[19,8,128]{2,1,0:T(8,128)S(1)} collective-permute-done((f32[19,8,128]{2,1,0:T(8,128)}, f32[19,8,128]{2,1,0:T(8,128)S(1)}, u32[]{:S(2)}, u32[]{:S(2)}) %collective-permute-start) | collective-permute-done | bytes 77856 | tf_op jit(solution)/shard_map/ppermute | solution.py:222
  11.3 0.9 %pad_maximum_fusion.own_ref = f32[76,8,128]{2,1,0:T(8,128)S(1)} fusion(f32[19,8,128]{2,1,0:T(8,128)S(1)} %collective-permute-done.2, f32[19,8,128]{2,1,0:T(8,128)S(1)} %collective-permute-done.1, f32[19,8,128]{2,1,0:T(8,128)S(1)} %collective-permute-done, f32[19,8,128]{2,1,0:T(8,128)} %pack.1), kind=kLoop, calls=%fused_computation | loop fusion | flops 233472 | bytes 622592 | tf_op jit(solution)/shard_map/concatenate | solution.py:241
  12.3 1.6 %collective-permute-done.3.other_ref = f32[76,8,128]{2,1,0:T(8,128)S(1)} collective-permute-done((f32[76,8,128]{2,1,0:T(8,128)S(1)}, f32[76,8,128]{2,1,0:T(8,128)S(1)}, u32[]{:S(2)}, u32[]{:S(2)}) %collective-permute-start.3) | collective-permute-done | bytes 311328 | tf_op jit(solution)/shard_map/ppermute | solution.py:222
  14.0 2.7 %collective-permute-start.4 = (f32[16,192]{1,0:T(8,128)S(1)}, f32[16,192]{1,0:T(8,128)S(1)}, u32[]{:S(2)}, u32[]{:S(2)}) collective-permute-start(f32[16,192]{1,0:T(8,128)S(1)} %half_coords.1.own_ref), channel_id=1, source_target_pairs={{0,8},{1,9},{2,10},{3,11},{4,12},{5,13},{6,14},{7,15},{8,0},{9,1},... | collective-permute-start | bytes 36872 | tf_op jit(solution)/shard_map/ppermute | solution.py:222
  16.6 0.3 half_rows.1
  16.9 1.8 %collective-permute-done.4.other_ref = f32[16,192]{1,0:T(8,128)S(1)} collective-permute-done((f32[16,192]{1,0:T(8,128)S(1)}, f32[16,192]{1,0:T(8,128)S(1)}, u32[]{:S(2)}, u32[]{:S(2)}) %collective-permute-start.4) | collective-permute-done | bytes 12320 | tf_op jit(solution)/shard_map/ppermute | solution.py:222
  18.7 0.5 %sweep.2 = (f32[16,192]{1,0:T(8,128)S(1)}, f32[192,384]{1,0:T(8,128)S(1)}) custom-call(f32[192,384]{1,0:T(8,128)S(1)} %get-tuple-element.12.dis_ref, f32[192,384]{1,0:T(8,128)S(1)} %get-tuple-element.13.weight_ref, f32[1,192]{1,0:T(1,128)S(1)} %get-tuple-element.14.scale_ref, f32[16,192]{1,0:T(8,128)S(1)} %half_coords.1.own_ref, ...), custom_call_target="tpu_custom_call" | custom-call | flops 73728 | bytes 294912 | tf_op jit(solution)/shard_map/sweep/pallas_call | solution.py:208
  19.2 2.7 %collective-permute-start.5 = (f32[16,192]{1,0:T(8,128)S(1)}, f32[16,192]{1,0:T(8,128)S(1)}, u32[]{:S(2)}, u32[]{:S(2)}) collective-permute-start(f32[16,192]{1,0:T(8,128)S(1)} %get-tuple-element.15.own_ref), channel_id=1, source_target_pairs={{0,8},{1,9},{2,10},{3,11},{4,12},{5,13},{6,14},{7,15},{8,0},{9,1},... | collective-permute-start | bytes 36872 | tf_op jit(solution)/shard_map/ppermute | solution.py:222
  21.9 2.0 %collective-permute-done.5.other_ref = f32[16,192]{1,0:T(8,128)S(1)} collective-permute-done((f32[16,192]{1,0:T(8,128)S(1)}, f32[16,192]{1,0:T(8,128)S(1)}, u32[]{:S(2)}, u32[]{:S(2)}) %collective-permute-start.5) | collective-permute-done | bytes 12320 | tf_op jit(solution)/shard_map/ppermute | solution.py:222
  23.9 0.5 %sweep.3 = (f32[16,192]{1,0:T(8,128)S(1)}, f32[192,384]{1,0:T(8,128)S(1)}) custom-call(f32[192,384]{1,0:T(8,128)S(1)} %get-tuple-element.12.dis_ref, f32[192,384]{1,0:T(8,128)S(1)} %get-tuple-element.13.weight_ref, f32[1,192]{1,0:T(1,128)S(1)} %get-tuple-element.14.scale_ref, f32[16,192]{1,0:T(8,128)S(1)} %get-tuple-element.15.own_ref, ...), custom_call_target="tpu_custom_call" | custom-call | flops 73728 | bytes 294912 | tf_op jit(solution)/shard_map/sweep/pallas_call | solution.py:208
  24.4 2.6 %collective-permute-start.6 = (f32[16,192]{1,0:T(8,128)S(1)}, f32[16,192]{1,0:T(8,128)S(1)}, u32[]{:S(2)}, u32[]{:S(2)}) collective-permute-start(f32[16,192]{1,0:T(8,128)S(1)} %get-tuple-element.16.own_ref), channel_id=1, source_target_pairs={{0,8},{1,9},{2,10},{3,11},{4,12},{5,13},{6,14},{7,15},{8,0},{9,1},... | collective-permute-start | bytes 36872 | tf_op jit(solution)/shard_map/ppermute | solution.py:222
  27.2 0.1 stress_sum.3.second_ref
  27.3 1.9 %collective-permute-done.6.other_ref = f32[16,192]{1,0:T(8,128)S(1)} collective-permute-done((f32[16,192]{1,0:T(8,128)S(1)}, f32[16,192]{1,0:T(8,128)S(1)}, u32[]{:S(2)}, u32[]{:S(2)}) %collective-permute-start.6) | collective-permute-done | bytes 12320 | tf_op jit(solution)/shard_map/ppermute | solution.py:222
  29.1 0.3 last_stress.1
  29.4 2.7 %collective-permute-start.7 = (f32[8,128]{1,0:T(8,128)S(1)}, f32[8,128]{1,0:T(8,128)S(1)}, u32[]{:S(2)}, u32[]{:S(2)}) collective-permute-start(f32[8,128]{1,0:T(8,128)S(1)} %get-tuple-element.21.own_ref), channel_id=1, source_target_pairs={{0,8},{1,9},{2,10},{3,11},{4,12},{5,13},{6,14},{7,15},{8,0},{9,1},... | collective-permute-start | bytes 12296 | tf_op jit(solution)/shard_map/ppermute | solution.py:222
  32.1 1.3 %final.1 = f32[16,24]{1,0:T(8,128)} custom-call(f32[192,384]{1,0:T(8,128)S(1)} %get-tuple-element.12.dis_ref, f32[192,384]{1,0:T(8,128)S(1)} %get-tuple-element.13.weight_ref, f32[192,384]{1,0:T(8,128)S(1)} %get-tuple-element.20.inverse_ref, f32[1,192]{1,0:T(1,128)S(1)} %get-tuple-element.14.scale_ref, f32[16,192]{1,0:T(8,128)S(1)} %get-tuple-element.16.own_ref, ...), custom_call_target="tpu_custom_call" | custom-call | flops 73728 | bytes 294912 | tf_op jit(solution)/shard_map/final/pallas_call | solution.py:208
  33.4 0.6 %collective-permute-done.7.other_ref = f32[8,128]{1,0:T(8,128)S(1)} collective-permute-done((f32[8,128]{1,0:T(8,128)S(1)}, f32[8,128]{1,0:T(8,128)S(1)}, u32[]{:S(2)}, u32[]{:S(2)}) %collective-permute-start.7) | collective-permute-done | bytes 4128 | tf_op jit(solution)/shard_map/ppermute | solution.py:222
  34.0 0.6 %total.1 = f32[3]{0:T(128)} custom-call(f32[8,128]{1,0:T(8,128)S(1)} %get-tuple-element.21.own_ref, f32[8,128]{1,0:T(8,128)S(1)} %collective-permute-done.7.other_ref), custom_call_target="tpu_custom_call" | custom-call | flops 73728 | bytes 294912 | tf_op jit(solution)/shard_map/total/pallas_call | solution.py:208
  (3 shorter events, 0.2 us)
Async XLA Ops:
  2.2 6.8 %collective-permute-start.2 = (f32[19,8,128]{2,1,0:T(8,128)}, f32[19,8,128]{2,1,0:T(8,128)S(1)}, u32[]{:S(2)}, u32[]{:S(2)}) collective-permute-start(f32[19,8,128]{2,1,0:T(8,128)} %pack.1), channel_id=1, source_target_pairs={{0,6},{1,7},{2,4},{3,5},{4,2},{5,3},{6,0},{7,1},{8,14},{9,15},{10,... | collective-permute-start | bytes 233480 | tf_op jit(solution)/shard_map/ppermute | solution.py:222
  6.2 4.6 %collective-permute-start.1 = (f32[19,8,128]{2,1,0:T(8,128)}, f32[19,8,128]{2,1,0:T(8,128)S(1)}, u32[]{:S(2)}, u32[]{:S(2)}) collective-permute-start(f32[19,8,128]{2,1,0:T(8,128)} %pack.1), channel_id=1, source_target_pairs={{0,2},{1,3},{2,0},{3,1},{4,6},{5,7},{6,4},{7,5},{8,10},{9,11},{10,... | collective-permute-start | bytes 233480 | tf_op jit(solution)/shard_map/ppermute | solution.py:222
  6.7 4.6 %collective-permute-start = (f32[19,8,128]{2,1,0:T(8,128)}, f32[19,8,128]{2,1,0:T(8,128)S(1)}, u32[]{:S(2)}, u32[]{:S(2)}) collective-permute-start(f32[19,8,128]{2,1,0:T(8,128)} %pack.1), channel_id=1, source_target_pairs={{0,4},{1,5},{2,6},{3,7},{4,0},{5,1},{6,2},{7,3},{8,12},{9,13},{10,... | collective-permute-start | bytes 233480 | tf_op jit(solution)/shard_map/ppermute | solution.py:222
  12.2 1.7 %collective-permute-start.3 = (f32[76,8,128]{2,1,0:T(8,128)S(1)}, f32[76,8,128]{2,1,0:T(8,128)S(1)}, u32[]{:S(2)}, u32[]{:S(2)}) collective-permute-start(f32[76,8,128]{2,1,0:T(8,128)S(1)} %pad_maximum_fusion.own_ref), channel_id=1, source_target_pairs={{0,1},{1,0},{2,3},{3,2},{4,5},{5,4},{6,7},{7,6},{8,9},{9,8},{10,11... | collective-permute-start | bytes 933896 | tf_op jit(solution)/shard_map/ppermute | solution.py:222
  14.0 4.7 %collective-permute-start.4 = (f32[16,192]{1,0:T(8,128)S(1)}, f32[16,192]{1,0:T(8,128)S(1)}, u32[]{:S(2)}, u32[]{:S(2)}) collective-permute-start(f32[16,192]{1,0:T(8,128)S(1)} %half_coords.1.own_ref), channel_id=1, source_target_pairs={{0,8},{1,9},{2,10},{3,11},{4,12},{5,13},{6,14},{7,15},{8,0},{9,1},... | collective-permute-start | bytes 36872 | tf_op jit(solution)/shard_map/ppermute | solution.py:222
  19.2 4.7 %collective-permute-start.5 = (f32[16,192]{1,0:T(8,128)S(1)}, f32[16,192]{1,0:T(8,128)S(1)}, u32[]{:S(2)}, u32[]{:S(2)}) collective-permute-start(f32[16,192]{1,0:T(8,128)S(1)} %get-tuple-element.15.own_ref), channel_id=1, source_target_pairs={{0,8},{1,9},{2,10},{3,11},{4,12},{5,13},{6,14},{7,15},{8,0},{9,1},... | collective-permute-start | bytes 36872 | tf_op jit(solution)/shard_map/ppermute | solution.py:222
  24.4 4.7 %collective-permute-start.6 = (f32[16,192]{1,0:T(8,128)S(1)}, f32[16,192]{1,0:T(8,128)S(1)}, u32[]{:S(2)}, u32[]{:S(2)}) collective-permute-start(f32[16,192]{1,0:T(8,128)S(1)} %get-tuple-element.16.own_ref), channel_id=1, source_target_pairs={{0,8},{1,9},{2,10},{3,11},{4,12},{5,13},{6,14},{7,15},{8,0},{9,1},... | collective-permute-start | bytes 36872 | tf_op jit(solution)/shard_map/ppermute | solution.py:222
  29.4 4.6 %collective-permute-start.7 = (f32[8,128]{1,0:T(8,128)S(1)}, f32[8,128]{1,0:T(8,128)S(1)}, u32[]{:S(2)}, u32[]{:S(2)}) collective-permute-start(f32[8,128]{1,0:T(8,128)S(1)} %get-tuple-element.21.own_ref), channel_id=1, source_target_pairs={{0,8},{1,9},{2,10},{3,11},{4,12},{5,13},{6,14},{7,15},{8,0},{9,1},... | collective-permute-start | bytes 12296 | tf_op jit(solution)/shard_map/ppermute | solution.py:222

commit v6 on v0

--- a/solution.py
+++ b/solution.py
@@ -1,9 +1,15 @@
+import functools
+
 import jax
 import jax.numpy as jnp
 from jax import lax
+from jax.experimental import pallas as pl
+from jax.experimental.pallas import tpu as pltpu
 from jax.sharding import PartitionSpec as P
 
 ITERS = 3
+LANES = 128
+MOST_PAIRS = 1 << 19
 
 
 def class_weight(class_codes):
@@ -14,7 +20,191 @@
     ).astype(jnp.float32)
 
 
-def body(dissim, classes, coords):
+def split_bf16(value, terms):
+    parts = []
+    for _ in range(terms):
+        part = value.astype(jnp.bfloat16)
+        parts.append(part)
+        value = value - part.astype(jnp.float32)
+    return parts
+
+
+SUBLANES = 8
+NT = (((1,), (1,)), ((), ()))
+TN = (((0,), (0,)), ((), ()))
+dot = functools.partial(lax.dot_general, preferred_element_type=jnp.float32)
+
+
+def lane_sums(value):
+    rows = jnp.sum(value, axis=0, keepdims=True)
+    return sum(rows[:, i : i + LANES] for i in range(0, rows.shape[1], LANES))
+
+
+def tile_spots(per_dev, points):
+    return [
+        (slice(row, row + SUBLANES), slice(column, column + LANES))
+        for row in range(0, per_dev, SUBLANES)
+        for column in range(0, points, LANES)
+    ]
+
+
+def pack_kernel(dis_hbm, cls_hbm, x_hbm, out_ref, dis_ref, cls_ref, x_ref, sems):
+    copies = [
+        pltpu.make_async_copy(src, dst, sems.at[i])
+        for i, (src, dst) in enumerate(
+            [(dis_hbm, dis_ref), (cls_hbm, cls_ref), (x_hbm, x_ref)]
+        )
+    ]
+    for copy in copies:
+        copy.start()
+    for copy in copies:
+        copy.wait()
+    spots = tile_spots(*dis_ref.shape)
+    for i, spot in enumerate(spots):
+        out_ref[i] = dis_ref[spot]
+        out_ref[len(spots) + i] = class_weight(cls_ref[spot])
+    half, per_dev = x_ref.shape[0] // 2, x_ref.shape[1]
+    pad = jnp.zeros((half, LANES - 2 * per_dev), jnp.float32)
+    out_ref[2 * len(spots)] = jnp.concatenate([x_ref[:half], x_ref[half:], pad], axis=1)
+
+
+def held_slots(offsets, refs, tiles):
+    me = lax.axis_index("wide")
+    for bit, ref in enumerate(refs):
+        for slot, offset in enumerate(offsets):
+            yield ref, slot * tiles, me ^ offset ^ bit
+
+
+def side_norm(top, bottom, coord_dims):
+    pad = jnp.zeros((coord_dims - 6, top[0].shape[1]), jnp.float32)
+    rows = [p.astype(jnp.float32) for p in (*top, *bottom)]
+    return jnp.concatenate([*rows, pad], axis=0).astype(jnp.bfloat16)
+
+
+def squares(own, x):
+    coord_dims = x.shape[0]
+    own_hi, own_mid, own_lo = (-2.0 * p for p in split_bf16(own, 3))
+    hi, mid, lo = split_bf16(x, 3)
+    own_norm = split_bf16(jnp.sum(own * own, axis=0, keepdims=True), 3)
+    norm = split_bf16(jnp.sum(x * x, axis=0, keepdims=True) + 1.0, 3)
+    left_ones = [jnp.ones((3, own.shape[1]), jnp.bfloat16)]
+    right_ones = [jnp.ones((3, x.shape[1]), jnp.bfloat16)]
+    left = [own_hi, own_hi, own_hi, own_mid, own_mid, own_lo]
+    right = [hi, mid, lo, hi, mid, hi]
+    left = jnp.concatenate([*left, side_norm(own_norm, left_ones, coord_dims)], axis=0)
+    right = jnp.concatenate([*right, side_norm(right_ones, norm, coord_dims)], axis=0)
+    return dot(left, right, TN), hi, mid
+
+
+def moved(own, hi, mid, pull, scale):
+    coord_dims, count = own.shape
+    ones = jnp.ones((coord_dims, hi.shape[1]), jnp.bfloat16)
+    sides = jnp.concatenate([hi, mid, ones], axis=0)
+    sums = dot(jnp.concatenate(split_bf16(pull, 2), axis=0), sides, NT)
+    sums = (sums[:count] + sums[count:]).T
+    pulled = sums[:coord_dims] + sums[coord_dims : 2 * coord_dims]
+    return own + (pulled - own * sums[2 * coord_dims : 2 * coord_dims + 1]) * scale
+
+
+def group_kernel(offsets, per_dev, mine_ref, theirs_ref, out_ref, stress_ref,
+                 dis_ref, weight_ref, tile_ref, inverse_ref):
+    points = dis_ref.shape[0]
+    spots = tile_spots(per_dev, points)
+    tiles = 2 * len(spots) + 1
+    for ref, base, place in held_slots(offsets, (mine_ref, theirs_ref), tiles):
+        tile_ref[place] = ref[base + tiles - 1]
+        for i, (rows, columns) in enumerate(spots):
+            start = pl.multiple_of(place * per_dev + rows.start, SUBLANES)
+            dis_ref[pl.ds(start, SUBLANES), columns] = ref[base + i]
+            weight_ref[pl.ds(start, SUBLANES), columns] = ref[base + len(spots) + i]
+    blocks = [tile_ref[i] for i in range(tile_ref.shape[0])]
+    halves = [
+        jnp.concatenate([t[:, low : low + per_dev] for t in blocks], axis=1)
+        for low in (0, per_dev)
+    ]
+    x = jnp.concatenate(halves, axis=0)
+    weight = weight_ref[...]
+    ones = jnp.ones((x.shape[0], points), jnp.bfloat16)
+    scale = 1.0 / (1.0 + dot(weight.astype(jnp.bfloat16), ones, NT).T[0:1])
+    sums = [lane_sums(weight * dis_ref[...] * dis_ref[...])]
+    for sweep in range(ITERS):
+        square, hi, mid = squares(x, x)
+        inverse = lax.rsqrt(square)
+        misfit = dis_ref[...] - square * inverse
+        weight = weight_ref[...]
+        sums.append(lane_sums(weight * misfit * misfit))
+        if sweep < ITERS - 1:
+            x = moved(x, hi, mid, weight - weight * dis_ref[...] * inverse, scale)
+    inverse_ref[...] = inverse
+    place = lax.axis_index("wide")
+    rows = pl.ds(pl.multiple_of(place * per_dev, SUBLANES), per_dev)
+    scaled = jnp.concatenate([x, jnp.broadcast_to(scale, (SUBLANES, points))], axis=0)
+    mine = jnp.zeros((scaled.shape[0], per_dev), jnp.float32)
+    for i in range(points // per_dev):
+        mine = jnp.where(place == i, scaled[:, i * per_dev : (i + 1) * per_dev], mine)
+    own, scale = mine[: x.shape[0]], mine[x.shape[0] : x.shape[0] + 1]
+    weight = weight_ref[rows, :]
+    pull = weight - weight * dis_ref[rows, :] * inverse_ref[rows, :]
+    out_ref[...] = moved(own, hi, mid, pull, scale)
+    total = jnp.sum(jnp.concatenate(sums, axis=0), axis=1, keepdims=True)
+    for sweep in range(ITERS):
+        stress_ref[sweep] = jnp.sum(total[sweep + 1 : sweep + 2] / total[0:1])
+
+
+def small_body(dissim, classes, coords):
+    coord_dims, _, per_dev = coords.shape
+    points = dissim.shape[2]
+    devices = points // per_dev
+    vmem = pl.BlockSpec(memory_space=pltpu.VMEM)
+    hbm = pl.BlockSpec(memory_space=pltpu.HBM)
+    f32 = functools.partial(jax.ShapeDtypeStruct, dtype=jnp.float32)
+    params = pltpu.CompilerParams(vmem_limit_bytes=16 << 20)
+
+    def swap(value, offset):
+        return lax.ppermute(value, "wide", [(i, i ^ offset) for i in range(devices)])
+
+    tiles = 2 * len(tile_spots(per_dev, points)) + 1
+    inputs = (dissim[0], classes[0], coords[:, 0, :])
+    packed = pl.pallas_call(
+        pack_kernel,
+        out_shape=f32((tiles, SUBLANES, LANES)),
+        in_specs=[hbm] * 3,
+        out_specs=vmem,
+        scratch_shapes=[
+            pltpu.VMEM((per_dev, points), jnp.float32),
+            pltpu.VMEM((per_dev, points), jnp.int32),
+            pltpu.VMEM((coord_dims, per_dev), jnp.float32),
+            pltpu.SemaphoreType.DMA((3,)),
+        ],
+        compiler_params=params,
+        name="pack",
+    )(*(pltpu.with_memory_space_constraint(array, pltpu.HBM) for array in inputs))
+    top, relay = devices // 2, 2
+    near, far = range(2, top, 2), range(top + relay + 2, devices, 2)
+    direct = [top, *reversed(far), *reversed(near)]
+    held = {0: packed, **{offset: swap(packed, offset) for offset in direct}}
+    held[top + relay] = swap(held[top], relay)
+    offsets = list(held)
+    mine = jnp.concatenate(list(held.values()), axis=0)
+    theirs = swap(mine, 1)
+    final, stress = pl.pallas_call(
+        functools.partial(group_kernel, offsets, per_dev),
+        out_shape=(f32((coord_dims, per_dev)), f32((ITERS,))),
+        in_specs=[vmem, vmem],
+        out_specs=(vmem, pl.BlockSpec(memory_space=pltpu.SMEM)),
+        scratch_shapes=[
+            pltpu.VMEM((points, points), jnp.float32),
+            pltpu.VMEM((points, points), jnp.float32),
+            pltpu.VMEM((devices, SUBLANES, LANES), jnp.float32),
+            pltpu.VMEM((points, points), jnp.float32),
+        ],
+        compiler_params=params,
+        name="group_smacof",
+    )(mine, theirs)
+    return (final[:, None, :], stress)
+
+
+def distributed_body(dissim, classes, coords):
     halves = dissim.shape[0]
     per_dev = dissim.shape[1]
     columns = dissim.shape[2]
@@ -79,6 +269,15 @@
 
 
 def solution(mesh):
+    def body(dissim, classes, coords):
+        coord_dims, halves, per_dev = coords.shape
+        points, devices = dissim.shape[2], mesh.shape["wide"]
+        small = halves == 1 and mesh.shape["narrow"] == 1 and points * points <= MOST_PAIRS
+        small = small and coord_dims == 2 * SUBLANES and 2 * per_dev <= LANES
+        small = small and per_dev % SUBLANES == 0 and points % LANES == 0
+        small = small and devices >= 8 and devices & (devices - 1) == 0
+        return (small_body if small else distributed_body)(dissim, classes, coords)
+
     return jax.shard_map(
         body,
         mesh=mesh,

time: 105 us -> 25 us (0.24)
  blocking collectives: 91.3 us -> 0 us
  starting transfers between devices: 0 us -> 13.5 us
  waiting for transfers between devices: 0 us -> 6.11 us
  matrix products: 5.06 us -> 0 us
  Pallas kernels: 0 us -> 4.22 us
  between operations: 4.42 us -> 0.66 us
  other arithmetic: 2.64 us -> 0 us
    all_gather x3 -> x0, blocking collectives: 60.8 us -> none  [body(): lax.all_gather(row_points, 'wide', axis=2, tiled=True)]
    psum x1 -> x0, blocking collectives: 30.5 us -> none  [body(): lax.psum(jnp.sum(weight * misfit * misfit), ('wide', 'narrow'))]
    ppermute x0 -> x8, starting transfers between devices: none -> 13.5 us  [swap(): lax.ppermute(value, 'wide', [(i, i ^ offset) for i in range(devices)])]
    ppermute x0 -> x8, waiting for transfers between devices: none -> 6.11 us  [swap(): lax.ppermute(value, 'wide', [(i, i ^ offset) for i in range(devices)])]
    dot_general x6 -> x0, matrix products: 5.06 us -> none  [the longest x3 3.07 us: body(): lax.dot_general(row_x, fold_column_x, (((0,), (0,)), ((), ())), precision...]
    pallas_call x0 -> x2, Pallas kernels: none -> 4.22 us  [the longest x1 3.33 us: small_body(): pl.pallas_call(functools.partial(group_kernel, offsets, per_dev), out_sha...]
    reduce_sum x5 -> x0, other arithmetic: 2.03 us -> none  [the longest x1 0.9 us: body(): jnp.sum(weight, axis=1).reshape(halves, per_dev)]
  transfers between devices with their start and end apart: 0 -> 8, of which waited for: 0 -> 6; matrix products, arithmetic and copies ran while one was open for 0% -> 0% of each run, Pallas kernels for 0% -> 0%
where the time goes in v6:
time: 25 us; the launch traced here: 24.5 us
  starting transfers between devices  13.5 us (54%)
  waiting for transfers between devices  6.11 us (24%)
  Pallas kernels  4.22 us (17%)
  between operations  0.66 us (3%)
    ppermute x8, starting transfers between devices, swap(): lax.ppermute(value, 'wide', [(i, i ^ offset) for i in range(devices)])  13.5 us
    ppermute x8, waiting for transfers between devices, swap(): lax.ppermute(value, 'wide', [(i, i ^ offset) for i in range(devices)])  6.11 us
    pallas_call x1, Pallas kernels, small_body(): pl.pallas_call(functools.partial(group_kernel, offsets, per_dev), out_sha...  3.33 us
    pallas_call x1, Pallas kernels, small_body(): pl.pallas_call(pack_kernel, out_shape=f32((tiles, SUBLANES, LANES)), in_s...  0.89 us
  transfers between devices with their start and end apart: 8, of which 6 were waited for; matrix products, arithmetic and copies ran while one was open for 0% of the time, Pallas kernels for 0%

profile of v6, /device:TPU:0, one launch (start us, length us, event | category | flops | bytes accessed | tf_op | source)
XLA Modules:
  0.0 24.5 jit_solution(3753330095546959554)
XLA Ops:
  0.6 0.9 %pack.1 = f32[19,8,128]{2,1,0:T(8,128)S(1)} custom-call(f32[24,384]{1,0:T(8,128)} %bitcast.6, s32[24,384]{1,0:T(8,128)} %bitcast.7, f32[16,24]{1,0:T(8,128)} %bitcast.8), custom_call_target="tpu_custom_call" | custom-call | tf_op jit(solution)/shard_map/pack/pallas_call | solution.py:168
  1.5 4.1 %collective-permute-start = (f32[19,8,128]{2,1,0:T(8,128)S(1)}, f32[19,8,128]{2,1,0:T(8,128)S(1)}, u32[]{:S(2)}, u32[]{:S(2)}) collective-permute-start(f32[19,8,128]{2,1,0:T(8,128)S(1)} %pack.1), channel_id=1, source_target_pairs={{0,8},{1,9},{2,10},{3,11},{4,12},{5,13},{6,14},{7,15},{8,0},{9,1},... | collective-permute-start | bytes 233480 | tf_op jit(solution)/shard_map/ppermute | solution.py:164
  5.6 2.3 %collective-permute-start.1 = (f32[19,8,128]{2,1,0:T(8,128)S(1)}, f32[19,8,128]{2,1,0:T(8,128)S(1)}, u32[]{:S(2)}, u32[]{:S(2)}) collective-permute-start(f32[19,8,128]{2,1,0:T(8,128)S(1)} %pack.1), channel_id=1, source_target_pairs={{0,14},{1,15},{2,12},{3,13},{4,10},{5,11},{6,8},{7,9},{8,6},{9,7},... | collective-permute-start | bytes 233480 | tf_op jit(solution)/shard_map/ppermute | solution.py:164
  7.9 2.5 %collective-permute-start.2 = (f32[19,8,128]{2,1,0:T(8,128)S(1)}, f32[19,8,128]{2,1,0:T(8,128)S(1)}, u32[]{:S(2)}, u32[]{:S(2)}) collective-permute-start(f32[19,8,128]{2,1,0:T(8,128)S(1)} %pack.1), channel_id=1, source_target_pairs={{0,12},{1,13},{2,14},{3,15},{4,8},{5,9},{6,10},{7,11},{8,4},{9,5},... | collective-permute-start | bytes 233480 | tf_op jit(solution)/shard_map/ppermute | solution.py:164
  10.4 0.0 collective-permute-start.3
  10.4 2.0 %collective-permute-start.4 = (f32[19,8,128]{2,1,0:T(8,128)S(1)}, f32[19,8,128]{2,1,0:T(8,128)S(1)}, u32[]{:S(2)}, u32[]{:S(2)}) collective-permute-start(f32[19,8,128]{2,1,0:T(8,128)S(1)} %pack.1), channel_id=1, source_target_pairs={{0,4},{1,5},{2,6},{3,7},{4,0},{5,1},{6,2},{7,3},{8,12},{9,13},{10,... | collective-permute-start | bytes 233480 | tf_op jit(solution)/shard_map/ppermute | solution.py:164
  12.4 0.0 collective-permute-done
  12.4 2.3 %collective-permute-start.5 = (f32[19,8,128]{2,1,0:T(8,128)S(1)}, f32[19,8,128]{2,1,0:T(8,128)S(1)}, u32[]{:S(2)}, u32[]{:S(2)}) collective-permute-start(f32[19,8,128]{2,1,0:T(8,128)S(1)} %pack.1), channel_id=1, source_target_pairs={{0,2},{1,3},{2,0},{3,1},{4,6},{5,7},{6,4},{7,5},{8,10},{9,11},{10,... | collective-permute-start | bytes 233480 | tf_op jit(solution)/shard_map/ppermute | solution.py:164
  14.7 0.0 collective-permute-done.1
  14.7 0.4 %collective-permute-start.6 = (f32[19,8,128]{2,1,0:T(8,128)S(1)}, f32[19,8,128]{2,1,0:T(8,128)S(1)}, u32[]{:S(2)}, u32[]{:S(2)}) collective-permute-start(f32[19,8,128]{2,1,0:T(8,128)S(1)} %collective-permute-done), channel_id=1, source_target_pairs={{0,2},{1,3},{2,0},{3,1},{4,6},{5,7},{6,4},{7,5},{8,10},{9,11},{10,... | collective-permute-start | bytes 233480 | tf_op jit(solution)/shard_map/ppermute | solution.py:164
  15.1 0.2 collective-permute-done.2
  15.3 1.5 %collective-permute-done.3 = f32[19,8,128]{2,1,0:T(8,128)S(1)} collective-permute-done((f32[19,8,128]{2,1,0:T(8,128)S(1)}, f32[19,8,128]{2,1,0:T(8,128)S(1)}, u32[]{:S(2)}, u32[]{:S(2)}) %collective-permute-start.3) | collective-permute-done | bytes 77856 | tf_op jit(solution)/shard_map/ppermute | solution.py:164
  16.8 0.7 %collective-permute-done.4 = f32[19,8,128]{2,1,0:T(8,128)S(1)} collective-permute-done((f32[19,8,128]{2,1,0:T(8,128)S(1)}, f32[19,8,128]{2,1,0:T(8,128)S(1)}, u32[]{:S(2)}, u32[]{:S(2)}) %collective-permute-start.4) | collective-permute-done | bytes 77856 | tf_op jit(solution)/shard_map/ppermute | solution.py:164
  17.4 0.1 collective-permute-done.5
  17.6 1.6 %collective-permute-done.6 = f32[19,8,128]{2,1,0:T(8,128)S(1)} collective-permute-done((f32[19,8,128]{2,1,0:T(8,128)S(1)}, f32[19,8,128]{2,1,0:T(8,128)S(1)}, u32[]{:S(2)}, u32[]{:S(2)}) %collective-permute-start.6) | collective-permute-done | bytes 77856 | tf_op jit(solution)/shard_map/ppermute | solution.py:164
  19.2 0.0 collective-permute-start.7
  19.2 2.0 %collective-permute-done.7.theirs_ref = f32[152,8,128]{2,1,0:T(8,128)S(1)} collective-permute-done((f32[152,8,128]{2,1,0:T(8,128)S(1)}, f32[152,8,128]{2,1,0:T(8,128)S(1)}, u32[]{:S(2)}, u32[]{:S(2)}) %collective-permute-start.7) | collective-permute-done | bytes 622624 | tf_op jit(solution)/shard_map/ppermute | solution.py:164
  21.2 3.3 %group_smacof.1 = (f32[16,24]{1,0:T(8,128)}, f32[3]{0:T(128)}) custom-call(f32[152,8,128]{2,1,0:T(8,128)S(1)} %constant_dynamic-update-slice_fusion.mine_ref, f32[152,8,128]{2,1,0:T(8,128)S(1)} %collective-permute-done.7.theirs_ref), custom_call_target="tpu_custom_call" | custom-call | tf_op jit(solution)/shard_map/group_smacof/pallas_call | solution.py:190
  (8 shorter events, 0.1 us)
Async XLA Ops:
  1.5 10.9 %collective-permute-start = (f32[19,8,128]{2,1,0:T(8,128)S(1)}, f32[19,8,128]{2,1,0:T(8,128)S(1)}, u32[]{:S(2)}, u32[]{:S(2)}) collective-permute-start(f32[19,8,128]{2,1,0:T(8,128)S(1)} %pack.1), channel_id=1, source_target_pairs={{0,8},{1,9},{2,10},{3,11},{4,12},{5,13},{6,14},{7,15},{8,0},{9,1},... | collective-permute-start | bytes 233480 | tf_op jit(solution)/shard_map/ppermute | solution.py:164
  5.6 9.1 %collective-permute-start.1 = (f32[19,8,128]{2,1,0:T(8,128)S(1)}, f32[19,8,128]{2,1,0:T(8,128)S(1)}, u32[]{:S(2)}, u32[]{:S(2)}) collective-permute-start(f32[19,8,128]{2,1,0:T(8,128)S(1)} %pack.1), channel_id=1, source_target_pairs={{0,14},{1,15},{2,12},{3,13},{4,10},{5,11},{6,8},{7,9},{8,6},{9,7},... | collective-permute-start | bytes 233480 | tf_op jit(solution)/shard_map/ppermute | solution.py:164
  7.9 7.4 %collective-permute-start.2 = (f32[19,8,128]{2,1,0:T(8,128)S(1)}, f32[19,8,128]{2,1,0:T(8,128)S(1)}, u32[]{:S(2)}, u32[]{:S(2)}) collective-permute-start(f32[19,8,128]{2,1,0:T(8,128)S(1)} %pack.1), channel_id=1, source_target_pairs={{0,12},{1,13},{2,14},{3,15},{4,8},{5,9},{6,10},{7,11},{8,4},{9,5},... | collective-permute-start | bytes 233480 | tf_op jit(solution)/shard_map/ppermute | solution.py:164
  10.4 6.4 %collective-permute-start.3 = (f32[19,8,128]{2,1,0:T(8,128)S(1)}, f32[19,8,128]{2,1,0:T(8,128)S(1)}, u32[]{:S(2)}, u32[]{:S(2)}) collective-permute-start(f32[19,8,128]{2,1,0:T(8,128)S(1)} %pack.1), channel_id=1, source_target_pairs={{0,6},{1,7},{2,4},{3,5},{4,2},{5,3},{6,0},{7,1},{8,14},{9,15},{10,... | collective-permute-start | bytes 233480 | tf_op jit(solution)/shard_map/ppermute | solution.py:164
  10.4 7.1 %collective-permute-start.4 = (f32[19,8,128]{2,1,0:T(8,128)S(1)}, f32[19,8,128]{2,1,0:T(8,128)S(1)}, u32[]{:S(2)}, u32[]{:S(2)}) collective-permute-start(f32[19,8,128]{2,1,0:T(8,128)S(1)} %pack.1), channel_id=1, source_target_pairs={{0,4},{1,5},{2,6},{3,7},{4,0},{5,1},{6,2},{7,3},{8,12},{9,13},{10,... | collective-permute-start | bytes 233480 | tf_op jit(solution)/shard_map/ppermute | solution.py:164
  12.4 5.2 %collective-permute-start.5 = (f32[19,8,128]{2,1,0:T(8,128)S(1)}, f32[19,8,128]{2,1,0:T(8,128)S(1)}, u32[]{:S(2)}, u32[]{:S(2)}) collective-permute-start(f32[19,8,128]{2,1,0:T(8,128)S(1)} %pack.1), channel_id=1, source_target_pairs={{0,2},{1,3},{2,0},{3,1},{4,6},{5,7},{6,4},{7,5},{8,10},{9,11},{10,... | collective-permute-start | bytes 233480 | tf_op jit(solution)/shard_map/ppermute | solution.py:164
  14.7 4.5 %collective-permute-start.6 = (f32[19,8,128]{2,1,0:T(8,128)S(1)}, f32[19,8,128]{2,1,0:T(8,128)S(1)}, u32[]{:S(2)}, u32[]{:S(2)}) collective-permute-start(f32[19,8,128]{2,1,0:T(8,128)S(1)} %collective-permute-done), channel_id=1, source_target_pairs={{0,2},{1,3},{2,0},{3,1},{4,6},{5,7},{6,4},{7,5},{8,10},{9,11},{10,... | collective-permute-start | bytes 233480 | tf_op jit(solution)/shard_map/ppermute | solution.py:164
  19.2 2.1 %collective-permute-start.7 = (f32[152,8,128]{2,1,0:T(8,128)S(1)}, f32[152,8,128]{2,1,0:T(8,128)S(1)}, u32[]{:S(2)}, u32[]{:S(2)}) collective-permute-start(f32[152,8,128]{2,1,0:T(8,128)S(1)} %constant_dynamic-update-slice_fusion.mine_ref), channel_id=1, source_target_pairs={{0,1},{1,0},{2,3},{3,2},{4,5},{5,4},{6,7},{7,6},{8,9},{9,8},{10,11... | collective-permute-start | bytes 1867784 | tf_op jit(solution)/shard_map/ppermute | solution.py:164

commit v7 on v6

--- a/solution.py
+++ b/solution.py
@@ -68,11 +68,11 @@
     out_ref[2 * len(spots)] = jnp.concatenate([x_ref[:half], x_ref[half:], pad], axis=1)
 
 
-def held_slots(offsets, refs, tiles):
-    me = lax.axis_index("wide")
+def held_slots(refs, tiles):
+    core = lax.rem(lax.axis_index("wide"), 2)
     for bit, ref in enumerate(refs):
-        for slot, offset in enumerate(offsets):
-            yield ref, slot * tiles, me ^ offset ^ bit
+        for slot in range(ref.shape[0] // tiles):
+            yield ref, slot * tiles, 2 * slot + (core ^ bit)
 
 
 def side_norm(top, bottom, coord_dims):
@@ -106,12 +106,12 @@
     return own + (pulled - own * sums[2 * coord_dims : 2 * coord_dims + 1]) * scale
 
 
-def group_kernel(offsets, per_dev, mine_ref, theirs_ref, out_ref, stress_ref,
+def group_kernel(per_dev, mine_ref, theirs_ref, out_ref, stress_ref,
                  dis_ref, weight_ref, tile_ref, inverse_ref):
     points = dis_ref.shape[0]
     spots = tile_spots(per_dev, points)
     tiles = 2 * len(spots) + 1
-    for ref, base, place in held_slots(offsets, (mine_ref, theirs_ref), tiles):
+    for ref, base, place in held_slots((mine_ref, theirs_ref), tiles):
         tile_ref[place] = ref[base + tiles - 1]
         for i, (rows, columns) in enumerate(spots):
             start = pl.multiple_of(place * per_dev + rows.start, SUBLANES)
@@ -179,16 +179,11 @@
         compiler_params=params,
         name="pack",
     )(*(pltpu.with_memory_space_constraint(array, pltpu.HBM) for array in inputs))
-    top, relay = devices // 2, 2
-    near, far = range(2, top, 2), range(top + relay + 2, devices, 2)
-    direct = [top, *reversed(far), *reversed(near)]
-    held = {0: packed, **{offset: swap(packed, offset) for offset in direct}}
-    held[top + relay] = swap(held[top], relay)
-    offsets = list(held)
-    mine = jnp.concatenate(list(held.values()), axis=0)
+    same_core = [list(range(core, devices, 2)) for core in range(2)]
+    mine = lax.all_gather(packed, "wide", axis=0, tiled=True, axis_index_groups=same_core)
     theirs = swap(mine, 1)
     final, stress = pl.pallas_call(
-        functools.partial(group_kernel, offsets, per_dev),
+        functools.partial(group_kernel, per_dev),
         out_shape=(f32((coord_dims, per_dev)), f32((ITERS,))),
         in_specs=[vmem, vmem],
         out_specs=(vmem, pl.BlockSpec(memory_space=pltpu.SMEM)),

time: 25 us -> 40.4 us (1.62)
  blocking collectives: 0 us -> 33.3 us
  starting transfers between devices: 13.5 us -> 0.01 us
  waiting for transfers between devices: 6.11 us -> 2.05 us
    all_gather x0 -> x1, blocking collectives: none -> 33.3 us  [small_body(): lax.all_gather(packed, 'wide', axis=0, tiled=True, axis_index_groups=same...]
    ppermute x8 -> x1, starting transfers between devices: 13.5 us -> 0.01 us  [swap(): lax.ppermute(value, 'wide', [(i, i ^ offset) for i in range(devices)])]
    ppermute x8 -> x1, waiting for transfers between devices: 6.11 us -> 2.05 us  [swap(): lax.ppermute(value, 'wide', [(i, i ^ offset) for i in range(devices)])]
  transfers between devices with their start and end apart: 8 -> 1, of which waited for: 6 -> 1; matrix products, arithmetic and copies ran while one was open for 0% -> 0% of each run, Pallas kernels for 0% -> 0%
where the time goes in v7:
time: 40.4 us; the launch traced here: 40.2 us
  blocking collectives  33.3 us (82%)
  Pallas kernels  4.22 us (10%)
  waiting for transfers between devices  2.05 us (5%)
  between operations  0.64 us (2%)
    all_gather x1, blocking collectives, small_body(): lax.all_gather(packed, 'wide', axis=0, tiled=True, axis_index_groups=same...  33.3 us
    pallas_call x1, Pallas kernels, small_body(): pl.pallas_call(functools.partial(group_kernel, per_dev), out_shape=(f32((...  3.33 us
    ppermute x1, waiting for transfers between devices, swap(): lax.ppermute(value, 'wide', [(i, i ^ offset) for i in range(devices)])  2.05 us
    pallas_call x1, Pallas kernels, small_body(): pl.pallas_call(pack_kernel, out_shape=f32((tiles, SUBLANES, LANES)), in_s...  0.89 us
  transfers between devices with their start and end apart: 1, of which 1 were waited for; matrix products, arithmetic and copies ran while one was open for 0% of the time, Pallas kernels for 0%

profile of v7, /device:TPU:0, one launch (start us, length us, event | category | flops | bytes accessed | tf_op | source)
XLA Modules:
  0.0 40.2 jit_solution(7010158273804030866)
XLA Ops:
  0.6 0.9 %pack.1 = f32[19,8,128]{2,1,0:T(8,128)S(1)} custom-call(f32[24,384]{1,0:T(8,128)} %bitcast.6, s32[24,384]{1,0:T(8,128)} %bitcast.7, f32[16,24]{1,0:T(8,128)} %bitcast.8), custom_call_target="tpu_custom_call" | custom-call | tf_op jit(solution)/shard_map/pack/pallas_call | solution.py:168
  1.5 33.3 %all_gather.3.mine_ref = f32[152,8,128]{2,1,0:T(8,128)S(1)} all-gather(f32[19,8,128]{2,1,0:T(8,128)S(1)} %pack.1), channel_id=1, replica_groups={{0,2,4,6,8,10,12,14},{1,3,5,7,9,11,13,15},{16,18,20,22,24,26,28,30},{17..., dimensions={0}, use_global_device_ids=true | all-gather | bytes 700416 | tf_op jit(solution)/shard_map/all_gather | solution.py:183
  34.8 0.0 collective-permute-start
  34.8 2.0 %collective-permute-done.theirs_ref = f32[152,8,128]{2,1,0:T(8,128)S(1)} collective-permute-done((f32[152,8,128]{2,1,0:T(8,128)S(1)}, f32[152,8,128]{2,1,0:T(8,128)S(1)}, u32[]{:S(2)}, u32[]{:S(2)}) %collective-permute-start) | collective-permute-done | bytes 622624 | tf_op jit(solution)/shard_map/ppermute | solution.py:164
  36.9 3.3 %group_smacof.1 = (f32[16,24]{1,0:T(8,128)}, f32[3]{0:T(128)}) custom-call(f32[152,8,128]{2,1,0:T(8,128)S(1)} %all_gather.3.mine_ref, f32[152,8,128]{2,1,0:T(8,128)S(1)} %collective-permute-done.theirs_ref), custom_call_target="tpu_custom_call" | custom-call | tf_op jit(solution)/shard_map/group_smacof/pallas_call | solution.py:185
Async XLA Ops:
  34.8 2.1 %collective-permute-start = (f32[152,8,128]{2,1,0:T(8,128)S(1)}, f32[152,8,128]{2,1,0:T(8,128)S(1)}, u32[]{:S(2)}, u32[]{:S(2)}) collective-permute-start(f32[152,8,128]{2,1,0:T(8,128)S(1)} %all_gather.3.mine_ref), channel_id=1, source_target_pairs={{0,1},{1,0},{2,3},{3,2},{4,5},{5,4},{6,7},{7,6},{8,9},{9,8},{10,11... | collective-permute-start | bytes 1867784 | tf_op jit(solution)/shard_map/ppermute | solution.py:164

commit v8 on v6

--- a/solution.py
+++ b/solution.py
@@ -179,11 +179,12 @@
         compiler_params=params,
         name="pack",
     )(*(pltpu.with_memory_space_constraint(array, pltpu.HBM) for array in inputs))
-    top, relay = devices // 2, 2
-    near, far = range(2, top, 2), range(top + relay + 2, devices, 2)
-    direct = [top, *reversed(far), *reversed(near)]
-    held = {0: packed, **{offset: swap(packed, offset) for offset in direct}}
-    held[top + relay] = swap(held[top], relay)
+    far, near, side = devices // 2, devices // 4, devices // 8
+    held = {0: packed}
+    for offset in (far, near, far | near | side, far | near, side):
+        held[offset] = swap(packed, offset)
+    for offset in (near, far):
+        held[offset | side] = swap(held[offset], side)
     offsets = list(held)
     mine = jnp.concatenate(list(held.values()), axis=0)
     theirs = swap(mine, 1)
@@ -275,7 +276,7 @@
         small = halves == 1 and mesh.shape["narrow"] == 1 and points * points <= MOST_PAIRS
         small = small and coord_dims == 2 * SUBLANES and 2 * per_dev <= LANES
         small = small and per_dev % SUBLANES == 0 and points % LANES == 0
-        small = small and devices >= 8 and devices & (devices - 1) == 0
+        small = small and devices == 16
         return (small_body if small else distributed_body)(dissim, classes, coords)
 
     return jax.shard_map(

time: 25 us -> 24.8 us (level)
  waiting for transfers between devices: 6.11 us -> 6.43 us
  starting transfers between devices: 13.5 us -> 13.2 us
    ppermute x8, waiting for transfers between devices: 6.11 us -> 6.43 us  [swap(): lax.ppermute(value, 'wide', [(i, i ^ offset) for i in range(devices)])]
    ppermute x8, starting transfers between devices: 13.5 us -> 13.2 us  [swap(): lax.ppermute(value, 'wide', [(i, i ^ offset) for i in range(devices)])]
  transfers between devices with their start and end apart: 8 -> 8, of which waited for: 6 -> 4; matrix products, arithmetic and copies ran while one was open for 0% -> 0% of each run, Pallas kernels for 0% -> 0%
where the time goes in v8:
time: 24.8 us; the launch traced here: 24.6 us
  starting transfers between devices  13.2 us (53%)
  waiting for transfers between devices  6.43 us (26%)
  Pallas kernels  4.21 us (17%)
  between operations  0.68 us (3%)
    ppermute x8, starting transfers between devices, swap(): lax.ppermute(value, 'wide', [(i, i ^ offset) for i in range(devices)])  13.2 us
    ppermute x8, waiting for transfers between devices, swap(): lax.ppermute(value, 'wide', [(i, i ^ offset) for i in range(devices)])  6.43 us
    pallas_call x1, Pallas kernels, small_body(): pl.pallas_call(functools.partial(group_kernel, offsets, per_dev), out_sha...  3.33 us
    pallas_call x1, Pallas kernels, small_body(): pl.pallas_call(pack_kernel, out_shape=f32((tiles, SUBLANES, LANES)), in_s...  0.89 us
  transfers between devices with their start and end apart: 8, of which 4 were waited for; matrix products, arithmetic and copies ran while one was open for 0% of the time, Pallas kernels for 0%

profile of v8, /device:TPU:0, one launch (start us, length us, event | category | flops | bytes accessed | tf_op | source)
XLA Modules:
  0.0 24.6 jit_solution(13340401192534234661)
XLA Ops:
  0.6 0.9 %pack.1 = f32[19,8,128]{2,1,0:T(8,128)S(1)} custom-call(f32[24,384]{1,0:T(8,128)} %bitcast.6, s32[24,384]{1,0:T(8,128)} %bitcast.7, f32[16,24]{1,0:T(8,128)} %bitcast.8), custom_call_target="tpu_custom_call" | custom-call | tf_op jit(solution)/shard_map/pack/pallas_call | solution.py:168
  1.5 4.1 %collective-permute-start = (f32[19,8,128]{2,1,0:T(8,128)S(1)}, f32[19,8,128]{2,1,0:T(8,128)S(1)}, u32[]{:S(2)}, u32[]{:S(2)}) collective-permute-start(f32[19,8,128]{2,1,0:T(8,128)S(1)} %pack.1), channel_id=1, source_target_pairs={{0,8},{1,9},{2,10},{3,11},{4,12},{5,13},{6,14},{7,15},{8,0},{9,1},... | collective-permute-start | bytes 233480 | tf_op jit(solution)/shard_map/ppermute | solution.py:164
  5.6 1.6 %collective-permute-start.1 = (f32[19,8,128]{2,1,0:T(8,128)S(1)}, f32[19,8,128]{2,1,0:T(8,128)S(1)}, u32[]{:S(2)}, u32[]{:S(2)}) collective-permute-start(f32[19,8,128]{2,1,0:T(8,128)S(1)} %pack.1), channel_id=1, source_target_pairs={{0,4},{1,5},{2,6},{3,7},{4,0},{5,1},{6,2},{7,3},{8,12},{9,13},{10,... | collective-permute-start | bytes 233480 | tf_op jit(solution)/shard_map/ppermute | solution.py:164
  7.2 1.1 %collective-permute-start.2 = (f32[19,8,128]{2,1,0:T(8,128)S(1)}, f32[19,8,128]{2,1,0:T(8,128)S(1)}, u32[]{:S(2)}, u32[]{:S(2)}) collective-permute-start(f32[19,8,128]{2,1,0:T(8,128)S(1)} %pack.1), channel_id=1, source_target_pairs={{0,14},{1,15},{2,12},{3,13},{4,10},{5,11},{6,8},{7,9},{8,6},{9,7},... | collective-permute-start | bytes 233480 | tf_op jit(solution)/shard_map/ppermute | solution.py:164
  8.4 3.6 %collective-permute-start.3 = (f32[19,8,128]{2,1,0:T(8,128)S(1)}, f32[19,8,128]{2,1,0:T(8,128)S(1)}, u32[]{:S(2)}, u32[]{:S(2)}) collective-permute-start(f32[19,8,128]{2,1,0:T(8,128)S(1)} %pack.1), channel_id=1, source_target_pairs={{0,12},{1,13},{2,14},{3,15},{4,8},{5,9},{6,10},{7,11},{8,4},{9,5},... | collective-permute-start | bytes 233480 | tf_op jit(solution)/shard_map/ppermute | solution.py:164
  12.0 0.5 %collective-permute-start.4 = (f32[19,8,128]{2,1,0:T(8,128)S(1)}, f32[19,8,128]{2,1,0:T(8,128)S(1)}, u32[]{:S(2)}, u32[]{:S(2)}) collective-permute-start(f32[19,8,128]{2,1,0:T(8,128)S(1)} %pack.1), channel_id=1, source_target_pairs={{0,2},{1,3},{2,0},{3,1},{4,6},{5,7},{6,4},{7,5},{8,10},{9,11},{10,... | collective-permute-start | bytes 233480 | tf_op jit(solution)/shard_map/ppermute | solution.py:164
  12.5 0.0 collective-permute-done
  12.5 1.6 %collective-permute-start.6 = (f32[19,8,128]{2,1,0:T(8,128)S(1)}, f32[19,8,128]{2,1,0:T(8,128)S(1)}, u32[]{:S(2)}, u32[]{:S(2)}) collective-permute-start(f32[19,8,128]{2,1,0:T(8,128)S(1)} %collective-permute-done), channel_id=1, source_target_pairs={{0,2},{1,3},{2,0},{3,1},{4,6},{5,7},{6,4},{7,5},{8,10},{9,11},{10,... | collective-permute-start | bytes 233480 | tf_op jit(solution)/shard_map/ppermute | solution.py:164
  14.1 0.0 collective-permute-done.1
  14.1 0.6 %collective-permute-start.5 = (f32[19,8,128]{2,1,0:T(8,128)S(1)}, f32[19,8,128]{2,1,0:T(8,128)S(1)}, u32[]{:S(2)}, u32[]{:S(2)}) collective-permute-start(f32[19,8,128]{2,1,0:T(8,128)S(1)} %collective-permute-done.1), channel_id=1, source_target_pairs={{0,2},{1,3},{2,0},{3,1},{4,6},{5,7},{6,4},{7,5},{8,10},{9,11},{10,... | collective-permute-start | bytes 233480 | tf_op jit(solution)/shard_map/ppermute | solution.py:164
  14.7 0.0 collective-permute-done.2
  14.7 0.5 %collective-permute-done.3 = f32[19,8,128]{2,1,0:T(8,128)S(1)} collective-permute-done((f32[19,8,128]{2,1,0:T(8,128)S(1)}, f32[19,8,128]{2,1,0:T(8,128)S(1)}, u32[]{:S(2)}, u32[]{:S(2)}) %collective-permute-start.3) | collective-permute-done | bytes 77856 | tf_op jit(solution)/shard_map/ppermute | solution.py:164
  15.2 2.0 %collective-permute-done.4 = f32[19,8,128]{2,1,0:T(8,128)S(1)} collective-permute-done((f32[19,8,128]{2,1,0:T(8,128)S(1)}, f32[19,8,128]{2,1,0:T(8,128)S(1)}, u32[]{:S(2)}, u32[]{:S(2)}) %collective-permute-start.4) | collective-permute-done | bytes 77856 | tf_op jit(solution)/shard_map/ppermute | solution.py:164
  17.3 1.8 %collective-permute-done.5 = f32[19,8,128]{2,1,0:T(8,128)S(1)} collective-permute-done((f32[19,8,128]{2,1,0:T(8,128)S(1)}, f32[19,8,128]{2,1,0:T(8,128)S(1)}, u32[]{:S(2)}, u32[]{:S(2)}) %collective-permute-start.5) | collective-permute-done | bytes 77856 | tf_op jit(solution)/shard_map/ppermute | solution.py:164
  19.1 0.0 collective-permute-done.6
  19.1 0.1 collective-permute-start.7
  19.2 2.0 %collective-permute-done.7.theirs_ref = f32[152,8,128]{2,1,0:T(8,128)S(1)} collective-permute-done((f32[152,8,128]{2,1,0:T(8,128)S(1)}, f32[152,8,128]{2,1,0:T(8,128)S(1)}, u32[]{:S(2)}, u32[]{:S(2)}) %collective-permute-start.7) | collective-permute-done | bytes 622624 | tf_op jit(solution)/shard_map/ppermute | solution.py:164
  21.2 3.3 %group_smacof.1 = (f32[16,24]{1,0:T(8,128)}, f32[3]{0:T(128)}) custom-call(f32[152,8,128]{2,1,0:T(8,128)S(1)} %constant_dynamic-update-slice_fusion.mine_ref, f32[152,8,128]{2,1,0:T(8,128)S(1)} %collective-permute-done.7.theirs_ref), custom_call_target="tpu_custom_call" | custom-call | tf_op jit(solution)/shard_map/group_smacof/pallas_call | solution.py:191
  (8 shorter events, 0.1 us)
Async XLA Ops:
  1.5 11.0 %collective-permute-start = (f32[19,8,128]{2,1,0:T(8,128)S(1)}, f32[19,8,128]{2,1,0:T(8,128)S(1)}, u32[]{:S(2)}, u32[]{:S(2)}) collective-permute-start(f32[19,8,128]{2,1,0:T(8,128)S(1)} %pack.1), channel_id=1, source_target_pairs={{0,8},{1,9},{2,10},{3,11},{4,12},{5,13},{6,14},{7,15},{8,0},{9,1},... | collective-permute-start | bytes 233480 | tf_op jit(solution)/shard_map/ppermute | solution.py:164
  5.6 8.4 %collective-permute-start.1 = (f32[19,8,128]{2,1,0:T(8,128)S(1)}, f32[19,8,128]{2,1,0:T(8,128)S(1)}, u32[]{:S(2)}, u32[]{:S(2)}) collective-permute-start(f32[19,8,128]{2,1,0:T(8,128)S(1)} %pack.1), channel_id=1, source_target_pairs={{0,4},{1,5},{2,6},{3,7},{4,0},{5,1},{6,2},{7,3},{8,12},{9,13},{10,... | collective-permute-start | bytes 233480 | tf_op jit(solution)/shard_map/ppermute | solution.py:164
  7.2 7.5 %collective-permute-start.2 = (f32[19,8,128]{2,1,0:T(8,128)S(1)}, f32[19,8,128]{2,1,0:T(8,128)S(1)}, u32[]{:S(2)}, u32[]{:S(2)}) collective-permute-start(f32[19,8,128]{2,1,0:T(8,128)S(1)} %pack.1), channel_id=1, source_target_pairs={{0,14},{1,15},{2,12},{3,13},{4,10},{5,11},{6,8},{7,9},{8,6},{9,7},... | collective-permute-start | bytes 233480 | tf_op jit(solution)/shard_map/ppermute | solution.py:164
  8.4 6.9 %collective-permute-start.3 = (f32[19,8,128]{2,1,0:T(8,128)S(1)}, f32[19,8,128]{2,1,0:T(8,128)S(1)}, u32[]{:S(2)}, u32[]{:S(2)}) collective-permute-start(f32[19,8,128]{2,1,0:T(8,128)S(1)} %pack.1), channel_id=1, source_target_pairs={{0,12},{1,13},{2,14},{3,15},{4,8},{5,9},{6,10},{7,11},{8,4},{9,5},... | collective-permute-start | bytes 233480 | tf_op jit(solution)/shard_map/ppermute | solution.py:164
  12.0 5.3 %collective-permute-start.4 = (f32[19,8,128]{2,1,0:T(8,128)S(1)}, f32[19,8,128]{2,1,0:T(8,128)S(1)}, u32[]{:S(2)}, u32[]{:S(2)}) collective-permute-start(f32[19,8,128]{2,1,0:T(8,128)S(1)} %pack.1), channel_id=1, source_target_pairs={{0,2},{1,3},{2,0},{3,1},{4,6},{5,7},{6,4},{7,5},{8,10},{9,11},{10,... | collective-permute-start | bytes 233480 | tf_op jit(solution)/shard_map/ppermute | solution.py:164
  12.5 6.6 %collective-permute-start.6 = (f32[19,8,128]{2,1,0:T(8,128)S(1)}, f32[19,8,128]{2,1,0:T(8,128)S(1)}, u32[]{:S(2)}, u32[]{:S(2)}) collective-permute-start(f32[19,8,128]{2,1,0:T(8,128)S(1)} %collective-permute-done), channel_id=1, source_target_pairs={{0,2},{1,3},{2,0},{3,1},{4,6},{5,7},{6,4},{7,5},{8,10},{9,11},{10,... | collective-permute-start | bytes 233480 | tf_op jit(solution)/shard_map/ppermute | solution.py:164
  14.1 5.0 %collective-permute-start.5 = (f32[19,8,128]{2,1,0:T(8,128)S(1)}, f32[19,8,128]{2,1,0:T(8,128)S(1)}, u32[]{:S(2)}, u32[]{:S(2)}) collective-permute-start(f32[19,8,128]{2,1,0:T(8,128)S(1)} %collective-permute-done.1), channel_id=1, source_target_pairs={{0,2},{1,3},{2,0},{3,1},{4,6},{5,7},{6,4},{7,5},{8,10},{9,11},{10,... | collective-permute-start | bytes 233480 | tf_op jit(solution)/shard_map/ppermute | solution.py:164
  19.1 2.1 %collective-permute-start.7 = (f32[152,8,128]{2,1,0:T(8,128)S(1)}, f32[152,8,128]{2,1,0:T(8,128)S(1)}, u32[]{:S(2)}, u32[]{:S(2)}) collective-permute-start(f32[152,8,128]{2,1,0:T(8,128)S(1)} %constant_dynamic-update-slice_fusion.mine_ref), channel_id=1, source_target_pairs={{0,1},{1,0},{2,3},{3,2},{4,5},{5,4},{6,7},{7,6},{8,9},{9,8},{10,11... | collective-permute-start | bytes 1867784 | tf_op jit(solution)/shard_map/ppermute | solution.py:164

commit v9 on v8

--- a/solution.py
+++ b/solution.py
@@ -181,10 +181,10 @@
     )(*(pltpu.with_memory_space_constraint(array, pltpu.HBM) for array in inputs))
     far, near, side = devices // 2, devices // 4, devices // 8
     held = {0: packed}
-    for offset in (far, near, far | near | side, far | near, side):
+    for offset in (far, near, side, far | near | side):
         held[offset] = swap(packed, offset)
-    for offset in (near, far):
-        held[offset | side] = swap(held[offset], side)
+    for source, step in ((far, side), (near, side), (far, near)):
+        held[source | step] = swap(held[source], step)
     offsets = list(held)
     mine = jnp.concatenate(list(held.values()), axis=0)
     theirs = swap(mine, 1)

time: 24.8 us -> 22.7 us (0.915)
  starting transfers between devices: 13.2 us -> 11.2 us
    ppermute x8, starting transfers between devices: 13.2 us -> 11.2 us  [swap(): lax.ppermute(value, 'wide', [(i, i ^ offset) for i in range(devices)])]
where the time goes in v9:
time: 22.7 us; the launch traced here: 22.5 us
  starting transfers between devices  11.2 us (49%)
  waiting for transfers between devices  6.4 us (28%)
  Pallas kernels  4.22 us (19%)
  between operations  0.69 us (3%)
    ppermute x8, starting transfers between devices, swap(): lax.ppermute(value, 'wide', [(i, i ^ offset) for i in range(devices)])  11.2 us
    ppermute x8, waiting for transfers between devices, swap(): lax.ppermute(value, 'wide', [(i, i ^ offset) for i in range(devices)])  6.4 us
    pallas_call x1, Pallas kernels, small_body(): pl.pallas_call(functools.partial(group_kernel, offsets, per_dev), out_sha...  3.33 us
    pallas_call x1, Pallas kernels, small_body(): pl.pallas_call(pack_kernel, out_shape=f32((tiles, SUBLANES, LANES)), in_s...  0.89 us
  transfers between devices with their start and end apart: 8, of which 4 were waited for; matrix products, arithmetic and copies ran while one was open for 0% of the time, Pallas kernels for 0%

profile of v9, /device:TPU:0, one launch (start us, length us, event | category | flops | bytes accessed | tf_op | source)
XLA Modules:
  0.0 22.5 jit_solution(15947821279649198554)
XLA Ops:
  0.6 0.9 %pack.1 = f32[19,8,128]{2,1,0:T(8,128)S(1)} custom-call(f32[24,384]{1,0:T(8,128)} %bitcast.6, s32[24,384]{1,0:T(8,128)} %bitcast.7, f32[16,24]{1,0:T(8,128)} %bitcast.8), custom_call_target="tpu_custom_call" | custom-call | tf_op jit(solution)/shard_map/pack/pallas_call | solution.py:168
  1.5 4.1 %collective-permute-start = (f32[19,8,128]{2,1,0:T(8,128)S(1)}, f32[19,8,128]{2,1,0:T(8,128)S(1)}, u32[]{:S(2)}, u32[]{:S(2)}) collective-permute-start(f32[19,8,128]{2,1,0:T(8,128)S(1)} %pack.1), channel_id=1, source_target_pairs={{0,8},{1,9},{2,10},{3,11},{4,12},{5,13},{6,14},{7,15},{8,0},{9,1},... | collective-permute-start | bytes 233480 | tf_op jit(solution)/shard_map/ppermute | solution.py:164
  5.6 1.6 %collective-permute-start.1 = (f32[19,8,128]{2,1,0:T(8,128)S(1)}, f32[19,8,128]{2,1,0:T(8,128)S(1)}, u32[]{:S(2)}, u32[]{:S(2)}) collective-permute-start(f32[19,8,128]{2,1,0:T(8,128)S(1)} %pack.1), channel_id=1, source_target_pairs={{0,4},{1,5},{2,6},{3,7},{4,0},{5,1},{6,2},{7,3},{8,12},{9,13},{10,... | collective-permute-start | bytes 233480 | tf_op jit(solution)/shard_map/ppermute | solution.py:164
  7.2 1.5 %collective-permute-start.2 = (f32[19,8,128]{2,1,0:T(8,128)S(1)}, f32[19,8,128]{2,1,0:T(8,128)S(1)}, u32[]{:S(2)}, u32[]{:S(2)}) collective-permute-start(f32[19,8,128]{2,1,0:T(8,128)S(1)} %pack.1), channel_id=1, source_target_pairs={{0,2},{1,3},{2,0},{3,1},{4,6},{5,7},{6,4},{7,5},{8,10},{9,11},{10,... | collective-permute-start | bytes 233480 | tf_op jit(solution)/shard_map/ppermute | solution.py:164
  8.7 0.0 collective-permute-start.3
  8.7 0.4 %collective-permute-done = f32[19,8,128]{2,1,0:T(8,128)S(1)} collective-permute-done((f32[19,8,128]{2,1,0:T(8,128)S(1)}, f32[19,8,128]{2,1,0:T(8,128)S(1)}, u32[]{:S(2)}, u32[]{:S(2)}) %collective-permute-start) | collective-permute-done | bytes 77856 | tf_op jit(solution)/shard_map/ppermute | solution.py:164
  9.1 1.9 %collective-permute-start.4 = (f32[19,8,128]{2,1,0:T(8,128)S(1)}, f32[19,8,128]{2,1,0:T(8,128)S(1)}, u32[]{:S(2)}, u32[]{:S(2)}) collective-permute-start(f32[19,8,128]{2,1,0:T(8,128)S(1)} %collective-permute-done), channel_id=1, source_target_pairs={{0,2},{1,3},{2,0},{3,1},{4,6},{5,7},{6,4},{7,5},{8,10},{9,11},{10,... | collective-permute-start | bytes 233480 | tf_op jit(solution)/shard_map/ppermute | solution.py:164
  11.1 1.4 %collective-permute-start.6 = (f32[19,8,128]{2,1,0:T(8,128)S(1)}, f32[19,8,128]{2,1,0:T(8,128)S(1)}, u32[]{:S(2)}, u32[]{:S(2)}) collective-permute-start(f32[19,8,128]{2,1,0:T(8,128)S(1)} %collective-permute-done), channel_id=1, source_target_pairs={{0,4},{1,5},{2,6},{3,7},{4,0},{5,1},{6,2},{7,3},{8,12},{9,13},{10,... | collective-permute-start | bytes 233480 | tf_op jit(solution)/shard_map/ppermute | solution.py:164
  12.5 0.0 collective-permute-done.1
  12.5 0.6 %collective-permute-start.5 = (f32[19,8,128]{2,1,0:T(8,128)S(1)}, f32[19,8,128]{2,1,0:T(8,128)S(1)}, u32[]{:S(2)}, u32[]{:S(2)}) collective-permute-start(f32[19,8,128]{2,1,0:T(8,128)S(1)} %collective-permute-done.1), channel_id=1, source_target_pairs={{0,2},{1,3},{2,0},{3,1},{4,6},{5,7},{6,4},{7,5},{8,10},{9,11},{10,... | collective-permute-start | bytes 233480 | tf_op jit(solution)/shard_map/ppermute | solution.py:164
  13.1 0.0 collective-permute-done.2
  13.1 3.2 %collective-permute-done.3 = f32[19,8,128]{2,1,0:T(8,128)S(1)} collective-permute-done((f32[19,8,128]{2,1,0:T(8,128)S(1)}, f32[19,8,128]{2,1,0:T(8,128)S(1)}, u32[]{:S(2)}, u32[]{:S(2)}) %collective-permute-start.3) | collective-permute-done | bytes 77856 | tf_op jit(solution)/shard_map/ppermute | solution.py:164
  16.4 0.0 collective-permute-done.4
  16.4 0.7 %collective-permute-done.5 = f32[19,8,128]{2,1,0:T(8,128)S(1)} collective-permute-done((f32[19,8,128]{2,1,0:T(8,128)S(1)}, f32[19,8,128]{2,1,0:T(8,128)S(1)}, u32[]{:S(2)}, u32[]{:S(2)}) %collective-permute-start.5) | collective-permute-done | bytes 77856 | tf_op jit(solution)/shard_map/ppermute | solution.py:164
  17.1 0.0 collective-permute-done.6
  17.1 0.1 collective-permute-start.7
  17.2 2.0 %collective-permute-done.7.theirs_ref = f32[152,8,128]{2,1,0:T(8,128)S(1)} collective-permute-done((f32[152,8,128]{2,1,0:T(8,128)S(1)}, f32[152,8,128]{2,1,0:T(8,128)S(1)}, u32[]{:S(2)}, u32[]{:S(2)}) %collective-permute-start.7) | collective-permute-done | bytes 622624 | tf_op jit(solution)/shard_map/ppermute | solution.py:164
  19.2 3.3 %group_smacof.1 = (f32[16,24]{1,0:T(8,128)}, f32[3]{0:T(128)}) custom-call(f32[152,8,128]{2,1,0:T(8,128)S(1)} %constant_dynamic-update-slice_fusion.mine_ref, f32[152,8,128]{2,1,0:T(8,128)S(1)} %collective-permute-done.7.theirs_ref), custom_call_target="tpu_custom_call" | custom-call | tf_op jit(solution)/shard_map/group_smacof/pallas_call | solution.py:191
  (8 shorter events, 0.1 us)
Async XLA Ops:
  1.5 7.6 %collective-permute-start = (f32[19,8,128]{2,1,0:T(8,128)S(1)}, f32[19,8,128]{2,1,0:T(8,128)S(1)}, u32[]{:S(2)}, u32[]{:S(2)}) collective-permute-start(f32[19,8,128]{2,1,0:T(8,128)S(1)} %pack.1), channel_id=1, source_target_pairs={{0,8},{1,9},{2,10},{3,11},{4,12},{5,13},{6,14},{7,15},{8,0},{9,1},... | collective-permute-start | bytes 233480 | tf_op jit(solution)/shard_map/ppermute | solution.py:164
  5.6 6.8 %collective-permute-start.1 = (f32[19,8,128]{2,1,0:T(8,128)S(1)}, f32[19,8,128]{2,1,0:T(8,128)S(1)}, u32[]{:S(2)}, u32[]{:S(2)}) collective-permute-start(f32[19,8,128]{2,1,0:T(8,128)S(1)} %pack.1), channel_id=1, source_target_pairs={{0,4},{1,5},{2,6},{3,7},{4,0},{5,1},{6,2},{7,3},{8,12},{9,13},{10,... | collective-permute-start | bytes 233480 | tf_op jit(solution)/shard_map/ppermute | solution.py:164
  7.2 5.9 %collective-permute-start.2 = (f32[19,8,128]{2,1,0:T(8,128)S(1)}, f32[19,8,128]{2,1,0:T(8,128)S(1)}, u32[]{:S(2)}, u32[]{:S(2)}) collective-permute-start(f32[19,8,128]{2,1,0:T(8,128)S(1)} %pack.1), channel_id=1, source_target_pairs={{0,2},{1,3},{2,0},{3,1},{4,6},{5,7},{6,4},{7,5},{8,10},{9,11},{10,... | collective-permute-start | bytes 233480 | tf_op jit(solution)/shard_map/ppermute | solution.py:164
  8.7 7.7 %collective-permute-start.3 = (f32[19,8,128]{2,1,0:T(8,128)S(1)}, f32[19,8,128]{2,1,0:T(8,128)S(1)}, u32[]{:S(2)}, u32[]{:S(2)}) collective-permute-start(f32[19,8,128]{2,1,0:T(8,128)S(1)} %pack.1), channel_id=1, source_target_pairs={{0,14},{1,15},{2,12},{3,13},{4,10},{5,11},{6,8},{7,9},{8,6},{9,7},... | collective-permute-start | bytes 233480 | tf_op jit(solution)/shard_map/ppermute | solution.py:164
  9.1 7.2 %collective-permute-start.4 = (f32[19,8,128]{2,1,0:T(8,128)S(1)}, f32[19,8,128]{2,1,0:T(8,128)S(1)}, u32[]{:S(2)}, u32[]{:S(2)}) collective-permute-start(f32[19,8,128]{2,1,0:T(8,128)S(1)} %collective-permute-done), channel_id=1, source_target_pairs={{0,2},{1,3},{2,0},{3,1},{4,6},{5,7},{6,4},{7,5},{8,10},{9,11},{10,... | collective-permute-start | bytes 233480 | tf_op jit(solution)/shard_map/ppermute | solution.py:164
  11.1 6.0 %collective-permute-start.6 = (f32[19,8,128]{2,1,0:T(8,128)S(1)}, f32[19,8,128]{2,1,0:T(8,128)S(1)}, u32[]{:S(2)}, u32[]{:S(2)}) collective-permute-start(f32[19,8,128]{2,1,0:T(8,128)S(1)} %collective-permute-done), channel_id=1, source_target_pairs={{0,4},{1,5},{2,6},{3,7},{4,0},{5,1},{6,2},{7,3},{8,12},{9,13},{10,... | collective-permute-start | bytes 233480 | tf_op jit(solution)/shard_map/ppermute | solution.py:164
  12.5 4.6 %collective-permute-start.5 = (f32[19,8,128]{2,1,0:T(8,128)S(1)}, f32[19,8,128]{2,1,0:T(8,128)S(1)}, u32[]{:S(2)}, u32[]{:S(2)}) collective-permute-start(f32[19,8,128]{2,1,0:T(8,128)S(1)} %collective-permute-done.1), channel_id=1, source_target_pairs={{0,2},{1,3},{2,0},{3,1},{4,6},{5,7},{6,4},{7,5},{8,10},{9,11},{10,... | collective-permute-start | bytes 233480 | tf_op jit(solution)/shard_map/ppermute | solution.py:164
  17.1 2.1 %collective-permute-start.7 = (f32[152,8,128]{2,1,0:T(8,128)S(1)}, f32[152,8,128]{2,1,0:T(8,128)S(1)}, u32[]{:S(2)}, u32[]{:S(2)}) collective-permute-start(f32[152,8,128]{2,1,0:T(8,128)S(1)} %constant_dynamic-update-slice_fusion.mine_ref), channel_id=1, source_target_pairs={{0,1},{1,0},{2,3},{3,2},{4,5},{5,4},{6,7},{7,6},{8,9},{9,8},{10,11... | collective-permute-start | bytes 1867784 | tf_op jit(solution)/shard_map/ppermute | solution.py:164

commit v10 on v9

--- a/solution.py
+++ b/solution.py
@@ -75,39 +75,35 @@
             yield ref, slot * tiles, me ^ offset ^ bit
 
 
-def side_norm(top, bottom, coord_dims):
+def norm_rows(top, bottom, coord_dims):
     pad = jnp.zeros((coord_dims - 6, top[0].shape[1]), jnp.float32)
     rows = [p.astype(jnp.float32) for p in (*top, *bottom)]
     return jnp.concatenate([*rows, pad], axis=0).astype(jnp.bfloat16)
 
 
-def squares(own, x):
+def left_side(x, parts):
+    hi, mid, lo = (-2.0 * p for p in parts)
+    norm = split_bf16(jnp.sum(x * x, axis=0, keepdims=True), 3)
+    ones = [jnp.ones((3, x.shape[1]), jnp.bfloat16)]
+    return jnp.concatenate([hi, hi, hi, mid, mid, lo, norm_rows(norm, ones, x.shape[0])], axis=0)
+
+
+def right_side(x, parts):
+    hi, mid, lo = parts
+    norm = split_bf16(jnp.sum(x * x, axis=0, keepdims=True) + 1.0, 3)
+    ones = [jnp.ones((3, x.shape[1]), jnp.bfloat16)]
+    return jnp.concatenate([hi, mid, lo, hi, mid, hi, norm_rows(ones, norm, x.shape[0])], axis=0)
+
+
+def moved(x, sides, pull, scale):
     coord_dims = x.shape[0]
-    own_hi, own_mid, own_lo = (-2.0 * p for p in split_bf16(own, 3))
-    hi, mid, lo = split_bf16(x, 3)
-    own_norm = split_bf16(jnp.sum(own * own, axis=0, keepdims=True), 3)
-    norm = split_bf16(jnp.sum(x * x, axis=0, keepdims=True) + 1.0, 3)
-    left_ones = [jnp.ones((3, own.shape[1]), jnp.bfloat16)]
-    right_ones = [jnp.ones((3, x.shape[1]), jnp.bfloat16)]
-    left = [own_hi, own_hi, own_hi, own_mid, own_mid, own_lo]
-    right = [hi, mid, lo, hi, mid, hi]
-    left = jnp.concatenate([*left, side_norm(own_norm, left_ones, coord_dims)], axis=0)
-    right = jnp.concatenate([*right, side_norm(right_ones, norm, coord_dims)], axis=0)
-    return dot(left, right, TN), hi, mid
-
-
-def moved(own, hi, mid, pull, scale):
-    coord_dims, count = own.shape
-    ones = jnp.ones((coord_dims, hi.shape[1]), jnp.bfloat16)
-    sides = jnp.concatenate([hi, mid, ones], axis=0)
-    sums = dot(jnp.concatenate(split_bf16(pull, 2), axis=0), sides, NT)
-    sums = (sums[:count] + sums[count:]).T
+    sums = sum(dot(sides, part, NT) for part in split_bf16(pull, 2))
     pulled = sums[:coord_dims] + sums[coord_dims : 2 * coord_dims]
-    return own + (pulled - own * sums[2 * coord_dims : 2 * coord_dims + 1]) * scale
+    return x + (pulled - x * sums[2 * coord_dims : 2 * coord_dims + 1]) * scale
 
 
 def group_kernel(offsets, per_dev, mine_ref, theirs_ref, out_ref, stress_ref,
-                 dis_ref, weight_ref, tile_ref, inverse_ref):
+                 dis_ref, weight_ref, tile_ref):
     points = dis_ref.shape[0]
     spots = tile_spots(per_dev, points)
     tiles = 2 * len(spots) + 1
@@ -123,32 +119,50 @@
         for low in (0, per_dev)
     ]
     x = jnp.concatenate(halves, axis=0)
-    weight = weight_ref[...]
-    ones = jnp.ones((x.shape[0], points), jnp.bfloat16)
-    scale = 1.0 / (1.0 + dot(weight.astype(jnp.bfloat16), ones, NT).T[0:1])
-    sums = [lane_sums(weight * dis_ref[...] * dis_ref[...])]
+    coord_dims = x.shape[0]
+    chunks = [slice(row, row + LANES) for row in range(0, points, LANES)]
+    ones = jnp.ones((coord_dims, points), jnp.bfloat16)
+    scales = [
+        1.0 / (1.0 + dot(ones, weight_ref[rows].astype(jnp.bfloat16), NT)[0:1]) for rows in chunks
+    ]
+    denom = sum(lane_sums(weight_ref[rows] * dis_ref[rows] * dis_ref[rows]) for rows in chunks)
+    place = lax.axis_index("wide")
+    own_rows = pl.ds(pl.multiple_of(place * per_dev, SUBLANES), per_dev)
+    shape = (points, per_dev)
+    pick = lax.broadcasted_iota(jnp.int32, shape, 0) - lax.broadcasted_iota(jnp.int32, shape, 1)
+    pick = (pick == place * per_dev).astype(jnp.float32).astype(jnp.bfloat16)
+    sums = [denom]
     for sweep in range(ITERS):
-        square, hi, mid = squares(x, x)
-        inverse = lax.rsqrt(square)
-        misfit = dis_ref[...] - square * inverse
-        weight = weight_ref[...]
-        sums.append(lane_sums(weight * misfit * misfit))
-        if sweep < ITERS - 1:
-            x = moved(x, hi, mid, weight - weight * dis_ref[...] * inverse, scale)
-    inverse_ref[...] = inverse
-    place = lax.axis_index("wide")
-    rows = pl.ds(pl.multiple_of(place * per_dev, SUBLANES), per_dev)
-    scaled = jnp.concatenate([x, jnp.broadcast_to(scale, (SUBLANES, points))], axis=0)
-    mine = jnp.zeros((scaled.shape[0], per_dev), jnp.float32)
-    for i in range(points // per_dev):
-        mine = jnp.where(place == i, scaled[:, i * per_dev : (i + 1) * per_dev], mine)
-    own, scale = mine[: x.shape[0]], mine[x.shape[0] : x.shape[0] + 1]
-    weight = weight_ref[rows, :]
-    pull = weight - weight * dis_ref[rows, :] * inverse_ref[rows, :]
-    out_ref[...] = moved(own, hi, mid, pull, scale)
+        parts = split_bf16(x, 3)
+        sides = jnp.concatenate([parts[0], parts[1], ones], axis=0)
+        left, right = left_side(x, parts), right_side(x, parts)
+        last = sweep == ITERS - 1
+        stress, following = 0.0, []
+        for rows, scale in zip(chunks, scales):
+            square = dot(left[:, rows], right, TN)
+            inverse = lax.rsqrt(square)
+            weight, dis = weight_ref[rows], dis_ref[rows]
+            misfit = dis - square * inverse
+            stress += lane_sums(weight * misfit * misfit)
+            if not last:
+                pull = weight - weight * dis * inverse
+                following.append(moved(x[:, rows], sides, pull, scale))
+        sums.append(stress)
+        if last:
+            own = dot(jnp.concatenate(parts, axis=0), pick, (((1,), (0,)), ((), ())))
+            own = sum(own[i * coord_dims : (i + 1) * coord_dims] for i in range(3))
+            inverse = lax.rsqrt(dot(left_side(own, split_bf16(own, 3)), right, TN))
+            weight = weight_ref[own_rows, :]
+            scale = 1.0 / (1.0 + dot(ones, weight.astype(jnp.bfloat16), NT)[0:1])
+            pull = weight - weight * dis_ref[own_rows, :] * inverse
+            out_ref[...] = moved(own, sides, pull, scale)
+        else:
+            x = jnp.concatenate(following, axis=1)
     total = jnp.sum(jnp.concatenate(sums, axis=0), axis=1, keepdims=True)
-    for sweep in range(ITERS):
-        stress_ref[sweep] = jnp.sum(total[sweep + 1 : sweep + 2] / total[0:1])
+    ratios = total[1:] / total[:1]
+    lanes = lax.broadcasted_iota(jnp.int32, (ITERS, LANES), 1)
+    lined = jnp.where(lanes == lax.broadcasted_iota(jnp.int32, (ITERS, LANES), 0), ratios, 0.0)
+    stress_ref[...] = jnp.sum(lined, axis=0, keepdims=True)[:, :ITERS]
 
 
 def small_body(dissim, classes, coords):
@@ -190,19 +204,18 @@
     theirs = swap(mine, 1)
     final, stress = pl.pallas_call(
         functools.partial(group_kernel, offsets, per_dev),
-        out_shape=(f32((coord_dims, per_dev)), f32((ITERS,))),
+        out_shape=(f32((coord_dims, per_dev)), f32((1, ITERS))),
         in_specs=[vmem, vmem],
-        out_specs=(vmem, pl.BlockSpec(memory_space=pltpu.SMEM)),
+        out_specs=(vmem, vmem),
         scratch_shapes=[
             pltpu.VMEM((points, points), jnp.float32),
             pltpu.VMEM((points, points), jnp.float32),
             pltpu.VMEM((devices, SUBLANES, LANES), jnp.float32),
-            pltpu.VMEM((points, points), jnp.float32),
         ],
         compiler_params=params,
         name="group_smacof",
     )(mine, theirs)
-    return (final[:, None, :], stress)
+    return (final[:, None, :], stress[0])
 
 
 def distributed_body(dissim, classes, coords):

time: 22.7 us -> 22.4 us (0.987)
  Pallas kernels: 4.22 us -> 3.91 us
    pallas_call x1, Pallas kernels: 3.33 us -> 3.02 us  [small_body(): pl.pallas_call(functools.partial(group_kernel, offsets, per_dev), out_sha...]
where the time goes in v10:
time: 22.4 us; the launch traced here: 22.2 us
  starting transfers between devices  11.2 us (50%)
  waiting for transfers between devices  6.4 us (29%)
  Pallas kernels  3.91 us (17%)
  between operations  0.69 us (3%)
    ppermute x8, starting transfers between devices, swap(): lax.ppermute(value, 'wide', [(i, i ^ offset) for i in range(devices)])  11.2 us
    ppermute x8, waiting for transfers between devices, swap(): lax.ppermute(value, 'wide', [(i, i ^ offset) for i in range(devices)])  6.4 us
    pallas_call x1, Pallas kernels, small_body(): pl.pallas_call(functools.partial(group_kernel, offsets, per_dev), out_sha...  3.02 us
    pallas_call x1, Pallas kernels, small_body(): pl.pallas_call(pack_kernel, out_shape=f32((tiles, SUBLANES, LANES)), in_s...  0.89 us
  transfers between devices with their start and end apart: 8, of which 4 were waited for; matrix products, arithmetic and copies ran while one was open for 0% of the time, Pallas kernels for 0%

profile of v10, /device:TPU:0, one launch (start us, length us, event | category | flops | bytes accessed | tf_op | source)
XLA Modules:
  0.0 22.2 jit_solution(3394344878275414219)
XLA Ops:
  0.6 0.9 %pack.1 = f32[19,8,128]{2,1,0:T(8,128)S(1)} custom-call(f32[24,384]{1,0:T(8,128)} %bitcast.7, s32[24,384]{1,0:T(8,128)} %bitcast.8, f32[16,24]{1,0:T(8,128)} %bitcast.9), custom_call_target="tpu_custom_call" | custom-call | tf_op jit(solution)/shard_map/pack/pallas_call | solution.py:182
  1.5 4.1 %collective-permute-start = (f32[19,8,128]{2,1,0:T(8,128)S(1)}, f32[19,8,128]{2,1,0:T(8,128)S(1)}, u32[]{:S(2)}, u32[]{:S(2)}) collective-permute-start(f32[19,8,128]{2,1,0:T(8,128)S(1)} %pack.1), channel_id=1, source_target_pairs={{0,8},{1,9},{2,10},{3,11},{4,12},{5,13},{6,14},{7,15},{8,0},{9,1},... | collective-permute-start | bytes 233480 | tf_op jit(solution)/shard_map/ppermute | solution.py:178
  5.6 1.6 %collective-permute-start.1 = (f32[19,8,128]{2,1,0:T(8,128)S(1)}, f32[19,8,128]{2,1,0:T(8,128)S(1)}, u32[]{:S(2)}, u32[]{:S(2)}) collective-permute-start(f32[19,8,128]{2,1,0:T(8,128)S(1)} %pack.1), channel_id=1, source_target_pairs={{0,4},{1,5},{2,6},{3,7},{4,0},{5,1},{6,2},{7,3},{8,12},{9,13},{10,... | collective-permute-start | bytes 233480 | tf_op jit(solution)/shard_map/ppermute | solution.py:178
  7.2 1.5 %collective-permute-start.2 = (f32[19,8,128]{2,1,0:T(8,128)S(1)}, f32[19,8,128]{2,1,0:T(8,128)S(1)}, u32[]{:S(2)}, u32[]{:S(2)}) collective-permute-start(f32[19,8,128]{2,1,0:T(8,128)S(1)} %pack.1), channel_id=1, source_target_pairs={{0,2},{1,3},{2,0},{3,1},{4,6},{5,7},{6,4},{7,5},{8,10},{9,11},{10,... | collective-permute-start | bytes 233480 | tf_op jit(solution)/shard_map/ppermute | solution.py:178
  8.7 0.0 collective-permute-start.3
  8.7 0.4 %collective-permute-done = f32[19,8,128]{2,1,0:T(8,128)S(1)} collective-permute-done((f32[19,8,128]{2,1,0:T(8,128)S(1)}, f32[19,8,128]{2,1,0:T(8,128)S(1)}, u32[]{:S(2)}, u32[]{:S(2)}) %collective-permute-start) | collective-permute-done | bytes 77856 | tf_op jit(solution)/shard_map/ppermute | solution.py:178
  9.1 1.9 %collective-permute-start.4 = (f32[19,8,128]{2,1,0:T(8,128)S(1)}, f32[19,8,128]{2,1,0:T(8,128)S(1)}, u32[]{:S(2)}, u32[]{:S(2)}) collective-permute-start(f32[19,8,128]{2,1,0:T(8,128)S(1)} %collective-permute-done), channel_id=1, source_target_pairs={{0,2},{1,3},{2,0},{3,1},{4,6},{5,7},{6,4},{7,5},{8,10},{9,11},{10,... | collective-permute-start | bytes 233480 | tf_op jit(solution)/shard_map/ppermute | solution.py:178
  11.1 1.4 %collective-permute-start.6 = (f32[19,8,128]{2,1,0:T(8,128)S(1)}, f32[19,8,128]{2,1,0:T(8,128)S(1)}, u32[]{:S(2)}, u32[]{:S(2)}) collective-permute-start(f32[19,8,128]{2,1,0:T(8,128)S(1)} %collective-permute-done), channel_id=1, source_target_pairs={{0,4},{1,5},{2,6},{3,7},{4,0},{5,1},{6,2},{7,3},{8,12},{9,13},{10,... | collective-permute-start | bytes 233480 | tf_op jit(solution)/shard_map/ppermute | solution.py:178
  12.5 0.0 collective-permute-done.1
  12.5 0.6 %collective-permute-start.5 = (f32[19,8,128]{2,1,0:T(8,128)S(1)}, f32[19,8,128]{2,1,0:T(8,128)S(1)}, u32[]{:S(2)}, u32[]{:S(2)}) collective-permute-start(f32[19,8,128]{2,1,0:T(8,128)S(1)} %collective-permute-done.1), channel_id=1, source_target_pairs={{0,2},{1,3},{2,0},{3,1},{4,6},{5,7},{6,4},{7,5},{8,10},{9,11},{10,... | collective-permute-start | bytes 233480 | tf_op jit(solution)/shard_map/ppermute | solution.py:178
  13.1 0.0 collective-permute-done.2
  13.1 3.2 %collective-permute-done.3 = f32[19,8,128]{2,1,0:T(8,128)S(1)} collective-permute-done((f32[19,8,128]{2,1,0:T(8,128)S(1)}, f32[19,8,128]{2,1,0:T(8,128)S(1)}, u32[]{:S(2)}, u32[]{:S(2)}) %collective-permute-start.3) | collective-permute-done | bytes 77856 | tf_op jit(solution)/shard_map/ppermute | solution.py:178
  16.4 0.0 collective-permute-done.4
  16.4 0.7 %collective-permute-done.5 = f32[19,8,128]{2,1,0:T(8,128)S(1)} collective-permute-done((f32[19,8,128]{2,1,0:T(8,128)S(1)}, f32[19,8,128]{2,1,0:T(8,128)S(1)}, u32[]{:S(2)}, u32[]{:S(2)}) %collective-permute-start.5) | collective-permute-done | bytes 77856 | tf_op jit(solution)/shard_map/ppermute | solution.py:178
  17.1 0.0 collective-permute-done.6
  17.1 0.1 collective-permute-start.7
  17.2 2.0 %collective-permute-done.7.theirs_ref = f32[152,8,128]{2,1,0:T(8,128)S(1)} collective-permute-done((f32[152,8,128]{2,1,0:T(8,128)S(1)}, f32[152,8,128]{2,1,0:T(8,128)S(1)}, u32[]{:S(2)}, u32[]{:S(2)}) %collective-permute-start.7) | collective-permute-done | bytes 622624 | tf_op jit(solution)/shard_map/ppermute | solution.py:178
  19.2 3.0 %group_smacof.1 = (f32[16,24]{1,0:T(8,128)}, f32[1,3]{1,0:T(1,128)}) custom-call(f32[152,8,128]{2,1,0:T(8,128)S(1)} %constant_dynamic-update-slice_fusion.mine_ref, f32[152,8,128]{2,1,0:T(8,128)S(1)} %collective-permute-done.7.theirs_ref), custom_call_target="tpu_custom_call" | custom-call | tf_op jit(solution)/shard_map/group_smacof/pallas_call | solution.py:205
  (8 shorter events, 0.1 us)
Async XLA Ops:
  1.5 7.6 %collective-permute-start = (f32[19,8,128]{2,1,0:T(8,128)S(1)}, f32[19,8,128]{2,1,0:T(8,128)S(1)}, u32[]{:S(2)}, u32[]{:S(2)}) collective-permute-start(f32[19,8,128]{2,1,0:T(8,128)S(1)} %pack.1), channel_id=1, source_target_pairs={{0,8},{1,9},{2,10},{3,11},{4,12},{5,13},{6,14},{7,15},{8,0},{9,1},... | collective-permute-start | bytes 233480 | tf_op jit(solution)/shard_map/ppermute | solution.py:178
  5.6 6.8 %collective-permute-start.1 = (f32[19,8,128]{2,1,0:T(8,128)S(1)}, f32[19,8,128]{2,1,0:T(8,128)S(1)}, u32[]{:S(2)}, u32[]{:S(2)}) collective-permute-start(f32[19,8,128]{2,1,0:T(8,128)S(1)} %pack.1), channel_id=1, source_target_pairs={{0,4},{1,5},{2,6},{3,7},{4,0},{5,1},{6,2},{7,3},{8,12},{9,13},{10,... | collective-permute-start | bytes 233480 | tf_op jit(solution)/shard_map/ppermute | solution.py:178
  7.2 5.9 %collective-permute-start.2 = (f32[19,8,128]{2,1,0:T(8,128)S(1)}, f32[19,8,128]{2,1,0:T(8,128)S(1)}, u32[]{:S(2)}, u32[]{:S(2)}) collective-permute-start(f32[19,8,128]{2,1,0:T(8,128)S(1)} %pack.1), channel_id=1, source_target_pairs={{0,2},{1,3},{2,0},{3,1},{4,6},{5,7},{6,4},{7,5},{8,10},{9,11},{10,... | collective-permute-start | bytes 233480 | tf_op jit(solution)/shard_map/ppermute | solution.py:178
  8.7 7.7 %collective-permute-start.3 = (f32[19,8,128]{2,1,0:T(8,128)S(1)}, f32[19,8,128]{2,1,0:T(8,128)S(1)}, u32[]{:S(2)}, u32[]{:S(2)}) collective-permute-start(f32[19,8,128]{2,1,0:T(8,128)S(1)} %pack.1), channel_id=1, source_target_pairs={{0,14},{1,15},{2,12},{3,13},{4,10},{5,11},{6,8},{7,9},{8,6},{9,7},... | collective-permute-start | bytes 233480 | tf_op jit(solution)/shard_map/ppermute | solution.py:178
  9.1 7.2 %collective-permute-start.4 = (f32[19,8,128]{2,1,0:T(8,128)S(1)}, f32[19,8,128]{2,1,0:T(8,128)S(1)}, u32[]{:S(2)}, u32[]{:S(2)}) collective-permute-start(f32[19,8,128]{2,1,0:T(8,128)S(1)} %collective-permute-done), channel_id=1, source_target_pairs={{0,2},{1,3},{2,0},{3,1},{4,6},{5,7},{6,4},{7,5},{8,10},{9,11},{10,... | collective-permute-start | bytes 233480 | tf_op jit(solution)/shard_map/ppermute | solution.py:178
  11.1 6.0 %collective-permute-start.6 = (f32[19,8,128]{2,1,0:T(8,128)S(1)}, f32[19,8,128]{2,1,0:T(8,128)S(1)}, u32[]{:S(2)}, u32[]{:S(2)}) collective-permute-start(f32[19,8,128]{2,1,0:T(8,128)S(1)} %collective-permute-done), channel_id=1, source_target_pairs={{0,4},{1,5},{2,6},{3,7},{4,0},{5,1},{6,2},{7,3},{8,12},{9,13},{10,... | collective-permute-start | bytes 233480 | tf_op jit(solution)/shard_map/ppermute | solution.py:178
  12.5 4.6 %collective-permute-start.5 = (f32[19,8,128]{2,1,0:T(8,128)S(1)}, f32[19,8,128]{2,1,0:T(8,128)S(1)}, u32[]{:S(2)}, u32[]{:S(2)}) collective-permute-start(f32[19,8,128]{2,1,0:T(8,128)S(1)} %collective-permute-done.1), channel_id=1, source_target_pairs={{0,2},{1,3},{2,0},{3,1},{4,6},{5,7},{6,4},{7,5},{8,10},{9,11},{10,... | collective-permute-start | bytes 233480 | tf_op jit(solution)/shard_map/ppermute | solution.py:178
  17.1 2.1 %collective-permute-start.7 = (f32[152,8,128]{2,1,0:T(8,128)S(1)}, f32[152,8,128]{2,1,0:T(8,128)S(1)}, u32[]{:S(2)}, u32[]{:S(2)}) collective-permute-start(f32[152,8,128]{2,1,0:T(8,128)S(1)} %constant_dynamic-update-slice_fusion.mine_ref), channel_id=1, source_target_pairs={{0,1},{1,0},{2,3},{3,2},{4,5},{5,4},{6,7},{7,6},{8,9},{9,8},{10,11... | collective-permute-start | bytes 1867784 | tf_op jit(solution)/shard_map/ppermute | solution.py:178

commit v11 on v10

--- a/solution.py
+++ b/solution.py
@@ -97,7 +97,8 @@
 
 def moved(x, sides, pull, scale):
     coord_dims = x.shape[0]
-    sums = sum(dot(sides, part, NT) for part in split_bf16(pull, 2))
+    parts = jnp.concatenate(split_bf16(pull, 2), axis=1)
+    sums = dot(parts, jnp.concatenate([sides, sides], axis=1), NT).T
     pulled = sums[:coord_dims] + sums[coord_dims : 2 * coord_dims]
     return x + (pulled - x * sums[2 * coord_dims : 2 * coord_dims + 1]) * scale
 
@@ -195,10 +196,10 @@
     )(*(pltpu.with_memory_space_constraint(array, pltpu.HBM) for array in inputs))
     far, near, side = devices // 2, devices // 4, devices // 8
     held = {0: packed}
-    for offset in (far, near, side, far | near | side):
+    for offset in (far, side, near, far | near | side, near | side):
         held[offset] = swap(packed, offset)
-    for source, step in ((far, side), (near, side), (far, near)):
-        held[source | step] = swap(held[source], step)
+    for step in (side, near):
+        held[far | step] = swap(held[far], step)
     offsets = list(held)
     mine = jnp.concatenate(list(held.values()), axis=0)
     theirs = swap(mine, 1)

time: 22.4 us -> 21.7 us (0.969)
  waiting for transfers between devices: 6.4 us -> 5.6 us
    ppermute x8, waiting for transfers between devices: 6.4 us -> 5.6 us  [swap(): lax.ppermute(value, 'wide', [(i, i ^ offset) for i in range(devices)])]
    ppermute x8, starting transfers between devices: 11.2 us -> 11.4 us  [swap(): lax.ppermute(value, 'wide', [(i, i ^ offset) for i in range(devices)])]
where the time goes in v11:
time: 21.7 us; the launch traced here: 21.5 us
  starting transfers between devices  11.4 us (53%)
  waiting for transfers between devices  5.6 us (26%)
  Pallas kernels  3.7 us (17%)
  between operations  0.68 us (3%)
    ppermute x8, starting transfers between devices, swap(): lax.ppermute(value, 'wide', [(i, i ^ offset) for i in range(devices)])  11.4 us
    ppermute x8, waiting for transfers between devices, swap(): lax.ppermute(value, 'wide', [(i, i ^ offset) for i in range(devices)])  5.6 us
    pallas_call x1, Pallas kernels, small_body(): pl.pallas_call(functools.partial(group_kernel, offsets, per_dev), out_sha...  2.81 us
    pallas_call x1, Pallas kernels, small_body(): pl.pallas_call(pack_kernel, out_shape=f32((tiles, SUBLANES, LANES)), in_s...  0.89 us
  transfers between devices with their start and end apart: 8, of which 4 were waited for; matrix products, arithmetic and copies ran while one was open for 0% of the time, Pallas kernels for 0%

profile of v11, /device:TPU:0, one launch (start us, length us, event | category | flops | bytes accessed | tf_op | source)
XLA Modules:
  0.0 21.5 jit_solution(8349440709560959685)
XLA Ops:
  0.6 0.9 %pack.1 = f32[19,8,128]{2,1,0:T(8,128)S(1)} custom-call(f32[24,384]{1,0:T(8,128)} %bitcast.7, s32[24,384]{1,0:T(8,128)} %bitcast.8, f32[16,24]{1,0:T(8,128)} %bitcast.9), custom_call_target="tpu_custom_call" | custom-call | tf_op jit(solution)/shard_map/pack/pallas_call | solution.py:183
  1.5 4.1 %collective-permute-start = (f32[19,8,128]{2,1,0:T(8,128)S(1)}, f32[19,8,128]{2,1,0:T(8,128)S(1)}, u32[]{:S(2)}, u32[]{:S(2)}) collective-permute-start(f32[19,8,128]{2,1,0:T(8,128)S(1)} %pack.1), channel_id=1, source_target_pairs={{0,8},{1,9},{2,10},{3,11},{4,12},{5,13},{6,14},{7,15},{8,0},{9,1},... | collective-permute-start | bytes 233480 | tf_op jit(solution)/shard_map/ppermute | solution.py:179
  5.6 1.5 %collective-permute-start.1 = (f32[19,8,128]{2,1,0:T(8,128)S(1)}, f32[19,8,128]{2,1,0:T(8,128)S(1)}, u32[]{:S(2)}, u32[]{:S(2)}) collective-permute-start(f32[19,8,128]{2,1,0:T(8,128)S(1)} %pack.1), channel_id=1, source_target_pairs={{0,2},{1,3},{2,0},{3,1},{4,6},{5,7},{6,4},{7,5},{8,10},{9,11},{10,... | collective-permute-start | bytes 233480 | tf_op jit(solution)/shard_map/ppermute | solution.py:179
  7.1 1.6 %collective-permute-start.2 = (f32[19,8,128]{2,1,0:T(8,128)S(1)}, f32[19,8,128]{2,1,0:T(8,128)S(1)}, u32[]{:S(2)}, u32[]{:S(2)}) collective-permute-start(f32[19,8,128]{2,1,0:T(8,128)S(1)} %pack.1), channel_id=1, source_target_pairs={{0,4},{1,5},{2,6},{3,7},{4,0},{5,1},{6,2},{7,3},{8,12},{9,13},{10,... | collective-permute-start | bytes 233480 | tf_op jit(solution)/shard_map/ppermute | solution.py:179
  8.7 0.0 collective-permute-start.3
  8.7 1.8 %collective-permute-start.4 = (f32[19,8,128]{2,1,0:T(8,128)S(1)}, f32[19,8,128]{2,1,0:T(8,128)S(1)}, u32[]{:S(2)}, u32[]{:S(2)}) collective-permute-start(f32[19,8,128]{2,1,0:T(8,128)S(1)} %pack.1), channel_id=1, source_target_pairs={{0,6},{1,7},{2,4},{3,5},{4,2},{5,3},{6,0},{7,1},{8,14},{9,15},{10,... | collective-permute-start | bytes 233480 | tf_op jit(solution)/shard_map/ppermute | solution.py:179
  10.5 0.0 collective-permute-done
  10.5 0.6 %collective-permute-start.5 = (f32[19,8,128]{2,1,0:T(8,128)S(1)}, f32[19,8,128]{2,1,0:T(8,128)S(1)}, u32[]{:S(2)}, u32[]{:S(2)}) collective-permute-start(f32[19,8,128]{2,1,0:T(8,128)S(1)} %collective-permute-done), channel_id=1, source_target_pairs={{0,2},{1,3},{2,0},{3,1},{4,6},{5,7},{6,4},{7,5},{8,10},{9,11},{10,... | collective-permute-start | bytes 233480 | tf_op jit(solution)/shard_map/ppermute | solution.py:179
  11.1 0.0 collective-permute-done.1
  11.1 1.8 %collective-permute-start.6 = (f32[19,8,128]{2,1,0:T(8,128)S(1)}, f32[19,8,128]{2,1,0:T(8,128)S(1)}, u32[]{:S(2)}, u32[]{:S(2)}) collective-permute-start(f32[19,8,128]{2,1,0:T(8,128)S(1)} %collective-permute-done), channel_id=1, source_target_pairs={{0,4},{1,5},{2,6},{3,7},{4,0},{5,1},{6,2},{7,3},{8,12},{9,13},{10,... | collective-permute-start | bytes 233480 | tf_op jit(solution)/shard_map/ppermute | solution.py:179
  12.9 0.0 collective-permute-done.2
  13.0 3.0 %collective-permute-done.3 = f32[19,8,128]{2,1,0:T(8,128)S(1)} collective-permute-done((f32[19,8,128]{2,1,0:T(8,128)S(1)}, f32[19,8,128]{2,1,0:T(8,128)S(1)}, u32[]{:S(2)}, u32[]{:S(2)}) %collective-permute-start.3) | collective-permute-done | bytes 77856 | tf_op jit(solution)/shard_map/ppermute | solution.py:179
  16.0 0.3 %collective-permute-done.4 = f32[19,8,128]{2,1,0:T(8,128)S(1)} collective-permute-done((f32[19,8,128]{2,1,0:T(8,128)S(1)}, f32[19,8,128]{2,1,0:T(8,128)S(1)}, u32[]{:S(2)}, u32[]{:S(2)}) %collective-permute-start.4) | collective-permute-done | bytes 77856 | tf_op jit(solution)/shard_map/ppermute | solution.py:179
  16.2 0.3 %collective-permute-done.5 = f32[19,8,128]{2,1,0:T(8,128)S(1)} collective-permute-done((f32[19,8,128]{2,1,0:T(8,128)S(1)}, f32[19,8,128]{2,1,0:T(8,128)S(1)}, u32[]{:S(2)}, u32[]{:S(2)}) %collective-permute-start.5) | collective-permute-done | bytes 77856 | tf_op jit(solution)/shard_map/ppermute | solution.py:179
  16.5 0.0 collective-permute-done.6
  16.6 0.1 collective-permute-start.7
  16.6 2.0 %collective-permute-done.7.theirs_ref = f32[152,8,128]{2,1,0:T(8,128)S(1)} collective-permute-done((f32[152,8,128]{2,1,0:T(8,128)S(1)}, f32[152,8,128]{2,1,0:T(8,128)S(1)}, u32[]{:S(2)}, u32[]{:S(2)}) %collective-permute-start.7) | collective-permute-done | bytes 622624 | tf_op jit(solution)/shard_map/ppermute | solution.py:179
  18.7 2.8 %group_smacof.1 = (f32[16,24]{1,0:T(8,128)}, f32[1,3]{1,0:T(1,128)}) custom-call(f32[152,8,128]{2,1,0:T(8,128)S(1)} %constant_dynamic-update-slice_fusion.mine_ref, f32[152,8,128]{2,1,0:T(8,128)S(1)} %collective-permute-done.7.theirs_ref), custom_call_target="tpu_custom_call" | custom-call | tf_op jit(solution)/shard_map/group_smacof/pallas_call | solution.py:206
  (8 shorter events, 0.1 us)
Async XLA Ops:
  1.5 9.0 %collective-permute-start = (f32[19,8,128]{2,1,0:T(8,128)S(1)}, f32[19,8,128]{2,1,0:T(8,128)S(1)}, u32[]{:S(2)}, u32[]{:S(2)}) collective-permute-start(f32[19,8,128]{2,1,0:T(8,128)S(1)} %pack.1), channel_id=1, source_target_pairs={{0,8},{1,9},{2,10},{3,11},{4,12},{5,13},{6,14},{7,15},{8,0},{9,1},... | collective-permute-start | bytes 233480 | tf_op jit(solution)/shard_map/ppermute | solution.py:179
  5.6 5.5 %collective-permute-start.1 = (f32[19,8,128]{2,1,0:T(8,128)S(1)}, f32[19,8,128]{2,1,0:T(8,128)S(1)}, u32[]{:S(2)}, u32[]{:S(2)}) collective-permute-start(f32[19,8,128]{2,1,0:T(8,128)S(1)} %pack.1), channel_id=1, source_target_pairs={{0,2},{1,3},{2,0},{3,1},{4,6},{5,7},{6,4},{7,5},{8,10},{9,11},{10,... | collective-permute-start | bytes 233480 | tf_op jit(solution)/shard_map/ppermute | solution.py:179
  7.1 5.8 %collective-permute-start.2 = (f32[19,8,128]{2,1,0:T(8,128)S(1)}, f32[19,8,128]{2,1,0:T(8,128)S(1)}, u32[]{:S(2)}, u32[]{:S(2)}) collective-permute-start(f32[19,8,128]{2,1,0:T(8,128)S(1)} %pack.1), channel_id=1, source_target_pairs={{0,4},{1,5},{2,6},{3,7},{4,0},{5,1},{6,2},{7,3},{8,12},{9,13},{10,... | collective-permute-start | bytes 233480 | tf_op jit(solution)/shard_map/ppermute | solution.py:179
  8.7 7.2 %collective-permute-start.3 = (f32[19,8,128]{2,1,0:T(8,128)S(1)}, f32[19,8,128]{2,1,0:T(8,128)S(1)}, u32[]{:S(2)}, u32[]{:S(2)}) collective-permute-start(f32[19,8,128]{2,1,0:T(8,128)S(1)} %pack.1), channel_id=1, source_target_pairs={{0,14},{1,15},{2,12},{3,13},{4,10},{5,11},{6,8},{7,9},{8,6},{9,7},... | collective-permute-start | bytes 233480 | tf_op jit(solution)/shard_map/ppermute | solution.py:179
  8.7 7.5 %collective-permute-start.4 = (f32[19,8,128]{2,1,0:T(8,128)S(1)}, f32[19,8,128]{2,1,0:T(8,128)S(1)}, u32[]{:S(2)}, u32[]{:S(2)}) collective-permute-start(f32[19,8,128]{2,1,0:T(8,128)S(1)} %pack.1), channel_id=1, source_target_pairs={{0,6},{1,7},{2,4},{3,5},{4,2},{5,3},{6,0},{7,1},{8,14},{9,15},{10,... | collective-permute-start | bytes 233480 | tf_op jit(solution)/shard_map/ppermute | solution.py:179
  10.5 6.0 %collective-permute-start.5 = (f32[19,8,128]{2,1,0:T(8,128)S(1)}, f32[19,8,128]{2,1,0:T(8,128)S(1)}, u32[]{:S(2)}, u32[]{:S(2)}) collective-permute-start(f32[19,8,128]{2,1,0:T(8,128)S(1)} %collective-permute-done), channel_id=1, source_target_pairs={{0,2},{1,3},{2,0},{3,1},{4,6},{5,7},{6,4},{7,5},{8,10},{9,11},{10,... | collective-permute-start | bytes 233480 | tf_op jit(solution)/shard_map/ppermute | solution.py:179
  11.1 5.4 %collective-permute-start.6 = (f32[19,8,128]{2,1,0:T(8,128)S(1)}, f32[19,8,128]{2,1,0:T(8,128)S(1)}, u32[]{:S(2)}, u32[]{:S(2)}) collective-permute-start(f32[19,8,128]{2,1,0:T(8,128)S(1)} %collective-permute-done), channel_id=1, source_target_pairs={{0,4},{1,5},{2,6},{3,7},{4,0},{5,1},{6,2},{7,3},{8,12},{9,13},{10,... | collective-permute-start | bytes 233480 | tf_op jit(solution)/shard_map/ppermute | solution.py:179
  16.6 2.1 %collective-permute-start.7 = (f32[152,8,128]{2,1,0:T(8,128)S(1)}, f32[152,8,128]{2,1,0:T(8,128)S(1)}, u32[]{:S(2)}, u32[]{:S(2)}) collective-permute-start(f32[152,8,128]{2,1,0:T(8,128)S(1)} %constant_dynamic-update-slice_fusion.mine_ref), channel_id=1, source_target_pairs={{0,1},{1,0},{2,3},{3,2},{4,5},{5,4},{6,7},{7,6},{8,9},{9,8},{10,11... | collective-permute-start | bytes 1867784 | tf_op jit(solution)/shard_map/ppermute | solution.py:179

commit v12 on v11

--- a/solution.py
+++ b/solution.py
@@ -70,8 +70,10 @@
 
 def held_slots(offsets, refs, tiles):
     me = lax.axis_index("wide")
+    core = lax.rem(me, 2)
     for bit, ref in enumerate(refs):
-        for slot, offset in enumerate(offsets):
+        for slot, pair in enumerate(zip(*offsets)):
+            offset = pair[bit] + core * (pair[1 - bit] - pair[bit])
             yield ref, slot * tiles, me ^ offset ^ bit
 
 
@@ -175,8 +177,8 @@
     f32 = functools.partial(jax.ShapeDtypeStruct, dtype=jnp.float32)
     params = pltpu.CompilerParams(vmem_limit_bytes=16 << 20)
 
-    def swap(value, offset):
-        return lax.ppermute(value, "wide", [(i, i ^ offset) for i in range(devices)])
+    def swap(value, steps):
+        return lax.ppermute(value, "wide", [(i, i ^ steps[i % 2]) for i in range(devices)])
 
     tiles = 2 * len(tile_spots(per_dev, points)) + 1
     inputs = (dissim[0], classes[0], coords[:, 0, :])
@@ -195,14 +197,18 @@
         name="pack",
     )(*(pltpu.with_memory_space_constraint(array, pltpu.HBM) for array in inputs))
     far, near, side = devices // 2, devices // 4, devices // 8
-    held = {0: packed}
-    for offset in (far, side, near, far | near | side, near | side):
-        held[offset] = swap(packed, offset)
-    for step in (side, near):
-        held[far | step] = swap(held[far], step)
-    offsets = list(held)
-    mine = jnp.concatenate(list(held.values()), axis=0)
-    theirs = swap(mine, 1)
+    firsts = (
+        (far | side, near, near | side, far | near, side),
+        (far | near, near, side, far | side, near | side),
+    )
+    relays = ((near, side), (side, near))
+    held = [packed] + [swap(packed, steps) for steps in zip(*firsts)]
+    held += [swap(held[1], steps) for steps in zip(*relays)]
+    offsets = [
+        (0, *first, *(first[0] ^ step for step in relay)) for first, relay in zip(firsts, relays)
+    ]
+    mine = jnp.concatenate(held, axis=0)
+    theirs = swap(mine, (1, 1))
     final, stress = pl.pallas_call(
         functools.partial(group_kernel, offsets, per_dev),
         out_shape=(f32((coord_dims, per_dev)), f32((1, ITERS))),

time: 21.7 us -> 21.7 us (level)
  transfers between devices with their start and end apart: 8 -> 8, of which waited for: 4 -> 6; matrix products, arithmetic and copies ran while one was open for 0% -> 0% of each run, Pallas kernels for 0% -> 0%
where the time goes in v12:
time: 21.7 us; the launch traced here: 21.5 us
  starting transfers between devices  11.4 us (53%)
  waiting for transfers between devices  5.72 us (26%)
  Pallas kernels  3.7 us (17%)
  between operations  0.66 us (3%)
    ppermute x8, starting transfers between devices, swap(): lax.ppermute(value, 'wide', [(i, i ^ steps[i % 2]) for i in range(devices)])  11.4 us
    ppermute x8, waiting for transfers between devices, swap(): lax.ppermute(value, 'wide', [(i, i ^ steps[i % 2]) for i in range(devices)])  5.72 us
    pallas_call x1, Pallas kernels, small_body(): pl.pallas_call(functools.partial(group_kernel, offsets, per_dev), out_sha...  2.81 us
    pallas_call x1, Pallas kernels, small_body(): pl.pallas_call(pack_kernel, out_shape=f32((tiles, SUBLANES, LANES)), in_s...  0.89 us
  transfers between devices with their start and end apart: 8, of which 6 were waited for; matrix products, arithmetic and copies ran while one was open for 0% of the time, Pallas kernels for 0%

profile of v12, /device:TPU:0, one launch (start us, length us, event | category | flops | bytes accessed | tf_op | source)
XLA Modules:
  0.0 21.5 jit_solution(7018231058265105214)
XLA Ops:
  0.6 0.9 %pack.1 = f32[19,8,128]{2,1,0:T(8,128)S(1)} custom-call(f32[24,384]{1,0:T(8,128)} %bitcast.7, s32[24,384]{1,0:T(8,128)} %bitcast.8, f32[16,24]{1,0:T(8,128)} %bitcast.9), custom_call_target="tpu_custom_call" | custom-call | tf_op jit(solution)/shard_map/pack/pallas_call | solution.py:185
  1.5 5.0 %collective-permute-start = (f32[19,8,128]{2,1,0:T(8,128)S(1)}, f32[19,8,128]{2,1,0:T(8,128)S(1)}, u32[]{:S(2)}, u32[]{:S(2)}) collective-permute-start(f32[19,8,128]{2,1,0:T(8,128)S(1)} %pack.1), channel_id=1, source_target_pairs={{0,10},{1,13},{2,8},{3,15},{4,14},{5,9},{6,12},{7,11},{8,2},{9,5},... | collective-permute-start | bytes 233480 | tf_op jit(solution)/shard_map/ppermute | solution.py:181
  6.6 1.6 %collective-permute-start.1 = (f32[19,8,128]{2,1,0:T(8,128)S(1)}, f32[19,8,128]{2,1,0:T(8,128)S(1)}, u32[]{:S(2)}, u32[]{:S(2)}) collective-permute-start(f32[19,8,128]{2,1,0:T(8,128)S(1)} %pack.1), channel_id=1, source_target_pairs={{0,4},{1,5},{2,6},{3,7},{4,0},{5,1},{6,2},{7,3},{8,12},{9,13},{10,... | collective-permute-start | bytes 233480 | tf_op jit(solution)/shard_map/ppermute | solution.py:181
  8.1 0.4 %collective-permute-start.2 = (f32[19,8,128]{2,1,0:T(8,128)S(1)}, f32[19,8,128]{2,1,0:T(8,128)S(1)}, u32[]{:S(2)}, u32[]{:S(2)}) collective-permute-start(f32[19,8,128]{2,1,0:T(8,128)S(1)} %pack.1), channel_id=1, source_target_pairs={{0,6},{1,3},{2,4},{3,1},{4,2},{5,7},{6,0},{7,5},{8,14},{9,11},{10,... | collective-permute-start | bytes 233480 | tf_op jit(solution)/shard_map/ppermute | solution.py:181
  8.6 1.3 %collective-permute-start.3 = (f32[19,8,128]{2,1,0:T(8,128)S(1)}, f32[19,8,128]{2,1,0:T(8,128)S(1)}, u32[]{:S(2)}, u32[]{:S(2)}) collective-permute-start(f32[19,8,128]{2,1,0:T(8,128)S(1)} %pack.1), channel_id=1, source_target_pairs={{0,12},{1,11},{2,14},{3,9},{4,8},{5,15},{6,10},{7,13},{8,4},{9,3},... | collective-permute-start | bytes 233480 | tf_op jit(solution)/shard_map/ppermute | solution.py:181
  9.9 1.5 %collective-permute-start.4 = (f32[19,8,128]{2,1,0:T(8,128)S(1)}, f32[19,8,128]{2,1,0:T(8,128)S(1)}, u32[]{:S(2)}, u32[]{:S(2)}) collective-permute-start(f32[19,8,128]{2,1,0:T(8,128)S(1)} %pack.1), channel_id=1, source_target_pairs={{0,2},{1,7},{2,0},{3,5},{4,6},{5,3},{6,4},{7,1},{8,10},{9,15},{10,... | collective-permute-start | bytes 233480 | tf_op jit(solution)/shard_map/ppermute | solution.py:181
  11.4 0.0 collective-permute-done
  11.4 0.7 %collective-permute-start.5 = (f32[19,8,128]{2,1,0:T(8,128)S(1)}, f32[19,8,128]{2,1,0:T(8,128)S(1)}, u32[]{:S(2)}, u32[]{:S(2)}) collective-permute-start(f32[19,8,128]{2,1,0:T(8,128)S(1)} %collective-permute-done), channel_id=1, source_target_pairs={{0,4},{1,3},{2,6},{3,1},{4,0},{5,7},{6,2},{7,5},{8,12},{9,11},{10,... | collective-permute-start | bytes 233480 | tf_op jit(solution)/shard_map/ppermute | solution.py:181
  12.2 0.0 collective-permute-done.1
  12.2 0.7 %collective-permute-start.6 = (f32[19,8,128]{2,1,0:T(8,128)S(1)}, f32[19,8,128]{2,1,0:T(8,128)S(1)}, u32[]{:S(2)}, u32[]{:S(2)}) collective-permute-start(f32[19,8,128]{2,1,0:T(8,128)S(1)} %collective-permute-done), channel_id=1, source_target_pairs={{0,2},{1,5},{2,0},{3,7},{4,6},{5,1},{6,4},{7,3},{8,10},{9,13},{10,... | collective-permute-start | bytes 233480 | tf_op jit(solution)/shard_map/ppermute | solution.py:181
  12.9 1.4 %collective-permute-done.2 = f32[19,8,128]{2,1,0:T(8,128)S(1)} collective-permute-done((f32[19,8,128]{2,1,0:T(8,128)S(1)}, f32[19,8,128]{2,1,0:T(8,128)S(1)}, u32[]{:S(2)}, u32[]{:S(2)}) %collective-permute-start.2) | collective-permute-done | bytes 77856 | tf_op jit(solution)/shard_map/ppermute | solution.py:181
  14.3 0.6 %collective-permute-done.3 = f32[19,8,128]{2,1,0:T(8,128)S(1)} collective-permute-done((f32[19,8,128]{2,1,0:T(8,128)S(1)}, f32[19,8,128]{2,1,0:T(8,128)S(1)}, u32[]{:S(2)}, u32[]{:S(2)}) %collective-permute-start.3) | collective-permute-done | bytes 77856 | tf_op jit(solution)/shard_map/ppermute | solution.py:181
  14.9 0.8 %collective-permute-done.4 = f32[19,8,128]{2,1,0:T(8,128)S(1)} collective-permute-done((f32[19,8,128]{2,1,0:T(8,128)S(1)}, f32[19,8,128]{2,1,0:T(8,128)S(1)}, u32[]{:S(2)}, u32[]{:S(2)}) %collective-permute-start.4) | collective-permute-done | bytes 77856 | tf_op jit(solution)/shard_map/ppermute | solution.py:181
  15.7 0.3 %collective-permute-done.5 = f32[19,8,128]{2,1,0:T(8,128)S(1)} collective-permute-done((f32[19,8,128]{2,1,0:T(8,128)S(1)}, f32[19,8,128]{2,1,0:T(8,128)S(1)}, u32[]{:S(2)}, u32[]{:S(2)}) %collective-permute-start.5) | collective-permute-done | bytes 77856 | tf_op jit(solution)/shard_map/ppermute | solution.py:181
  16.0 0.6 %collective-permute-done.6 = f32[19,8,128]{2,1,0:T(8,128)S(1)} collective-permute-done((f32[19,8,128]{2,1,0:T(8,128)S(1)}, f32[19,8,128]{2,1,0:T(8,128)S(1)}, u32[]{:S(2)}, u32[]{:S(2)}) %collective-permute-start.6) | collective-permute-done | bytes 77856 | tf_op jit(solution)/shard_map/ppermute | solution.py:181
  16.6 0.0 collective-permute-start.7
  16.6 2.0 %collective-permute-done.7.theirs_ref = f32[152,8,128]{2,1,0:T(8,128)S(1)} collective-permute-done((f32[152,8,128]{2,1,0:T(8,128)S(1)}, f32[152,8,128]{2,1,0:T(8,128)S(1)}, u32[]{:S(2)}, u32[]{:S(2)}) %collective-permute-start.7) | collective-permute-done | bytes 622624 | tf_op jit(solution)/shard_map/ppermute | solution.py:181
  18.7 2.8 %group_smacof.1 = (f32[16,24]{1,0:T(8,128)}, f32[1,3]{1,0:T(1,128)}) custom-call(f32[152,8,128]{2,1,0:T(8,128)S(1)} %constant_dynamic-update-slice_fusion.mine_ref, f32[152,8,128]{2,1,0:T(8,128)S(1)} %collective-permute-done.7.theirs_ref), custom_call_target="tpu_custom_call" | custom-call | tf_op jit(solution)/shard_map/group_smacof/pallas_call | solution.py:212
  (8 shorter events, 0.1 us)
Async XLA Ops:
  1.5 9.9 %collective-permute-start = (f32[19,8,128]{2,1,0:T(8,128)S(1)}, f32[19,8,128]{2,1,0:T(8,128)S(1)}, u32[]{:S(2)}, u32[]{:S(2)}) collective-permute-start(f32[19,8,128]{2,1,0:T(8,128)S(1)} %pack.1), channel_id=1, source_target_pairs={{0,10},{1,13},{2,8},{3,15},{4,14},{5,9},{6,12},{7,11},{8,2},{9,5},... | collective-permute-start | bytes 233480 | tf_op jit(solution)/shard_map/ppermute | solution.py:181
  6.6 5.6 %collective-permute-start.1 = (f32[19,8,128]{2,1,0:T(8,128)S(1)}, f32[19,8,128]{2,1,0:T(8,128)S(1)}, u32[]{:S(2)}, u32[]{:S(2)}) collective-permute-start(f32[19,8,128]{2,1,0:T(8,128)S(1)} %pack.1), channel_id=1, source_target_pairs={{0,4},{1,5},{2,6},{3,7},{4,0},{5,1},{6,2},{7,3},{8,12},{9,13},{10,... | collective-permute-start | bytes 233480 | tf_op jit(solution)/shard_map/ppermute | solution.py:181
  8.1 6.1 %collective-permute-start.2 = (f32[19,8,128]{2,1,0:T(8,128)S(1)}, f32[19,8,128]{2,1,0:T(8,128)S(1)}, u32[]{:S(2)}, u32[]{:S(2)}) collective-permute-start(f32[19,8,128]{2,1,0:T(8,128)S(1)} %pack.1), channel_id=1, source_target_pairs={{0,6},{1,3},{2,4},{3,1},{4,2},{5,7},{6,0},{7,5},{8,14},{9,11},{10,... | collective-permute-start | bytes 233480 | tf_op jit(solution)/shard_map/ppermute | solution.py:181
  8.6 6.3 %collective-permute-start.3 = (f32[19,8,128]{2,1,0:T(8,128)S(1)}, f32[19,8,128]{2,1,0:T(8,128)S(1)}, u32[]{:S(2)}, u32[]{:S(2)}) collective-permute-start(f32[19,8,128]{2,1,0:T(8,128)S(1)} %pack.1), channel_id=1, source_target_pairs={{0,12},{1,11},{2,14},{3,9},{4,8},{5,15},{6,10},{7,13},{8,4},{9,3},... | collective-permute-start | bytes 233480 | tf_op jit(solution)/shard_map/ppermute | solution.py:181
  9.9 5.8 %collective-permute-start.4 = (f32[19,8,128]{2,1,0:T(8,128)S(1)}, f32[19,8,128]{2,1,0:T(8,128)S(1)}, u32[]{:S(2)}, u32[]{:S(2)}) collective-permute-start(f32[19,8,128]{2,1,0:T(8,128)S(1)} %pack.1), channel_id=1, source_target_pairs={{0,2},{1,7},{2,0},{3,5},{4,6},{5,3},{6,4},{7,1},{8,10},{9,15},{10,... | collective-permute-start | bytes 233480 | tf_op jit(solution)/shard_map/ppermute | solution.py:181
  11.4 4.6 %collective-permute-start.5 = (f32[19,8,128]{2,1,0:T(8,128)S(1)}, f32[19,8,128]{2,1,0:T(8,128)S(1)}, u32[]{:S(2)}, u32[]{:S(2)}) collective-permute-start(f32[19,8,128]{2,1,0:T(8,128)S(1)} %collective-permute-done), channel_id=1, source_target_pairs={{0,4},{1,3},{2,6},{3,1},{4,0},{5,7},{6,2},{7,5},{8,12},{9,11},{10,... | collective-permute-start | bytes 233480 | tf_op jit(solution)/shard_map/ppermute | solution.py:181
  12.2 4.5 %collective-permute-start.6 = (f32[19,8,128]{2,1,0:T(8,128)S(1)}, f32[19,8,128]{2,1,0:T(8,128)S(1)}, u32[]{:S(2)}, u32[]{:S(2)}) collective-permute-start(f32[19,8,128]{2,1,0:T(8,128)S(1)} %collective-permute-done), channel_id=1, source_target_pairs={{0,2},{1,5},{2,0},{3,7},{4,6},{5,1},{6,4},{7,3},{8,10},{9,13},{10,... | collective-permute-start | bytes 233480 | tf_op jit(solution)/shard_map/ppermute | solution.py:181
  16.6 2.1 %collective-permute-start.7 = (f32[152,8,128]{2,1,0:T(8,128)S(1)}, f32[152,8,128]{2,1,0:T(8,128)S(1)}, u32[]{:S(2)}, u32[]{:S(2)}) collective-permute-start(f32[152,8,128]{2,1,0:T(8,128)S(1)} %constant_dynamic-update-slice_fusion.mine_ref), channel_id=1, source_target_pairs={{0,1},{1,0},{2,3},{3,2},{4,5},{5,4},{6,7},{7,6},{8,9},{9,8},{10,11... | collective-permute-start | bytes 1867784 | tf_op jit(solution)/shard_map/ppermute | solution.py:181

commit v13 on v11

--- a/solution.py
+++ b/solution.py
@@ -95,12 +95,16 @@
     return jnp.concatenate([hi, mid, lo, hi, mid, hi, norm_rows(ones, norm, x.shape[0])], axis=0)
 
 
-def moved(x, sides, pull, scale):
+def inverse_weight(weight, ones):
+    return 1.0 / (1.0 + dot(weight.astype(jnp.bfloat16), ones, NT).T[0:1])
+
+
+def moved(x, sides, push, scale):
     coord_dims = x.shape[0]
-    parts = jnp.concatenate(split_bf16(pull, 2), axis=1)
+    parts = jnp.concatenate(split_bf16(push, 2), axis=1)
     sums = dot(parts, jnp.concatenate([sides, sides], axis=1), NT).T
-    pulled = sums[:coord_dims] + sums[coord_dims : 2 * coord_dims]
-    return x + (pulled - x * sums[2 * coord_dims : 2 * coord_dims + 1]) * scale
+    pushed = sums[:coord_dims] + sums[coord_dims : 2 * coord_dims]
+    return x + (x * sums[2 * coord_dims : 2 * coord_dims + 1] - pushed) * scale
 
 
 def group_kernel(offsets, per_dev, mine_ref, theirs_ref, out_ref, stress_ref,
@@ -123,9 +127,7 @@
     coord_dims = x.shape[0]
     chunks = [slice(row, row + LANES) for row in range(0, points, LANES)]
     ones = jnp.ones((coord_dims, points), jnp.bfloat16)
-    scales = [
-        1.0 / (1.0 + dot(ones, weight_ref[rows].astype(jnp.bfloat16), NT)[0:1]) for rows in chunks
-    ]
+    scales = [inverse_weight(weight_ref[rows], ones) for rows in chunks]
     denom = sum(lane_sums(weight_ref[rows] * dis_ref[rows] * dis_ref[rows]) for rows in chunks)
     place = lax.axis_index("wide")
     own_rows = pl.ds(pl.multiple_of(place * per_dev, SUBLANES), per_dev)
@@ -144,19 +146,19 @@
             inverse = lax.rsqrt(square)
             weight, dis = weight_ref[rows], dis_ref[rows]
             misfit = dis - square * inverse
-            stress += lane_sums(weight * misfit * misfit)
+            weighted = weight * misfit
+            stress += lane_sums(weighted * misfit)
             if not last:
-                pull = weight - weight * dis * inverse
-                following.append(moved(x[:, rows], sides, pull, scale))
+                following.append(moved(x[:, rows], sides, weighted * inverse, scale))
         sums.append(stress)
         if last:
             own = dot(jnp.concatenate(parts, axis=0), pick, (((1,), (0,)), ((), ())))
             own = sum(own[i * coord_dims : (i + 1) * coord_dims] for i in range(3))
-            inverse = lax.rsqrt(dot(left_side(own, split_bf16(own, 3)), right, TN))
+            square = dot(left_side(own, split_bf16(own, 3)), right, TN)
+            inverse = lax.rsqrt(square)
             weight = weight_ref[own_rows, :]
-            scale = 1.0 / (1.0 + dot(ones, weight.astype(jnp.bfloat16), NT)[0:1])
-            pull = weight - weight * dis_ref[own_rows, :] * inverse
-            out_ref[...] = moved(own, sides, pull, scale)
+            push = weight * (dis_ref[own_rows, :] - square * inverse) * inverse
+            out_ref[...] = moved(own, sides, push, inverse_weight(weight, ones))
         else:
             x = jnp.concatenate(following, axis=1)
     total = jnp.sum(jnp.concatenate(sums, axis=0), axis=1, keepdims=True)

time: 21.7 us -> 21.7 us (level)
  no operation moved by 1% of the time
where the time goes in v13:
time: 21.7 us; the launch traced here: 21.5 us
  starting transfers between devices  11.4 us (53%)
  waiting for transfers between devices  5.6 us (26%)
  Pallas kernels  3.69 us (17%)
  between operations  0.68 us (3%)
    ppermute x8, starting transfers between devices, swap(): lax.ppermute(value, 'wide', [(i, i ^ offset) for i in range(devices)])  11.4 us
    ppermute x8, waiting for transfers between devices, swap(): lax.ppermute(value, 'wide', [(i, i ^ offset) for i in range(devices)])  5.6 us
    pallas_call x1, Pallas kernels, small_body(): pl.pallas_call(functools.partial(group_kernel, offsets, per_dev), out_sha...  2.81 us
    pallas_call x1, Pallas kernels, small_body(): pl.pallas_call(pack_kernel, out_shape=f32((tiles, SUBLANES, LANES)), in_s...  0.89 us
  transfers between devices with their start and end apart: 8, of which 4 were waited for; matrix products, arithmetic and copies ran while one was open for 0% of the time, Pallas kernels for 0%

profile of v13, /device:TPU:0, one launch (start us, length us, event | category | flops | bytes accessed | tf_op | source)
XLA Modules:
  0.0 21.5 jit_solution(9515837569172592697)
XLA Ops:
  0.6 0.9 %pack.1 = f32[19,8,128]{2,1,0:T(8,128)S(1)} custom-call(f32[24,384]{1,0:T(8,128)} %bitcast.7, s32[24,384]{1,0:T(8,128)} %bitcast.8, f32[16,24]{1,0:T(8,128)} %bitcast.9), custom_call_target="tpu_custom_call" | custom-call | tf_op jit(solution)/shard_map/pack/pallas_call | solution.py:185
  1.5 4.1 %collective-permute-start = (f32[19,8,128]{2,1,0:T(8,128)S(1)}, f32[19,8,128]{2,1,0:T(8,128)S(1)}, u32[]{:S(2)}, u32[]{:S(2)}) collective-permute-start(f32[19,8,128]{2,1,0:T(8,128)S(1)} %pack.1), channel_id=1, source_target_pairs={{0,8},{1,9},{2,10},{3,11},{4,12},{5,13},{6,14},{7,15},{8,0},{9,1},... | collective-permute-start | bytes 233480 | tf_op jit(solution)/shard_map/ppermute | solution.py:181
  5.6 1.5 %collective-permute-start.1 = (f32[19,8,128]{2,1,0:T(8,128)S(1)}, f32[19,8,128]{2,1,0:T(8,128)S(1)}, u32[]{:S(2)}, u32[]{:S(2)}) collective-permute-start(f32[19,8,128]{2,1,0:T(8,128)S(1)} %pack.1), channel_id=1, source_target_pairs={{0,2},{1,3},{2,0},{3,1},{4,6},{5,7},{6,4},{7,5},{8,10},{9,11},{10,... | collective-permute-start | bytes 233480 | tf_op jit(solution)/shard_map/ppermute | solution.py:181
  7.1 1.6 %collective-permute-start.2 = (f32[19,8,128]{2,1,0:T(8,128)S(1)}, f32[19,8,128]{2,1,0:T(8,128)S(1)}, u32[]{:S(2)}, u32[]{:S(2)}) collective-permute-start(f32[19,8,128]{2,1,0:T(8,128)S(1)} %pack.1), channel_id=1, source_target_pairs={{0,4},{1,5},{2,6},{3,7},{4,0},{5,1},{6,2},{7,3},{8,12},{9,13},{10,... | collective-permute-start | bytes 233480 | tf_op jit(solution)/shard_map/ppermute | solution.py:181
  8.7 0.0 collective-permute-start.3
  8.7 1.8 %collective-permute-start.4 = (f32[19,8,128]{2,1,0:T(8,128)S(1)}, f32[19,8,128]{2,1,0:T(8,128)S(1)}, u32[]{:S(2)}, u32[]{:S(2)}) collective-permute-start(f32[19,8,128]{2,1,0:T(8,128)S(1)} %pack.1), channel_id=1, source_target_pairs={{0,6},{1,7},{2,4},{3,5},{4,2},{5,3},{6,0},{7,1},{8,14},{9,15},{10,... | collective-permute-start | bytes 233480 | tf_op jit(solution)/shard_map/ppermute | solution.py:181
  10.5 0.0 collective-permute-done
  10.5 0.6 %collective-permute-start.5 = (f32[19,8,128]{2,1,0:T(8,128)S(1)}, f32[19,8,128]{2,1,0:T(8,128)S(1)}, u32[]{:S(2)}, u32[]{:S(2)}) collective-permute-start(f32[19,8,128]{2,1,0:T(8,128)S(1)} %collective-permute-done), channel_id=1, source_target_pairs={{0,2},{1,3},{2,0},{3,1},{4,6},{5,7},{6,4},{7,5},{8,10},{9,11},{10,... | collective-permute-start | bytes 233480 | tf_op jit(solution)/shard_map/ppermute | solution.py:181
  11.1 0.0 collective-permute-done.1
  11.1 1.8 %collective-permute-start.6 = (f32[19,8,128]{2,1,0:T(8,128)S(1)}, f32[19,8,128]{2,1,0:T(8,128)S(1)}, u32[]{:S(2)}, u32[]{:S(2)}) collective-permute-start(f32[19,8,128]{2,1,0:T(8,128)S(1)} %collective-permute-done), channel_id=1, source_target_pairs={{0,4},{1,5},{2,6},{3,7},{4,0},{5,1},{6,2},{7,3},{8,12},{9,13},{10,... | collective-permute-start | bytes 233480 | tf_op jit(solution)/shard_map/ppermute | solution.py:181
  12.9 0.0 collective-permute-done.2
  13.0 3.0 %collective-permute-done.3 = f32[19,8,128]{2,1,0:T(8,128)S(1)} collective-permute-done((f32[19,8,128]{2,1,0:T(8,128)S(1)}, f32[19,8,128]{2,1,0:T(8,128)S(1)}, u32[]{:S(2)}, u32[]{:S(2)}) %collective-permute-start.3) | collective-permute-done | bytes 77856 | tf_op jit(solution)/shard_map/ppermute | solution.py:181
  16.0 0.3 %collective-permute-done.4 = f32[19,8,128]{2,1,0:T(8,128)S(1)} collective-permute-done((f32[19,8,128]{2,1,0:T(8,128)S(1)}, f32[19,8,128]{2,1,0:T(8,128)S(1)}, u32[]{:S(2)}, u32[]{:S(2)}) %collective-permute-start.4) | collective-permute-done | bytes 77856 | tf_op jit(solution)/shard_map/ppermute | solution.py:181
  16.2 0.3 %collective-permute-done.5 = f32[19,8,128]{2,1,0:T(8,128)S(1)} collective-permute-done((f32[19,8,128]{2,1,0:T(8,128)S(1)}, f32[19,8,128]{2,1,0:T(8,128)S(1)}, u32[]{:S(2)}, u32[]{:S(2)}) %collective-permute-start.5) | collective-permute-done | bytes 77856 | tf_op jit(solution)/shard_map/ppermute | solution.py:181
  16.5 0.0 collective-permute-done.6
  16.6 0.1 collective-permute-start.7
  16.6 2.0 %collective-permute-done.7.theirs_ref = f32[152,8,128]{2,1,0:T(8,128)S(1)} collective-permute-done((f32[152,8,128]{2,1,0:T(8,128)S(1)}, f32[152,8,128]{2,1,0:T(8,128)S(1)}, u32[]{:S(2)}, u32[]{:S(2)}) %collective-permute-start.7) | collective-permute-done | bytes 622624 | tf_op jit(solution)/shard_map/ppermute | solution.py:181
  18.7 2.8 %group_smacof.1 = (f32[16,24]{1,0:T(8,128)}, f32[1,3]{1,0:T(1,128)}) custom-call(f32[152,8,128]{2,1,0:T(8,128)S(1)} %constant_dynamic-update-slice_fusion.mine_ref, f32[152,8,128]{2,1,0:T(8,128)S(1)} %collective-permute-done.7.theirs_ref), custom_call_target="tpu_custom_call" | custom-call | tf_op jit(solution)/shard_map/group_smacof/pallas_call | solution.py:208
  (8 shorter events, 0.1 us)
Async XLA Ops:
  1.5 9.0 %collective-permute-start = (f32[19,8,128]{2,1,0:T(8,128)S(1)}, f32[19,8,128]{2,1,0:T(8,128)S(1)}, u32[]{:S(2)}, u32[]{:S(2)}) collective-permute-start(f32[19,8,128]{2,1,0:T(8,128)S(1)} %pack.1), channel_id=1, source_target_pairs={{0,8},{1,9},{2,10},{3,11},{4,12},{5,13},{6,14},{7,15},{8,0},{9,1},... | collective-permute-start | bytes 233480 | tf_op jit(solution)/shard_map/ppermute | solution.py:181
  5.6 5.5 %collective-permute-start.1 = (f32[19,8,128]{2,1,0:T(8,128)S(1)}, f32[19,8,128]{2,1,0:T(8,128)S(1)}, u32[]{:S(2)}, u32[]{:S(2)}) collective-permute-start(f32[19,8,128]{2,1,0:T(8,128)S(1)} %pack.1), channel_id=1, source_target_pairs={{0,2},{1,3},{2,0},{3,1},{4,6},{5,7},{6,4},{7,5},{8,10},{9,11},{10,... | collective-permute-start | bytes 233480 | tf_op jit(solution)/shard_map/ppermute | solution.py:181
  7.1 5.8 %collective-permute-start.2 = (f32[19,8,128]{2,1,0:T(8,128)S(1)}, f32[19,8,128]{2,1,0:T(8,128)S(1)}, u32[]{:S(2)}, u32[]{:S(2)}) collective-permute-start(f32[19,8,128]{2,1,0:T(8,128)S(1)} %pack.1), channel_id=1, source_target_pairs={{0,4},{1,5},{2,6},{3,7},{4,0},{5,1},{6,2},{7,3},{8,12},{9,13},{10,... | collective-permute-start | bytes 233480 | tf_op jit(solution)/shard_map/ppermute | solution.py:181
  8.7 7.2 %collective-permute-start.3 = (f32[19,8,128]{2,1,0:T(8,128)S(1)}, f32[19,8,128]{2,1,0:T(8,128)S(1)}, u32[]{:S(2)}, u32[]{:S(2)}) collective-permute-start(f32[19,8,128]{2,1,0:T(8,128)S(1)} %pack.1), channel_id=1, source_target_pairs={{0,14},{1,15},{2,12},{3,13},{4,10},{5,11},{6,8},{7,9},{8,6},{9,7},... | collective-permute-start | bytes 233480 | tf_op jit(solution)/shard_map/ppermute | solution.py:181
  8.7 7.5 %collective-permute-start.4 = (f32[19,8,128]{2,1,0:T(8,128)S(1)}, f32[19,8,128]{2,1,0:T(8,128)S(1)}, u32[]{:S(2)}, u32[]{:S(2)}) collective-permute-start(f32[19,8,128]{2,1,0:T(8,128)S(1)} %pack.1), channel_id=1, source_target_pairs={{0,6},{1,7},{2,4},{3,5},{4,2},{5,3},{6,0},{7,1},{8,14},{9,15},{10,... | collective-permute-start | bytes 233480 | tf_op jit(solution)/shard_map/ppermute | solution.py:181
  10.5 6.0 %collective-permute-start.5 = (f32[19,8,128]{2,1,0:T(8,128)S(1)}, f32[19,8,128]{2,1,0:T(8,128)S(1)}, u32[]{:S(2)}, u32[]{:S(2)}) collective-permute-start(f32[19,8,128]{2,1,0:T(8,128)S(1)} %collective-permute-done), channel_id=1, source_target_pairs={{0,2},{1,3},{2,0},{3,1},{4,6},{5,7},{6,4},{7,5},{8,10},{9,11},{10,... | collective-permute-start | bytes 233480 | tf_op jit(solution)/shard_map/ppermute | solution.py:181
  11.1 5.4 %collective-permute-start.6 = (f32[19,8,128]{2,1,0:T(8,128)S(1)}, f32[19,8,128]{2,1,0:T(8,128)S(1)}, u32[]{:S(2)}, u32[]{:S(2)}) collective-permute-start(f32[19,8,128]{2,1,0:T(8,128)S(1)} %collective-permute-done), channel_id=1, source_target_pairs={{0,4},{1,5},{2,6},{3,7},{4,0},{5,1},{6,2},{7,3},{8,12},{9,13},{10,... | collective-permute-start | bytes 233480 | tf_op jit(solution)/shard_map/ppermute | solution.py:181
  16.6 2.1 %collective-permute-start.7 = (f32[152,8,128]{2,1,0:T(8,128)S(1)}, f32[152,8,128]{2,1,0:T(8,128)S(1)}, u32[]{:S(2)}, u32[]{:S(2)}) collective-permute-start(f32[152,8,128]{2,1,0:T(8,128)S(1)} %constant_dynamic-update-slice_fusion.mine_ref), channel_id=1, source_target_pairs={{0,1},{1,0},{2,3},{3,2},{4,5},{5,4},{6,7},{7,6},{8,9},{9,8},{10,11... | collective-permute-start | bytes 1867784 | tf_op jit(solution)/shard_map/ppermute | solution.py:181

commit v14 on v13

--- a/solution.py
+++ b/solution.py
@@ -68,13 +68,6 @@
     out_ref[2 * len(spots)] = jnp.concatenate([x_ref[:half], x_ref[half:], pad], axis=1)
 
 
-def held_slots(offsets, refs, tiles):
-    me = lax.axis_index("wide")
-    for bit, ref in enumerate(refs):
-        for slot, offset in enumerate(offsets):
-            yield ref, slot * tiles, me ^ offset ^ bit
-
-
 def norm_rows(top, bottom, coord_dims):
     pad = jnp.zeros((coord_dims - 6, top[0].shape[1]), jnp.float32)
     rows = [p.astype(jnp.float32) for p in (*top, *bottom)]
@@ -107,62 +100,152 @@
     return x + (x * sums[2 * coord_dims : 2 * coord_dims + 1] - pushed) * scale
 
 
-def group_kernel(offsets, per_dev, mine_ref, theirs_ref, out_ref, stress_ref,
+def place_of(offset, bit):
+    return lax.axis_index("wide") ^ offset ^ bit
+
+
+def sweep_rows(x, dis, weight, square, sides, scale):
+    inverse = lax.rsqrt(square)
+    misfit = dis - square * inverse
+    weighted = weight * misfit
+    return lane_sums(weighted * misfit), moved(x, sides, weighted * inverse, scale)
+
+
+def sides_of(parts, points):
+    ones = jnp.ones((parts[0].shape[0], points), jnp.bfloat16)
+    return jnp.concatenate([parts[0], parts[1], ones], axis=0), ones
+
+
+def row_chunks(count):
+    return [slice(row, min(row + LANES, count)) for row in range(0, count, LANES)]
+
+
+def from_tiles(tiles, per_dev):
+    halves = [
+        jnp.concatenate([t[:, low : low + per_dev] for t in tiles], axis=1) for low in (0, per_dev)
+    ]
+    return jnp.concatenate(halves, axis=0)
+
+
+def static_rows(ref, per_dev, dis_ref, weight_ref):
+    spots = tile_spots(per_dev, dis_ref.shape[1])
+    tiles = 2 * len(spots) + 1
+    for slot in range(ref.shape[0] // tiles):
+        for i, (rows, columns) in enumerate(spots):
+            spot = slice(slot * per_dev + rows.start, slot * per_dev + rows.stop)
+            dis_ref[spot, columns] = ref[slot * tiles + i]
+            weight_ref[spot, columns] = ref[slot * tiles + len(spots) + i]
+
+
+def first_kernel(offsets, per_dev, mine_ref, tiles_ref, their_tiles_ref, x_ref, moved_ref, rest_ref,
+                 inverse_ref, distance_ref, stress_ref, order_ref,
                  dis_ref, weight_ref, tile_ref):
-    points = dis_ref.shape[0]
+    held, points = dis_ref.shape
+    order = []
+    shape = (per_dev, points)
+    lanes = lax.broadcasted_iota(jnp.int32, shape, 1) - lax.broadcasted_iota(jnp.int32, shape, 0)
+    for bit, ref in enumerate((tiles_ref, their_tiles_ref)):
+        for slot, offset in enumerate(offsets):
+            place = place_of(offset, bit)
+            tile_ref[place] = ref[slot]
+            order.append((lanes == place * per_dev).astype(jnp.float32))
+    order_ref[...] = jnp.concatenate(order, axis=0).astype(jnp.bfloat16)
+    static_rows(mine_ref, per_dev, dis_ref, weight_ref)
+    mine = from_tiles([tiles_ref[i] for i in range(len(offsets))], per_dev)
+    rest = from_tiles([their_tiles_ref[i] for i in range(len(offsets))], per_dev)
+    x = from_tiles([tile_ref[i] for i in range(tile_ref.shape[0])], per_dev)
+    x_ref[...] = x
+    rest_ref[...] = rest
+    parts = split_bf16(x, 3)
+    sides, ones = sides_of(parts, points)
+    right = right_side(x, parts)
+    left = left_side(mine, split_bf16(mine, 3))
+    rest_left = left_side(rest, split_bf16(rest, 3))
+    stress, following = 0.0, []
+    for rows in row_chunks(held):
+        weight = weight_ref[rows]
+        part, new = sweep_rows(
+            mine[:, rows], dis_ref[rows], weight, dot(left[:, rows], right, TN), sides,
+            inverse_weight(weight, ones),
+        )
+        stress += part
+        following.append(new)
+    moved_ref[...] = jnp.concatenate(following, axis=1)
+    stress_ref[...] = stress
+    for rows in row_chunks(held):
+        square = dot(rest_left[:, rows], right, TN)
+        inverse = lax.rsqrt(square)
+        inverse_ref[rows] = inverse
+        distance_ref[rows] = square * inverse
+
+
+def second_kernel(offsets, per_dev, mine_ref, theirs_ref, x_ref, moved_ref, rest_ref, inverse_ref,
+                  distance_ref, first_ref, order_ref, out_ref, stress_ref,
+                  dis_ref, weight_ref, rest_dis_ref, rest_weight_ref, push_ref):
+    held, points = rest_dis_ref.shape
+    coord_dims = x_ref.shape[0]
+    static_rows(theirs_ref, per_dev, rest_dis_ref, rest_weight_ref)
+    sides, ones = sides_of(split_bf16(x_ref[...], 2), points)
+    stress, following = first_ref[...], [moved_ref[...]]
+    for rows in row_chunks(held):
+        weight = rest_weight_ref[rows]
+        misfit = rest_dis_ref[rows] - distance_ref[rows]
+        weighted = weight * misfit
+        stress += lane_sums(weighted * misfit)
+        push = weighted * inverse_ref[rows]
+        following.append(moved(rest_ref[:, rows], sides, push, inverse_weight(weight, ones)))
+    sums = [stress]
+    slots = jnp.concatenate(following, axis=1)
     spots = tile_spots(per_dev, points)
     tiles = 2 * len(spots) + 1
-    for ref, base, place in held_slots(offsets, (mine_ref, theirs_ref), tiles):
-        tile_ref[place] = ref[base + tiles - 1]
-        for i, (rows, columns) in enumerate(spots):
-            start = pl.multiple_of(place * per_dev + rows.start, SUBLANES)
-            dis_ref[pl.ds(start, SUBLANES), columns] = ref[base + i]
-            weight_ref[pl.ds(start, SUBLANES), columns] = ref[base + len(spots) + i]
-    blocks = [tile_ref[i] for i in range(tile_ref.shape[0])]
-    halves = [
-        jnp.concatenate([t[:, low : low + per_dev] for t in blocks], axis=1)
-        for low in (0, per_dev)
-    ]
-    x = jnp.concatenate(halves, axis=0)
-    coord_dims = x.shape[0]
-    chunks = [slice(row, row + LANES) for row in range(0, points, LANES)]
-    ones = jnp.ones((coord_dims, points), jnp.bfloat16)
+    for bit, ref in enumerate((mine_ref, theirs_ref)):
+        for slot, offset in enumerate(offsets):
+            for i, (rows, columns) in enumerate(spots):
+                start = place_of(offset, bit) * per_dev + rows.start
+                spot = pl.ds(pl.multiple_of(start, SUBLANES), SUBLANES)
+                dis_ref[spot, columns] = ref[slot * tiles + i]
+                weight_ref[spot, columns] = ref[slot * tiles + len(spots) + i]
+    chunks = row_chunks(points)
     scales = [inverse_weight(weight_ref[rows], ones) for rows in chunks]
     denom = sum(lane_sums(weight_ref[rows] * dis_ref[rows] * dis_ref[rows]) for rows in chunks)
+    ordered = dot(jnp.concatenate(split_bf16(slots, 3), axis=0), order_ref[...], (((1,), (0,)), ((), ())))
+    parts = [ordered[i * coord_dims : (i + 1) * coord_dims] for i in range(3)]
+    x = sum(parts)
+    parts = [p.astype(jnp.bfloat16) for p in parts]
+    for sweep in range(1, ITERS):
+        last = sweep == ITERS - 1
+        sides, _ = sides_of(parts, points)
+        left, right = left_side(x, parts), right_side(x, parts)
+        stress, following = 0.0, []
+        for rows, scale in zip(chunks, scales):
+            square = dot(left[:, rows], right, TN)
+            if last:
+                inverse = lax.rsqrt(square)
+                misfit = dis_ref[rows] - square * inverse
+                weighted = weight_ref[rows] * misfit
+                stress += lane_sums(weighted * misfit)
+                push_ref[rows] = weighted * inverse
+            else:
+                part, new = sweep_rows(
+                    x[:, rows], dis_ref[rows], weight_ref[rows], square, sides, scale
+                )
+                stress += part
+                following.append(new)
+        sums.append(stress)
+        if not last:
+            x = jnp.concatenate(following, axis=1)
+            parts = split_bf16(x, 3)
     place = lax.axis_index("wide")
-    own_rows = pl.ds(pl.multiple_of(place * per_dev, SUBLANES), per_dev)
     shape = (points, per_dev)
     pick = lax.broadcasted_iota(jnp.int32, shape, 0) - lax.broadcasted_iota(jnp.int32, shape, 1)
     pick = (pick == place * per_dev).astype(jnp.float32).astype(jnp.bfloat16)
-    sums = [denom]
-    for sweep in range(ITERS):
-        parts = split_bf16(x, 3)
-        sides = jnp.concatenate([parts[0], parts[1], ones], axis=0)
-        left, right = left_side(x, parts), right_side(x, parts)
-        last = sweep == ITERS - 1
-        stress, following = 0.0, []
-        for rows, scale in zip(chunks, scales):
-            square = dot(left[:, rows], right, TN)
-            inverse = lax.rsqrt(square)
-            weight, dis = weight_ref[rows], dis_ref[rows]
-            misfit = dis - square * inverse
-            weighted = weight * misfit
-            stress += lane_sums(weighted * misfit)
-            if not last:
-                following.append(moved(x[:, rows], sides, weighted * inverse, scale))
-        sums.append(stress)
-        if last:
-            own = dot(jnp.concatenate(parts, axis=0), pick, (((1,), (0,)), ((), ())))
-            own = sum(own[i * coord_dims : (i + 1) * coord_dims] for i in range(3))
-            square = dot(left_side(own, split_bf16(own, 3)), right, TN)
-            inverse = lax.rsqrt(square)
-            weight = weight_ref[own_rows, :]
-            push = weight * (dis_ref[own_rows, :] - square * inverse) * inverse
-            out_ref[...] = moved(own, sides, push, inverse_weight(weight, ones))
-        else:
-            x = jnp.concatenate(following, axis=1)
-    total = jnp.sum(jnp.concatenate(sums, axis=0), axis=1, keepdims=True)
-    ratios = total[1:] / total[:1]
+    own = dot(jnp.concatenate(parts, axis=0), pick, (((1,), (0,)), ((), ())))
+    own = sum(own[i * coord_dims : (i + 1) * coord_dims] for i in range(3))
+    own_rows = pl.ds(pl.multiple_of(place * per_dev, SUBLANES), per_dev)
+    scale = inverse_weight(weight_ref[own_rows, :], ones)
+    out_ref[...] = moved(own, sides, push_ref[own_rows, :], scale)
+    total = jnp.sum(jnp.concatenate([*sums, denom], axis=0), axis=1, keepdims=True)
+    ratios = total[:ITERS] / total[ITERS:]
     lanes = lax.broadcasted_iota(jnp.int32, (ITERS, LANES), 1)
     lined = jnp.where(lanes == lax.broadcasted_iota(jnp.int32, (ITERS, LANES), 0), ratios, 0.0)
     stress_ref[...] = jnp.sum(lined, axis=0, keepdims=True)[:, :ITERS]
@@ -204,20 +287,47 @@
         held[far | step] = swap(held[far], step)
     offsets = list(held)
     mine = jnp.concatenate(list(held.values()), axis=0)
+    mine_tiles = jnp.stack([block[-1] for block in held.values()])
+    their_tiles = swap(mine_tiles, 1)
     theirs = swap(mine, 1)
+    rows = per_dev * len(offsets)
+    shadow = pl.pallas_call(
+        functools.partial(first_kernel, offsets, per_dev),
+        out_shape=(
+            f32((coord_dims, points)),
+            f32((coord_dims, rows)),
+            f32((coord_dims, rows)),
+            f32((rows, points)),
+            f32((rows, points)),
+            f32((1, LANES)),
+            jax.ShapeDtypeStruct((points, points), jnp.bfloat16),
+        ),
+        in_specs=[vmem] * 3,
+        out_specs=(vmem,) * 7,
+        scratch_shapes=[
+            pltpu.VMEM((rows, points), jnp.float32),
+            pltpu.VMEM((rows, points), jnp.float32),
+            pltpu.VMEM((devices, SUBLANES, LANES), jnp.float32),
+        ],
+        compiler_params=params,
+        cost_estimate=pl.CostEstimate(flops=10**7, bytes_accessed=0, transcendentals=0),
+        name="first_sweep",
+    )(mine, mine_tiles, their_tiles)
     final, stress = pl.pallas_call(
-        functools.partial(group_kernel, offsets, per_dev),
+        functools.partial(second_kernel, offsets, per_dev),
         out_shape=(f32((coord_dims, per_dev)), f32((1, ITERS))),
-        in_specs=[vmem, vmem],
+        in_specs=[vmem] * 9,
         out_specs=(vmem, vmem),
         scratch_shapes=[
             pltpu.VMEM((points, points), jnp.float32),
             pltpu.VMEM((points, points), jnp.float32),
-            pltpu.VMEM((devices, SUBLANES, LANES), jnp.float32),
+            pltpu.VMEM((rows, points), jnp.float32),
+            pltpu.VMEM((rows, points), jnp.float32),
+            pltpu.VMEM((points, points), jnp.float32),
         ],
         compiler_params=params,
         name="group_smacof",
-    )(mine, theirs)
+    )(mine, theirs, *shadow)
     return (final[:, None, :], stress[0])
 
 

time: 21.7 us -> 22 us (1.014)
  starting transfers between devices: 11.4 us -> 11.9 us
  waiting for transfers between devices: 5.6 us -> 5.12 us
  Pallas kernels: 3.69 us -> 3.94 us
    ppermute x8 -> x9, waiting for transfers between devices: 5.6 us -> 5.12 us  [swap(): lax.ppermute(value, 'wide', [(i, i ^ offset) for i in range(devices)])]
    ppermute x8 -> x9, starting transfers between devices: 11.4 us -> 11.9 us  [swap(): lax.ppermute(value, 'wide', [(i, i ^ offset) for i in range(devices)])]
    pallas_call x1 -> x2, Pallas kernels: 2.81 us -> 3.05 us  [the longest x1 2.46 us: small_body(): pl.pallas_call(functools.partial(second_kernel, offsets, per_dev), out_sh...]
  transfers between devices with their start and end apart: 8 -> 9, of which waited for: 4 -> 4; matrix products, arithmetic and copies ran while one was open for 0% -> 0% of each run, Pallas kernels for 0% -> 3%
where the time goes in v14:
time: 22 us; the launch traced here: 21.8 us
  starting transfers between devices  11.9 us (54%)
  waiting for transfers between devices  5.12 us (23%)
  Pallas kernels  3.94 us (18%)
  between operations  0.75 us (3%)
    ppermute x9, starting transfers between devices, swap(): lax.ppermute(value, 'wide', [(i, i ^ offset) for i in range(devices)])  11.9 us
    ppermute x9, waiting for transfers between devices, swap(): lax.ppermute(value, 'wide', [(i, i ^ offset) for i in range(devices)])  5.12 us
    pallas_call x1, Pallas kernels, small_body(): pl.pallas_call(functools.partial(second_kernel, offsets, per_dev), out_sh...  2.46 us
    pallas_call x1, Pallas kernels, small_body(): pl.pallas_call(pack_kernel, out_shape=f32((tiles, SUBLANES, LANES)), in_s...  0.89 us
    pallas_call x1, Pallas kernels, small_body(): pl.pallas_call(functools.partial(first_kernel, offsets, per_dev), out_sha...  0.59 us
  transfers between devices with their start and end apart: 9, of which 4 were waited for; matrix products, arithmetic and copies ran while one was open for 0% of the time, Pallas kernels for 3%

profile of v14, /device:TPU:0, one launch (start us, length us, event | category | flops | bytes accessed | tf_op | source)
XLA Modules:
  0.0 21.8 jit_solution(8482876195138642924)
XLA Ops:
  0.6 0.9 %pack.1 = f32[19,8,128]{2,1,0:T(8,128)S(1)} custom-call(f32[24,384]{1,0:T(8,128)} %bitcast.7, s32[24,384]{1,0:T(8,128)} %bitcast.8, f32[16,24]{1,0:T(8,128)} %bitcast.9), custom_call_target="tpu_custom_call" | custom-call | tf_op jit(solution)/shard_map/pack/pallas_call | solution.py:268
  1.5 4.1 %collective-permute-start = (f32[19,8,128]{2,1,0:T(8,128)S(1)}, f32[19,8,128]{2,1,0:T(8,128)S(1)}, u32[]{:S(2)}, u32[]{:S(2)}) collective-permute-start(f32[19,8,128]{2,1,0:T(8,128)S(1)} %pack.1), channel_id=1, source_target_pairs={{0,8},{1,9},{2,10},{3,11},{4,12},{5,13},{6,14},{7,15},{8,0},{9,1},... | collective-permute-start | bytes 233480 | tf_op jit(solution)/shard_map/ppermute | solution.py:264
  5.6 1.5 %collective-permute-start.1 = (f32[19,8,128]{2,1,0:T(8,128)S(1)}, f32[19,8,128]{2,1,0:T(8,128)S(1)}, u32[]{:S(2)}, u32[]{:S(2)}) collective-permute-start(f32[19,8,128]{2,1,0:T(8,128)S(1)} %pack.1), channel_id=1, source_target_pairs={{0,2},{1,3},{2,0},{3,1},{4,6},{5,7},{6,4},{7,5},{8,10},{9,11},{10,... | collective-permute-start | bytes 233480 | tf_op jit(solution)/shard_map/ppermute | solution.py:264
  7.1 1.6 %collective-permute-start.2 = (f32[19,8,128]{2,1,0:T(8,128)S(1)}, f32[19,8,128]{2,1,0:T(8,128)S(1)}, u32[]{:S(2)}, u32[]{:S(2)}) collective-permute-start(f32[19,8,128]{2,1,0:T(8,128)S(1)} %pack.1), channel_id=1, source_target_pairs={{0,4},{1,5},{2,6},{3,7},{4,0},{5,1},{6,2},{7,3},{8,12},{9,13},{10,... | collective-permute-start | bytes 233480 | tf_op jit(solution)/shard_map/ppermute | solution.py:264
  8.7 0.0 collective-permute-start.3
  8.7 1.8 %collective-permute-start.4 = (f32[19,8,128]{2,1,0:T(8,128)S(1)}, f32[19,8,128]{2,1,0:T(8,128)S(1)}, u32[]{:S(2)}, u32[]{:S(2)}) collective-permute-start(f32[19,8,128]{2,1,0:T(8,128)S(1)} %pack.1), channel_id=1, source_target_pairs={{0,6},{1,7},{2,4},{3,5},{4,2},{5,3},{6,0},{7,1},{8,14},{9,15},{10,... | collective-permute-start | bytes 233480 | tf_op jit(solution)/shard_map/ppermute | solution.py:264
  10.5 0.0 collective-permute-done
  10.5 0.6 %collective-permute-start.5 = (f32[19,8,128]{2,1,0:T(8,128)S(1)}, f32[19,8,128]{2,1,0:T(8,128)S(1)}, u32[]{:S(2)}, u32[]{:S(2)}) collective-permute-start(f32[19,8,128]{2,1,0:T(8,128)S(1)} %collective-permute-done), channel_id=1, source_target_pairs={{0,2},{1,3},{2,0},{3,1},{4,6},{5,7},{6,4},{7,5},{8,10},{9,11},{10,... | collective-permute-start | bytes 233480 | tf_op jit(solution)/shard_map/ppermute | solution.py:264
  11.1 0.0 collective-permute-done.1
  11.1 1.8 %collective-permute-start.6 = (f32[19,8,128]{2,1,0:T(8,128)S(1)}, f32[19,8,128]{2,1,0:T(8,128)S(1)}, u32[]{:S(2)}, u32[]{:S(2)}) collective-permute-start(f32[19,8,128]{2,1,0:T(8,128)S(1)} %collective-permute-done), channel_id=1, source_target_pairs={{0,4},{1,5},{2,6},{3,7},{4,0},{5,1},{6,2},{7,3},{8,12},{9,13},{10,... | collective-permute-start | bytes 233480 | tf_op jit(solution)/shard_map/ppermute | solution.py:264
  13.0 0.0 collective-permute-done.2
  13.0 3.0 %collective-permute-done.3 = f32[19,8,128]{2,1,0:T(8,128)S(1)} collective-permute-done((f32[19,8,128]{2,1,0:T(8,128)S(1)}, f32[19,8,128]{2,1,0:T(8,128)S(1)}, u32[]{:S(2)}, u32[]{:S(2)}) %collective-permute-start.3) | collective-permute-done | bytes 77856 | tf_op jit(solution)/shard_map/ppermute | solution.py:264
  16.0 0.3 %collective-permute-done.4 = f32[19,8,128]{2,1,0:T(8,128)S(1)} collective-permute-done((f32[19,8,128]{2,1,0:T(8,128)S(1)}, f32[19,8,128]{2,1,0:T(8,128)S(1)}, u32[]{:S(2)}, u32[]{:S(2)}) %collective-permute-start.4) | collective-permute-done | bytes 77856 | tf_op jit(solution)/shard_map/ppermute | solution.py:264
  16.3 0.3 %collective-permute-done.5 = f32[19,8,128]{2,1,0:T(8,128)S(1)} collective-permute-done((f32[19,8,128]{2,1,0:T(8,128)S(1)}, f32[19,8,128]{2,1,0:T(8,128)S(1)}, u32[]{:S(2)}, u32[]{:S(2)}) %collective-permute-start.5) | collective-permute-done | bytes 77856 | tf_op jit(solution)/shard_map/ppermute | solution.py:264
  16.5 0.0 collective-permute-done.6
  16.6 0.1 collective-permute-start.7
  16.7 0.5 %collective-permute-start.8 = (f32[8,8,128]{2,1,0:T(8,128)S(1)}, f32[8,8,128]{2,1,0:T(8,128)S(1)}, u32[]{:S(2)}, u32[]{:S(2)}) collective-permute-start(f32[8,8,128]{2,1,0:T(8,128)S(1)} %constant_dynamic-update-slice_fusion.8.tiles_ref), channel_id=1, source_target_pairs={{0,1},{1,0},{2,3},{3,2},{4,5},{5,4},{6,7},{7,6},{8,9},{9,8},{10,11... | collective-permute-start | bytes 98312 | tf_op jit(solution)/shard_map/ppermute | solution.py:264
  17.1 1.6 %collective-permute-done.8.their_tiles_ref = f32[8,8,128]{2,1,0:T(8,128)S(1)} collective-permute-done((f32[8,8,128]{2,1,0:T(8,128)S(1)}, f32[8,8,128]{2,1,0:T(8,128)S(1)}, u32[]{:S(2)}, u32[]{:S(2)}) %collective-permute-start.8) | collective-permute-done | bytes 32800 | tf_op jit(solution)/shard_map/ppermute | solution.py:264
  18.7 0.6 %first_sweep.1 = (f32[16,384]{1,0:T(8,128)S(1)}, f32[16,192]{1,0:T(8,128)S(1)}, f32[16,192]{1,0:T(8,128)S(1)}, f32[192,384]{1,0:T(8,128)S(1)}, f32[192,384]{1,0:...) custom-call(f32[152,8,128]{2,1,0:T(8,128)S(1)} %constant_dynamic-update-slice_fusion.mine_ref, ...), custom_call_target="tpu_custom_call" | custom-call | flops 10000000 | tf_op jit(solution)/shard_map/first_sweep/pallas_call | solution.py:294
  19.3 0.0 collective-permute-done.7.theirs_ref
  19.3 2.5 %group_smacof.1 = (f32[16,24]{1,0:T(8,128)}, f32[1,3]{1,0:T(1,128)}) custom-call(f32[152,8,128]{2,1,0:T(8,128)S(1)} %constant_dynamic-update-slice_fusion.mine_ref, f32[152,8,128]{2,1,0:T(8,128)S(1)} %collective-permute-done.7.theirs_ref, f32[16,384]{1,0:T(8,128)S(1)} %get-tuple-element.11.x_ref, f32[16,192]{1,0:T(8,128)S(1)} %get-tuple-element.12.moved_ref, ...), custom_call_target="tpu_custom_call" | custom-call | tf_op jit(solution)/shard_map/group_smacof/pallas_call | solution.py:316
  (16 shorter events, 0.1 us)
Async XLA Ops:
  1.5 9.0 %collective-permute-start = (f32[19,8,128]{2,1,0:T(8,128)S(1)}, f32[19,8,128]{2,1,0:T(8,128)S(1)}, u32[]{:S(2)}, u32[]{:S(2)}) collective-permute-start(f32[19,8,128]{2,1,0:T(8,128)S(1)} %pack.1), channel_id=1, source_target_pairs={{0,8},{1,9},{2,10},{3,11},{4,12},{5,13},{6,14},{7,15},{8,0},{9,1},... | collective-permute-start | bytes 233480 | tf_op jit(solution)/shard_map/ppermute | solution.py:264
  5.6 5.5 %collective-permute-start.1 = (f32[19,8,128]{2,1,0:T(8,128)S(1)}, f32[19,8,128]{2,1,0:T(8,128)S(1)}, u32[]{:S(2)}, u32[]{:S(2)}) collective-permute-start(f32[19,8,128]{2,1,0:T(8,128)S(1)} %pack.1), channel_id=1, source_target_pairs={{0,2},{1,3},{2,0},{3,1},{4,6},{5,7},{6,4},{7,5},{8,10},{9,11},{10,... | collective-permute-start | bytes 233480 | tf_op jit(solution)/shard_map/ppermute | solution.py:264
  7.1 5.8 %collective-permute-start.2 = (f32[19,8,128]{2,1,0:T(8,128)S(1)}, f32[19,8,128]{2,1,0:T(8,128)S(1)}, u32[]{:S(2)}, u32[]{:S(2)}) collective-permute-start(f32[19,8,128]{2,1,0:T(8,128)S(1)} %pack.1), channel_id=1, source_target_pairs={{0,4},{1,5},{2,6},{3,7},{4,0},{5,1},{6,2},{7,3},{8,12},{9,13},{10,... | collective-permute-start | bytes 233480 | tf_op jit(solution)/shard_map/ppermute | solution.py:264
  8.7 7.2 %collective-permute-start.3 = (f32[19,8,128]{2,1,0:T(8,128)S(1)}, f32[19,8,128]{2,1,0:T(8,128)S(1)}, u32[]{:S(2)}, u32[]{:S(2)}) collective-permute-start(f32[19,8,128]{2,1,0:T(8,128)S(1)} %pack.1), channel_id=1, source_target_pairs={{0,14},{1,15},{2,12},{3,13},{4,10},{5,11},{6,8},{7,9},{8,6},{9,7},... | collective-permute-start | bytes 233480 | tf_op jit(solution)/shard_map/ppermute | solution.py:264
  8.7 7.6 %collective-permute-start.4 = (f32[19,8,128]{2,1,0:T(8,128)S(1)}, f32[19,8,128]{2,1,0:T(8,128)S(1)}, u32[]{:S(2)}, u32[]{:S(2)}) collective-permute-start(f32[19,8,128]{2,1,0:T(8,128)S(1)} %pack.1), channel_id=1, source_target_pairs={{0,6},{1,7},{2,4},{3,5},{4,2},{5,3},{6,0},{7,1},{8,14},{9,15},{10,... | collective-permute-start | bytes 233480 | tf_op jit(solution)/shard_map/ppermute | solution.py:264
  10.5 6.0 %collective-permute-start.5 = (f32[19,8,128]{2,1,0:T(8,128)S(1)}, f32[19,8,128]{2,1,0:T(8,128)S(1)}, u32[]{:S(2)}, u32[]{:S(2)}) collective-permute-start(f32[19,8,128]{2,1,0:T(8,128)S(1)} %collective-permute-done), channel_id=1, source_target_pairs={{0,2},{1,3},{2,0},{3,1},{4,6},{5,7},{6,4},{7,5},{8,10},{9,11},{10,... | collective-permute-start | bytes 233480 | tf_op jit(solution)/shard_map/ppermute | solution.py:264
  11.1 5.4 %collective-permute-start.6 = (f32[19,8,128]{2,1,0:T(8,128)S(1)}, f32[19,8,128]{2,1,0:T(8,128)S(1)}, u32[]{:S(2)}, u32[]{:S(2)}) collective-permute-start(f32[19,8,128]{2,1,0:T(8,128)S(1)} %collective-permute-done), channel_id=1, source_target_pairs={{0,4},{1,5},{2,6},{3,7},{4,0},{5,1},{6,2},{7,3},{8,12},{9,13},{10,... | collective-permute-start | bytes 233480 | tf_op jit(solution)/shard_map/ppermute | solution.py:264
  16.6 2.8 %collective-permute-start.7 = (f32[152,8,128]{2,1,0:T(8,128)S(1)}, f32[152,8,128]{2,1,0:T(8,128)S(1)}, u32[]{:S(2)}, u32[]{:S(2)}) collective-permute-start(f32[152,8,128]{2,1,0:T(8,128)S(1)} %constant_dynamic-update-slice_fusion.mine_ref), channel_id=1, source_target_pairs={{0,1},{1,0},{2,3},{3,2},{4,5},{5,4},{6,7},{7,6},{8,9},{9,8},{10,11... | collective-permute-start | bytes 1867784 | tf_op jit(solution)/shard_map/ppermute | solution.py:264
  16.7 2.1 %collective-permute-start.8 = (f32[8,8,128]{2,1,0:T(8,128)S(1)}, f32[8,8,128]{2,1,0:T(8,128)S(1)}, u32[]{:S(2)}, u32[]{:S(2)}) collective-permute-start(f32[8,8,128]{2,1,0:T(8,128)S(1)} %constant_dynamic-update-slice_fusion.8.tiles_ref), channel_id=1, source_target_pairs={{0,1},{1,0},{2,3},{3,2},{4,5},{5,4},{6,7},{7,6},{8,9},{9,8},{10,11... | collective-permute-start | bytes 98312 | tf_op jit(solution)/shard_map/ppermute | solution.py:264

commit v15 on v13

--- a/solution.py
+++ b/solution.py
@@ -70,9 +70,9 @@
 
 def held_slots(offsets, refs, tiles):
     me = lax.axis_index("wide")
-    for bit, ref in enumerate(refs):
-        for slot, offset in enumerate(offsets):
-            yield ref, slot * tiles, me ^ offset ^ bit
+    for group, ref in zip(offsets, refs):
+        for slot, offset in enumerate(group):
+            yield ref, slot * tiles, me ^ offset
 
 
 def norm_rows(top, bottom, coord_dims):
@@ -107,12 +107,20 @@
     return x + (x * sums[2 * coord_dims : 2 * coord_dims + 1] - pushed) * scale
 
 
-def group_kernel(offsets, per_dev, mine_ref, theirs_ref, out_ref, stress_ref,
-                 dis_ref, weight_ref, tile_ref):
+def join_kernel(*refs):
+    *block_refs, out_ref = refs
+    size = block_refs[0].shape[0]
+    for i, ref in enumerate(block_refs):
+        out_ref[i * size : (i + 1) * size] = ref[...]
+
+
+def group_kernel(offsets, per_dev, *refs):
+    slot_refs = refs[: len(offsets)]
+    out_ref, stress_ref, dis_ref, weight_ref, tile_ref = refs[len(offsets) :]
     points = dis_ref.shape[0]
     spots = tile_spots(per_dev, points)
     tiles = 2 * len(spots) + 1
-    for ref, base, place in held_slots(offsets, (mine_ref, theirs_ref), tiles):
+    for ref, base, place in held_slots(offsets, slot_refs, tiles):
         tile_ref[place] = ref[base + tiles - 1]
         for i, (rows, columns) in enumerate(spots):
             start = pl.multiple_of(place * per_dev + rows.start, SUBLANES)
@@ -198,17 +206,34 @@
     )(*(pltpu.with_memory_space_constraint(array, pltpu.HBM) for array in inputs))
     far, near, side = devices // 2, devices // 4, devices // 8
     held = {0: packed}
-    for offset in (far, side, near, far | near | side, near | side):
+    for offset in (far, side, near, near | side, far | near | side):
         held[offset] = swap(packed, offset)
-    for step in (side, near):
+    for step in (near, side):
         held[far | step] = swap(held[far], step)
-    offsets = list(held)
-    mine = jnp.concatenate(list(held.values()), axis=0)
-    theirs = swap(mine, 1)
+    early = [0, far, near, side]
+    late = [offset for offset in held if offset not in early]
+    block = packed.shape[0]
+
+    def join(group, flops):
+        return pl.pallas_call(
+            join_kernel,
+            out_shape=f32((len(group) * block, SUBLANES, LANES)),
+            in_specs=[vmem] * len(group),
+            out_specs=vmem,
+            compiler_params=params,
+            cost_estimate=pl.CostEstimate(flops=flops, bytes_accessed=0, transcendentals=0),
+            name="join",
+        )(*(held[offset] for offset in group))
+
+    first, second = join(early, 1), join(late, 1)
+    first_swapped = swap(first, 1)
+
+    slots = [first, first_swapped, second, swap(second, 1)]
+    offsets = [early, [o ^ 1 for o in early], late, [o ^ 1 for o in late]]
     final, stress = pl.pallas_call(
         functools.partial(group_kernel, offsets, per_dev),
         out_shape=(f32((coord_dims, per_dev)), f32((1, ITERS))),
-        in_specs=[vmem, vmem],
+        in_specs=[vmem] * len(slots),
         out_specs=(vmem, vmem),
         scratch_shapes=[
             pltpu.VMEM((points, points), jnp.float32),
@@ -217,7 +242,7 @@
         ],
         compiler_params=params,
         name="group_smacof",
-    )(mine, theirs)
+    )(*slots)
     return (final[:, None, :], stress[0])
 
 

time: 21.7 us -> 21.2 us (0.977)
  waiting for transfers between devices: 5.6 us -> 5.15 us
    ppermute x8 -> x9, waiting for transfers between devices: 5.6 us -> 5.15 us  [swap(): lax.ppermute(value, 'wide', [(i, i ^ offset) for i in range(devices)])]
    ppermute x8 -> x9, starting transfers between devices: 11.4 us -> 11.5 us  [swap(): lax.ppermute(value, 'wide', [(i, i ^ offset) for i in range(devices)])]
  transfers between devices with their start and end apart: 8 -> 9, of which waited for: 4 -> 4; matrix products, arithmetic and copies ran while one was open for 0% -> 0% of each run, Pallas kernels for 0% -> 0%
where the time goes in v15:
time: 21.2 us; the launch traced here: 21 us
  starting transfers between devices  11.5 us (54%)
  waiting for transfers between devices  5.15 us (24%)
  Pallas kernels  3.74 us (18%)
  between operations  0.68 us (3%)
    ppermute x9, starting transfers between devices, swap(): lax.ppermute(value, 'wide', [(i, i ^ offset) for i in range(devices)])  11.5 us
    ppermute x9, waiting for transfers between devices, swap(): lax.ppermute(value, 'wide', [(i, i ^ offset) for i in range(devices)])  5.15 us
    pallas_call x1, Pallas kernels, small_body(): pl.pallas_call(functools.partial(group_kernel, offsets, per_dev), out_sha...  2.81 us
    pallas_call x1, Pallas kernels, small_body(): pl.pallas_call(pack_kernel, out_shape=f32((tiles, SUBLANES, LANES)), in_s...  0.89 us
  transfers between devices with their start and end apart: 9, of which 4 were waited for; matrix products, arithmetic and copies ran while one was open for 0% of the time, Pallas kernels for 0%

profile of v15, /device:TPU:0, one launch (start us, length us, event | category | flops | bytes accessed | tf_op | source)
XLA Modules:
  0.0 21.0 jit_solution(3796015921131270497)
XLA Ops:
  0.6 0.9 %pack.1.refs_0_ = f32[19,8,128]{2,1,0:T(8,128)S(1)} custom-call(f32[24,384]{1,0:T(8,128)} %bitcast.7, s32[24,384]{1,0:T(8,128)} %bitcast.8, f32[16,24]{1,0:T(8,128)} %bitcast.9), custom_call_target="tpu_custom_call" | custom-call | tf_op jit(solution)/shard_map/pack/pallas_call | solution.py:193
  1.5 4.1 %collective-permute-start = (f32[19,8,128]{2,1,0:T(8,128)S(1)}, f32[19,8,128]{2,1,0:T(8,128)S(1)}, u32[]{:S(2)}, u32[]{:S(2)}) collective-permute-start(f32[19,8,128]{2,1,0:T(8,128)S(1)} %pack.1.refs_0_), channel_id=1, source_target_pairs={{0,8},{1,9},{2,10},{3,11},{4,12},{5,13},{6,14},{7,15},{8,0},{9,1},... | collective-permute-start | bytes 233480 | tf_op jit(solution)/shard_map/ppermute | solution.py:189
  5.6 1.5 %collective-permute-start.2 = (f32[19,8,128]{2,1,0:T(8,128)S(1)}, f32[19,8,128]{2,1,0:T(8,128)S(1)}, u32[]{:S(2)}, u32[]{:S(2)}) collective-permute-start(f32[19,8,128]{2,1,0:T(8,128)S(1)} %pack.1.refs_0_), channel_id=1, source_target_pairs={{0,2},{1,3},{2,0},{3,1},{4,6},{5,7},{6,4},{7,5},{8,10},{9,11},{10,... | collective-permute-start | bytes 233480 | tf_op jit(solution)/shard_map/ppermute | solution.py:189
  7.1 1.6 %collective-permute-start.1 = (f32[19,8,128]{2,1,0:T(8,128)S(1)}, f32[19,8,128]{2,1,0:T(8,128)S(1)}, u32[]{:S(2)}, u32[]{:S(2)}) collective-permute-start(f32[19,8,128]{2,1,0:T(8,128)S(1)} %pack.1.refs_0_), channel_id=1, source_target_pairs={{0,4},{1,5},{2,6},{3,7},{4,0},{5,1},{6,2},{7,3},{8,12},{9,13},{10,... | collective-permute-start | bytes 233480 | tf_op jit(solution)/shard_map/ppermute | solution.py:189
  8.7 0.0 collective-permute-start.5
  8.7 1.8 %collective-permute-start.4 = (f32[19,8,128]{2,1,0:T(8,128)S(1)}, f32[19,8,128]{2,1,0:T(8,128)S(1)}, u32[]{:S(2)}, u32[]{:S(2)}) collective-permute-start(f32[19,8,128]{2,1,0:T(8,128)S(1)} %pack.1.refs_0_), channel_id=1, source_target_pairs={{0,6},{1,7},{2,4},{3,5},{4,2},{5,3},{6,0},{7,1},{8,14},{9,15},{10,... | collective-permute-start | bytes 233480 | tf_op jit(solution)/shard_map/ppermute | solution.py:189
  10.5 0.0 collective-permute-done.refs_1_
  10.5 0.6 %collective-permute-start.7 = (f32[19,8,128]{2,1,0:T(8,128)S(1)}, f32[19,8,128]{2,1,0:T(8,128)S(1)}, u32[]{:S(2)}, u32[]{:S(2)}) collective-permute-start(f32[19,8,128]{2,1,0:T(8,128)S(1)} %collective-permute-done.refs_1_), channel_id=1, source_target_pairs={{0,2},{1,3},{2,0},{3,1},{4,6},{5,7},{6,4},{7,5},{8,10},{9,11},{10,... | collective-permute-start | bytes 233480 | tf_op jit(solution)/shard_map/ppermute | solution.py:189
  11.1 0.0 collective-permute-done.2.refs_3_
  11.1 1.8 %collective-permute-start.6 = (f32[19,8,128]{2,1,0:T(8,128)S(1)}, f32[19,8,128]{2,1,0:T(8,128)S(1)}, u32[]{:S(2)}, u32[]{:S(2)}) collective-permute-start(f32[19,8,128]{2,1,0:T(8,128)S(1)} %collective-permute-done.refs_1_), channel_id=1, source_target_pairs={{0,4},{1,5},{2,6},{3,7},{4,0},{5,1},{6,2},{7,3},{8,12},{9,13},{10,... | collective-permute-start | bytes 233480 | tf_op jit(solution)/shard_map/ppermute | solution.py:189
  12.9 0.0 collective-permute-done.1.refs_2_
  12.9 0.1 collective-permute-start.3
  13.0 3.1 %collective-permute-done.5.refs_1_ = f32[19,8,128]{2,1,0:T(8,128)S(1)} collective-permute-done((f32[19,8,128]{2,1,0:T(8,128)S(1)}, f32[19,8,128]{2,1,0:T(8,128)S(1)}, u32[]{:S(2)}, u32[]{:S(2)}) %collective-permute-start.5) | collective-permute-done | bytes 77856 | tf_op jit(solution)/shard_map/ppermute | solution.py:189
  16.0 0.1 collective-permute-done.4.refs_0_
  16.1 0.4 %collective-permute-done.7.refs_3_ = f32[19,8,128]{2,1,0:T(8,128)S(1)} collective-permute-done((f32[19,8,128]{2,1,0:T(8,128)S(1)}, f32[19,8,128]{2,1,0:T(8,128)S(1)}, u32[]{:S(2)}, u32[]{:S(2)}) %collective-permute-start.7) | collective-permute-done | bytes 77856 | tf_op jit(solution)/shard_map/ppermute | solution.py:189
  16.5 0.0 collective-permute-done.6.refs_2_
  16.5 0.1 collective-permute-start.8
  16.6 0.0 collective-permute-done.3.refs_1_
  16.6 1.6 %collective-permute-done.8.refs_3_ = f32[76,8,128]{2,1,0:T(8,128)S(1)} collective-permute-done((f32[76,8,128]{2,1,0:T(8,128)S(1)}, f32[76,8,128]{2,1,0:T(8,128)S(1)}, u32[]{:S(2)}, u32[]{:S(2)}) %collective-permute-start.8) | collective-permute-done | bytes 311328 | tf_op jit(solution)/shard_map/ppermute | solution.py:189
  18.2 2.8 %group_smacof.1 = (f32[16,24]{1,0:T(8,128)}, f32[1,3]{1,0:T(1,128)}) custom-call(f32[76,8,128]{2,1,0:T(8,128)S(1)} %join.2.refs_0_, f32[76,8,128]{2,1,0:T(8,128)S(1)} %collective-permute-done.3.refs_1_, f32[76,8,128]{2,1,0:T(8,128)S(1)} %join.3.refs_2_, f32[76,8,128]{2,1,0:T(8,128)S(1)} %collective-permute-done.8.refs_3_), custom_call_target="tpu_custom_call" | custom-call | tf_op jit(solution)/shard_map/group_smacof/pallas_call | solution.py:233
  (2 shorter events, 0.0 us)
Async XLA Ops:
  1.5 9.0 %collective-permute-start = (f32[19,8,128]{2,1,0:T(8,128)S(1)}, f32[19,8,128]{2,1,0:T(8,128)S(1)}, u32[]{:S(2)}, u32[]{:S(2)}) collective-permute-start(f32[19,8,128]{2,1,0:T(8,128)S(1)} %pack.1.refs_0_), channel_id=1, source_target_pairs={{0,8},{1,9},{2,10},{3,11},{4,12},{5,13},{6,14},{7,15},{8,0},{9,1},... | collective-permute-start | bytes 233480 | tf_op jit(solution)/shard_map/ppermute | solution.py:189
  5.6 5.4 %collective-permute-start.2 = (f32[19,8,128]{2,1,0:T(8,128)S(1)}, f32[19,8,128]{2,1,0:T(8,128)S(1)}, u32[]{:S(2)}, u32[]{:S(2)}) collective-permute-start(f32[19,8,128]{2,1,0:T(8,128)S(1)} %pack.1.refs_0_), channel_id=1, source_target_pairs={{0,2},{1,3},{2,0},{3,1},{4,6},{5,7},{6,4},{7,5},{8,10},{9,11},{10,... | collective-permute-start | bytes 233480 | tf_op jit(solution)/shard_map/ppermute | solution.py:189
  7.1 5.7 %collective-permute-start.1 = (f32[19,8,128]{2,1,0:T(8,128)S(1)}, f32[19,8,128]{2,1,0:T(8,128)S(1)}, u32[]{:S(2)}, u32[]{:S(2)}) collective-permute-start(f32[19,8,128]{2,1,0:T(8,128)S(1)} %pack.1.refs_0_), channel_id=1, source_target_pairs={{0,4},{1,5},{2,6},{3,7},{4,0},{5,1},{6,2},{7,3},{8,12},{9,13},{10,... | collective-permute-start | bytes 233480 | tf_op jit(solution)/shard_map/ppermute | solution.py:189
  8.7 7.3 %collective-permute-start.5 = (f32[19,8,128]{2,1,0:T(8,128)S(1)}, f32[19,8,128]{2,1,0:T(8,128)S(1)}, u32[]{:S(2)}, u32[]{:S(2)}) collective-permute-start(f32[19,8,128]{2,1,0:T(8,128)S(1)} %pack.1.refs_0_), channel_id=1, source_target_pairs={{0,14},{1,15},{2,12},{3,13},{4,10},{5,11},{6,8},{7,9},{8,6},{9,7},... | collective-permute-start | bytes 233480 | tf_op jit(solution)/shard_map/ppermute | solution.py:189
  8.7 7.4 %collective-permute-start.4 = (f32[19,8,128]{2,1,0:T(8,128)S(1)}, f32[19,8,128]{2,1,0:T(8,128)S(1)}, u32[]{:S(2)}, u32[]{:S(2)}) collective-permute-start(f32[19,8,128]{2,1,0:T(8,128)S(1)} %pack.1.refs_0_), channel_id=1, source_target_pairs={{0,6},{1,7},{2,4},{3,5},{4,2},{5,3},{6,0},{7,1},{8,14},{9,15},{10,... | collective-permute-start | bytes 233480 | tf_op jit(solution)/shard_map/ppermute | solution.py:189
  10.5 6.0 %collective-permute-start.7 = (f32[19,8,128]{2,1,0:T(8,128)S(1)}, f32[19,8,128]{2,1,0:T(8,128)S(1)}, u32[]{:S(2)}, u32[]{:S(2)}) collective-permute-start(f32[19,8,128]{2,1,0:T(8,128)S(1)} %collective-permute-done.refs_1_), channel_id=1, source_target_pairs={{0,2},{1,3},{2,0},{3,1},{4,6},{5,7},{6,4},{7,5},{8,10},{9,11},{10,... | collective-permute-start | bytes 233480 | tf_op jit(solution)/shard_map/ppermute | solution.py:189
  11.1 5.5 %collective-permute-start.6 = (f32[19,8,128]{2,1,0:T(8,128)S(1)}, f32[19,8,128]{2,1,0:T(8,128)S(1)}, u32[]{:S(2)}, u32[]{:S(2)}) collective-permute-start(f32[19,8,128]{2,1,0:T(8,128)S(1)} %collective-permute-done.refs_1_), channel_id=1, source_target_pairs={{0,4},{1,5},{2,6},{3,7},{4,0},{5,1},{6,2},{7,3},{8,12},{9,13},{10,... | collective-permute-start | bytes 233480 | tf_op jit(solution)/shard_map/ppermute | solution.py:189
  12.9 3.7 %collective-permute-start.3 = (f32[76,8,128]{2,1,0:T(8,128)S(1)}, f32[76,8,128]{2,1,0:T(8,128)S(1)}, u32[]{:S(2)}, u32[]{:S(2)}) collective-permute-start(f32[76,8,128]{2,1,0:T(8,128)S(1)} %join.2.refs_0_), channel_id=1, source_target_pairs={{0,1},{1,0},{2,3},{3,2},{4,5},{5,4},{6,7},{7,6},{8,9},{9,8},{10,11... | collective-permute-start | bytes 933896 | tf_op jit(solution)/shard_map/ppermute | solution.py:189
  16.5 1.7 %collective-permute-start.8 = (f32[76,8,128]{2,1,0:T(8,128)S(1)}, f32[76,8,128]{2,1,0:T(8,128)S(1)}, u32[]{:S(2)}, u32[]{:S(2)}) collective-permute-start(f32[76,8,128]{2,1,0:T(8,128)S(1)} %join.3.refs_2_), channel_id=1, source_target_pairs={{0,1},{1,0},{2,3},{3,2},{4,5},{5,4},{6,7},{7,6},{8,9},{9,8},{10,11... | collective-permute-start | bytes 933896 | tf_op jit(solution)/shard_map/ppermute | solution.py:189

commit v16 on v15

--- a/solution.py
+++ b/solution.py
@@ -205,12 +205,13 @@
         name="pack",
     )(*(pltpu.with_memory_space_constraint(array, pltpu.HBM) for array in inputs))
     far, near, side = devices // 2, devices // 4, devices // 8
+    cross = 1
     held = {0: packed}
     for offset in (far, side, near, near | side, far | near | side):
-        held[offset] = swap(packed, offset)
+        held[offset | cross] = swap(packed, offset | cross)
     for step in (near, side):
-        held[far | step] = swap(held[far], step)
-    early = [0, far, near, side]
+        held[far | step] = swap(held[far | cross], step | cross)
+    early = [0, far | cross, near | cross, side | cross]
     late = [offset for offset in held if offset not in early]
     block = packed.shape[0]
 
@@ -226,9 +227,7 @@
         )(*(held[offset] for offset in group))
 
     first, second = join(early, 1), join(late, 1)
-    first_swapped = swap(first, 1)
-
-    slots = [first, first_swapped, second, swap(second, 1)]
+    slots = [first, swap(first, 1), second, swap(second, 1)]
     offsets = [early, [o ^ 1 for o in early], late, [o ^ 1 for o in late]]
     final, stress = pl.pallas_call(
         functools.partial(group_kernel, offsets, per_dev),

time: 21.2 us -> 21.7 us (1.024)
  waiting for transfers between devices: 5.15 us -> 6.14 us
  starting transfers between devices: 11.5 us -> 11 us
    ppermute x9, waiting for transfers between devices: 5.15 us -> 6.14 us  [swap(): lax.ppermute(value, 'wide', [(i, i ^ offset) for i in range(devices)])]
    ppermute x9, starting transfers between devices: 11.5 us -> 11 us  [swap(): lax.ppermute(value, 'wide', [(i, i ^ offset) for i in range(devices)])]
where the time goes in v16:
time: 21.7 us; the launch traced here: 21.5 us
  starting transfers between devices  11 us (51%)
  waiting for transfers between devices  6.14 us (28%)
  Pallas kernels  3.74 us (17%)
  between operations  0.66 us (3%)
    ppermute x9, starting transfers between devices, swap(): lax.ppermute(value, 'wide', [(i, i ^ offset) for i in range(devices)])  11 us
    ppermute x9, waiting for transfers between devices, swap(): lax.ppermute(value, 'wide', [(i, i ^ offset) for i in range(devices)])  6.14 us
    pallas_call x1, Pallas kernels, small_body(): pl.pallas_call(functools.partial(group_kernel, offsets, per_dev), out_sha...  2.81 us
    pallas_call x1, Pallas kernels, small_body(): pl.pallas_call(pack_kernel, out_shape=f32((tiles, SUBLANES, LANES)), in_s...  0.89 us
  transfers between devices with their start and end apart: 9, of which 4 were waited for; matrix products, arithmetic and copies ran while one was open for 0% of the time, Pallas kernels for 0%

profile of v16, /device:TPU:0, one launch (start us, length us, event | category | flops | bytes accessed | tf_op | source)
XLA Modules:
  0.0 21.5 jit_solution(4863464897991617770)
XLA Ops:
  0.6 0.9 %pack.1.refs_0_ = f32[19,8,128]{2,1,0:T(8,128)S(1)} custom-call(f32[24,384]{1,0:T(8,128)} %bitcast.7, s32[24,384]{1,0:T(8,128)} %bitcast.8, f32[16,24]{1,0:T(8,128)} %bitcast.9), custom_call_target="tpu_custom_call" | custom-call | tf_op jit(solution)/shard_map/pack/pallas_call | solution.py:193
  1.5 3.5 %collective-permute-start = (f32[19,8,128]{2,1,0:T(8,128)S(1)}, f32[19,8,128]{2,1,0:T(8,128)S(1)}, u32[]{:S(2)}, u32[]{:S(2)}) collective-permute-start(f32[19,8,128]{2,1,0:T(8,128)S(1)} %pack.1.refs_0_), channel_id=1, source_target_pairs={{0,9},{1,8},{2,11},{3,10},{4,13},{5,12},{6,15},{7,14},{8,1},{9,0},... | collective-permute-start | bytes 233480 | tf_op jit(solution)/shard_map/ppermute | solution.py:189
  5.1 1.8 %collective-permute-start.2 = (f32[19,8,128]{2,1,0:T(8,128)S(1)}, f32[19,8,128]{2,1,0:T(8,128)S(1)}, u32[]{:S(2)}, u32[]{:S(2)}) collective-permute-start(f32[19,8,128]{2,1,0:T(8,128)S(1)} %pack.1.refs_0_), channel_id=1, source_target_pairs={{0,3},{1,2},{2,1},{3,0},{4,7},{5,6},{6,5},{7,4},{8,11},{9,10},{10,... | collective-permute-start | bytes 233480 | tf_op jit(solution)/shard_map/ppermute | solution.py:189
  6.8 1.0 %collective-permute-start.1 = (f32[19,8,128]{2,1,0:T(8,128)S(1)}, f32[19,8,128]{2,1,0:T(8,128)S(1)}, u32[]{:S(2)}, u32[]{:S(2)}) collective-permute-start(f32[19,8,128]{2,1,0:T(8,128)S(1)} %pack.1.refs_0_), channel_id=1, source_target_pairs={{0,5},{1,4},{2,7},{3,6},{4,1},{5,0},{6,3},{7,2},{8,13},{9,12},{10,... | collective-permute-start | bytes 233480 | tf_op jit(solution)/shard_map/ppermute | solution.py:189
  7.9 0.1 collective-permute-start.5
  7.9 1.8 %collective-permute-start.4 = (f32[19,8,128]{2,1,0:T(8,128)S(1)}, f32[19,8,128]{2,1,0:T(8,128)S(1)}, u32[]{:S(2)}, u32[]{:S(2)}) collective-permute-start(f32[19,8,128]{2,1,0:T(8,128)S(1)} %pack.1.refs_0_), channel_id=1, source_target_pairs={{0,7},{1,6},{2,5},{3,4},{4,3},{5,2},{6,1},{7,0},{8,15},{9,14},{10,... | collective-permute-start | bytes 233480 | tf_op jit(solution)/shard_map/ppermute | solution.py:189
  9.7 0.0 collective-permute-done.refs_1_
  9.7 1.6 %collective-permute-start.7 = (f32[19,8,128]{2,1,0:T(8,128)S(1)}, f32[19,8,128]{2,1,0:T(8,128)S(1)}, u32[]{:S(2)}, u32[]{:S(2)}) collective-permute-start(f32[19,8,128]{2,1,0:T(8,128)S(1)} %collective-permute-done.refs_1_), channel_id=1, source_target_pairs={{0,3},{1,2},{2,1},{3,0},{4,7},{5,6},{6,5},{7,4},{8,11},{9,10},{10,... | collective-permute-start | bytes 233480 | tf_op jit(solution)/shard_map/ppermute | solution.py:189
  11.3 0.0 collective-permute-done.2.refs_3_
  11.3 0.9 %collective-permute-start.6 = (f32[19,8,128]{2,1,0:T(8,128)S(1)}, f32[19,8,128]{2,1,0:T(8,128)S(1)}, u32[]{:S(2)}, u32[]{:S(2)}) collective-permute-start(f32[19,8,128]{2,1,0:T(8,128)S(1)} %collective-permute-done.refs_1_), channel_id=1, source_target_pairs={{0,5},{1,4},{2,7},{3,6},{4,1},{5,0},{6,3},{7,2},{8,13},{9,12},{10,... | collective-permute-start | bytes 233480 | tf_op jit(solution)/shard_map/ppermute | solution.py:189
  12.1 0.0 collective-permute-done.1.refs_2_
  12.2 0.2 collective-permute-start.3
  12.4 2.2 %collective-permute-done.5.refs_1_ = f32[19,8,128]{2,1,0:T(8,128)S(1)} collective-permute-done((f32[19,8,128]{2,1,0:T(8,128)S(1)}, f32[19,8,128]{2,1,0:T(8,128)S(1)}, u32[]{:S(2)}, u32[]{:S(2)}) %collective-permute-start.5) | collective-permute-done | bytes 77856 | tf_op jit(solution)/shard_map/ppermute | solution.py:189
  14.6 0.0 collective-permute-done.4.refs_0_
  14.6 2.4 %collective-permute-done.7.refs_3_ = f32[19,8,128]{2,1,0:T(8,128)S(1)} collective-permute-done((f32[19,8,128]{2,1,0:T(8,128)S(1)}, f32[19,8,128]{2,1,0:T(8,128)S(1)}, u32[]{:S(2)}, u32[]{:S(2)}) %collective-permute-start.7) | collective-permute-done | bytes 77856 | tf_op jit(solution)/shard_map/ppermute | solution.py:189
  17.0 0.1 collective-permute-done.6.refs_2_
  17.1 0.2 collective-permute-start.8
  17.2 0.0 collective-permute-done.3.refs_1_
  17.2 1.5 %collective-permute-done.8.refs_3_ = f32[76,8,128]{2,1,0:T(8,128)S(1)} collective-permute-done((f32[76,8,128]{2,1,0:T(8,128)S(1)}, f32[76,8,128]{2,1,0:T(8,128)S(1)}, u32[]{:S(2)}, u32[]{:S(2)}) %collective-permute-start.8) | collective-permute-done | bytes 311328 | tf_op jit(solution)/shard_map/ppermute | solution.py:189
  18.7 2.8 %group_smacof.1 = (f32[16,24]{1,0:T(8,128)}, f32[1,3]{1,0:T(1,128)}) custom-call(f32[76,8,128]{2,1,0:T(8,128)S(1)} %join.2.refs_0_, f32[76,8,128]{2,1,0:T(8,128)S(1)} %collective-permute-done.3.refs_1_, f32[76,8,128]{2,1,0:T(8,128)S(1)} %join.3.refs_2_, f32[76,8,128]{2,1,0:T(8,128)S(1)} %collective-permute-done.8.refs_3_), custom_call_target="tpu_custom_call" | custom-call | tf_op jit(solution)/shard_map/group_smacof/pallas_call | solution.py:232
  (2 shorter events, 0.0 us)
Async XLA Ops:
  1.5 8.2 %collective-permute-start = (f32[19,8,128]{2,1,0:T(8,128)S(1)}, f32[19,8,128]{2,1,0:T(8,128)S(1)}, u32[]{:S(2)}, u32[]{:S(2)}) collective-permute-start(f32[19,8,128]{2,1,0:T(8,128)S(1)} %pack.1.refs_0_), channel_id=1, source_target_pairs={{0,9},{1,8},{2,11},{3,10},{4,13},{5,12},{6,15},{7,14},{8,1},{9,0},... | collective-permute-start | bytes 233480 | tf_op jit(solution)/shard_map/ppermute | solution.py:189
  5.1 6.2 %collective-permute-start.2 = (f32[19,8,128]{2,1,0:T(8,128)S(1)}, f32[19,8,128]{2,1,0:T(8,128)S(1)}, u32[]{:S(2)}, u32[]{:S(2)}) collective-permute-start(f32[19,8,128]{2,1,0:T(8,128)S(1)} %pack.1.refs_0_), channel_id=1, source_target_pairs={{0,3},{1,2},{2,1},{3,0},{4,7},{5,6},{6,5},{7,4},{8,11},{9,10},{10,... | collective-permute-start | bytes 233480 | tf_op jit(solution)/shard_map/ppermute | solution.py:189
  6.8 5.3 %collective-permute-start.1 = (f32[19,8,128]{2,1,0:T(8,128)S(1)}, f32[19,8,128]{2,1,0:T(8,128)S(1)}, u32[]{:S(2)}, u32[]{:S(2)}) collective-permute-start(f32[19,8,128]{2,1,0:T(8,128)S(1)} %pack.1.refs_0_), channel_id=1, source_target_pairs={{0,5},{1,4},{2,7},{3,6},{4,1},{5,0},{6,3},{7,2},{8,13},{9,12},{10,... | collective-permute-start | bytes 233480 | tf_op jit(solution)/shard_map/ppermute | solution.py:189
  7.9 6.7 %collective-permute-start.5 = (f32[19,8,128]{2,1,0:T(8,128)S(1)}, f32[19,8,128]{2,1,0:T(8,128)S(1)}, u32[]{:S(2)}, u32[]{:S(2)}) collective-permute-start(f32[19,8,128]{2,1,0:T(8,128)S(1)} %pack.1.refs_0_), channel_id=1, source_target_pairs={{0,15},{1,14},{2,13},{3,12},{4,11},{5,10},{6,9},{7,8},{8,7},{9,6},... | collective-permute-start | bytes 233480 | tf_op jit(solution)/shard_map/ppermute | solution.py:189
  7.9 6.7 %collective-permute-start.4 = (f32[19,8,128]{2,1,0:T(8,128)S(1)}, f32[19,8,128]{2,1,0:T(8,128)S(1)}, u32[]{:S(2)}, u32[]{:S(2)}) collective-permute-start(f32[19,8,128]{2,1,0:T(8,128)S(1)} %pack.1.refs_0_), channel_id=1, source_target_pairs={{0,7},{1,6},{2,5},{3,4},{4,3},{5,2},{6,1},{7,0},{8,15},{9,14},{10,... | collective-permute-start | bytes 233480 | tf_op jit(solution)/shard_map/ppermute | solution.py:189
  9.7 7.3 %collective-permute-start.7 = (f32[19,8,128]{2,1,0:T(8,128)S(1)}, f32[19,8,128]{2,1,0:T(8,128)S(1)}, u32[]{:S(2)}, u32[]{:S(2)}) collective-permute-start(f32[19,8,128]{2,1,0:T(8,128)S(1)} %collective-permute-done.refs_1_), channel_id=1, source_target_pairs={{0,3},{1,2},{2,1},{3,0},{4,7},{5,6},{6,5},{7,4},{8,11},{9,10},{10,... | collective-permute-start | bytes 233480 | tf_op jit(solution)/shard_map/ppermute | solution.py:189
  11.3 5.7 %collective-permute-start.6 = (f32[19,8,128]{2,1,0:T(8,128)S(1)}, f32[19,8,128]{2,1,0:T(8,128)S(1)}, u32[]{:S(2)}, u32[]{:S(2)}) collective-permute-start(f32[19,8,128]{2,1,0:T(8,128)S(1)} %collective-permute-done.refs_1_), channel_id=1, source_target_pairs={{0,5},{1,4},{2,7},{3,6},{4,1},{5,0},{6,3},{7,2},{8,13},{9,12},{10,... | collective-permute-start | bytes 233480 | tf_op jit(solution)/shard_map/ppermute | solution.py:189
  12.2 5.1 %collective-permute-start.3 = (f32[76,8,128]{2,1,0:T(8,128)S(1)}, f32[76,8,128]{2,1,0:T(8,128)S(1)}, u32[]{:S(2)}, u32[]{:S(2)}) collective-permute-start(f32[76,8,128]{2,1,0:T(8,128)S(1)} %join.2.refs_0_), channel_id=1, source_target_pairs={{0,1},{1,0},{2,3},{3,2},{4,5},{5,4},{6,7},{7,6},{8,9},{9,8},{10,11... | collective-permute-start | bytes 933896 | tf_op jit(solution)/shard_map/ppermute | solution.py:189
  17.1 1.7 %collective-permute-start.8 = (f32[76,8,128]{2,1,0:T(8,128)S(1)}, f32[76,8,128]{2,1,0:T(8,128)S(1)}, u32[]{:S(2)}, u32[]{:S(2)}) collective-permute-start(f32[76,8,128]{2,1,0:T(8,128)S(1)} %join.3.refs_2_), channel_id=1, source_target_pairs={{0,1},{1,0},{2,3},{3,2},{4,5},{5,4},{6,7},{7,6},{8,9},{9,8},{10,11... | collective-permute-start | bytes 933896 | tf_op jit(solution)/shard_map/ppermute | solution.py:189

commit v17 on v15

--- a/solution.py
+++ b/solution.py
@@ -206,10 +206,10 @@
     )(*(pltpu.with_memory_space_constraint(array, pltpu.HBM) for array in inputs))
     far, near, side = devices // 2, devices // 4, devices // 8
     held = {0: packed}
-    for offset in (far, side, near, near | side, far | near | side):
+    for offset in (far, side, near, far | near | side):
         held[offset] = swap(packed, offset)
-    for step in (near, side):
-        held[far | step] = swap(held[far], step)
+    for source, step in ((far, near), (far, side), (side, near)):
+        held[source | step] = swap(held[source], step)
     early = [0, far, near, side]
     late = [offset for offset in held if offset not in early]
     block = packed.shape[0]
@@ -226,9 +226,7 @@
         )(*(held[offset] for offset in group))
 
     first, second = join(early, 1), join(late, 1)
-    first_swapped = swap(first, 1)
-
-    slots = [first, first_swapped, second, swap(second, 1)]
+    slots = [first, swap(first, 1), second, swap(second, 1)]
     offsets = [early, [o ^ 1 for o in early], late, [o ^ 1 for o in late]]
     final, stress = pl.pallas_call(
         functools.partial(group_kernel, offsets, per_dev),

time: 21.2 us -> 21.2 us (level)
  starting transfers between devices: 11.5 us -> 10.4 us
  waiting for transfers between devices: 5.15 us -> 6.15 us
    ppermute x9, starting transfers between devices: 11.5 us -> 10.4 us  [swap(): lax.ppermute(value, 'wide', [(i, i ^ offset) for i in range(devices)])]
    ppermute x9, waiting for transfers between devices: 5.15 us -> 6.15 us  [swap(): lax.ppermute(value, 'wide', [(i, i ^ offset) for i in range(devices)])]
where the time goes in v17:
time: 21.2 us; the launch traced here: 21 us
  starting transfers between devices  10.4 us (49%)
  waiting for transfers between devices  6.15 us (29%)
  Pallas kernels  3.73 us (18%)
  between operations  0.68 us (3%)
    ppermute x9, starting transfers between devices, swap(): lax.ppermute(value, 'wide', [(i, i ^ offset) for i in range(devices)])  10.4 us
    ppermute x9, waiting for transfers between devices, swap(): lax.ppermute(value, 'wide', [(i, i ^ offset) for i in range(devices)])  6.15 us
    pallas_call x1, Pallas kernels, small_body(): pl.pallas_call(functools.partial(group_kernel, offsets, per_dev), out_sha...  2.8 us
    pallas_call x1, Pallas kernels, small_body(): pl.pallas_call(pack_kernel, out_shape=f32((tiles, SUBLANES, LANES)), in_s...  0.89 us
  transfers between devices with their start and end apart: 9, of which 4 were waited for; matrix products, arithmetic and copies ran while one was open for 0% of the time, Pallas kernels for 0%

profile of v17, /device:TPU:0, one launch (start us, length us, event | category | flops | bytes accessed | tf_op | source)
XLA Modules:
  0.0 21.0 jit_solution(609505129428107810)
XLA Ops:
  0.6 0.9 %pack.1.refs_0_ = f32[19,8,128]{2,1,0:T(8,128)S(1)} custom-call(f32[24,384]{1,0:T(8,128)} %bitcast.7, s32[24,384]{1,0:T(8,128)} %bitcast.8, f32[16,24]{1,0:T(8,128)} %bitcast.9), custom_call_target="tpu_custom_call" | custom-call | tf_op jit(solution)/shard_map/pack/pallas_call | solution.py:193
  1.5 3.0 %collective-permute-start.2 = (f32[19,8,128]{2,1,0:T(8,128)S(1)}, f32[19,8,128]{2,1,0:T(8,128)S(1)}, u32[]{:S(2)}, u32[]{:S(2)}) collective-permute-start(f32[19,8,128]{2,1,0:T(8,128)S(1)} %pack.1.refs_0_), channel_id=1, source_target_pairs={{0,2},{1,3},{2,0},{3,1},{4,6},{5,7},{6,4},{7,5},{8,10},{9,11},{10,... | collective-permute-start | bytes 233480 | tf_op jit(solution)/shard_map/ppermute | solution.py:189
  4.5 2.6 %collective-permute-start = (f32[19,8,128]{2,1,0:T(8,128)S(1)}, f32[19,8,128]{2,1,0:T(8,128)S(1)}, u32[]{:S(2)}, u32[]{:S(2)}) collective-permute-start(f32[19,8,128]{2,1,0:T(8,128)S(1)} %pack.1.refs_0_), channel_id=1, source_target_pairs={{0,8},{1,9},{2,10},{3,11},{4,12},{5,13},{6,14},{7,15},{8,0},{9,1},... | collective-permute-start | bytes 233480 | tf_op jit(solution)/shard_map/ppermute | solution.py:189
  7.1 1.6 %collective-permute-start.1 = (f32[19,8,128]{2,1,0:T(8,128)S(1)}, f32[19,8,128]{2,1,0:T(8,128)S(1)}, u32[]{:S(2)}, u32[]{:S(2)}) collective-permute-start(f32[19,8,128]{2,1,0:T(8,128)S(1)} %pack.1.refs_0_), channel_id=1, source_target_pairs={{0,4},{1,5},{2,6},{3,7},{4,0},{5,1},{6,2},{7,3},{8,12},{9,13},{10,... | collective-permute-start | bytes 233480 | tf_op jit(solution)/shard_map/ppermute | solution.py:189
  8.7 0.0 collective-permute-start.4
  8.7 0.0 collective-permute-done.2.refs_3_
  8.7 0.9 %collective-permute-start.7 = (f32[19,8,128]{2,1,0:T(8,128)S(1)}, f32[19,8,128]{2,1,0:T(8,128)S(1)}, u32[]{:S(2)}, u32[]{:S(2)}) collective-permute-start(f32[19,8,128]{2,1,0:T(8,128)S(1)} %collective-permute-done.2.refs_3_), channel_id=1, source_target_pairs={{0,4},{1,5},{2,6},{3,7},{4,0},{5,1},{6,2},{7,3},{8,12},{9,13},{10,... | collective-permute-start | bytes 233480 | tf_op jit(solution)/shard_map/ppermute | solution.py:189
  9.6 1.7 %collective-permute-done.refs_1_ = f32[19,8,128]{2,1,0:T(8,128)S(1)} collective-permute-done((f32[19,8,128]{2,1,0:T(8,128)S(1)}, f32[19,8,128]{2,1,0:T(8,128)S(1)}, u32[]{:S(2)}, u32[]{:S(2)}) %collective-permute-start) | collective-permute-done | bytes 77856 | tf_op jit(solution)/shard_map/ppermute | solution.py:189
  11.2 0.0 collective-permute-start.6
  11.2 2.3 %collective-permute-start.5 = (f32[19,8,128]{2,1,0:T(8,128)S(1)}, f32[19,8,128]{2,1,0:T(8,128)S(1)}, u32[]{:S(2)}, u32[]{:S(2)}) collective-permute-start(f32[19,8,128]{2,1,0:T(8,128)S(1)} %collective-permute-done.refs_1_), channel_id=1, source_target_pairs={{0,4},{1,5},{2,6},{3,7},{4,0},{5,1},{6,2},{7,3},{8,12},{9,13},{10,... | collective-permute-start | bytes 233480 | tf_op jit(solution)/shard_map/ppermute | solution.py:189
  13.5 0.0 collective-permute-done.1.refs_2_
  13.5 0.1 collective-permute-start.3
  13.6 2.7 %collective-permute-done.4.refs_0_ = f32[19,8,128]{2,1,0:T(8,128)S(1)} collective-permute-done((f32[19,8,128]{2,1,0:T(8,128)S(1)}, f32[19,8,128]{2,1,0:T(8,128)S(1)}, u32[]{:S(2)}, u32[]{:S(2)}) %collective-permute-start.4) | collective-permute-done | bytes 77856 | tf_op jit(solution)/shard_map/ppermute | solution.py:189
  16.3 0.0 collective-permute-done.7.refs_3_
  16.3 0.2 collective-permute-done.6.refs_2_
  16.5 0.0 collective-permute-done.5.refs_1_
  16.5 0.1 collective-permute-start.8
  16.6 0.0 collective-permute-done.3.refs_1_
  16.6 1.6 %collective-permute-done.8.refs_3_ = f32[76,8,128]{2,1,0:T(8,128)S(1)} collective-permute-done((f32[76,8,128]{2,1,0:T(8,128)S(1)}, f32[76,8,128]{2,1,0:T(8,128)S(1)}, u32[]{:S(2)}, u32[]{:S(2)}) %collective-permute-start.8) | collective-permute-done | bytes 311328 | tf_op jit(solution)/shard_map/ppermute | solution.py:189
  18.2 2.8 %group_smacof.1 = (f32[16,24]{1,0:T(8,128)}, f32[1,3]{1,0:T(1,128)}) custom-call(f32[76,8,128]{2,1,0:T(8,128)S(1)} %join.2.refs_0_, f32[76,8,128]{2,1,0:T(8,128)S(1)} %collective-permute-done.3.refs_1_, f32[76,8,128]{2,1,0:T(8,128)S(1)} %join.3.refs_2_, f32[76,8,128]{2,1,0:T(8,128)S(1)} %collective-permute-done.8.refs_3_), custom_call_target="tpu_custom_call" | custom-call | tf_op jit(solution)/shard_map/group_smacof/pallas_call | solution.py:231
  (2 shorter events, 0.0 us)
Async XLA Ops:
  1.5 7.2 %collective-permute-start.2 = (f32[19,8,128]{2,1,0:T(8,128)S(1)}, f32[19,8,128]{2,1,0:T(8,128)S(1)}, u32[]{:S(2)}, u32[]{:S(2)}) collective-permute-start(f32[19,8,128]{2,1,0:T(8,128)S(1)} %pack.1.refs_0_), channel_id=1, source_target_pairs={{0,2},{1,3},{2,0},{3,1},{4,6},{5,7},{6,4},{7,5},{8,10},{9,11},{10,... | collective-permute-start | bytes 233480 | tf_op jit(solution)/shard_map/ppermute | solution.py:189
  4.5 6.7 %collective-permute-start = (f32[19,8,128]{2,1,0:T(8,128)S(1)}, f32[19,8,128]{2,1,0:T(8,128)S(1)}, u32[]{:S(2)}, u32[]{:S(2)}) collective-permute-start(f32[19,8,128]{2,1,0:T(8,128)S(1)} %pack.1.refs_0_), channel_id=1, source_target_pairs={{0,8},{1,9},{2,10},{3,11},{4,12},{5,13},{6,14},{7,15},{8,0},{9,1},... | collective-permute-start | bytes 233480 | tf_op jit(solution)/shard_map/ppermute | solution.py:189
  7.1 6.4 %collective-permute-start.1 = (f32[19,8,128]{2,1,0:T(8,128)S(1)}, f32[19,8,128]{2,1,0:T(8,128)S(1)}, u32[]{:S(2)}, u32[]{:S(2)}) collective-permute-start(f32[19,8,128]{2,1,0:T(8,128)S(1)} %pack.1.refs_0_), channel_id=1, source_target_pairs={{0,4},{1,5},{2,6},{3,7},{4,0},{5,1},{6,2},{7,3},{8,12},{9,13},{10,... | collective-permute-start | bytes 233480 | tf_op jit(solution)/shard_map/ppermute | solution.py:189
  8.7 7.6 %collective-permute-start.4 = (f32[19,8,128]{2,1,0:T(8,128)S(1)}, f32[19,8,128]{2,1,0:T(8,128)S(1)}, u32[]{:S(2)}, u32[]{:S(2)}) collective-permute-start(f32[19,8,128]{2,1,0:T(8,128)S(1)} %pack.1.refs_0_), channel_id=1, source_target_pairs={{0,14},{1,15},{2,12},{3,13},{4,10},{5,11},{6,8},{7,9},{8,6},{9,7},... | collective-permute-start | bytes 233480 | tf_op jit(solution)/shard_map/ppermute | solution.py:189
  8.7 7.6 %collective-permute-start.7 = (f32[19,8,128]{2,1,0:T(8,128)S(1)}, f32[19,8,128]{2,1,0:T(8,128)S(1)}, u32[]{:S(2)}, u32[]{:S(2)}) collective-permute-start(f32[19,8,128]{2,1,0:T(8,128)S(1)} %collective-permute-done.2.refs_3_), channel_id=1, source_target_pairs={{0,4},{1,5},{2,6},{3,7},{4,0},{5,1},{6,2},{7,3},{8,12},{9,13},{10,... | collective-permute-start | bytes 233480 | tf_op jit(solution)/shard_map/ppermute | solution.py:189
  11.2 5.2 %collective-permute-start.6 = (f32[19,8,128]{2,1,0:T(8,128)S(1)}, f32[19,8,128]{2,1,0:T(8,128)S(1)}, u32[]{:S(2)}, u32[]{:S(2)}) collective-permute-start(f32[19,8,128]{2,1,0:T(8,128)S(1)} %collective-permute-done.refs_1_), channel_id=1, source_target_pairs={{0,2},{1,3},{2,0},{3,1},{4,6},{5,7},{6,4},{7,5},{8,10},{9,11},{10,... | collective-permute-start | bytes 233480 | tf_op jit(solution)/shard_map/ppermute | solution.py:189
  11.2 5.3 %collective-permute-start.5 = (f32[19,8,128]{2,1,0:T(8,128)S(1)}, f32[19,8,128]{2,1,0:T(8,128)S(1)}, u32[]{:S(2)}, u32[]{:S(2)}) collective-permute-start(f32[19,8,128]{2,1,0:T(8,128)S(1)} %collective-permute-done.refs_1_), channel_id=1, source_target_pairs={{0,4},{1,5},{2,6},{3,7},{4,0},{5,1},{6,2},{7,3},{8,12},{9,13},{10,... | collective-permute-start | bytes 233480 | tf_op jit(solution)/shard_map/ppermute | solution.py:189
  13.5 3.1 %collective-permute-start.3 = (f32[76,8,128]{2,1,0:T(8,128)S(1)}, f32[76,8,128]{2,1,0:T(8,128)S(1)}, u32[]{:S(2)}, u32[]{:S(2)}) collective-permute-start(f32[76,8,128]{2,1,0:T(8,128)S(1)} %join.2.refs_0_), channel_id=1, source_target_pairs={{0,1},{1,0},{2,3},{3,2},{4,5},{5,4},{6,7},{7,6},{8,9},{9,8},{10,11... | collective-permute-start | bytes 933896 | tf_op jit(solution)/shard_map/ppermute | solution.py:189
  16.5 1.7 %collective-permute-start.8 = (f32[76,8,128]{2,1,0:T(8,128)S(1)}, f32[76,8,128]{2,1,0:T(8,128)S(1)}, u32[]{:S(2)}, u32[]{:S(2)}) collective-permute-start(f32[76,8,128]{2,1,0:T(8,128)S(1)} %join.3.refs_2_), channel_id=1, source_target_pairs={{0,1},{1,0},{2,3},{3,2},{4,5},{5,4},{6,7},{7,6},{8,9},{9,8},{10,11... | collective-permute-start | bytes 933896 | tf_op jit(solution)/shard_map/ppermute | solution.py:189

commit v18 on v17

--- a/solution.py
+++ b/solution.py
@@ -206,11 +206,11 @@
     )(*(pltpu.with_memory_space_constraint(array, pltpu.HBM) for array in inputs))
     far, near, side = devices // 2, devices // 4, devices // 8
     held = {0: packed}
-    for offset in (far, side, near, far | near | side):
+    for offset in (side, far, near, far | near | side):
         held[offset] = swap(packed, offset)
-    for source, step in ((far, near), (far, side), (side, near)):
+    for source, step in ((far, side), (side, near), (far, near)):
         held[source | step] = swap(held[source], step)
-    early = [0, far, near, side]
+    early = [0, side, near, far]
     late = [offset for offset in held if offset not in early]
     block = packed.shape[0]
 

time: 21.2 us -> 21.9 us (1.033)
  starting transfers between devices: 10.4 us -> 11 us
  waiting for transfers between devices: 6.15 us -> 6.38 us
    ppermute x9, starting transfers between devices: 10.4 us -> 11 us  [swap(): lax.ppermute(value, 'wide', [(i, i ^ offset) for i in range(devices)])]
    ppermute x9, waiting for transfers between devices: 6.15 us -> 6.38 us  [swap(): lax.ppermute(value, 'wide', [(i, i ^ offset) for i in range(devices)])]
where the time goes in v18:
time: 21.9 us; the launch traced here: 21.8 us
  starting transfers between devices  11 us (50%)
  waiting for transfers between devices  6.38 us (29%)
  Pallas kernels  3.74 us (17%)
  between operations  0.68 us (3%)
    ppermute x9, starting transfers between devices, swap(): lax.ppermute(value, 'wide', [(i, i ^ offset) for i in range(devices)])  11 us
    ppermute x9, waiting for transfers between devices, swap(): lax.ppermute(value, 'wide', [(i, i ^ offset) for i in range(devices)])  6.38 us
    pallas_call x1, Pallas kernels, small_body(): pl.pallas_call(functools.partial(group_kernel, offsets, per_dev), out_sha...  2.81 us
    pallas_call x1, Pallas kernels, small_body(): pl.pallas_call(pack_kernel, out_shape=f32((tiles, SUBLANES, LANES)), in_s...  0.89 us
  transfers between devices with their start and end apart: 9, of which 4 were waited for; matrix products, arithmetic and copies ran while one was open for 0% of the time, Pallas kernels for 0%

profile of v18, /device:TPU:0, one launch (start us, length us, event | category | flops | bytes accessed | tf_op | source)
XLA Modules:
  0.0 21.8 jit_solution(15632818635870183650)
XLA Ops:
  0.6 0.9 %pack.1.refs_0_ = f32[19,8,128]{2,1,0:T(8,128)S(1)} custom-call(f32[24,384]{1,0:T(8,128)} %bitcast.7, s32[24,384]{1,0:T(8,128)} %bitcast.8, f32[16,24]{1,0:T(8,128)} %bitcast.9), custom_call_target="tpu_custom_call" | custom-call | tf_op jit(solution)/shard_map/pack/pallas_call | solution.py:193
  1.5 4.1 %collective-permute-start.2 = (f32[19,8,128]{2,1,0:T(8,128)S(1)}, f32[19,8,128]{2,1,0:T(8,128)S(1)}, u32[]{:S(2)}, u32[]{:S(2)}) collective-permute-start(f32[19,8,128]{2,1,0:T(8,128)S(1)} %pack.1.refs_0_), channel_id=1, source_target_pairs={{0,8},{1,9},{2,10},{3,11},{4,12},{5,13},{6,14},{7,15},{8,0},{9,1},... | collective-permute-start | bytes 233480 | tf_op jit(solution)/shard_map/ppermute | solution.py:189
  5.6 1.5 %collective-permute-start = (f32[19,8,128]{2,1,0:T(8,128)S(1)}, f32[19,8,128]{2,1,0:T(8,128)S(1)}, u32[]{:S(2)}, u32[]{:S(2)}) collective-permute-start(f32[19,8,128]{2,1,0:T(8,128)S(1)} %pack.1.refs_0_), channel_id=1, source_target_pairs={{0,2},{1,3},{2,0},{3,1},{4,6},{5,7},{6,4},{7,5},{8,10},{9,11},{10,... | collective-permute-start | bytes 233480 | tf_op jit(solution)/shard_map/ppermute | solution.py:189
  7.1 1.6 %collective-permute-start.1 = (f32[19,8,128]{2,1,0:T(8,128)S(1)}, f32[19,8,128]{2,1,0:T(8,128)S(1)}, u32[]{:S(2)}, u32[]{:S(2)}) collective-permute-start(f32[19,8,128]{2,1,0:T(8,128)S(1)} %pack.1.refs_0_), channel_id=1, source_target_pairs={{0,4},{1,5},{2,6},{3,7},{4,0},{5,1},{6,2},{7,3},{8,12},{9,13},{10,... | collective-permute-start | bytes 233480 | tf_op jit(solution)/shard_map/ppermute | solution.py:189
  8.7 0.0 collective-permute-start.4
  8.7 0.7 %collective-permute-done.2.refs_3_ = f32[19,8,128]{2,1,0:T(8,128)S(1)} collective-permute-done((f32[19,8,128]{2,1,0:T(8,128)S(1)}, f32[19,8,128]{2,1,0:T(8,128)S(1)}, u32[]{:S(2)}, u32[]{:S(2)}) %collective-permute-start.2) | collective-permute-done | bytes 77856 | tf_op jit(solution)/shard_map/ppermute | solution.py:189
  9.4 1.2 %collective-permute-start.7 = (f32[19,8,128]{2,1,0:T(8,128)S(1)}, f32[19,8,128]{2,1,0:T(8,128)S(1)}, u32[]{:S(2)}, u32[]{:S(2)}) collective-permute-start(f32[19,8,128]{2,1,0:T(8,128)S(1)} %collective-permute-done.2.refs_3_), channel_id=1, source_target_pairs={{0,4},{1,5},{2,6},{3,7},{4,0},{5,1},{6,2},{7,3},{8,12},{9,13},{10,... | collective-permute-start | bytes 233480 | tf_op jit(solution)/shard_map/ppermute | solution.py:189
  10.6 2.3 %collective-permute-start.5 = (f32[19,8,128]{2,1,0:T(8,128)S(1)}, f32[19,8,128]{2,1,0:T(8,128)S(1)}, u32[]{:S(2)}, u32[]{:S(2)}) collective-permute-start(f32[19,8,128]{2,1,0:T(8,128)S(1)} %collective-permute-done.2.refs_3_), channel_id=1, source_target_pairs={{0,2},{1,3},{2,0},{3,1},{4,6},{5,7},{6,4},{7,5},{8,10},{9,11},{10,... | collective-permute-start | bytes 233480 | tf_op jit(solution)/shard_map/ppermute | solution.py:189
  12.9 0.0 collective-permute-done.refs_1_
  12.9 0.2 %collective-permute-start.6 = (f32[19,8,128]{2,1,0:T(8,128)S(1)}, f32[19,8,128]{2,1,0:T(8,128)S(1)}, u32[]{:S(2)}, u32[]{:S(2)}) collective-permute-start(f32[19,8,128]{2,1,0:T(8,128)S(1)} %collective-permute-done.refs_1_), channel_id=1, source_target_pairs={{0,4},{1,5},{2,6},{3,7},{4,0},{5,1},{6,2},{7,3},{8,12},{9,13},{10,... | collective-permute-start | bytes 233480 | tf_op jit(solution)/shard_map/ppermute | solution.py:189
  13.1 0.0 collective-permute-done.1.refs_2_
  13.1 0.1 collective-permute-start.3
  13.2 2.9 %collective-permute-done.4.refs_0_ = f32[19,8,128]{2,1,0:T(8,128)S(1)} collective-permute-done((f32[19,8,128]{2,1,0:T(8,128)S(1)}, f32[19,8,128]{2,1,0:T(8,128)S(1)}, u32[]{:S(2)}, u32[]{:S(2)}) %collective-permute-start.4) | collective-permute-done | bytes 77856 | tf_op jit(solution)/shard_map/ppermute | solution.py:189
  16.1 0.0 collective-permute-done.7.refs_3_
  16.1 0.0 collective-permute-done.5.refs_1_
  16.1 1.1 %collective-permute-done.6.refs_2_ = f32[19,8,128]{2,1,0:T(8,128)S(1)} collective-permute-done((f32[19,8,128]{2,1,0:T(8,128)S(1)}, f32[19,8,128]{2,1,0:T(8,128)S(1)}, u32[]{:S(2)}, u32[]{:S(2)}) %collective-permute-start.6) | collective-permute-done | bytes 77856 | tf_op jit(solution)/shard_map/ppermute | solution.py:189
  17.3 0.1 collective-permute-start.8
  17.4 0.0 collective-permute-done.3.refs_1_
  17.4 1.6 %collective-permute-done.8.refs_3_ = f32[76,8,128]{2,1,0:T(8,128)S(1)} collective-permute-done((f32[76,8,128]{2,1,0:T(8,128)S(1)}, f32[76,8,128]{2,1,0:T(8,128)S(1)}, u32[]{:S(2)}, u32[]{:S(2)}) %collective-permute-start.8) | collective-permute-done | bytes 311328 | tf_op jit(solution)/shard_map/ppermute | solution.py:189
  19.0 2.8 %group_smacof.1 = (f32[16,24]{1,0:T(8,128)}, f32[1,3]{1,0:T(1,128)}) custom-call(f32[76,8,128]{2,1,0:T(8,128)S(1)} %join.2.refs_0_, f32[76,8,128]{2,1,0:T(8,128)S(1)} %collective-permute-done.3.refs_1_, f32[76,8,128]{2,1,0:T(8,128)S(1)} %join.3.refs_2_, f32[76,8,128]{2,1,0:T(8,128)S(1)} %collective-permute-done.8.refs_3_), custom_call_target="tpu_custom_call" | custom-call | tf_op jit(solution)/shard_map/group_smacof/pallas_call | solution.py:231
  (2 shorter events, 0.0 us)
Async XLA Ops:
  1.5 7.9 %collective-permute-start.2 = (f32[19,8,128]{2,1,0:T(8,128)S(1)}, f32[19,8,128]{2,1,0:T(8,128)S(1)}, u32[]{:S(2)}, u32[]{:S(2)}) collective-permute-start(f32[19,8,128]{2,1,0:T(8,128)S(1)} %pack.1.refs_0_), channel_id=1, source_target_pairs={{0,8},{1,9},{2,10},{3,11},{4,12},{5,13},{6,14},{7,15},{8,0},{9,1},... | collective-permute-start | bytes 233480 | tf_op jit(solution)/shard_map/ppermute | solution.py:189
  5.6 7.2 %collective-permute-start = (f32[19,8,128]{2,1,0:T(8,128)S(1)}, f32[19,8,128]{2,1,0:T(8,128)S(1)}, u32[]{:S(2)}, u32[]{:S(2)}) collective-permute-start(f32[19,8,128]{2,1,0:T(8,128)S(1)} %pack.1.refs_0_), channel_id=1, source_target_pairs={{0,2},{1,3},{2,0},{3,1},{4,6},{5,7},{6,4},{7,5},{8,10},{9,11},{10,... | collective-permute-start | bytes 233480 | tf_op jit(solution)/shard_map/ppermute | solution.py:189
  7.1 6.0 %collective-permute-start.1 = (f32[19,8,128]{2,1,0:T(8,128)S(1)}, f32[19,8,128]{2,1,0:T(8,128)S(1)}, u32[]{:S(2)}, u32[]{:S(2)}) collective-permute-start(f32[19,8,128]{2,1,0:T(8,128)S(1)} %pack.1.refs_0_), channel_id=1, source_target_pairs={{0,4},{1,5},{2,6},{3,7},{4,0},{5,1},{6,2},{7,3},{8,12},{9,13},{10,... | collective-permute-start | bytes 233480 | tf_op jit(solution)/shard_map/ppermute | solution.py:189
  8.7 7.4 %collective-permute-start.4 = (f32[19,8,128]{2,1,0:T(8,128)S(1)}, f32[19,8,128]{2,1,0:T(8,128)S(1)}, u32[]{:S(2)}, u32[]{:S(2)}) collective-permute-start(f32[19,8,128]{2,1,0:T(8,128)S(1)} %pack.1.refs_0_), channel_id=1, source_target_pairs={{0,14},{1,15},{2,12},{3,13},{4,10},{5,11},{6,8},{7,9},{8,6},{9,7},... | collective-permute-start | bytes 233480 | tf_op jit(solution)/shard_map/ppermute | solution.py:189
  9.4 6.7 %collective-permute-start.7 = (f32[19,8,128]{2,1,0:T(8,128)S(1)}, f32[19,8,128]{2,1,0:T(8,128)S(1)}, u32[]{:S(2)}, u32[]{:S(2)}) collective-permute-start(f32[19,8,128]{2,1,0:T(8,128)S(1)} %collective-permute-done.2.refs_3_), channel_id=1, source_target_pairs={{0,4},{1,5},{2,6},{3,7},{4,0},{5,1},{6,2},{7,3},{8,12},{9,13},{10,... | collective-permute-start | bytes 233480 | tf_op jit(solution)/shard_map/ppermute | solution.py:189
  10.6 5.5 %collective-permute-start.5 = (f32[19,8,128]{2,1,0:T(8,128)S(1)}, f32[19,8,128]{2,1,0:T(8,128)S(1)}, u32[]{:S(2)}, u32[]{:S(2)}) collective-permute-start(f32[19,8,128]{2,1,0:T(8,128)S(1)} %collective-permute-done.2.refs_3_), channel_id=1, source_target_pairs={{0,2},{1,3},{2,0},{3,1},{4,6},{5,7},{6,4},{7,5},{8,10},{9,11},{10,... | collective-permute-start | bytes 233480 | tf_op jit(solution)/shard_map/ppermute | solution.py:189
  12.9 4.4 %collective-permute-start.6 = (f32[19,8,128]{2,1,0:T(8,128)S(1)}, f32[19,8,128]{2,1,0:T(8,128)S(1)}, u32[]{:S(2)}, u32[]{:S(2)}) collective-permute-start(f32[19,8,128]{2,1,0:T(8,128)S(1)} %collective-permute-done.refs_1_), channel_id=1, source_target_pairs={{0,4},{1,5},{2,6},{3,7},{4,0},{5,1},{6,2},{7,3},{8,12},{9,13},{10,... | collective-permute-start | bytes 233480 | tf_op jit(solution)/shard_map/ppermute | solution.py:189
  13.1 4.2 %collective-permute-start.3 = (f32[76,8,128]{2,1,0:T(8,128)S(1)}, f32[76,8,128]{2,1,0:T(8,128)S(1)}, u32[]{:S(2)}, u32[]{:S(2)}) collective-permute-start(f32[76,8,128]{2,1,0:T(8,128)S(1)} %join.2.refs_0_), channel_id=1, source_target_pairs={{0,1},{1,0},{2,3},{3,2},{4,5},{5,4},{6,7},{7,6},{8,9},{9,8},{10,11... | collective-permute-start | bytes 933896 | tf_op jit(solution)/shard_map/ppermute | solution.py:189
  17.3 1.7 %collective-permute-start.8 = (f32[76,8,128]{2,1,0:T(8,128)S(1)}, f32[76,8,128]{2,1,0:T(8,128)S(1)}, u32[]{:S(2)}, u32[]{:S(2)}) collective-permute-start(f32[76,8,128]{2,1,0:T(8,128)S(1)} %join.3.refs_2_), channel_id=1, source_target_pairs={{0,1},{1,0},{2,3},{3,2},{4,5},{5,4},{6,7},{7,6},{8,9},{9,8},{10,11... | collective-permute-start | bytes 933896 | tf_op jit(solution)/shard_map/ppermute | solution.py:189

commit v19 on v17

--- a/solution.py
+++ b/solution.py
@@ -206,7 +206,7 @@
     )(*(pltpu.with_memory_space_constraint(array, pltpu.HBM) for array in inputs))
     far, near, side = devices // 2, devices // 4, devices // 8
     held = {0: packed}
-    for offset in (far, side, near, far | near | side):
+    for offset in (far, side, near, far | near | side | 1):
         held[offset] = swap(packed, offset)
     for source, step in ((far, near), (far, side), (side, near)):
         held[source | step] = swap(held[source], step)

time: 21.2 us -> 21.2 us (level)
  transfers between devices with their start and end apart: 9 -> 9, of which waited for: 4 -> 5; matrix products, arithmetic and copies ran while one was open for 0% -> 0% of each run, Pallas kernels for 0% -> 0%
where the time goes in v19:
time: 21.2 us; the launch traced here: 21 us
  starting transfers between devices  10.3 us (49%)
  waiting for transfers between devices  6.34 us (30%)
  Pallas kernels  3.74 us (18%)
  between operations  0.68 us (3%)
    ppermute x9, starting transfers between devices, swap(): lax.ppermute(value, 'wide', [(i, i ^ offset) for i in range(devices)])  10.3 us
    ppermute x9, waiting for transfers between devices, swap(): lax.ppermute(value, 'wide', [(i, i ^ offset) for i in range(devices)])  6.34 us
    pallas_call x1, Pallas kernels, small_body(): pl.pallas_call(functools.partial(group_kernel, offsets, per_dev), out_sha...  2.81 us
    pallas_call x1, Pallas kernels, small_body(): pl.pallas_call(pack_kernel, out_shape=f32((tiles, SUBLANES, LANES)), in_s...  0.89 us
  transfers between devices with their start and end apart: 9, of which 5 were waited for; matrix products, arithmetic and copies ran while one was open for 0% of the time, Pallas kernels for 0%

profile of v19, /device:TPU:0, one launch (start us, length us, event | category | flops | bytes accessed | tf_op | source)
XLA Modules:
  0.0 21.0 jit_solution(14817321292152484902)
XLA Ops:
  0.6 0.9 %pack.1.refs_0_ = f32[19,8,128]{2,1,0:T(8,128)S(1)} custom-call(f32[24,384]{1,0:T(8,128)} %bitcast.7, s32[24,384]{1,0:T(8,128)} %bitcast.8, f32[16,24]{1,0:T(8,128)} %bitcast.9), custom_call_target="tpu_custom_call" | custom-call | tf_op jit(solution)/shard_map/pack/pallas_call | solution.py:193
  1.5 3.0 %collective-permute-start.2 = (f32[19,8,128]{2,1,0:T(8,128)S(1)}, f32[19,8,128]{2,1,0:T(8,128)S(1)}, u32[]{:S(2)}, u32[]{:S(2)}) collective-permute-start(f32[19,8,128]{2,1,0:T(8,128)S(1)} %pack.1.refs_0_), channel_id=1, source_target_pairs={{0,2},{1,3},{2,0},{3,1},{4,6},{5,7},{6,4},{7,5},{8,10},{9,11},{10,... | collective-permute-start | bytes 233480 | tf_op jit(solution)/shard_map/ppermute | solution.py:189
  4.5 2.6 %collective-permute-start = (f32[19,8,128]{2,1,0:T(8,128)S(1)}, f32[19,8,128]{2,1,0:T(8,128)S(1)}, u32[]{:S(2)}, u32[]{:S(2)}) collective-permute-start(f32[19,8,128]{2,1,0:T(8,128)S(1)} %pack.1.refs_0_), channel_id=1, source_target_pairs={{0,8},{1,9},{2,10},{3,11},{4,12},{5,13},{6,14},{7,15},{8,0},{9,1},... | collective-permute-start | bytes 233480 | tf_op jit(solution)/shard_map/ppermute | solution.py:189
  7.1 1.6 %collective-permute-start.1 = (f32[19,8,128]{2,1,0:T(8,128)S(1)}, f32[19,8,128]{2,1,0:T(8,128)S(1)}, u32[]{:S(2)}, u32[]{:S(2)}) collective-permute-start(f32[19,8,128]{2,1,0:T(8,128)S(1)} %pack.1.refs_0_), channel_id=1, source_target_pairs={{0,4},{1,5},{2,6},{3,7},{4,0},{5,1},{6,2},{7,3},{8,12},{9,13},{10,... | collective-permute-start | bytes 233480 | tf_op jit(solution)/shard_map/ppermute | solution.py:189
  8.7 0.0 collective-permute-start.4
  8.7 0.0 collective-permute-done.2.refs_3_
  8.7 0.5 %collective-permute-start.7 = (f32[19,8,128]{2,1,0:T(8,128)S(1)}, f32[19,8,128]{2,1,0:T(8,128)S(1)}, u32[]{:S(2)}, u32[]{:S(2)}) collective-permute-start(f32[19,8,128]{2,1,0:T(8,128)S(1)} %collective-permute-done.2.refs_3_), channel_id=1, source_target_pairs={{0,4},{1,5},{2,6},{3,7},{4,0},{5,1},{6,2},{7,3},{8,12},{9,13},{10,... | collective-permute-start | bytes 233480 | tf_op jit(solution)/shard_map/ppermute | solution.py:189
  9.2 1.3 %collective-permute-done.refs_1_ = f32[19,8,128]{2,1,0:T(8,128)S(1)} collective-permute-done((f32[19,8,128]{2,1,0:T(8,128)S(1)}, f32[19,8,128]{2,1,0:T(8,128)S(1)}, u32[]{:S(2)}, u32[]{:S(2)}) %collective-permute-start) | collective-permute-done | bytes 77856 | tf_op jit(solution)/shard_map/ppermute | solution.py:189
  10.5 0.5 %collective-permute-start.6 = (f32[19,8,128]{2,1,0:T(8,128)S(1)}, f32[19,8,128]{2,1,0:T(8,128)S(1)}, u32[]{:S(2)}, u32[]{:S(2)}) collective-permute-start(f32[19,8,128]{2,1,0:T(8,128)S(1)} %collective-permute-done.refs_1_), channel_id=1, source_target_pairs={{0,2},{1,3},{2,0},{3,1},{4,6},{5,7},{6,4},{7,5},{8,10},{9,11},{10,... | collective-permute-start | bytes 233480 | tf_op jit(solution)/shard_map/ppermute | solution.py:189
  11.0 2.0 %collective-permute-start.5 = (f32[19,8,128]{2,1,0:T(8,128)S(1)}, f32[19,8,128]{2,1,0:T(8,128)S(1)}, u32[]{:S(2)}, u32[]{:S(2)}) collective-permute-start(f32[19,8,128]{2,1,0:T(8,128)S(1)} %collective-permute-done.refs_1_), channel_id=1, source_target_pairs={{0,4},{1,5},{2,6},{3,7},{4,0},{5,1},{6,2},{7,3},{8,12},{9,13},{10,... | collective-permute-start | bytes 233480 | tf_op jit(solution)/shard_map/ppermute | solution.py:189
  13.0 0.0 collective-permute-done.1.refs_2_
  13.0 0.1 collective-permute-start.3
  13.1 3.0 %collective-permute-done.4.refs_0_ = f32[19,8,128]{2,1,0:T(8,128)S(1)} collective-permute-done((f32[19,8,128]{2,1,0:T(8,128)S(1)}, f32[19,8,128]{2,1,0:T(8,128)S(1)}, u32[]{:S(2)}, u32[]{:S(2)}) %collective-permute-start.4) | collective-permute-done | bytes 77856 | tf_op jit(solution)/shard_map/ppermute | solution.py:189
  16.0 0.0 collective-permute-done.7.refs_3_
  16.0 0.1 collective-permute-done.6.refs_2_
  16.2 0.4 %collective-permute-done.5.refs_1_ = f32[19,8,128]{2,1,0:T(8,128)S(1)} collective-permute-done((f32[19,8,128]{2,1,0:T(8,128)S(1)}, f32[19,8,128]{2,1,0:T(8,128)S(1)}, u32[]{:S(2)}, u32[]{:S(2)}) %collective-permute-start.5) | collective-permute-done | bytes 77856 | tf_op jit(solution)/shard_map/ppermute | solution.py:189
  16.5 0.1 collective-permute-start.8
  16.6 0.0 collective-permute-done.3.refs_1_
  16.6 1.6 %collective-permute-done.8.refs_3_ = f32[76,8,128]{2,1,0:T(8,128)S(1)} collective-permute-done((f32[76,8,128]{2,1,0:T(8,128)S(1)}, f32[76,8,128]{2,1,0:T(8,128)S(1)}, u32[]{:S(2)}, u32[]{:S(2)}) %collective-permute-start.8) | collective-permute-done | bytes 311328 | tf_op jit(solution)/shard_map/ppermute | solution.py:189
  18.2 2.8 %group_smacof.1 = (f32[16,24]{1,0:T(8,128)}, f32[1,3]{1,0:T(1,128)}) custom-call(f32[76,8,128]{2,1,0:T(8,128)S(1)} %join.2.refs_0_, f32[76,8,128]{2,1,0:T(8,128)S(1)} %collective-permute-done.3.refs_1_, f32[76,8,128]{2,1,0:T(8,128)S(1)} %join.3.refs_2_, f32[76,8,128]{2,1,0:T(8,128)S(1)} %collective-permute-done.8.refs_3_), custom_call_target="tpu_custom_call" | custom-call | tf_op jit(solution)/shard_map/group_smacof/pallas_call | solution.py:231
  (2 shorter events, 0.0 us)
Async XLA Ops:
  1.5 7.2 %collective-permute-start.2 = (f32[19,8,128]{2,1,0:T(8,128)S(1)}, f32[19,8,128]{2,1,0:T(8,128)S(1)}, u32[]{:S(2)}, u32[]{:S(2)}) collective-permute-start(f32[19,8,128]{2,1,0:T(8,128)S(1)} %pack.1.refs_0_), channel_id=1, source_target_pairs={{0,2},{1,3},{2,0},{3,1},{4,6},{5,7},{6,4},{7,5},{8,10},{9,11},{10,... | collective-permute-start | bytes 233480 | tf_op jit(solution)/shard_map/ppermute | solution.py:189
  4.5 5.9 %collective-permute-start = (f32[19,8,128]{2,1,0:T(8,128)S(1)}, f32[19,8,128]{2,1,0:T(8,128)S(1)}, u32[]{:S(2)}, u32[]{:S(2)}) collective-permute-start(f32[19,8,128]{2,1,0:T(8,128)S(1)} %pack.1.refs_0_), channel_id=1, source_target_pairs={{0,8},{1,9},{2,10},{3,11},{4,12},{5,13},{6,14},{7,15},{8,0},{9,1},... | collective-permute-start | bytes 233480 | tf_op jit(solution)/shard_map/ppermute | solution.py:189
  7.1 5.8 %collective-permute-start.1 = (f32[19,8,128]{2,1,0:T(8,128)S(1)}, f32[19,8,128]{2,1,0:T(8,128)S(1)}, u32[]{:S(2)}, u32[]{:S(2)}) collective-permute-start(f32[19,8,128]{2,1,0:T(8,128)S(1)} %pack.1.refs_0_), channel_id=1, source_target_pairs={{0,4},{1,5},{2,6},{3,7},{4,0},{5,1},{6,2},{7,3},{8,12},{9,13},{10,... | collective-permute-start | bytes 233480 | tf_op jit(solution)/shard_map/ppermute | solution.py:189
  8.7 7.3 %collective-permute-start.4 = (f32[19,8,128]{2,1,0:T(8,128)S(1)}, f32[19,8,128]{2,1,0:T(8,128)S(1)}, u32[]{:S(2)}, u32[]{:S(2)}) collective-permute-start(f32[19,8,128]{2,1,0:T(8,128)S(1)} %pack.1.refs_0_), channel_id=1, source_target_pairs={{0,15},{1,14},{2,13},{3,12},{4,11},{5,10},{6,9},{7,8},{8,7},{9,6},... | collective-permute-start | bytes 233480 | tf_op jit(solution)/shard_map/ppermute | solution.py:189
  8.7 7.3 %collective-permute-start.7 = (f32[19,8,128]{2,1,0:T(8,128)S(1)}, f32[19,8,128]{2,1,0:T(8,128)S(1)}, u32[]{:S(2)}, u32[]{:S(2)}) collective-permute-start(f32[19,8,128]{2,1,0:T(8,128)S(1)} %collective-permute-done.2.refs_3_), channel_id=1, source_target_pairs={{0,4},{1,5},{2,6},{3,7},{4,0},{5,1},{6,2},{7,3},{8,12},{9,13},{10,... | collective-permute-start | bytes 233480 | tf_op jit(solution)/shard_map/ppermute | solution.py:189
  10.5 5.7 %collective-permute-start.6 = (f32[19,8,128]{2,1,0:T(8,128)S(1)}, f32[19,8,128]{2,1,0:T(8,128)S(1)}, u32[]{:S(2)}, u32[]{:S(2)}) collective-permute-start(f32[19,8,128]{2,1,0:T(8,128)S(1)} %collective-permute-done.refs_1_), channel_id=1, source_target_pairs={{0,2},{1,3},{2,0},{3,1},{4,6},{5,7},{6,4},{7,5},{8,10},{9,11},{10,... | collective-permute-start | bytes 233480 | tf_op jit(solution)/shard_map/ppermute | solution.py:189
  11.0 5.5 %collective-permute-start.5 = (f32[19,8,128]{2,1,0:T(8,128)S(1)}, f32[19,8,128]{2,1,0:T(8,128)S(1)}, u32[]{:S(2)}, u32[]{:S(2)}) collective-permute-start(f32[19,8,128]{2,1,0:T(8,128)S(1)} %collective-permute-done.refs_1_), channel_id=1, source_target_pairs={{0,4},{1,5},{2,6},{3,7},{4,0},{5,1},{6,2},{7,3},{8,12},{9,13},{10,... | collective-permute-start | bytes 233480 | tf_op jit(solution)/shard_map/ppermute | solution.py:189
  13.0 3.6 %collective-permute-start.3 = (f32[76,8,128]{2,1,0:T(8,128)S(1)}, f32[76,8,128]{2,1,0:T(8,128)S(1)}, u32[]{:S(2)}, u32[]{:S(2)}) collective-permute-start(f32[76,8,128]{2,1,0:T(8,128)S(1)} %join.2.refs_0_), channel_id=1, source_target_pairs={{0,1},{1,0},{2,3},{3,2},{4,5},{5,4},{6,7},{7,6},{8,9},{9,8},{10,11... | collective-permute-start | bytes 933896 | tf_op jit(solution)/shard_map/ppermute | solution.py:189
  16.5 1.7 %collective-permute-start.8 = (f32[76,8,128]{2,1,0:T(8,128)S(1)}, f32[76,8,128]{2,1,0:T(8,128)S(1)}, u32[]{:S(2)}, u32[]{:S(2)}) collective-permute-start(f32[76,8,128]{2,1,0:T(8,128)S(1)} %join.3.refs_2_), channel_id=1, source_target_pairs={{0,1},{1,0},{2,3},{3,2},{4,5},{5,4},{6,7},{7,6},{8,9},{9,8},{10,11... | collective-permute-start | bytes 933896 | tf_op jit(solution)/shard_map/ppermute | solution.py:189

commit v20 on v17

--- a/solution.py
+++ b/solution.py
@@ -133,7 +133,7 @@
     ]
     x = jnp.concatenate(halves, axis=0)
     coord_dims = x.shape[0]
-    chunks = [slice(row, row + LANES) for row in range(0, points, LANES)]
+    chunks = [slice(0, points)]
     ones = jnp.ones((coord_dims, points), jnp.bfloat16)
     scales = [inverse_weight(weight_ref[rows], ones) for rows in chunks]
     denom = sum(lane_sums(weight_ref[rows] * dis_ref[rows] * dis_ref[rows]) for rows in chunks)

time: 21.2 us -> 21.2 us (level)
  no operation moved by 1% of the time
where the time goes in v20:
time: 21.2 us; the launch traced here: 21 us
  starting transfers between devices  10.4 us (49%)
  waiting for transfers between devices  6.15 us (29%)
  Pallas kernels  3.75 us (18%)
  between operations  0.68 us (3%)
    ppermute x9, starting transfers between devices, swap(): lax.ppermute(value, 'wide', [(i, i ^ offset) for i in range(devices)])  10.4 us
    ppermute x9, waiting for transfers between devices, swap(): lax.ppermute(value, 'wide', [(i, i ^ offset) for i in range(devices)])  6.15 us
    pallas_call x1, Pallas kernels, small_body(): pl.pallas_call(functools.partial(group_kernel, offsets, per_dev), out_sha...  2.82 us
    pallas_call x1, Pallas kernels, small_body(): pl.pallas_call(pack_kernel, out_shape=f32((tiles, SUBLANES, LANES)), in_s...  0.89 us
  transfers between devices with their start and end apart: 9, of which 4 were waited for; matrix products, arithmetic and copies ran while one was open for 0% of the time, Pallas kernels for 0%

profile of v20, /device:TPU:0, one launch (start us, length us, event | category | flops | bytes accessed | tf_op | source)
XLA Modules:
  0.0 21.0 jit_solution(12212195833068135457)
XLA Ops:
  0.6 0.9 %pack.1.refs_0_ = f32[19,8,128]{2,1,0:T(8,128)S(1)} custom-call(f32[24,384]{1,0:T(8,128)} %bitcast.7, s32[24,384]{1,0:T(8,128)} %bitcast.8, f32[16,24]{1,0:T(8,128)} %bitcast.9), custom_call_target="tpu_custom_call" | custom-call | tf_op jit(solution)/shard_map/pack/pallas_call | solution.py:193
  1.5 3.0 %collective-permute-start.2 = (f32[19,8,128]{2,1,0:T(8,128)S(1)}, f32[19,8,128]{2,1,0:T(8,128)S(1)}, u32[]{:S(2)}, u32[]{:S(2)}) collective-permute-start(f32[19,8,128]{2,1,0:T(8,128)S(1)} %pack.1.refs_0_), channel_id=1, source_target_pairs={{0,2},{1,3},{2,0},{3,1},{4,6},{5,7},{6,4},{7,5},{8,10},{9,11},{10,... | collective-permute-start | bytes 233480 | tf_op jit(solution)/shard_map/ppermute | solution.py:189
  4.5 2.6 %collective-permute-start = (f32[19,8,128]{2,1,0:T(8,128)S(1)}, f32[19,8,128]{2,1,0:T(8,128)S(1)}, u32[]{:S(2)}, u32[]{:S(2)}) collective-permute-start(f32[19,8,128]{2,1,0:T(8,128)S(1)} %pack.1.refs_0_), channel_id=1, source_target_pairs={{0,8},{1,9},{2,10},{3,11},{4,12},{5,13},{6,14},{7,15},{8,0},{9,1},... | collective-permute-start | bytes 233480 | tf_op jit(solution)/shard_map/ppermute | solution.py:189
  7.1 1.6 %collective-permute-start.1 = (f32[19,8,128]{2,1,0:T(8,128)S(1)}, f32[19,8,128]{2,1,0:T(8,128)S(1)}, u32[]{:S(2)}, u32[]{:S(2)}) collective-permute-start(f32[19,8,128]{2,1,0:T(8,128)S(1)} %pack.1.refs_0_), channel_id=1, source_target_pairs={{0,4},{1,5},{2,6},{3,7},{4,0},{5,1},{6,2},{7,3},{8,12},{9,13},{10,... | collective-permute-start | bytes 233480 | tf_op jit(solution)/shard_map/ppermute | solution.py:189
  8.7 0.0 collective-permute-start.4
  8.7 0.0 collective-permute-done.2.refs_3_
  8.7 0.9 %collective-permute-start.7 = (f32[19,8,128]{2,1,0:T(8,128)S(1)}, f32[19,8,128]{2,1,0:T(8,128)S(1)}, u32[]{:S(2)}, u32[]{:S(2)}) collective-permute-start(f32[19,8,128]{2,1,0:T(8,128)S(1)} %collective-permute-done.2.refs_3_), channel_id=1, source_target_pairs={{0,4},{1,5},{2,6},{3,7},{4,0},{5,1},{6,2},{7,3},{8,12},{9,13},{10,... | collective-permute-start | bytes 233480 | tf_op jit(solution)/shard_map/ppermute | solution.py:189
  9.6 1.7 %collective-permute-done.refs_1_ = f32[19,8,128]{2,1,0:T(8,128)S(1)} collective-permute-done((f32[19,8,128]{2,1,0:T(8,128)S(1)}, f32[19,8,128]{2,1,0:T(8,128)S(1)}, u32[]{:S(2)}, u32[]{:S(2)}) %collective-permute-start) | collective-permute-done | bytes 77856 | tf_op jit(solution)/shard_map/ppermute | solution.py:189
  11.2 0.0 collective-permute-start.6
  11.2 2.3 %collective-permute-start.5 = (f32[19,8,128]{2,1,0:T(8,128)S(1)}, f32[19,8,128]{2,1,0:T(8,128)S(1)}, u32[]{:S(2)}, u32[]{:S(2)}) collective-permute-start(f32[19,8,128]{2,1,0:T(8,128)S(1)} %collective-permute-done.refs_1_), channel_id=1, source_target_pairs={{0,4},{1,5},{2,6},{3,7},{4,0},{5,1},{6,2},{7,3},{8,12},{9,13},{10,... | collective-permute-start | bytes 233480 | tf_op jit(solution)/shard_map/ppermute | solution.py:189
  13.5 0.0 collective-permute-done.1.refs_2_
  13.5 0.1 collective-permute-start.3
  13.6 2.7 %collective-permute-done.4.refs_0_ = f32[19,8,128]{2,1,0:T(8,128)S(1)} collective-permute-done((f32[19,8,128]{2,1,0:T(8,128)S(1)}, f32[19,8,128]{2,1,0:T(8,128)S(1)}, u32[]{:S(2)}, u32[]{:S(2)}) %collective-permute-start.4) | collective-permute-done | bytes 77856 | tf_op jit(solution)/shard_map/ppermute | solution.py:189
  16.3 0.0 collective-permute-done.7.refs_3_
  16.3 0.2 collective-permute-done.6.refs_2_
  16.5 0.0 collective-permute-done.5.refs_1_
  16.5 0.1 collective-permute-start.8
  16.6 0.0 collective-permute-done.3.refs_1_
  16.6 1.6 %collective-permute-done.8.refs_3_ = f32[76,8,128]{2,1,0:T(8,128)S(1)} collective-permute-done((f32[76,8,128]{2,1,0:T(8,128)S(1)}, f32[76,8,128]{2,1,0:T(8,128)S(1)}, u32[]{:S(2)}, u32[]{:S(2)}) %collective-permute-start.8) | collective-permute-done | bytes 311328 | tf_op jit(solution)/shard_map/ppermute | solution.py:189
  18.2 2.8 %group_smacof.1 = (f32[16,24]{1,0:T(8,128)}, f32[1,3]{1,0:T(1,128)}) custom-call(f32[76,8,128]{2,1,0:T(8,128)S(1)} %join.2.refs_0_, f32[76,8,128]{2,1,0:T(8,128)S(1)} %collective-permute-done.3.refs_1_, f32[76,8,128]{2,1,0:T(8,128)S(1)} %join.3.refs_2_, f32[76,8,128]{2,1,0:T(8,128)S(1)} %collective-permute-done.8.refs_3_), custom_call_target="tpu_custom_call" | custom-call | tf_op jit(solution)/shard_map/group_smacof/pallas_call | solution.py:231
  (2 shorter events, 0.0 us)
Async XLA Ops:
  1.5 7.2 %collective-permute-start.2 = (f32[19,8,128]{2,1,0:T(8,128)S(1)}, f32[19,8,128]{2,1,0:T(8,128)S(1)}, u32[]{:S(2)}, u32[]{:S(2)}) collective-permute-start(f32[19,8,128]{2,1,0:T(8,128)S(1)} %pack.1.refs_0_), channel_id=1, source_target_pairs={{0,2},{1,3},{2,0},{3,1},{4,6},{5,7},{6,4},{7,5},{8,10},{9,11},{10,... | collective-permute-start | bytes 233480 | tf_op jit(solution)/shard_map/ppermute | solution.py:189
  4.5 6.7 %collective-permute-start = (f32[19,8,128]{2,1,0:T(8,128)S(1)}, f32[19,8,128]{2,1,0:T(8,128)S(1)}, u32[]{:S(2)}, u32[]{:S(2)}) collective-permute-start(f32[19,8,128]{2,1,0:T(8,128)S(1)} %pack.1.refs_0_), channel_id=1, source_target_pairs={{0,8},{1,9},{2,10},{3,11},{4,12},{5,13},{6,14},{7,15},{8,0},{9,1},... | collective-permute-start | bytes 233480 | tf_op jit(solution)/shard_map/ppermute | solution.py:189
  7.1 6.4 %collective-permute-start.1 = (f32[19,8,128]{2,1,0:T(8,128)S(1)}, f32[19,8,128]{2,1,0:T(8,128)S(1)}, u32[]{:S(2)}, u32[]{:S(2)}) collective-permute-start(f32[19,8,128]{2,1,0:T(8,128)S(1)} %pack.1.refs_0_), channel_id=1, source_target_pairs={{0,4},{1,5},{2,6},{3,7},{4,0},{5,1},{6,2},{7,3},{8,12},{9,13},{10,... | collective-permute-start | bytes 233480 | tf_op jit(solution)/shard_map/ppermute | solution.py:189
  8.7 7.6 %collective-permute-start.4 = (f32[19,8,128]{2,1,0:T(8,128)S(1)}, f32[19,8,128]{2,1,0:T(8,128)S(1)}, u32[]{:S(2)}, u32[]{:S(2)}) collective-permute-start(f32[19,8,128]{2,1,0:T(8,128)S(1)} %pack.1.refs_0_), channel_id=1, source_target_pairs={{0,14},{1,15},{2,12},{3,13},{4,10},{5,11},{6,8},{7,9},{8,6},{9,7},... | collective-permute-start | bytes 233480 | tf_op jit(solution)/shard_map/ppermute | solution.py:189
  8.7 7.6 %collective-permute-start.7 = (f32[19,8,128]{2,1,0:T(8,128)S(1)}, f32[19,8,128]{2,1,0:T(8,128)S(1)}, u32[]{:S(2)}, u32[]{:S(2)}) collective-permute-start(f32[19,8,128]{2,1,0:T(8,128)S(1)} %collective-permute-done.2.refs_3_), channel_id=1, source_target_pairs={{0,4},{1,5},{2,6},{3,7},{4,0},{5,1},{6,2},{7,3},{8,12},{9,13},{10,... | collective-permute-start | bytes 233480 | tf_op jit(solution)/shard_map/ppermute | solution.py:189
  11.2 5.2 %collective-permute-start.6 = (f32[19,8,128]{2,1,0:T(8,128)S(1)}, f32[19,8,128]{2,1,0:T(8,128)S(1)}, u32[]{:S(2)}, u32[]{:S(2)}) collective-permute-start(f32[19,8,128]{2,1,0:T(8,128)S(1)} %collective-permute-done.refs_1_), channel_id=1, source_target_pairs={{0,2},{1,3},{2,0},{3,1},{4,6},{5,7},{6,4},{7,5},{8,10},{9,11},{10,... | collective-permute-start | bytes 233480 | tf_op jit(solution)/shard_map/ppermute | solution.py:189
  11.2 5.3 %collective-permute-start.5 = (f32[19,8,128]{2,1,0:T(8,128)S(1)}, f32[19,8,128]{2,1,0:T(8,128)S(1)}, u32[]{:S(2)}, u32[]{:S(2)}) collective-permute-start(f32[19,8,128]{2,1,0:T(8,128)S(1)} %collective-permute-done.refs_1_), channel_id=1, source_target_pairs={{0,4},{1,5},{2,6},{3,7},{4,0},{5,1},{6,2},{7,3},{8,12},{9,13},{10,... | collective-permute-start | bytes 233480 | tf_op jit(solution)/shard_map/ppermute | solution.py:189
  13.5 3.1 %collective-permute-start.3 = (f32[76,8,128]{2,1,0:T(8,128)S(1)}, f32[76,8,128]{2,1,0:T(8,128)S(1)}, u32[]{:S(2)}, u32[]{:S(2)}) collective-permute-start(f32[76,8,128]{2,1,0:T(8,128)S(1)} %join.2.refs_0_), channel_id=1, source_target_pairs={{0,1},{1,0},{2,3},{3,2},{4,5},{5,4},{6,7},{7,6},{8,9},{9,8},{10,11... | collective-permute-start | bytes 933896 | tf_op jit(solution)/shard_map/ppermute | solution.py:189
  16.5 1.7 %collective-permute-start.8 = (f32[76,8,128]{2,1,0:T(8,128)S(1)}, f32[76,8,128]{2,1,0:T(8,128)S(1)}, u32[]{:S(2)}, u32[]{:S(2)}) collective-permute-start(f32[76,8,128]{2,1,0:T(8,128)S(1)} %join.3.refs_2_), channel_id=1, source_target_pairs={{0,1},{1,0},{2,3},{3,2},{4,5},{5,4},{6,7},{7,6},{8,9},{9,8},{10,11... | collective-permute-start | bytes 933896 | tf_op jit(solution)/shard_map/ppermute | solution.py:189

commit v21 on v20

--- a/solution.py
+++ b/solution.py
@@ -68,13 +68,6 @@
     out_ref[2 * len(spots)] = jnp.concatenate([x_ref[:half], x_ref[half:], pad], axis=1)
 
 
-def held_slots(offsets, refs, tiles):
-    me = lax.axis_index("wide")
-    for group, ref in zip(offsets, refs):
-        for slot, offset in enumerate(group):
-            yield ref, slot * tiles, me ^ offset
-
-
 def norm_rows(top, bottom, coord_dims):
     pad = jnp.zeros((coord_dims - 6, top[0].shape[1]), jnp.float32)
     rows = [p.astype(jnp.float32) for p in (*top, *bottom)]
@@ -116,59 +109,48 @@
 
 def group_kernel(offsets, per_dev, *refs):
     slot_refs = refs[: len(offsets)]
-    out_ref, stress_ref, dis_ref, weight_ref, tile_ref = refs[len(offsets) :]
+    out_ref, stress_ref, dis_ref, weight_ref = refs[len(offsets) :]
     points = dis_ref.shape[0]
     spots = tile_spots(per_dev, points)
     tiles = 2 * len(spots) + 1
-    for ref, base, place in held_slots(offsets, slot_refs, tiles):
-        tile_ref[place] = ref[base + tiles - 1]
-        for i, (rows, columns) in enumerate(spots):
-            start = pl.multiple_of(place * per_dev + rows.start, SUBLANES)
-            dis_ref[pl.ds(start, SUBLANES), columns] = ref[base + i]
-            weight_ref[pl.ds(start, SUBLANES), columns] = ref[base + len(spots) + i]
-    blocks = [tile_ref[i] for i in range(tile_ref.shape[0])]
+    me = lax.axis_index("wide")
+    shape = (per_dev, points)
+    lanes = lax.broadcasted_iota(jnp.int32, shape, 1) - lax.broadcasted_iota(jnp.int32, shape, 0)
+    blocks, order = [], []
+    for group, ref in zip(offsets, slot_refs):
+        for slot, offset in enumerate(group):
+            base, first = slot * tiles, len(blocks) * per_dev
+            blocks.append(ref[base + tiles - 1])
+            order.append((lanes == (me ^ offset) * per_dev).astype(jnp.float32))
+            for i, (rows, columns) in enumerate(spots):
+                spot = slice(first + rows.start, first + rows.stop)
+                dis_ref[spot, columns] = ref[base + i]
+                weight_ref[spot, columns] = ref[base + len(spots) + i]
+    order = jnp.concatenate(order, axis=0).astype(jnp.bfloat16)
     halves = [
         jnp.concatenate([t[:, low : low + per_dev] for t in blocks], axis=1)
         for low in (0, per_dev)
     ]
     x = jnp.concatenate(halves, axis=0)
     coord_dims = x.shape[0]
-    chunks = [slice(0, points)]
     ones = jnp.ones((coord_dims, points), jnp.bfloat16)
-    scales = [inverse_weight(weight_ref[rows], ones) for rows in chunks]
-    denom = sum(lane_sums(weight_ref[rows] * dis_ref[rows] * dis_ref[rows]) for rows in chunks)
-    place = lax.axis_index("wide")
-    own_rows = pl.ds(pl.multiple_of(place * per_dev, SUBLANES), per_dev)
-    shape = (points, per_dev)
-    pick = lax.broadcasted_iota(jnp.int32, shape, 0) - lax.broadcasted_iota(jnp.int32, shape, 1)
-    pick = (pick == place * per_dev).astype(jnp.float32).astype(jnp.bfloat16)
-    sums = [denom]
+    scale = inverse_weight(weight_ref[...], ones)
+    sums = [lane_sums(weight_ref[...] * dis_ref[...] * dis_ref[...])]
     for sweep in range(ITERS):
         parts = split_bf16(x, 3)
-        sides = jnp.concatenate([parts[0], parts[1], ones], axis=0)
-        left, right = left_side(x, parts), right_side(x, parts)
-        last = sweep == ITERS - 1
-        stress, following = 0.0, []
-        for rows, scale in zip(chunks, scales):
-            square = dot(left[:, rows], right, TN)
-            inverse = lax.rsqrt(square)
-            weight, dis = weight_ref[rows], dis_ref[rows]
-            misfit = dis - square * inverse
-            weighted = weight * misfit
-            stress += lane_sums(weighted * misfit)
-            if not last:
-                following.append(moved(x[:, rows], sides, weighted * inverse, scale))
-        sums.append(stress)
-        if last:
-            own = dot(jnp.concatenate(parts, axis=0), pick, (((1,), (0,)), ((), ())))
-            own = sum(own[i * coord_dims : (i + 1) * coord_dims] for i in range(3))
-            square = dot(left_side(own, split_bf16(own, 3)), right, TN)
-            inverse = lax.rsqrt(square)
-            weight = weight_ref[own_rows, :]
-            push = weight * (dis_ref[own_rows, :] - square * inverse) * inverse
-            out_ref[...] = moved(own, sides, push, inverse_weight(weight, ones))
-        else:
-            x = jnp.concatenate(following, axis=1)
+        ordered = dot(jnp.concatenate(parts, axis=0), order, (((1,), (0,)), ((), ())))
+        ordered = [ordered[i * coord_dims : (i + 1) * coord_dims] for i in range(3)]
+        columns = [part.astype(jnp.bfloat16) for part in ordered]
+        sides = jnp.concatenate([columns[0], columns[1], ones], axis=0)
+        square = dot(left_side(x, parts), right_side(sum(ordered), columns), TN)
+        inverse = lax.rsqrt(square)
+        misfit = dis_ref[...] - square * inverse
+        weighted = weight_ref[...] * misfit
+        sums.append(lane_sums(weighted * misfit))
+        if sweep < ITERS - 1:
+            x = moved(x, sides, weighted * inverse, scale)
+    push = weighted[:per_dev] * inverse[:per_dev]
+    out_ref[...] = moved(x[:, :per_dev], sides, push, scale[:, :per_dev])
     total = jnp.sum(jnp.concatenate(sums, axis=0), axis=1, keepdims=True)
     ratios = total[1:] / total[:1]
     lanes = lax.broadcasted_iota(jnp.int32, (ITERS, LANES), 1)
@@ -236,7 +218,6 @@
         scratch_shapes=[
             pltpu.VMEM((points, points), jnp.float32),
             pltpu.VMEM((points, points), jnp.float32),
-            pltpu.VMEM((devices, SUBLANES, LANES), jnp.float32),
         ],
         compiler_params=params,
         name="group_smacof",

time: 21.2 us -> 21.2 us (level)
  no operation moved by 1% of the time
where the time goes in v21:
time: 21.2 us; the launch traced here: 21.1 us
  starting transfers between devices  10.4 us (49%)
  waiting for transfers between devices  6.15 us (29%)
  Pallas kernels  3.8 us (18%)
  between operations  0.68 us (3%)
    ppermute x9, starting transfers between devices, swap(): lax.ppermute(value, 'wide', [(i, i ^ offset) for i in range(devices)])  10.4 us
    ppermute x9, waiting for transfers between devices, swap(): lax.ppermute(value, 'wide', [(i, i ^ offset) for i in range(devices)])  6.15 us
    pallas_call x1, Pallas kernels, small_body(): pl.pallas_call(functools.partial(group_kernel, offsets, per_dev), out_sha...  2.87 us
    pallas_call x1, Pallas kernels, small_body(): pl.pallas_call(pack_kernel, out_shape=f32((tiles, SUBLANES, LANES)), in_s...  0.89 us
  transfers between devices with their start and end apart: 9, of which 4 were waited for; matrix products, arithmetic and copies ran while one was open for 0% of the time, Pallas kernels for 0%

profile of v21, /device:TPU:0, one launch (start us, length us, event | category | flops | bytes accessed | tf_op | source)
XLA Modules:
  0.0 21.1 jit_solution(996751060407606564)
XLA Ops:
  0.6 0.9 %pack.1.refs_0_ = f32[19,8,128]{2,1,0:T(8,128)S(1)} custom-call(f32[24,384]{1,0:T(8,128)} %bitcast.7, s32[24,384]{1,0:T(8,128)} %bitcast.8, f32[16,24]{1,0:T(8,128)} %bitcast.9), custom_call_target="tpu_custom_call" | custom-call | tf_op jit(solution)/shard_map/pack/pallas_call | solution.py:175
  1.5 3.0 %collective-permute-start.2 = (f32[19,8,128]{2,1,0:T(8,128)S(1)}, f32[19,8,128]{2,1,0:T(8,128)S(1)}, u32[]{:S(2)}, u32[]{:S(2)}) collective-permute-start(f32[19,8,128]{2,1,0:T(8,128)S(1)} %pack.1.refs_0_), channel_id=1, source_target_pairs={{0,2},{1,3},{2,0},{3,1},{4,6},{5,7},{6,4},{7,5},{8,10},{9,11},{10,... | collective-permute-start | bytes 233480 | tf_op jit(solution)/shard_map/ppermute | solution.py:171
  4.5 2.6 %collective-permute-start = (f32[19,8,128]{2,1,0:T(8,128)S(1)}, f32[19,8,128]{2,1,0:T(8,128)S(1)}, u32[]{:S(2)}, u32[]{:S(2)}) collective-permute-start(f32[19,8,128]{2,1,0:T(8,128)S(1)} %pack.1.refs_0_), channel_id=1, source_target_pairs={{0,8},{1,9},{2,10},{3,11},{4,12},{5,13},{6,14},{7,15},{8,0},{9,1},... | collective-permute-start | bytes 233480 | tf_op jit(solution)/shard_map/ppermute | solution.py:171
  7.1 1.6 %collective-permute-start.1 = (f32[19,8,128]{2,1,0:T(8,128)S(1)}, f32[19,8,128]{2,1,0:T(8,128)S(1)}, u32[]{:S(2)}, u32[]{:S(2)}) collective-permute-start(f32[19,8,128]{2,1,0:T(8,128)S(1)} %pack.1.refs_0_), channel_id=1, source_target_pairs={{0,4},{1,5},{2,6},{3,7},{4,0},{5,1},{6,2},{7,3},{8,12},{9,13},{10,... | collective-permute-start | bytes 233480 | tf_op jit(solution)/shard_map/ppermute | solution.py:171
  8.7 0.0 collective-permute-start.4
  8.7 0.0 collective-permute-done.2.refs_3_
  8.7 0.9 %collective-permute-start.7 = (f32[19,8,128]{2,1,0:T(8,128)S(1)}, f32[19,8,128]{2,1,0:T(8,128)S(1)}, u32[]{:S(2)}, u32[]{:S(2)}) collective-permute-start(f32[19,8,128]{2,1,0:T(8,128)S(1)} %collective-permute-done.2.refs_3_), channel_id=1, source_target_pairs={{0,4},{1,5},{2,6},{3,7},{4,0},{5,1},{6,2},{7,3},{8,12},{9,13},{10,... | collective-permute-start | bytes 233480 | tf_op jit(solution)/shard_map/ppermute | solution.py:171
  9.6 1.7 %collective-permute-done.refs_1_ = f32[19,8,128]{2,1,0:T(8,128)S(1)} collective-permute-done((f32[19,8,128]{2,1,0:T(8,128)S(1)}, f32[19,8,128]{2,1,0:T(8,128)S(1)}, u32[]{:S(2)}, u32[]{:S(2)}) %collective-permute-start) | collective-permute-done | bytes 77856 | tf_op jit(solution)/shard_map/ppermute | solution.py:171
  11.2 0.0 collective-permute-start.6
  11.2 2.3 %collective-permute-start.5 = (f32[19,8,128]{2,1,0:T(8,128)S(1)}, f32[19,8,128]{2,1,0:T(8,128)S(1)}, u32[]{:S(2)}, u32[]{:S(2)}) collective-permute-start(f32[19,8,128]{2,1,0:T(8,128)S(1)} %collective-permute-done.refs_1_), channel_id=1, source_target_pairs={{0,4},{1,5},{2,6},{3,7},{4,0},{5,1},{6,2},{7,3},{8,12},{9,13},{10,... | collective-permute-start | bytes 233480 | tf_op jit(solution)/shard_map/ppermute | solution.py:171
  13.5 0.0 collective-permute-done.1.refs_2_
  13.5 0.1 collective-permute-start.3
  13.6 2.7 %collective-permute-done.4.refs_0_ = f32[19,8,128]{2,1,0:T(8,128)S(1)} collective-permute-done((f32[19,8,128]{2,1,0:T(8,128)S(1)}, f32[19,8,128]{2,1,0:T(8,128)S(1)}, u32[]{:S(2)}, u32[]{:S(2)}) %collective-permute-start.4) | collective-permute-done | bytes 77856 | tf_op jit(solution)/shard_map/ppermute | solution.py:171
  16.3 0.0 collective-permute-done.7.refs_3_
  16.3 0.2 collective-permute-done.6.refs_2_
  16.5 0.0 collective-permute-done.5.refs_1_
  16.5 0.1 collective-permute-start.8
  16.6 0.0 collective-permute-done.3.refs_1_
  16.6 1.6 %collective-permute-done.8.refs_3_ = f32[76,8,128]{2,1,0:T(8,128)S(1)} collective-permute-done((f32[76,8,128]{2,1,0:T(8,128)S(1)}, f32[76,8,128]{2,1,0:T(8,128)S(1)}, u32[]{:S(2)}, u32[]{:S(2)}) %collective-permute-start.8) | collective-permute-done | bytes 311328 | tf_op jit(solution)/shard_map/ppermute | solution.py:171
  18.2 2.9 %group_smacof.1 = (f32[16,24]{1,0:T(8,128)}, f32[1,3]{1,0:T(1,128)}) custom-call(f32[76,8,128]{2,1,0:T(8,128)S(1)} %join.2.refs_0_, f32[76,8,128]{2,1,0:T(8,128)S(1)} %collective-permute-done.3.refs_1_, f32[76,8,128]{2,1,0:T(8,128)S(1)} %join.3.refs_2_, f32[76,8,128]{2,1,0:T(8,128)S(1)} %collective-permute-done.8.refs_3_), custom_call_target="tpu_custom_call" | custom-call | tf_op jit(solution)/shard_map/group_smacof/pallas_call | solution.py:213
  (2 shorter events, 0.0 us)
Async XLA Ops:
  1.5 7.2 %collective-permute-start.2 = (f32[19,8,128]{2,1,0:T(8,128)S(1)}, f32[19,8,128]{2,1,0:T(8,128)S(1)}, u32[]{:S(2)}, u32[]{:S(2)}) collective-permute-start(f32[19,8,128]{2,1,0:T(8,128)S(1)} %pack.1.refs_0_), channel_id=1, source_target_pairs={{0,2},{1,3},{2,0},{3,1},{4,6},{5,7},{6,4},{7,5},{8,10},{9,11},{10,... | collective-permute-start | bytes 233480 | tf_op jit(solution)/shard_map/ppermute | solution.py:171
  4.5 6.7 %collective-permute-start = (f32[19,8,128]{2,1,0:T(8,128)S(1)}, f32[19,8,128]{2,1,0:T(8,128)S(1)}, u32[]{:S(2)}, u32[]{:S(2)}) collective-permute-start(f32[19,8,128]{2,1,0:T(8,128)S(1)} %pack.1.refs_0_), channel_id=1, source_target_pairs={{0,8},{1,9},{2,10},{3,11},{4,12},{5,13},{6,14},{7,15},{8,0},{9,1},... | collective-permute-start | bytes 233480 | tf_op jit(solution)/shard_map/ppermute | solution.py:171
  7.1 6.4 %collective-permute-start.1 = (f32[19,8,128]{2,1,0:T(8,128)S(1)}, f32[19,8,128]{2,1,0:T(8,128)S(1)}, u32[]{:S(2)}, u32[]{:S(2)}) collective-permute-start(f32[19,8,128]{2,1,0:T(8,128)S(1)} %pack.1.refs_0_), channel_id=1, source_target_pairs={{0,4},{1,5},{2,6},{3,7},{4,0},{5,1},{6,2},{7,3},{8,12},{9,13},{10,... | collective-permute-start | bytes 233480 | tf_op jit(solution)/shard_map/ppermute | solution.py:171
  8.7 7.6 %collective-permute-start.4 = (f32[19,8,128]{2,1,0:T(8,128)S(1)}, f32[19,8,128]{2,1,0:T(8,128)S(1)}, u32[]{:S(2)}, u32[]{:S(2)}) collective-permute-start(f32[19,8,128]{2,1,0:T(8,128)S(1)} %pack.1.refs_0_), channel_id=1, source_target_pairs={{0,14},{1,15},{2,12},{3,13},{4,10},{5,11},{6,8},{7,9},{8,6},{9,7},... | collective-permute-start | bytes 233480 | tf_op jit(solution)/shard_map/ppermute | solution.py:171
  8.7 7.6 %collective-permute-start.7 = (f32[19,8,128]{2,1,0:T(8,128)S(1)}, f32[19,8,128]{2,1,0:T(8,128)S(1)}, u32[]{:S(2)}, u32[]{:S(2)}) collective-permute-start(f32[19,8,128]{2,1,0:T(8,128)S(1)} %collective-permute-done.2.refs_3_), channel_id=1, source_target_pairs={{0,4},{1,5},{2,6},{3,7},{4,0},{5,1},{6,2},{7,3},{8,12},{9,13},{10,... | collective-permute-start | bytes 233480 | tf_op jit(solution)/shard_map/ppermute | solution.py:171
  11.2 5.2 %collective-permute-start.6 = (f32[19,8,128]{2,1,0:T(8,128)S(1)}, f32[19,8,128]{2,1,0:T(8,128)S(1)}, u32[]{:S(2)}, u32[]{:S(2)}) collective-permute-start(f32[19,8,128]{2,1,0:T(8,128)S(1)} %collective-permute-done.refs_1_), channel_id=1, source_target_pairs={{0,2},{1,3},{2,0},{3,1},{4,6},{5,7},{6,4},{7,5},{8,10},{9,11},{10,... | collective-permute-start | bytes 233480 | tf_op jit(solution)/shard_map/ppermute | solution.py:171
  11.2 5.3 %collective-permute-start.5 = (f32[19,8,128]{2,1,0:T(8,128)S(1)}, f32[19,8,128]{2,1,0:T(8,128)S(1)}, u32[]{:S(2)}, u32[]{:S(2)}) collective-permute-start(f32[19,8,128]{2,1,0:T(8,128)S(1)} %collective-permute-done.refs_1_), channel_id=1, source_target_pairs={{0,4},{1,5},{2,6},{3,7},{4,0},{5,1},{6,2},{7,3},{8,12},{9,13},{10,... | collective-permute-start | bytes 233480 | tf_op jit(solution)/shard_map/ppermute | solution.py:171
  13.5 3.1 %collective-permute-start.3 = (f32[76,8,128]{2,1,0:T(8,128)S(1)}, f32[76,8,128]{2,1,0:T(8,128)S(1)}, u32[]{:S(2)}, u32[]{:S(2)}) collective-permute-start(f32[76,8,128]{2,1,0:T(8,128)S(1)} %join.2.refs_0_), channel_id=1, source_target_pairs={{0,1},{1,0},{2,3},{3,2},{4,5},{5,4},{6,7},{7,6},{8,9},{9,8},{10,11... | collective-permute-start | bytes 933896 | tf_op jit(solution)/shard_map/ppermute | solution.py:171
  16.5 1.7 %collective-permute-start.8 = (f32[76,8,128]{2,1,0:T(8,128)S(1)}, f32[76,8,128]{2,1,0:T(8,128)S(1)}, u32[]{:S(2)}, u32[]{:S(2)}) collective-permute-start(f32[76,8,128]{2,1,0:T(8,128)S(1)} %join.3.refs_2_), channel_id=1, source_target_pairs={{0,1},{1,0},{2,3},{3,2},{4,5},{5,4},{6,7},{7,6},{8,9},{9,8},{10,11... | collective-permute-start | bytes 933896 | tf_op jit(solution)/shard_map/ppermute | solution.py:171

commit v22 on v19

--- a/solution.py
+++ b/solution.py
@@ -206,11 +206,11 @@
     )(*(pltpu.with_memory_space_constraint(array, pltpu.HBM) for array in inputs))
     far, near, side = devices // 2, devices // 4, devices // 8
     held = {0: packed}
-    for offset in (far, side, near, far | near | side | 1):
+    for offset in (far, near, side, far | near | side):
         held[offset] = swap(packed, offset)
-    for source, step in ((far, near), (far, side), (side, near)):
+    for source, step in ((far, side), (far, near), (near, side)):
         held[source | step] = swap(held[source], step)
-    early = [0, far, near, side]
+    early = [0, far, side, near]
     late = [offset for offset in held if offset not in early]
     block = packed.shape[0]
 

time: 21.2 us -> 22.4 us (1.057)
  starting transfers between devices: 10.3 us -> 12.6 us
  waiting for transfers between devices: 6.34 us -> 5.23 us
    ppermute x9, starting transfers between devices: 10.3 us -> 12.6 us  [swap(): lax.ppermute(value, 'wide', [(i, i ^ offset) for i in range(devices)])]
    ppermute x9, waiting for transfers between devices: 6.34 us -> 5.23 us  [swap(): lax.ppermute(value, 'wide', [(i, i ^ offset) for i in range(devices)])]
  transfers between devices with their start and end apart: 9 -> 9, of which waited for: 5 -> 4; matrix products, arithmetic and copies ran while one was open for 0% -> 0% of each run, Pallas kernels for 0% -> 0%
where the time goes in v22:
time: 22.4 us; the launch traced here: 22.2 us
  starting transfers between devices  12.6 us (56%)
  waiting for transfers between devices  5.23 us (23%)
  Pallas kernels  3.74 us (17%)
  between operations  0.68 us (3%)
    ppermute x9, starting transfers between devices, swap(): lax.ppermute(value, 'wide', [(i, i ^ offset) for i in range(devices)])  12.6 us
    ppermute x9, waiting for transfers between devices, swap(): lax.ppermute(value, 'wide', [(i, i ^ offset) for i in range(devices)])  5.23 us
    pallas_call x1, Pallas kernels, small_body(): pl.pallas_call(functools.partial(group_kernel, offsets, per_dev), out_sha...  2.81 us
    pallas_call x1, Pallas kernels, small_body(): pl.pallas_call(pack_kernel, out_shape=f32((tiles, SUBLANES, LANES)), in_s...  0.89 us
  transfers between devices with their start and end apart: 9, of which 4 were waited for; matrix products, arithmetic and copies ran while one was open for 0% of the time, Pallas kernels for 0%

profile of v22, /device:TPU:0, one launch (start us, length us, event | category | flops | bytes accessed | tf_op | source)
XLA Modules:
  0.0 22.2 jit_solution(11910503733180129956)
XLA Ops:
  0.6 0.9 %pack.1.refs_0_ = f32[19,8,128]{2,1,0:T(8,128)S(1)} custom-call(f32[24,384]{1,0:T(8,128)} %bitcast.7, s32[24,384]{1,0:T(8,128)} %bitcast.8, f32[16,24]{1,0:T(8,128)} %bitcast.9), custom_call_target="tpu_custom_call" | custom-call | tf_op jit(solution)/shard_map/pack/pallas_call | solution.py:193
  1.5 3.1 %collective-permute-start.2 = (f32[19,8,128]{2,1,0:T(8,128)S(1)}, f32[19,8,128]{2,1,0:T(8,128)S(1)}, u32[]{:S(2)}, u32[]{:S(2)}) collective-permute-start(f32[19,8,128]{2,1,0:T(8,128)S(1)} %pack.1.refs_0_), channel_id=1, source_target_pairs={{0,4},{1,5},{2,6},{3,7},{4,0},{5,1},{6,2},{7,3},{8,12},{9,13},{10,... | collective-permute-start | bytes 233480 | tf_op jit(solution)/shard_map/ppermute | solution.py:189
  4.6 2.6 %collective-permute-start = (f32[19,8,128]{2,1,0:T(8,128)S(1)}, f32[19,8,128]{2,1,0:T(8,128)S(1)}, u32[]{:S(2)}, u32[]{:S(2)}) collective-permute-start(f32[19,8,128]{2,1,0:T(8,128)S(1)} %pack.1.refs_0_), channel_id=1, source_target_pairs={{0,8},{1,9},{2,10},{3,11},{4,12},{5,13},{6,14},{7,15},{8,0},{9,1},... | collective-permute-start | bytes 233480 | tf_op jit(solution)/shard_map/ppermute | solution.py:189
  7.2 1.5 %collective-permute-start.1 = (f32[19,8,128]{2,1,0:T(8,128)S(1)}, f32[19,8,128]{2,1,0:T(8,128)S(1)}, u32[]{:S(2)}, u32[]{:S(2)}) collective-permute-start(f32[19,8,128]{2,1,0:T(8,128)S(1)} %pack.1.refs_0_), channel_id=1, source_target_pairs={{0,2},{1,3},{2,0},{3,1},{4,6},{5,7},{6,4},{7,5},{8,10},{9,11},{10,... | collective-permute-start | bytes 233480 | tf_op jit(solution)/shard_map/ppermute | solution.py:189
  8.7 0.0 collective-permute-start.4
  8.7 0.0 collective-permute-done.2.refs_3_
  8.7 1.7 %collective-permute-start.7 = (f32[19,8,128]{2,1,0:T(8,128)S(1)}, f32[19,8,128]{2,1,0:T(8,128)S(1)}, u32[]{:S(2)}, u32[]{:S(2)}) collective-permute-start(f32[19,8,128]{2,1,0:T(8,128)S(1)} %collective-permute-done.2.refs_3_), channel_id=1, source_target_pairs={{0,2},{1,3},{2,0},{3,1},{4,6},{5,7},{6,4},{7,5},{8,10},{9,11},{10,... | collective-permute-start | bytes 233480 | tf_op jit(solution)/shard_map/ppermute | solution.py:189
  10.4 0.9 %collective-permute-done.refs_1_ = f32[19,8,128]{2,1,0:T(8,128)S(1)} collective-permute-done((f32[19,8,128]{2,1,0:T(8,128)S(1)}, f32[19,8,128]{2,1,0:T(8,128)S(1)}, u32[]{:S(2)}, u32[]{:S(2)}) %collective-permute-start) | collective-permute-done | bytes 77856 | tf_op jit(solution)/shard_map/ppermute | solution.py:189
  11.3 2.1 %collective-permute-start.6 = (f32[19,8,128]{2,1,0:T(8,128)S(1)}, f32[19,8,128]{2,1,0:T(8,128)S(1)}, u32[]{:S(2)}, u32[]{:S(2)}) collective-permute-start(f32[19,8,128]{2,1,0:T(8,128)S(1)} %collective-permute-done.refs_1_), channel_id=1, source_target_pairs={{0,4},{1,5},{2,6},{3,7},{4,0},{5,1},{6,2},{7,3},{8,12},{9,13},{10,... | collective-permute-start | bytes 233480 | tf_op jit(solution)/shard_map/ppermute | solution.py:189
  13.3 1.5 %collective-permute-start.5 = (f32[19,8,128]{2,1,0:T(8,128)S(1)}, f32[19,8,128]{2,1,0:T(8,128)S(1)}, u32[]{:S(2)}, u32[]{:S(2)}) collective-permute-start(f32[19,8,128]{2,1,0:T(8,128)S(1)} %collective-permute-done.refs_1_), channel_id=1, source_target_pairs={{0,2},{1,3},{2,0},{3,1},{4,6},{5,7},{6,4},{7,5},{8,10},{9,11},{10,... | collective-permute-start | bytes 233480 | tf_op jit(solution)/shard_map/ppermute | solution.py:189
  14.9 0.0 collective-permute-done.1.refs_2_
  14.9 0.1 collective-permute-start.3
  15.0 0.8 %collective-permute-done.4.refs_0_ = f32[19,8,128]{2,1,0:T(8,128)S(1)} collective-permute-done((f32[19,8,128]{2,1,0:T(8,128)S(1)}, f32[19,8,128]{2,1,0:T(8,128)S(1)}, u32[]{:S(2)}, u32[]{:S(2)}) %collective-permute-start.4) | collective-permute-done | bytes 77856 | tf_op jit(solution)/shard_map/ppermute | solution.py:189
  15.8 0.0 collective-permute-done.7.refs_3_
  15.8 0.0 collective-permute-done.6.refs_2_
  15.8 1.9 %collective-permute-done.5.refs_1_ = f32[19,8,128]{2,1,0:T(8,128)S(1)} collective-permute-done((f32[19,8,128]{2,1,0:T(8,128)S(1)}, f32[19,8,128]{2,1,0:T(8,128)S(1)}, u32[]{:S(2)}, u32[]{:S(2)}) %collective-permute-start.5) | collective-permute-done | bytes 77856 | tf_op jit(solution)/shard_map/ppermute | solution.py:189
  17.8 0.1 collective-permute-start.8
  17.8 0.0 collective-permute-done.3.refs_1_
  17.9 1.6 %collective-permute-done.8.refs_3_ = f32[76,8,128]{2,1,0:T(8,128)S(1)} collective-permute-done((f32[76,8,128]{2,1,0:T(8,128)S(1)}, f32[76,8,128]{2,1,0:T(8,128)S(1)}, u32[]{:S(2)}, u32[]{:S(2)}) %collective-permute-start.8) | collective-permute-done | bytes 311328 | tf_op jit(solution)/shard_map/ppermute | solution.py:189
  19.4 2.8 %group_smacof.1 = (f32[16,24]{1,0:T(8,128)}, f32[1,3]{1,0:T(1,128)}) custom-call(f32[76,8,128]{2,1,0:T(8,128)S(1)} %join.2.refs_0_, f32[76,8,128]{2,1,0:T(8,128)S(1)} %collective-permute-done.3.refs_1_, f32[76,8,128]{2,1,0:T(8,128)S(1)} %join.3.refs_2_, f32[76,8,128]{2,1,0:T(8,128)S(1)} %collective-permute-done.8.refs_3_), custom_call_target="tpu_custom_call" | custom-call | tf_op jit(solution)/shard_map/group_smacof/pallas_call | solution.py:231
  (2 shorter events, 0.0 us)
Async XLA Ops:
  1.5 7.2 %collective-permute-start.2 = (f32[19,8,128]{2,1,0:T(8,128)S(1)}, f32[19,8,128]{2,1,0:T(8,128)S(1)}, u32[]{:S(2)}, u32[]{:S(2)}) collective-permute-start(f32[19,8,128]{2,1,0:T(8,128)S(1)} %pack.1.refs_0_), channel_id=1, source_target_pairs={{0,4},{1,5},{2,6},{3,7},{4,0},{5,1},{6,2},{7,3},{8,12},{9,13},{10,... | collective-permute-start | bytes 233480 | tf_op jit(solution)/shard_map/ppermute | solution.py:189
  4.6 6.6 %collective-permute-start = (f32[19,8,128]{2,1,0:T(8,128)S(1)}, f32[19,8,128]{2,1,0:T(8,128)S(1)}, u32[]{:S(2)}, u32[]{:S(2)}) collective-permute-start(f32[19,8,128]{2,1,0:T(8,128)S(1)} %pack.1.refs_0_), channel_id=1, source_target_pairs={{0,8},{1,9},{2,10},{3,11},{4,12},{5,13},{6,14},{7,15},{8,0},{9,1},... | collective-permute-start | bytes 233480 | tf_op jit(solution)/shard_map/ppermute | solution.py:189
  7.2 7.7 %collective-permute-start.1 = (f32[19,8,128]{2,1,0:T(8,128)S(1)}, f32[19,8,128]{2,1,0:T(8,128)S(1)}, u32[]{:S(2)}, u32[]{:S(2)}) collective-permute-start(f32[19,8,128]{2,1,0:T(8,128)S(1)} %pack.1.refs_0_), channel_id=1, source_target_pairs={{0,2},{1,3},{2,0},{3,1},{4,6},{5,7},{6,4},{7,5},{8,10},{9,11},{10,... | collective-permute-start | bytes 233480 | tf_op jit(solution)/shard_map/ppermute | solution.py:189
  8.7 7.1 %collective-permute-start.4 = (f32[19,8,128]{2,1,0:T(8,128)S(1)}, f32[19,8,128]{2,1,0:T(8,128)S(1)}, u32[]{:S(2)}, u32[]{:S(2)}) collective-permute-start(f32[19,8,128]{2,1,0:T(8,128)S(1)} %pack.1.refs_0_), channel_id=1, source_target_pairs={{0,14},{1,15},{2,12},{3,13},{4,10},{5,11},{6,8},{7,9},{8,6},{9,7},... | collective-permute-start | bytes 233480 | tf_op jit(solution)/shard_map/ppermute | solution.py:189
  8.7 7.1 %collective-permute-start.7 = (f32[19,8,128]{2,1,0:T(8,128)S(1)}, f32[19,8,128]{2,1,0:T(8,128)S(1)}, u32[]{:S(2)}, u32[]{:S(2)}) collective-permute-start(f32[19,8,128]{2,1,0:T(8,128)S(1)} %collective-permute-done.2.refs_3_), channel_id=1, source_target_pairs={{0,2},{1,3},{2,0},{3,1},{4,6},{5,7},{6,4},{7,5},{8,10},{9,11},{10,... | collective-permute-start | bytes 233480 | tf_op jit(solution)/shard_map/ppermute | solution.py:189
  11.3 4.5 %collective-permute-start.6 = (f32[19,8,128]{2,1,0:T(8,128)S(1)}, f32[19,8,128]{2,1,0:T(8,128)S(1)}, u32[]{:S(2)}, u32[]{:S(2)}) collective-permute-start(f32[19,8,128]{2,1,0:T(8,128)S(1)} %collective-permute-done.refs_1_), channel_id=1, source_target_pairs={{0,4},{1,5},{2,6},{3,7},{4,0},{5,1},{6,2},{7,3},{8,12},{9,13},{10,... | collective-permute-start | bytes 233480 | tf_op jit(solution)/shard_map/ppermute | solution.py:189
  13.3 4.4 %collective-permute-start.5 = (f32[19,8,128]{2,1,0:T(8,128)S(1)}, f32[19,8,128]{2,1,0:T(8,128)S(1)}, u32[]{:S(2)}, u32[]{:S(2)}) collective-permute-start(f32[19,8,128]{2,1,0:T(8,128)S(1)} %collective-permute-done.refs_1_), channel_id=1, source_target_pairs={{0,2},{1,3},{2,0},{3,1},{4,6},{5,7},{6,4},{7,5},{8,10},{9,11},{10,... | collective-permute-start | bytes 233480 | tf_op jit(solution)/shard_map/ppermute | solution.py:189
  14.9 3.0 %collective-permute-start.3 = (f32[76,8,128]{2,1,0:T(8,128)S(1)}, f32[76,8,128]{2,1,0:T(8,128)S(1)}, u32[]{:S(2)}, u32[]{:S(2)}) collective-permute-start(f32[76,8,128]{2,1,0:T(8,128)S(1)} %join.2.refs_0_), channel_id=1, source_target_pairs={{0,1},{1,0},{2,3},{3,2},{4,5},{5,4},{6,7},{7,6},{8,9},{9,8},{10,11... | collective-permute-start | bytes 933896 | tf_op jit(solution)/shard_map/ppermute | solution.py:189
  17.8 1.7 %collective-permute-start.8 = (f32[76,8,128]{2,1,0:T(8,128)S(1)}, f32[76,8,128]{2,1,0:T(8,128)S(1)}, u32[]{:S(2)}, u32[]{:S(2)}) collective-permute-start(f32[76,8,128]{2,1,0:T(8,128)S(1)} %join.3.refs_2_), channel_id=1, source_target_pairs={{0,1},{1,0},{2,3},{3,2},{4,5},{5,4},{6,7},{7,6},{8,9},{9,8},{10,11... | collective-permute-start | bytes 933896 | tf_op jit(solution)/shard_map/ppermute | solution.py:189

commit v23 on v22

--- a/solution.py
+++ b/solution.py
@@ -208,7 +208,7 @@
     held = {0: packed}
     for offset in (far, near, side, far | near | side):
         held[offset] = swap(packed, offset)
-    for source, step in ((far, side), (far, near), (near, side)):
+    for source, step in ((far, near), (far, side), (near, side)):
         held[source | step] = swap(held[source], step)
     early = [0, far, side, near]
     late = [offset for offset in held if offset not in early]

time: 22.4 us -> 22 us (0.982)
  waiting for transfers between devices: 5.23 us -> 4.73 us
    ppermute x9, waiting for transfers between devices: 5.23 us -> 4.73 us  [swap(): lax.ppermute(value, 'wide', [(i, i ^ offset) for i in range(devices)])]
  transfers between devices with their start and end apart: 9 -> 9, of which waited for: 4 -> 5; matrix products, arithmetic and copies ran while one was open for 0% -> 0% of each run, Pallas kernels for 0% -> 0%
where the time goes in v23:
time: 22 us; the launch traced here: 21.7 us
  starting transfers between devices  12.6 us (57%)
  waiting for transfers between devices  4.73 us (22%)
  Pallas kernels  3.74 us (17%)
  between operations  0.68 us (3%)
    ppermute x9, starting transfers between devices, swap(): lax.ppermute(value, 'wide', [(i, i ^ offset) for i in range(devices)])  12.6 us
    ppermute x9, waiting for transfers between devices, swap(): lax.ppermute(value, 'wide', [(i, i ^ offset) for i in range(devices)])  4.73 us
    pallas_call x1, Pallas kernels, small_body(): pl.pallas_call(functools.partial(group_kernel, offsets, per_dev), out_sha...  2.81 us
    pallas_call x1, Pallas kernels, small_body(): pl.pallas_call(pack_kernel, out_shape=f32((tiles, SUBLANES, LANES)), in_s...  0.89 us
  transfers between devices with their start and end apart: 9, of which 5 were waited for; matrix products, arithmetic and copies ran while one was open for 0% of the time, Pallas kernels for 0%

profile of v23, /device:TPU:0, one launch (start us, length us, event | category | flops | bytes accessed | tf_op | source)
XLA Modules:
  0.0 21.7 jit_solution(7972385953741362822)
XLA Ops:
  0.6 0.9 %pack.1.refs_0_ = f32[19,8,128]{2,1,0:T(8,128)S(1)} custom-call(f32[24,384]{1,0:T(8,128)} %bitcast.7, s32[24,384]{1,0:T(8,128)} %bitcast.8, f32[16,24]{1,0:T(8,128)} %bitcast.9), custom_call_target="tpu_custom_call" | custom-call | tf_op jit(solution)/shard_map/pack/pallas_call | solution.py:193
  1.5 3.1 %collective-permute-start.2 = (f32[19,8,128]{2,1,0:T(8,128)S(1)}, f32[19,8,128]{2,1,0:T(8,128)S(1)}, u32[]{:S(2)}, u32[]{:S(2)}) collective-permute-start(f32[19,8,128]{2,1,0:T(8,128)S(1)} %pack.1.refs_0_), channel_id=1, source_target_pairs={{0,4},{1,5},{2,6},{3,7},{4,0},{5,1},{6,2},{7,3},{8,12},{9,13},{10,... | collective-permute-start | bytes 233480 | tf_op jit(solution)/shard_map/ppermute | solution.py:189
  4.6 2.6 %collective-permute-start = (f32[19,8,128]{2,1,0:T(8,128)S(1)}, f32[19,8,128]{2,1,0:T(8,128)S(1)}, u32[]{:S(2)}, u32[]{:S(2)}) collective-permute-start(f32[19,8,128]{2,1,0:T(8,128)S(1)} %pack.1.refs_0_), channel_id=1, source_target_pairs={{0,8},{1,9},{2,10},{3,11},{4,12},{5,13},{6,14},{7,15},{8,0},{9,1},... | collective-permute-start | bytes 233480 | tf_op jit(solution)/shard_map/ppermute | solution.py:189
  7.2 1.5 %collective-permute-start.1 = (f32[19,8,128]{2,1,0:T(8,128)S(1)}, f32[19,8,128]{2,1,0:T(8,128)S(1)}, u32[]{:S(2)}, u32[]{:S(2)}) collective-permute-start(f32[19,8,128]{2,1,0:T(8,128)S(1)} %pack.1.refs_0_), channel_id=1, source_target_pairs={{0,2},{1,3},{2,0},{3,1},{4,6},{5,7},{6,4},{7,5},{8,10},{9,11},{10,... | collective-permute-start | bytes 233480 | tf_op jit(solution)/shard_map/ppermute | solution.py:189
  8.7 0.0 collective-permute-start.4
  8.7 0.0 collective-permute-done.2.refs_3_
  8.7 1.7 %collective-permute-start.7 = (f32[19,8,128]{2,1,0:T(8,128)S(1)}, f32[19,8,128]{2,1,0:T(8,128)S(1)}, u32[]{:S(2)}, u32[]{:S(2)}) collective-permute-start(f32[19,8,128]{2,1,0:T(8,128)S(1)} %collective-permute-done.2.refs_3_), channel_id=1, source_target_pairs={{0,2},{1,3},{2,0},{3,1},{4,6},{5,7},{6,4},{7,5},{8,10},{9,11},{10,... | collective-permute-start | bytes 233480 | tf_op jit(solution)/shard_map/ppermute | solution.py:189
  10.4 0.9 %collective-permute-done.refs_1_ = f32[19,8,128]{2,1,0:T(8,128)S(1)} collective-permute-done((f32[19,8,128]{2,1,0:T(8,128)S(1)}, f32[19,8,128]{2,1,0:T(8,128)S(1)}, u32[]{:S(2)}, u32[]{:S(2)}) %collective-permute-start) | collective-permute-done | bytes 77856 | tf_op jit(solution)/shard_map/ppermute | solution.py:189
  11.3 1.5 %collective-permute-start.6 = (f32[19,8,128]{2,1,0:T(8,128)S(1)}, f32[19,8,128]{2,1,0:T(8,128)S(1)}, u32[]{:S(2)}, u32[]{:S(2)}) collective-permute-start(f32[19,8,128]{2,1,0:T(8,128)S(1)} %collective-permute-done.refs_1_), channel_id=1, source_target_pairs={{0,2},{1,3},{2,0},{3,1},{4,6},{5,7},{6,4},{7,5},{8,10},{9,11},{10,... | collective-permute-start | bytes 233480 | tf_op jit(solution)/shard_map/ppermute | solution.py:189
  12.8 2.1 %collective-permute-start.5 = (f32[19,8,128]{2,1,0:T(8,128)S(1)}, f32[19,8,128]{2,1,0:T(8,128)S(1)}, u32[]{:S(2)}, u32[]{:S(2)}) collective-permute-start(f32[19,8,128]{2,1,0:T(8,128)S(1)} %collective-permute-done.refs_1_), channel_id=1, source_target_pairs={{0,4},{1,5},{2,6},{3,7},{4,0},{5,1},{6,2},{7,3},{8,12},{9,13},{10,... | collective-permute-start | bytes 233480 | tf_op jit(solution)/shard_map/ppermute | solution.py:189
  14.9 0.0 collective-permute-done.1.refs_2_
  14.9 0.1 collective-permute-start.3
  15.0 1.2 %collective-permute-done.4.refs_0_ = f32[19,8,128]{2,1,0:T(8,128)S(1)} collective-permute-done((f32[19,8,128]{2,1,0:T(8,128)S(1)}, f32[19,8,128]{2,1,0:T(8,128)S(1)}, u32[]{:S(2)}, u32[]{:S(2)}) %collective-permute-start.4) | collective-permute-done | bytes 77856 | tf_op jit(solution)/shard_map/ppermute | solution.py:189
  16.2 0.0 collective-permute-done.7.refs_3_
  16.2 0.3 %collective-permute-done.6.refs_2_ = f32[19,8,128]{2,1,0:T(8,128)S(1)} collective-permute-done((f32[19,8,128]{2,1,0:T(8,128)S(1)}, f32[19,8,128]{2,1,0:T(8,128)S(1)}, u32[]{:S(2)}, u32[]{:S(2)}) %collective-permute-start.6) | collective-permute-done | bytes 77856 | tf_op jit(solution)/shard_map/ppermute | solution.py:189
  16.5 0.7 %collective-permute-done.5.refs_1_ = f32[19,8,128]{2,1,0:T(8,128)S(1)} collective-permute-done((f32[19,8,128]{2,1,0:T(8,128)S(1)}, f32[19,8,128]{2,1,0:T(8,128)S(1)}, u32[]{:S(2)}, u32[]{:S(2)}) %collective-permute-start.5) | collective-permute-done | bytes 77856 | tf_op jit(solution)/shard_map/ppermute | solution.py:189
  17.3 0.1 collective-permute-start.8
  17.3 0.0 collective-permute-done.3.refs_1_
  17.4 1.6 %collective-permute-done.8.refs_3_ = f32[76,8,128]{2,1,0:T(8,128)S(1)} collective-permute-done((f32[76,8,128]{2,1,0:T(8,128)S(1)}, f32[76,8,128]{2,1,0:T(8,128)S(1)}, u32[]{:S(2)}, u32[]{:S(2)}) %collective-permute-start.8) | collective-permute-done | bytes 311328 | tf_op jit(solution)/shard_map/ppermute | solution.py:189
  18.9 2.8 %group_smacof.1 = (f32[16,24]{1,0:T(8,128)}, f32[1,3]{1,0:T(1,128)}) custom-call(f32[76,8,128]{2,1,0:T(8,128)S(1)} %join.2.refs_0_, f32[76,8,128]{2,1,0:T(8,128)S(1)} %collective-permute-done.3.refs_1_, f32[76,8,128]{2,1,0:T(8,128)S(1)} %join.3.refs_2_, f32[76,8,128]{2,1,0:T(8,128)S(1)} %collective-permute-done.8.refs_3_), custom_call_target="tpu_custom_call" | custom-call | tf_op jit(solution)/shard_map/group_smacof/pallas_call | solution.py:231
  (2 shorter events, 0.0 us)
Async XLA Ops:
  1.5 7.2 %collective-permute-start.2 = (f32[19,8,128]{2,1,0:T(8,128)S(1)}, f32[19,8,128]{2,1,0:T(8,128)S(1)}, u32[]{:S(2)}, u32[]{:S(2)}) collective-permute-start(f32[19,8,128]{2,1,0:T(8,128)S(1)} %pack.1.refs_0_), channel_id=1, source_target_pairs={{0,4},{1,5},{2,6},{3,7},{4,0},{5,1},{6,2},{7,3},{8,12},{9,13},{10,... | collective-permute-start | bytes 233480 | tf_op jit(solution)/shard_map/ppermute | solution.py:189
  4.6 6.6 %collective-permute-start = (f32[19,8,128]{2,1,0:T(8,128)S(1)}, f32[19,8,128]{2,1,0:T(8,128)S(1)}, u32[]{:S(2)}, u32[]{:S(2)}) collective-permute-start(f32[19,8,128]{2,1,0:T(8,128)S(1)} %pack.1.refs_0_), channel_id=1, source_target_pairs={{0,8},{1,9},{2,10},{3,11},{4,12},{5,13},{6,14},{7,15},{8,0},{9,1},... | collective-permute-start | bytes 233480 | tf_op jit(solution)/shard_map/ppermute | solution.py:189
  7.2 7.7 %collective-permute-start.1 = (f32[19,8,128]{2,1,0:T(8,128)S(1)}, f32[19,8,128]{2,1,0:T(8,128)S(1)}, u32[]{:S(2)}, u32[]{:S(2)}) collective-permute-start(f32[19,8,128]{2,1,0:T(8,128)S(1)} %pack.1.refs_0_), channel_id=1, source_target_pairs={{0,2},{1,3},{2,0},{3,1},{4,6},{5,7},{6,4},{7,5},{8,10},{9,11},{10,... | collective-permute-start | bytes 233480 | tf_op jit(solution)/shard_map/ppermute | solution.py:189
  8.7 7.5 %collective-permute-start.4 = (f32[19,8,128]{2,1,0:T(8,128)S(1)}, f32[19,8,128]{2,1,0:T(8,128)S(1)}, u32[]{:S(2)}, u32[]{:S(2)}) collective-permute-start(f32[19,8,128]{2,1,0:T(8,128)S(1)} %pack.1.refs_0_), channel_id=1, source_target_pairs={{0,14},{1,15},{2,12},{3,13},{4,10},{5,11},{6,8},{7,9},{8,6},{9,7},... | collective-permute-start | bytes 233480 | tf_op jit(solution)/shard_map/ppermute | solution.py:189
  8.7 7.5 %collective-permute-start.7 = (f32[19,8,128]{2,1,0:T(8,128)S(1)}, f32[19,8,128]{2,1,0:T(8,128)S(1)}, u32[]{:S(2)}, u32[]{:S(2)}) collective-permute-start(f32[19,8,128]{2,1,0:T(8,128)S(1)} %collective-permute-done.2.refs_3_), channel_id=1, source_target_pairs={{0,2},{1,3},{2,0},{3,1},{4,6},{5,7},{6,4},{7,5},{8,10},{9,11},{10,... | collective-permute-start | bytes 233480 | tf_op jit(solution)/shard_map/ppermute | solution.py:189
  11.3 5.2 %collective-permute-start.6 = (f32[19,8,128]{2,1,0:T(8,128)S(1)}, f32[19,8,128]{2,1,0:T(8,128)S(1)}, u32[]{:S(2)}, u32[]{:S(2)}) collective-permute-start(f32[19,8,128]{2,1,0:T(8,128)S(1)} %collective-permute-done.refs_1_), channel_id=1, source_target_pairs={{0,2},{1,3},{2,0},{3,1},{4,6},{5,7},{6,4},{7,5},{8,10},{9,11},{10,... | collective-permute-start | bytes 233480 | tf_op jit(solution)/shard_map/ppermute | solution.py:189
  12.8 4.5 %collective-permute-start.5 = (f32[19,8,128]{2,1,0:T(8,128)S(1)}, f32[19,8,128]{2,1,0:T(8,128)S(1)}, u32[]{:S(2)}, u32[]{:S(2)}) collective-permute-start(f32[19,8,128]{2,1,0:T(8,128)S(1)} %collective-permute-done.refs_1_), channel_id=1, source_target_pairs={{0,4},{1,5},{2,6},{3,7},{4,0},{5,1},{6,2},{7,3},{8,12},{9,13},{10,... | collective-permute-start | bytes 233480 | tf_op jit(solution)/shard_map/ppermute | solution.py:189
  14.9 2.5 %collective-permute-start.3 = (f32[76,8,128]{2,1,0:T(8,128)S(1)}, f32[76,8,128]{2,1,0:T(8,128)S(1)}, u32[]{:S(2)}, u32[]{:S(2)}) collective-permute-start(f32[76,8,128]{2,1,0:T(8,128)S(1)} %join.2.refs_0_), channel_id=1, source_target_pairs={{0,1},{1,0},{2,3},{3,2},{4,5},{5,4},{6,7},{7,6},{8,9},{9,8},{10,11... | collective-permute-start | bytes 933896 | tf_op jit(solution)/shard_map/ppermute | solution.py:189
  17.3 1.7 %collective-permute-start.8 = (f32[76,8,128]{2,1,0:T(8,128)S(1)}, f32[76,8,128]{2,1,0:T(8,128)S(1)}, u32[]{:S(2)}, u32[]{:S(2)}) collective-permute-start(f32[76,8,128]{2,1,0:T(8,128)S(1)} %join.3.refs_2_), channel_id=1, source_target_pairs={{0,1},{1,0},{2,3},{3,2},{4,5},{5,4},{6,7},{7,6},{8,9},{9,8},{10,11... | collective-permute-start | bytes 933896 | tf_op jit(solution)/shard_map/ppermute | solution.py:189

commit v24 on v18

--- a/solution.py
+++ b/solution.py
@@ -208,8 +208,10 @@
     held = {0: packed}
     for offset in (side, far, near, far | near | side):
         held[offset] = swap(packed, offset)
-    for source, step in ((far, side), (side, near), (far, near)):
-        held[source | step] = swap(held[source], step)
+    ordered, _ = lax.optimization_barrier((held[far], held[side]))
+    held[side | near] = swap(held[side], near)
+    held[far | side] = swap(ordered, side)
+    held[far | near] = swap(ordered, near)
     early = [0, side, near, far]
     late = [offset for offset in held if offset not in early]
     block = packed.shape[0]

time: 21.9 us -> 22.8 us (1.041)
  waiting for transfers between devices: 6.38 us -> 7.2 us
    ppermute x9, waiting for transfers between devices: 6.38 us -> 7.2 us  [swap(): lax.ppermute(value, 'wide', [(i, i ^ offset) for i in range(devices)])]
  transfers between devices with their start and end apart: 9 -> 9, of which waited for: 4 -> 7; matrix products, arithmetic and copies ran while one was open for 0% -> 0% of each run, Pallas kernels for 0% -> 0%
where the time goes in v24:
time: 22.8 us; the launch traced here: 22.6 us
  starting transfers between devices  11 us (48%)
  waiting for transfers between devices  7.2 us (32%)
  Pallas kernels  3.74 us (16%)
  between operations  0.68 us (3%)
    ppermute x9, starting transfers between devices, swap(): lax.ppermute(value, 'wide', [(i, i ^ offset) for i in range(devices)])  11 us
    ppermute x9, waiting for transfers between devices, swap(): lax.ppermute(value, 'wide', [(i, i ^ offset) for i in range(devices)])  7.2 us
    pallas_call x1, Pallas kernels, small_body(): pl.pallas_call(functools.partial(group_kernel, offsets, per_dev), out_sha...  2.81 us
    pallas_call x1, Pallas kernels, small_body(): pl.pallas_call(pack_kernel, out_shape=f32((tiles, SUBLANES, LANES)), in_s...  0.89 us
  transfers between devices with their start and end apart: 9, of which 7 were waited for; matrix products, arithmetic and copies ran while one was open for 0% of the time, Pallas kernels for 0%

profile of v24, /device:TPU:0, one launch (start us, length us, event | category | flops | bytes accessed | tf_op | source)
XLA Modules:
  0.0 22.6 jit_solution(17724469339202547678)
XLA Ops:
  0.6 0.9 %pack.1.refs_0_ = f32[19,8,128]{2,1,0:T(8,128)S(1)} custom-call(f32[24,384]{1,0:T(8,128)} %bitcast.7, s32[24,384]{1,0:T(8,128)} %bitcast.8, f32[16,24]{1,0:T(8,128)} %bitcast.9), custom_call_target="tpu_custom_call" | custom-call | tf_op jit(solution)/shard_map/pack/pallas_call | solution.py:193
  1.5 4.1 %collective-permute-start.2 = (f32[19,8,128]{2,1,0:T(8,128)S(1)}, f32[19,8,128]{2,1,0:T(8,128)S(1)}, u32[]{:S(2)}, u32[]{:S(2)}) collective-permute-start(f32[19,8,128]{2,1,0:T(8,128)S(1)} %pack.1.refs_0_), channel_id=1, source_target_pairs={{0,8},{1,9},{2,10},{3,11},{4,12},{5,13},{6,14},{7,15},{8,0},{9,1},... | collective-permute-start | bytes 233480 | tf_op jit(solution)/shard_map/ppermute | solution.py:189
  5.6 1.5 %collective-permute-start = (f32[19,8,128]{2,1,0:T(8,128)S(1)}, f32[19,8,128]{2,1,0:T(8,128)S(1)}, u32[]{:S(2)}, u32[]{:S(2)}) collective-permute-start(f32[19,8,128]{2,1,0:T(8,128)S(1)} %pack.1.refs_0_), channel_id=1, source_target_pairs={{0,2},{1,3},{2,0},{3,1},{4,6},{5,7},{6,4},{7,5},{8,10},{9,11},{10,... | collective-permute-start | bytes 233480 | tf_op jit(solution)/shard_map/ppermute | solution.py:189
  7.1 1.3 %collective-permute-start.4 = (f32[19,8,128]{2,1,0:T(8,128)S(1)}, f32[19,8,128]{2,1,0:T(8,128)S(1)}, u32[]{:S(2)}, u32[]{:S(2)}) collective-permute-start(f32[19,8,128]{2,1,0:T(8,128)S(1)} %pack.1.refs_0_), channel_id=1, source_target_pairs={{0,14},{1,15},{2,12},{3,13},{4,10},{5,11},{6,8},{7,9},{8,6},{9,7},... | collective-permute-start | bytes 233480 | tf_op jit(solution)/shard_map/ppermute | solution.py:189
  8.4 0.3 %collective-permute-start.1 = (f32[19,8,128]{2,1,0:T(8,128)S(1)}, f32[19,8,128]{2,1,0:T(8,128)S(1)}, u32[]{:S(2)}, u32[]{:S(2)}) collective-permute-start(f32[19,8,128]{2,1,0:T(8,128)S(1)} %pack.1.refs_0_), channel_id=1, source_target_pairs={{0,4},{1,5},{2,6},{3,7},{4,0},{5,1},{6,2},{7,3},{8,12},{9,13},{10,... | collective-permute-start | bytes 233480 | tf_op jit(solution)/shard_map/ppermute | solution.py:189
  8.7 1.0 %collective-permute-done.2.refs_3_ = f32[19,8,128]{2,1,0:T(8,128)S(1)} collective-permute-done((f32[19,8,128]{2,1,0:T(8,128)S(1)}, f32[19,8,128]{2,1,0:T(8,128)S(1)}, u32[]{:S(2)}, u32[]{:S(2)}) %collective-permute-start.2) | collective-permute-done | bytes 77856 | tf_op jit(solution)/shard_map/ppermute | solution.py:189
  9.7 0.4 %collective-permute-done.refs_1_ = f32[19,8,128]{2,1,0:T(8,128)S(1)} collective-permute-done((f32[19,8,128]{2,1,0:T(8,128)S(1)}, f32[19,8,128]{2,1,0:T(8,128)S(1)}, u32[]{:S(2)}, u32[]{:S(2)}) %collective-permute-start) | collective-permute-done | bytes 77856 | tf_op jit(solution)/shard_map/ppermute | solution.py:189
  10.0 2.4 %collective-permute-start.7 = (f32[19,8,128]{2,1,0:T(8,128)S(1)}, f32[19,8,128]{2,1,0:T(8,128)S(1)}, u32[]{:S(2)}, u32[]{:S(2)}) collective-permute-start(f32[19,8,128]{2,1,0:T(8,128)S(1)} %collective-permute-done.2.refs_3_), channel_id=1, source_target_pairs={{0,4},{1,5},{2,6},{3,7},{4,0},{5,1},{6,2},{7,3},{8,12},{9,13},{10,... | collective-permute-start | bytes 233480 | tf_op jit(solution)/shard_map/ppermute | solution.py:189
  12.4 1.3 %collective-permute-start.6 = (f32[19,8,128]{2,1,0:T(8,128)S(1)}, f32[19,8,128]{2,1,0:T(8,128)S(1)}, u32[]{:S(2)}, u32[]{:S(2)}) collective-permute-start(f32[19,8,128]{2,1,0:T(8,128)S(1)} %collective-permute-done.2.refs_3_), channel_id=1, source_target_pairs={{0,2},{1,3},{2,0},{3,1},{4,6},{5,7},{6,4},{7,5},{8,10},{9,11},{10,... | collective-permute-start | bytes 233480 | tf_op jit(solution)/shard_map/ppermute | solution.py:189
  13.7 0.0 collective-permute-start.5
  13.7 0.5 %collective-permute-done.1.refs_2_ = f32[19,8,128]{2,1,0:T(8,128)S(1)} collective-permute-done((f32[19,8,128]{2,1,0:T(8,128)S(1)}, f32[19,8,128]{2,1,0:T(8,128)S(1)}, u32[]{:S(2)}, u32[]{:S(2)}) %collective-permute-start.1) | collective-permute-done | bytes 77856 | tf_op jit(solution)/shard_map/ppermute | solution.py:189
  14.3 0.1 collective-permute-start.3
  14.3 0.0 collective-permute-done.4.refs_0_
  14.4 1.3 %collective-permute-done.7.refs_3_ = f32[19,8,128]{2,1,0:T(8,128)S(1)} collective-permute-done((f32[19,8,128]{2,1,0:T(8,128)S(1)}, f32[19,8,128]{2,1,0:T(8,128)S(1)}, u32[]{:S(2)}, u32[]{:S(2)}) %collective-permute-start.7) | collective-permute-done | bytes 77856 | tf_op jit(solution)/shard_map/ppermute | solution.py:189
  15.7 1.2 %collective-permute-done.6.refs_2_ = f32[19,8,128]{2,1,0:T(8,128)S(1)} collective-permute-done((f32[19,8,128]{2,1,0:T(8,128)S(1)}, f32[19,8,128]{2,1,0:T(8,128)S(1)}, u32[]{:S(2)}, u32[]{:S(2)}) %collective-permute-start.6) | collective-permute-done | bytes 77856 | tf_op jit(solution)/shard_map/ppermute | solution.py:189
  16.8 1.3 %collective-permute-done.5.refs_1_ = f32[19,8,128]{2,1,0:T(8,128)S(1)} collective-permute-done((f32[19,8,128]{2,1,0:T(8,128)S(1)}, f32[19,8,128]{2,1,0:T(8,128)S(1)}, u32[]{:S(2)}, u32[]{:S(2)}) %collective-permute-start.5) | collective-permute-done | bytes 77856 | tf_op jit(solution)/shard_map/ppermute | solution.py:189
  18.1 0.1 collective-permute-start.8
  18.2 0.0 collective-permute-done.3.refs_1_
  18.2 1.6 %collective-permute-done.8.refs_3_ = f32[76,8,128]{2,1,0:T(8,128)S(1)} collective-permute-done((f32[76,8,128]{2,1,0:T(8,128)S(1)}, f32[76,8,128]{2,1,0:T(8,128)S(1)}, u32[]{:S(2)}, u32[]{:S(2)}) %collective-permute-start.8) | collective-permute-done | bytes 311328 | tf_op jit(solution)/shard_map/ppermute | solution.py:189
  19.8 2.8 %group_smacof.1 = (f32[16,24]{1,0:T(8,128)}, f32[1,3]{1,0:T(1,128)}) custom-call(f32[76,8,128]{2,1,0:T(8,128)S(1)} %join.2.refs_0_, f32[76,8,128]{2,1,0:T(8,128)S(1)} %collective-permute-done.3.refs_1_, f32[76,8,128]{2,1,0:T(8,128)S(1)} %join.3.refs_2_, f32[76,8,128]{2,1,0:T(8,128)S(1)} %collective-permute-done.8.refs_3_), custom_call_target="tpu_custom_call" | custom-call | tf_op jit(solution)/shard_map/group_smacof/pallas_call | solution.py:233
  (2 shorter events, 0.0 us)
Async XLA Ops:
  1.5 8.1 %collective-permute-start.2 = (f32[19,8,128]{2,1,0:T(8,128)S(1)}, f32[19,8,128]{2,1,0:T(8,128)S(1)}, u32[]{:S(2)}, u32[]{:S(2)}) collective-permute-start(f32[19,8,128]{2,1,0:T(8,128)S(1)} %pack.1.refs_0_), channel_id=1, source_target_pairs={{0,8},{1,9},{2,10},{3,11},{4,12},{5,13},{6,14},{7,15},{8,0},{9,1},... | collective-permute-start | bytes 233480 | tf_op jit(solution)/shard_map/ppermute | solution.py:189
  5.6 4.4 %collective-permute-start = (f32[19,8,128]{2,1,0:T(8,128)S(1)}, f32[19,8,128]{2,1,0:T(8,128)S(1)}, u32[]{:S(2)}, u32[]{:S(2)}) collective-permute-start(f32[19,8,128]{2,1,0:T(8,128)S(1)} %pack.1.refs_0_), channel_id=1, source_target_pairs={{0,2},{1,3},{2,0},{3,1},{4,6},{5,7},{6,4},{7,5},{8,10},{9,11},{10,... | collective-permute-start | bytes 233480 | tf_op jit(solution)/shard_map/ppermute | solution.py:189
  7.1 7.3 %collective-permute-start.4 = (f32[19,8,128]{2,1,0:T(8,128)S(1)}, f32[19,8,128]{2,1,0:T(8,128)S(1)}, u32[]{:S(2)}, u32[]{:S(2)}) collective-permute-start(f32[19,8,128]{2,1,0:T(8,128)S(1)} %pack.1.refs_0_), channel_id=1, source_target_pairs={{0,14},{1,15},{2,12},{3,13},{4,10},{5,11},{6,8},{7,9},{8,6},{9,7},... | collective-permute-start | bytes 233480 | tf_op jit(solution)/shard_map/ppermute | solution.py:189
  8.4 5.8 %collective-permute-start.1 = (f32[19,8,128]{2,1,0:T(8,128)S(1)}, f32[19,8,128]{2,1,0:T(8,128)S(1)}, u32[]{:S(2)}, u32[]{:S(2)}) collective-permute-start(f32[19,8,128]{2,1,0:T(8,128)S(1)} %pack.1.refs_0_), channel_id=1, source_target_pairs={{0,4},{1,5},{2,6},{3,7},{4,0},{5,1},{6,2},{7,3},{8,12},{9,13},{10,... | collective-permute-start | bytes 233480 | tf_op jit(solution)/shard_map/ppermute | solution.py:189
  10.0 5.6 %collective-permute-start.7 = (f32[19,8,128]{2,1,0:T(8,128)S(1)}, f32[19,8,128]{2,1,0:T(8,128)S(1)}, u32[]{:S(2)}, u32[]{:S(2)}) collective-permute-start(f32[19,8,128]{2,1,0:T(8,128)S(1)} %collective-permute-done.2.refs_3_), channel_id=1, source_target_pairs={{0,4},{1,5},{2,6},{3,7},{4,0},{5,1},{6,2},{7,3},{8,12},{9,13},{10,... | collective-permute-start | bytes 233480 | tf_op jit(solution)/shard_map/ppermute | solution.py:189
  12.4 4.4 %collective-permute-start.6 = (f32[19,8,128]{2,1,0:T(8,128)S(1)}, f32[19,8,128]{2,1,0:T(8,128)S(1)}, u32[]{:S(2)}, u32[]{:S(2)}) collective-permute-start(f32[19,8,128]{2,1,0:T(8,128)S(1)} %collective-permute-done.2.refs_3_), channel_id=1, source_target_pairs={{0,2},{1,3},{2,0},{3,1},{4,6},{5,7},{6,4},{7,5},{8,10},{9,11},{10,... | collective-permute-start | bytes 233480 | tf_op jit(solution)/shard_map/ppermute | solution.py:189
  13.7 4.4 %collective-permute-start.5 = (f32[19,8,128]{2,1,0:T(8,128)S(1)}, f32[19,8,128]{2,1,0:T(8,128)S(1)}, u32[]{:S(2)}, u32[]{:S(2)}) collective-permute-start(f32[19,8,128]{2,1,0:T(8,128)S(1)} %collective-permute-done.refs_1_), channel_id=1, source_target_pairs={{0,4},{1,5},{2,6},{3,7},{4,0},{5,1},{6,2},{7,3},{8,12},{9,13},{10,... | collective-permute-start | bytes 233480 | tf_op jit(solution)/shard_map/ppermute | solution.py:189
  14.3 3.9 %collective-permute-start.3 = (f32[76,8,128]{2,1,0:T(8,128)S(1)}, f32[76,8,128]{2,1,0:T(8,128)S(1)}, u32[]{:S(2)}, u32[]{:S(2)}) collective-permute-start(f32[76,8,128]{2,1,0:T(8,128)S(1)} %join.2.refs_0_), channel_id=1, source_target_pairs={{0,1},{1,0},{2,3},{3,2},{4,5},{5,4},{6,7},{7,6},{8,9},{9,8},{10,11... | collective-permute-start | bytes 933896 | tf_op jit(solution)/shard_map/ppermute | solution.py:189
  18.1 1.7 %collective-permute-start.8 = (f32[76,8,128]{2,1,0:T(8,128)S(1)}, f32[76,8,128]{2,1,0:T(8,128)S(1)}, u32[]{:S(2)}, u32[]{:S(2)}) collective-permute-start(f32[76,8,128]{2,1,0:T(8,128)S(1)} %join.3.refs_2_), channel_id=1, source_target_pairs={{0,1},{1,0},{2,3},{3,2},{4,5},{5,4},{6,7},{7,6},{8,9},{9,8},{10,11... | collective-permute-start | bytes 933896 | tf_op jit(solution)/shard_map/ppermute | solution.py:189

commit v25 on v17

--- a/solution.py
+++ b/solution.py
@@ -208,8 +208,10 @@
     held = {0: packed}
     for offset in (far, side, near, far | near | side):
         held[offset] = swap(packed, offset)
-    for source, step in ((far, near), (far, side), (side, near)):
-        held[source | step] = swap(held[source], step)
+    ordered, _ = lax.optimization_barrier((held[far], held[side]))
+    held[far | near] = swap(ordered, near)
+    held[far | side] = swap(ordered, side)
+    held[side | near] = swap(held[side], near)
     early = [0, far, near, side]
     late = [offset for offset in held if offset not in early]
     block = packed.shape[0]

time: 21.2 us -> 23.4 us (1.10)
  waiting for transfers between devices: 6.15 us -> 9.38 us
  starting transfers between devices: 10.4 us -> 9.42 us
    ppermute x9, waiting for transfers between devices: 6.15 us -> 9.38 us  [swap(): lax.ppermute(value, 'wide', [(i, i ^ offset) for i in range(devices)])]
    ppermute x9, starting transfers between devices: 10.4 us -> 9.42 us  [swap(): lax.ppermute(value, 'wide', [(i, i ^ offset) for i in range(devices)])]
  transfers between devices with their start and end apart: 9 -> 9, of which waited for: 4 -> 5; matrix products, arithmetic and copies ran while one was open for 0% -> 0% of each run, Pallas kernels for 0% -> 0%
where the time goes in v25:
time: 23.4 us; the launch traced here: 23.2 us
  starting transfers between devices  9.42 us (40%)
  waiting for transfers between devices  9.38 us (40%)
  Pallas kernels  3.74 us (16%)
  between operations  0.69 us (3%)
    ppermute x9, starting transfers between devices, swap(): lax.ppermute(value, 'wide', [(i, i ^ offset) for i in range(devices)])  9.42 us
    ppermute x9, waiting for transfers between devices, swap(): lax.ppermute(value, 'wide', [(i, i ^ offset) for i in range(devices)])  9.38 us
    pallas_call x1, Pallas kernels, small_body(): pl.pallas_call(functools.partial(group_kernel, offsets, per_dev), out_sha...  2.81 us
    pallas_call x1, Pallas kernels, small_body(): pl.pallas_call(pack_kernel, out_shape=f32((tiles, SUBLANES, LANES)), in_s...  0.89 us
  transfers between devices with their start and end apart: 9, of which 5 were waited for; matrix products, arithmetic and copies ran while one was open for 0% of the time, Pallas kernels for 0%

profile of v25, /device:TPU:0, one launch (start us, length us, event | category | flops | bytes accessed | tf_op | source)
XLA Modules:
  0.0 23.2 jit_solution(10919395774173245035)
XLA Ops:
  0.6 0.9 %pack.1.refs_0_ = f32[19,8,128]{2,1,0:T(8,128)S(1)} custom-call(f32[24,384]{1,0:T(8,128)} %bitcast.7, s32[24,384]{1,0:T(8,128)} %bitcast.8, f32[16,24]{1,0:T(8,128)} %bitcast.9), custom_call_target="tpu_custom_call" | custom-call | tf_op jit(solution)/shard_map/pack/pallas_call | solution.py:193
  1.5 3.0 %collective-permute-start.2 = (f32[19,8,128]{2,1,0:T(8,128)S(1)}, f32[19,8,128]{2,1,0:T(8,128)S(1)}, u32[]{:S(2)}, u32[]{:S(2)}) collective-permute-start(f32[19,8,128]{2,1,0:T(8,128)S(1)} %pack.1.refs_0_), channel_id=1, source_target_pairs={{0,2},{1,3},{2,0},{3,1},{4,6},{5,7},{6,4},{7,5},{8,10},{9,11},{10,... | collective-permute-start | bytes 233480 | tf_op jit(solution)/shard_map/ppermute | solution.py:189
  4.5 2.6 %collective-permute-start = (f32[19,8,128]{2,1,0:T(8,128)S(1)}, f32[19,8,128]{2,1,0:T(8,128)S(1)}, u32[]{:S(2)}, u32[]{:S(2)}) collective-permute-start(f32[19,8,128]{2,1,0:T(8,128)S(1)} %pack.1.refs_0_), channel_id=1, source_target_pairs={{0,8},{1,9},{2,10},{3,11},{4,12},{5,13},{6,14},{7,15},{8,0},{9,1},... | collective-permute-start | bytes 233480 | tf_op jit(solution)/shard_map/ppermute | solution.py:189
  7.1 1.3 %collective-permute-start.4 = (f32[19,8,128]{2,1,0:T(8,128)S(1)}, f32[19,8,128]{2,1,0:T(8,128)S(1)}, u32[]{:S(2)}, u32[]{:S(2)}) collective-permute-start(f32[19,8,128]{2,1,0:T(8,128)S(1)} %pack.1.refs_0_), channel_id=1, source_target_pairs={{0,14},{1,15},{2,12},{3,13},{4,10},{5,11},{6,8},{7,9},{8,6},{9,7},... | collective-permute-start | bytes 233480 | tf_op jit(solution)/shard_map/ppermute | solution.py:189
  8.4 0.3 %collective-permute-start.1 = (f32[19,8,128]{2,1,0:T(8,128)S(1)}, f32[19,8,128]{2,1,0:T(8,128)S(1)}, u32[]{:S(2)}, u32[]{:S(2)}) collective-permute-start(f32[19,8,128]{2,1,0:T(8,128)S(1)} %pack.1.refs_0_), channel_id=1, source_target_pairs={{0,4},{1,5},{2,6},{3,7},{4,0},{5,1},{6,2},{7,3},{8,12},{9,13},{10,... | collective-permute-start | bytes 233480 | tf_op jit(solution)/shard_map/ppermute | solution.py:189
  8.7 0.0 collective-permute-done.2.refs_3_
  8.7 3.5 %collective-permute-done.refs_1_ = f32[19,8,128]{2,1,0:T(8,128)S(1)} collective-permute-done((f32[19,8,128]{2,1,0:T(8,128)S(1)}, f32[19,8,128]{2,1,0:T(8,128)S(1)}, u32[]{:S(2)}, u32[]{:S(2)}) %collective-permute-start) | collective-permute-done | bytes 77856 | tf_op jit(solution)/shard_map/ppermute | solution.py:189
  12.2 1.2 %collective-permute-start.7 = (f32[19,8,128]{2,1,0:T(8,128)S(1)}, f32[19,8,128]{2,1,0:T(8,128)S(1)}, u32[]{:S(2)}, u32[]{:S(2)}) collective-permute-start(f32[19,8,128]{2,1,0:T(8,128)S(1)} %collective-permute-done.2.refs_3_), channel_id=1, source_target_pairs={{0,4},{1,5},{2,6},{3,7},{4,0},{5,1},{6,2},{7,3},{8,12},{9,13},{10,... | collective-permute-start | bytes 233480 | tf_op jit(solution)/shard_map/ppermute | solution.py:189
  13.5 0.9 %collective-permute-start.6 = (f32[19,8,128]{2,1,0:T(8,128)S(1)}, f32[19,8,128]{2,1,0:T(8,128)S(1)}, u32[]{:S(2)}, u32[]{:S(2)}) collective-permute-start(f32[19,8,128]{2,1,0:T(8,128)S(1)} %collective-permute-done.refs_1_), channel_id=1, source_target_pairs={{0,2},{1,3},{2,0},{3,1},{4,6},{5,7},{6,4},{7,5},{8,10},{9,11},{10,... | collective-permute-start | bytes 233480 | tf_op jit(solution)/shard_map/ppermute | solution.py:189
  14.3 0.0 collective-permute-start.5
  14.3 0.0 collective-permute-done.1.refs_2_
  14.4 0.1 collective-permute-start.3
  14.4 0.0 collective-permute-done.4.refs_0_
  14.4 2.6 %collective-permute-done.7.refs_3_ = f32[19,8,128]{2,1,0:T(8,128)S(1)} collective-permute-done((f32[19,8,128]{2,1,0:T(8,128)S(1)}, f32[19,8,128]{2,1,0:T(8,128)S(1)}, u32[]{:S(2)}, u32[]{:S(2)}) %collective-permute-start.7) | collective-permute-done | bytes 77856 | tf_op jit(solution)/shard_map/ppermute | solution.py:189
  17.0 0.9 %collective-permute-done.6.refs_2_ = f32[19,8,128]{2,1,0:T(8,128)S(1)} collective-permute-done((f32[19,8,128]{2,1,0:T(8,128)S(1)}, f32[19,8,128]{2,1,0:T(8,128)S(1)}, u32[]{:S(2)}, u32[]{:S(2)}) %collective-permute-start.6) | collective-permute-done | bytes 77856 | tf_op jit(solution)/shard_map/ppermute | solution.py:189
  17.9 0.9 %collective-permute-done.5.refs_1_ = f32[19,8,128]{2,1,0:T(8,128)S(1)} collective-permute-done((f32[19,8,128]{2,1,0:T(8,128)S(1)}, f32[19,8,128]{2,1,0:T(8,128)S(1)}, u32[]{:S(2)}, u32[]{:S(2)}) %collective-permute-start.5) | collective-permute-done | bytes 77856 | tf_op jit(solution)/shard_map/ppermute | solution.py:189
  18.7 0.1 collective-permute-start.8
  18.8 0.0 collective-permute-done.3.refs_1_
  18.8 1.6 %collective-permute-done.8.refs_3_ = f32[76,8,128]{2,1,0:T(8,128)S(1)} collective-permute-done((f32[76,8,128]{2,1,0:T(8,128)S(1)}, f32[76,8,128]{2,1,0:T(8,128)S(1)}, u32[]{:S(2)}, u32[]{:S(2)}) %collective-permute-start.8) | collective-permute-done | bytes 311328 | tf_op jit(solution)/shard_map/ppermute | solution.py:189
  20.4 2.8 %group_smacof.1 = (f32[16,24]{1,0:T(8,128)}, f32[1,3]{1,0:T(1,128)}) custom-call(f32[76,8,128]{2,1,0:T(8,128)S(1)} %join.2.refs_0_, f32[76,8,128]{2,1,0:T(8,128)S(1)} %collective-permute-done.3.refs_1_, f32[76,8,128]{2,1,0:T(8,128)S(1)} %join.3.refs_2_, f32[76,8,128]{2,1,0:T(8,128)S(1)} %collective-permute-done.8.refs_3_), custom_call_target="tpu_custom_call" | custom-call | tf_op jit(solution)/shard_map/group_smacof/pallas_call | solution.py:233
  (2 shorter events, 0.0 us)
Async XLA Ops:
  1.5 7.2 %collective-permute-start.2 = (f32[19,8,128]{2,1,0:T(8,128)S(1)}, f32[19,8,128]{2,1,0:T(8,128)S(1)}, u32[]{:S(2)}, u32[]{:S(2)}) collective-permute-start(f32[19,8,128]{2,1,0:T(8,128)S(1)} %pack.1.refs_0_), channel_id=1, source_target_pairs={{0,2},{1,3},{2,0},{3,1},{4,6},{5,7},{6,4},{7,5},{8,10},{9,11},{10,... | collective-permute-start | bytes 233480 | tf_op jit(solution)/shard_map/ppermute | solution.py:189
  4.5 7.7 %collective-permute-start = (f32[19,8,128]{2,1,0:T(8,128)S(1)}, f32[19,8,128]{2,1,0:T(8,128)S(1)}, u32[]{:S(2)}, u32[]{:S(2)}) collective-permute-start(f32[19,8,128]{2,1,0:T(8,128)S(1)} %pack.1.refs_0_), channel_id=1, source_target_pairs={{0,8},{1,9},{2,10},{3,11},{4,12},{5,13},{6,14},{7,15},{8,0},{9,1},... | collective-permute-start | bytes 233480 | tf_op jit(solution)/shard_map/ppermute | solution.py:189
  7.1 7.3 %collective-permute-start.4 = (f32[19,8,128]{2,1,0:T(8,128)S(1)}, f32[19,8,128]{2,1,0:T(8,128)S(1)}, u32[]{:S(2)}, u32[]{:S(2)}) collective-permute-start(f32[19,8,128]{2,1,0:T(8,128)S(1)} %pack.1.refs_0_), channel_id=1, source_target_pairs={{0,14},{1,15},{2,12},{3,13},{4,10},{5,11},{6,8},{7,9},{8,6},{9,7},... | collective-permute-start | bytes 233480 | tf_op jit(solution)/shard_map/ppermute | solution.py:189
  8.4 5.9 %collective-permute-start.1 = (f32[19,8,128]{2,1,0:T(8,128)S(1)}, f32[19,8,128]{2,1,0:T(8,128)S(1)}, u32[]{:S(2)}, u32[]{:S(2)}) collective-permute-start(f32[19,8,128]{2,1,0:T(8,128)S(1)} %pack.1.refs_0_), channel_id=1, source_target_pairs={{0,4},{1,5},{2,6},{3,7},{4,0},{5,1},{6,2},{7,3},{8,12},{9,13},{10,... | collective-permute-start | bytes 233480 | tf_op jit(solution)/shard_map/ppermute | solution.py:189
  12.2 4.8 %collective-permute-start.7 = (f32[19,8,128]{2,1,0:T(8,128)S(1)}, f32[19,8,128]{2,1,0:T(8,128)S(1)}, u32[]{:S(2)}, u32[]{:S(2)}) collective-permute-start(f32[19,8,128]{2,1,0:T(8,128)S(1)} %collective-permute-done.2.refs_3_), channel_id=1, source_target_pairs={{0,4},{1,5},{2,6},{3,7},{4,0},{5,1},{6,2},{7,3},{8,12},{9,13},{10,... | collective-permute-start | bytes 233480 | tf_op jit(solution)/shard_map/ppermute | solution.py:189
  13.5 4.4 %collective-permute-start.6 = (f32[19,8,128]{2,1,0:T(8,128)S(1)}, f32[19,8,128]{2,1,0:T(8,128)S(1)}, u32[]{:S(2)}, u32[]{:S(2)}) collective-permute-start(f32[19,8,128]{2,1,0:T(8,128)S(1)} %collective-permute-done.refs_1_), channel_id=1, source_target_pairs={{0,2},{1,3},{2,0},{3,1},{4,6},{5,7},{6,4},{7,5},{8,10},{9,11},{10,... | collective-permute-start | bytes 233480 | tf_op jit(solution)/shard_map/ppermute | solution.py:189
  14.3 4.4 %collective-permute-start.5 = (f32[19,8,128]{2,1,0:T(8,128)S(1)}, f32[19,8,128]{2,1,0:T(8,128)S(1)}, u32[]{:S(2)}, u32[]{:S(2)}) collective-permute-start(f32[19,8,128]{2,1,0:T(8,128)S(1)} %collective-permute-done.refs_1_), channel_id=1, source_target_pairs={{0,4},{1,5},{2,6},{3,7},{4,0},{5,1},{6,2},{7,3},{8,12},{9,13},{10,... | collective-permute-start | bytes 233480 | tf_op jit(solution)/shard_map/ppermute | solution.py:189
  14.4 4.5 %collective-permute-start.3 = (f32[76,8,128]{2,1,0:T(8,128)S(1)}, f32[76,8,128]{2,1,0:T(8,128)S(1)}, u32[]{:S(2)}, u32[]{:S(2)}) collective-permute-start(f32[76,8,128]{2,1,0:T(8,128)S(1)} %join.2.refs_0_), channel_id=1, source_target_pairs={{0,1},{1,0},{2,3},{3,2},{4,5},{5,4},{6,7},{7,6},{8,9},{9,8},{10,11... | collective-permute-start | bytes 933896 | tf_op jit(solution)/shard_map/ppermute | solution.py:189
  18.7 1.7 %collective-permute-start.8 = (f32[76,8,128]{2,1,0:T(8,128)S(1)}, f32[76,8,128]{2,1,0:T(8,128)S(1)}, u32[]{:S(2)}, u32[]{:S(2)}) collective-permute-start(f32[76,8,128]{2,1,0:T(8,128)S(1)} %join.3.refs_2_), channel_id=1, source_target_pairs={{0,1},{1,0},{2,3},{3,2},{4,5},{5,4},{6,7},{7,6},{8,9},{9,8},{10,11... | collective-permute-start | bytes 933896 | tf_op jit(solution)/shard_map/ppermute | solution.py:189

commit v26 on v17

--- a/solution.py
+++ b/solution.py
@@ -208,7 +208,7 @@
     held = {0: packed}
     for offset in (far, side, near, far | near | side):
         held[offset] = swap(packed, offset)
-    for source, step in ((far, near), (far, side), (side, near)):
+    for source, step in ((far, near | 1), (far, side), (side, near)):
         held[source | step] = swap(held[source], step)
     early = [0, far, near, side]
     late = [offset for offset in held if offset not in early]

time: 21.2 us -> 21.2 us (level)
  waiting for transfers between devices: 6.15 us -> 7.84 us
  starting transfers between devices: 10.4 us -> 8.74 us
    ppermute x9, waiting for transfers between devices: 6.15 us -> 7.84 us  [swap(): lax.ppermute(value, 'wide', [(i, i ^ offset) for i in range(devices)])]
    ppermute x9, starting transfers between devices: 10.4 us -> 8.74 us  [swap(): lax.ppermute(value, 'wide', [(i, i ^ offset) for i in range(devices)])]
  transfers between devices with their start and end apart: 9 -> 9, of which waited for: 4 -> 5; matrix products, arithmetic and copies ran while one was open for 0% -> 0% of each run, Pallas kernels for 0% -> 0%
where the time goes in v26:
time: 21.2 us; the launch traced here: 21 us
  starting transfers between devices  8.74 us (41%)
  waiting for transfers between devices  7.84 us (37%)
  Pallas kernels  3.74 us (18%)
  between operations  0.66 us (3%)
    ppermute x9, starting transfers between devices, swap(): lax.ppermute(value, 'wide', [(i, i ^ offset) for i in range(devices)])  8.74 us
    ppermute x9, waiting for transfers between devices, swap(): lax.ppermute(value, 'wide', [(i, i ^ offset) for i in range(devices)])  7.84 us
    pallas_call x1, Pallas kernels, small_body(): pl.pallas_call(functools.partial(group_kernel, offsets, per_dev), out_sha...  2.81 us
    pallas_call x1, Pallas kernels, small_body(): pl.pallas_call(pack_kernel, out_shape=f32((tiles, SUBLANES, LANES)), in_s...  0.89 us
  transfers between devices with their start and end apart: 9, of which 5 were waited for; matrix products, arithmetic and copies ran while one was open for 0% of the time, Pallas kernels for 0%

profile of v26, /device:TPU:0, one launch (start us, length us, event | category | flops | bytes accessed | tf_op | source)
XLA Modules:
  0.0 21.0 jit_solution(102390516784341128)
XLA Ops:
  0.6 0.9 %pack.1.refs_0_ = f32[19,8,128]{2,1,0:T(8,128)S(1)} custom-call(f32[24,384]{1,0:T(8,128)} %bitcast.7, s32[24,384]{1,0:T(8,128)} %bitcast.8, f32[16,24]{1,0:T(8,128)} %bitcast.9), custom_call_target="tpu_custom_call" | custom-call | tf_op jit(solution)/shard_map/pack/pallas_call | solution.py:193
  1.5 3.0 %collective-permute-start.2 = (f32[19,8,128]{2,1,0:T(8,128)S(1)}, f32[19,8,128]{2,1,0:T(8,128)S(1)}, u32[]{:S(2)}, u32[]{:S(2)}) collective-permute-start(f32[19,8,128]{2,1,0:T(8,128)S(1)} %pack.1.refs_0_), channel_id=1, source_target_pairs={{0,2},{1,3},{2,0},{3,1},{4,6},{5,7},{6,4},{7,5},{8,10},{9,11},{10,... | collective-permute-start | bytes 233480 | tf_op jit(solution)/shard_map/ppermute | solution.py:189
  4.5 2.6 %collective-permute-start = (f32[19,8,128]{2,1,0:T(8,128)S(1)}, f32[19,8,128]{2,1,0:T(8,128)S(1)}, u32[]{:S(2)}, u32[]{:S(2)}) collective-permute-start(f32[19,8,128]{2,1,0:T(8,128)S(1)} %pack.1.refs_0_), channel_id=1, source_target_pairs={{0,8},{1,9},{2,10},{3,11},{4,12},{5,13},{6,14},{7,15},{8,0},{9,1},... | collective-permute-start | bytes 233480 | tf_op jit(solution)/shard_map/ppermute | solution.py:189
  7.1 1.6 %collective-permute-start.1 = (f32[19,8,128]{2,1,0:T(8,128)S(1)}, f32[19,8,128]{2,1,0:T(8,128)S(1)}, u32[]{:S(2)}, u32[]{:S(2)}) collective-permute-start(f32[19,8,128]{2,1,0:T(8,128)S(1)} %pack.1.refs_0_), channel_id=1, source_target_pairs={{0,4},{1,5},{2,6},{3,7},{4,0},{5,1},{6,2},{7,3},{8,12},{9,13},{10,... | collective-permute-start | bytes 233480 | tf_op jit(solution)/shard_map/ppermute | solution.py:189
  8.7 0.0 collective-permute-start.4
  8.7 0.0 collective-permute-done.2.refs_3_
  8.7 0.9 %collective-permute-start.7 = (f32[19,8,128]{2,1,0:T(8,128)S(1)}, f32[19,8,128]{2,1,0:T(8,128)S(1)}, u32[]{:S(2)}, u32[]{:S(2)}) collective-permute-start(f32[19,8,128]{2,1,0:T(8,128)S(1)} %collective-permute-done.2.refs_3_), channel_id=1, source_target_pairs={{0,4},{1,5},{2,6},{3,7},{4,0},{5,1},{6,2},{7,3},{8,12},{9,13},{10,... | collective-permute-start | bytes 233480 | tf_op jit(solution)/shard_map/ppermute | solution.py:189
  9.6 1.7 %collective-permute-done.refs_1_ = f32[19,8,128]{2,1,0:T(8,128)S(1)} collective-permute-done((f32[19,8,128]{2,1,0:T(8,128)S(1)}, f32[19,8,128]{2,1,0:T(8,128)S(1)}, u32[]{:S(2)}, u32[]{:S(2)}) %collective-permute-start) | collective-permute-done | bytes 77856 | tf_op jit(solution)/shard_map/ppermute | solution.py:189
  11.2 0.0 collective-permute-start.6
  11.2 0.0 collective-permute-start.5
  11.2 1.9 %collective-permute-done.1.refs_2_ = f32[19,8,128]{2,1,0:T(8,128)S(1)} collective-permute-done((f32[19,8,128]{2,1,0:T(8,128)S(1)}, f32[19,8,128]{2,1,0:T(8,128)S(1)}, u32[]{:S(2)}, u32[]{:S(2)}) %collective-permute-start.1) | collective-permute-done | bytes 77856 | tf_op jit(solution)/shard_map/ppermute | solution.py:189
  13.2 0.5 %collective-permute-start.3 = (f32[76,8,128]{2,1,0:T(8,128)S(1)}, f32[76,8,128]{2,1,0:T(8,128)S(1)}, u32[]{:S(2)}, u32[]{:S(2)}) collective-permute-start(f32[76,8,128]{2,1,0:T(8,128)S(1)} %join.2.refs_0_), channel_id=1, source_target_pairs={{0,1},{1,0},{2,3},{3,2},{4,5},{5,4},{6,7},{7,6},{8,9},{9,8},{10,11... | collective-permute-start | bytes 933896 | tf_op jit(solution)/shard_map/ppermute | solution.py:189
  13.7 2.2 %collective-permute-done.4.refs_0_ = f32[19,8,128]{2,1,0:T(8,128)S(1)} collective-permute-done((f32[19,8,128]{2,1,0:T(8,128)S(1)}, f32[19,8,128]{2,1,0:T(8,128)S(1)}, u32[]{:S(2)}, u32[]{:S(2)}) %collective-permute-start.4) | collective-permute-done | bytes 77856 | tf_op jit(solution)/shard_map/ppermute | solution.py:189
  15.9 0.0 collective-permute-done.7.refs_3_
  15.9 0.6 %collective-permute-done.6.refs_2_ = f32[19,8,128]{2,1,0:T(8,128)S(1)} collective-permute-done((f32[19,8,128]{2,1,0:T(8,128)S(1)}, f32[19,8,128]{2,1,0:T(8,128)S(1)}, u32[]{:S(2)}, u32[]{:S(2)}) %collective-permute-start.6) | collective-permute-done | bytes 77856 | tf_op jit(solution)/shard_map/ppermute | solution.py:189
  16.5 0.0 collective-permute-done.5.refs_1_
  16.5 0.2 collective-permute-start.8
  16.7 0.0 collective-permute-done.3.refs_1_
  16.7 1.5 %collective-permute-done.8.refs_3_ = f32[76,8,128]{2,1,0:T(8,128)S(1)} collective-permute-done((f32[76,8,128]{2,1,0:T(8,128)S(1)}, f32[76,8,128]{2,1,0:T(8,128)S(1)}, u32[]{:S(2)}, u32[]{:S(2)}) %collective-permute-start.8) | collective-permute-done | bytes 311328 | tf_op jit(solution)/shard_map/ppermute | solution.py:189
  18.2 2.8 %group_smacof.1 = (f32[16,24]{1,0:T(8,128)}, f32[1,3]{1,0:T(1,128)}) custom-call(f32[76,8,128]{2,1,0:T(8,128)S(1)} %join.2.refs_0_, f32[76,8,128]{2,1,0:T(8,128)S(1)} %collective-permute-done.3.refs_1_, f32[76,8,128]{2,1,0:T(8,128)S(1)} %join.3.refs_2_, f32[76,8,128]{2,1,0:T(8,128)S(1)} %collective-permute-done.8.refs_3_), custom_call_target="tpu_custom_call" | custom-call | tf_op jit(solution)/shard_map/group_smacof/pallas_call | solution.py:231
  (2 shorter events, 0.0 us)
Async XLA Ops:
  1.5 7.2 %collective-permute-start.2 = (f32[19,8,128]{2,1,0:T(8,128)S(1)}, f32[19,8,128]{2,1,0:T(8,128)S(1)}, u32[]{:S(2)}, u32[]{:S(2)}) collective-permute-start(f32[19,8,128]{2,1,0:T(8,128)S(1)} %pack.1.refs_0_), channel_id=1, source_target_pairs={{0,2},{1,3},{2,0},{3,1},{4,6},{5,7},{6,4},{7,5},{8,10},{9,11},{10,... | collective-permute-start | bytes 233480 | tf_op jit(solution)/shard_map/ppermute | solution.py:189
  4.5 6.7 %collective-permute-start = (f32[19,8,128]{2,1,0:T(8,128)S(1)}, f32[19,8,128]{2,1,0:T(8,128)S(1)}, u32[]{:S(2)}, u32[]{:S(2)}) collective-permute-start(f32[19,8,128]{2,1,0:T(8,128)S(1)} %pack.1.refs_0_), channel_id=1, source_target_pairs={{0,8},{1,9},{2,10},{3,11},{4,12},{5,13},{6,14},{7,15},{8,0},{9,1},... | collective-permute-start | bytes 233480 | tf_op jit(solution)/shard_map/ppermute | solution.py:189
  7.1 6.0 %collective-permute-start.1 = (f32[19,8,128]{2,1,0:T(8,128)S(1)}, f32[19,8,128]{2,1,0:T(8,128)S(1)}, u32[]{:S(2)}, u32[]{:S(2)}) collective-permute-start(f32[19,8,128]{2,1,0:T(8,128)S(1)} %pack.1.refs_0_), channel_id=1, source_target_pairs={{0,4},{1,5},{2,6},{3,7},{4,0},{5,1},{6,2},{7,3},{8,12},{9,13},{10,... | collective-permute-start | bytes 233480 | tf_op jit(solution)/shard_map/ppermute | solution.py:189
  8.7 7.2 %collective-permute-start.4 = (f32[19,8,128]{2,1,0:T(8,128)S(1)}, f32[19,8,128]{2,1,0:T(8,128)S(1)}, u32[]{:S(2)}, u32[]{:S(2)}) collective-permute-start(f32[19,8,128]{2,1,0:T(8,128)S(1)} %pack.1.refs_0_), channel_id=1, source_target_pairs={{0,14},{1,15},{2,12},{3,13},{4,10},{5,11},{6,8},{7,9},{8,6},{9,7},... | collective-permute-start | bytes 233480 | tf_op jit(solution)/shard_map/ppermute | solution.py:189
  8.7 7.2 %collective-permute-start.7 = (f32[19,8,128]{2,1,0:T(8,128)S(1)}, f32[19,8,128]{2,1,0:T(8,128)S(1)}, u32[]{:S(2)}, u32[]{:S(2)}) collective-permute-start(f32[19,8,128]{2,1,0:T(8,128)S(1)} %collective-permute-done.2.refs_3_), channel_id=1, source_target_pairs={{0,4},{1,5},{2,6},{3,7},{4,0},{5,1},{6,2},{7,3},{8,12},{9,13},{10,... | collective-permute-start | bytes 233480 | tf_op jit(solution)/shard_map/ppermute | solution.py:189
  11.2 5.2 %collective-permute-start.6 = (f32[19,8,128]{2,1,0:T(8,128)S(1)}, f32[19,8,128]{2,1,0:T(8,128)S(1)}, u32[]{:S(2)}, u32[]{:S(2)}) collective-permute-start(f32[19,8,128]{2,1,0:T(8,128)S(1)} %collective-permute-done.refs_1_), channel_id=1, source_target_pairs={{0,2},{1,3},{2,0},{3,1},{4,6},{5,7},{6,4},{7,5},{8,10},{9,11},{10,... | collective-permute-start | bytes 233480 | tf_op jit(solution)/shard_map/ppermute | solution.py:189
  11.2 5.2 %collective-permute-start.5 = (f32[19,8,128]{2,1,0:T(8,128)S(1)}, f32[19,8,128]{2,1,0:T(8,128)S(1)}, u32[]{:S(2)}, u32[]{:S(2)}) collective-permute-start(f32[19,8,128]{2,1,0:T(8,128)S(1)} %collective-permute-done.refs_1_), channel_id=1, source_target_pairs={{0,5},{1,4},{2,7},{3,6},{4,1},{5,0},{6,3},{7,2},{8,13},{9,12},{10,... | collective-permute-start | bytes 233480 | tf_op jit(solution)/shard_map/ppermute | solution.py:189
  13.2 3.5 %collective-permute-start.3 = (f32[76,8,128]{2,1,0:T(8,128)S(1)}, f32[76,8,128]{2,1,0:T(8,128)S(1)}, u32[]{:S(2)}, u32[]{:S(2)}) collective-permute-start(f32[76,8,128]{2,1,0:T(8,128)S(1)} %join.2.refs_0_), channel_id=1, source_target_pairs={{0,1},{1,0},{2,3},{3,2},{4,5},{5,4},{6,7},{7,6},{8,9},{9,8},{10,11... | collective-permute-start | bytes 933896 | tf_op jit(solution)/shard_map/ppermute | solution.py:189
  16.5 1.7 %collective-permute-start.8 = (f32[76,8,128]{2,1,0:T(8,128)S(1)}, f32[76,8,128]{2,1,0:T(8,128)S(1)}, u32[]{:S(2)}, u32[]{:S(2)}) collective-permute-start(f32[76,8,128]{2,1,0:T(8,128)S(1)} %join.3.refs_2_), channel_id=1, source_target_pairs={{0,1},{1,0},{2,3},{3,2},{4,5},{5,4},{6,7},{7,6},{8,9},{9,8},{10,11... | collective-permute-start | bytes 933896 | tf_op jit(solution)/shard_map/ppermute | solution.py:189

commit v27 on v26

--- a/solution.py
+++ b/solution.py
@@ -206,7 +206,7 @@
     )(*(pltpu.with_memory_space_constraint(array, pltpu.HBM) for array in inputs))
     far, near, side = devices // 2, devices // 4, devices // 8
     held = {0: packed}
-    for offset in (far, side, near, far | near | side):
+    for offset in (far, side, near, far | near | side | 1):
         held[offset] = swap(packed, offset)
     for source, step in ((far, near | 1), (far, side), (side, near)):
         held[source | step] = swap(held[source], step)

time: 21.2 us -> 21 us (level)
  waiting for transfers between devices: 7.84 us -> 6.14 us
  starting transfers between devices: 8.74 us -> 10.2 us
    ppermute x9, waiting for transfers between devices: 7.84 us -> 6.14 us  [swap(): lax.ppermute(value, 'wide', [(i, i ^ offset) for i in range(devices)])]
    ppermute x9, starting transfers between devices: 8.74 us -> 10.2 us  [swap(): lax.ppermute(value, 'wide', [(i, i ^ offset) for i in range(devices)])]
  transfers between devices with their start and end apart: 9 -> 9, of which waited for: 5 -> 6; matrix products, arithmetic and copies ran while one was open for 0% -> 0% of each run, Pallas kernels for 0% -> 0%
where the time goes in v27:
time: 21 us; the launch traced here: 20.8 us
  starting transfers between devices  10.2 us (49%)
  waiting for transfers between devices  6.14 us (29%)
  Pallas kernels  3.74 us (18%)
  between operations  0.65 us (3%)
    ppermute x9, starting transfers between devices, swap(): lax.ppermute(value, 'wide', [(i, i ^ offset) for i in range(devices)])  10.2 us
    ppermute x9, waiting for transfers between devices, swap(): lax.ppermute(value, 'wide', [(i, i ^ offset) for i in range(devices)])  6.14 us
    pallas_call x1, Pallas kernels, small_body(): pl.pallas_call(functools.partial(group_kernel, offsets, per_dev), out_sha...  2.81 us
    pallas_call x1, Pallas kernels, small_body(): pl.pallas_call(pack_kernel, out_shape=f32((tiles, SUBLANES, LANES)), in_s...  0.89 us
  transfers between devices with their start and end apart: 9, of which 6 were waited for; matrix products, arithmetic and copies ran while one was open for 0% of the time, Pallas kernels for 0%

profile of v27, /device:TPU:0, one launch (start us, length us, event | category | flops | bytes accessed | tf_op | source)
XLA Modules:
  0.0 20.8 jit_solution(8175541967730145213)
XLA Ops:
  0.6 0.9 %pack.1.refs_0_ = f32[19,8,128]{2,1,0:T(8,128)S(1)} custom-call(f32[24,384]{1,0:T(8,128)} %bitcast.7, s32[24,384]{1,0:T(8,128)} %bitcast.8, f32[16,24]{1,0:T(8,128)} %bitcast.9), custom_call_target="tpu_custom_call" | custom-call | tf_op jit(solution)/shard_map/pack/pallas_call | solution.py:193
  1.5 3.0 %collective-permute-start.2 = (f32[19,8,128]{2,1,0:T(8,128)S(1)}, f32[19,8,128]{2,1,0:T(8,128)S(1)}, u32[]{:S(2)}, u32[]{:S(2)}) collective-permute-start(f32[19,8,128]{2,1,0:T(8,128)S(1)} %pack.1.refs_0_), channel_id=1, source_target_pairs={{0,2},{1,3},{2,0},{3,1},{4,6},{5,7},{6,4},{7,5},{8,10},{9,11},{10,... | collective-permute-start | bytes 233480 | tf_op jit(solution)/shard_map/ppermute | solution.py:189
  4.5 2.6 %collective-permute-start = (f32[19,8,128]{2,1,0:T(8,128)S(1)}, f32[19,8,128]{2,1,0:T(8,128)S(1)}, u32[]{:S(2)}, u32[]{:S(2)}) collective-permute-start(f32[19,8,128]{2,1,0:T(8,128)S(1)} %pack.1.refs_0_), channel_id=1, source_target_pairs={{0,8},{1,9},{2,10},{3,11},{4,12},{5,13},{6,14},{7,15},{8,0},{9,1},... | collective-permute-start | bytes 233480 | tf_op jit(solution)/shard_map/ppermute | solution.py:189
  7.1 1.6 %collective-permute-start.1 = (f32[19,8,128]{2,1,0:T(8,128)S(1)}, f32[19,8,128]{2,1,0:T(8,128)S(1)}, u32[]{:S(2)}, u32[]{:S(2)}) collective-permute-start(f32[19,8,128]{2,1,0:T(8,128)S(1)} %pack.1.refs_0_), channel_id=1, source_target_pairs={{0,4},{1,5},{2,6},{3,7},{4,0},{5,1},{6,2},{7,3},{8,12},{9,13},{10,... | collective-permute-start | bytes 233480 | tf_op jit(solution)/shard_map/ppermute | solution.py:189
  8.7 0.0 collective-permute-start.4
  8.7 0.0 collective-permute-done.2.refs_3_
  8.7 0.5 %collective-permute-start.7 = (f32[19,8,128]{2,1,0:T(8,128)S(1)}, f32[19,8,128]{2,1,0:T(8,128)S(1)}, u32[]{:S(2)}, u32[]{:S(2)}) collective-permute-start(f32[19,8,128]{2,1,0:T(8,128)S(1)} %collective-permute-done.2.refs_3_), channel_id=1, source_target_pairs={{0,4},{1,5},{2,6},{3,7},{4,0},{5,1},{6,2},{7,3},{8,12},{9,13},{10,... | collective-permute-start | bytes 233480 | tf_op jit(solution)/shard_map/ppermute | solution.py:189
  9.2 1.3 %collective-permute-done.refs_1_ = f32[19,8,128]{2,1,0:T(8,128)S(1)} collective-permute-done((f32[19,8,128]{2,1,0:T(8,128)S(1)}, f32[19,8,128]{2,1,0:T(8,128)S(1)}, u32[]{:S(2)}, u32[]{:S(2)}) %collective-permute-start) | collective-permute-done | bytes 77856 | tf_op jit(solution)/shard_map/ppermute | solution.py:189
  10.5 0.5 %collective-permute-start.6 = (f32[19,8,128]{2,1,0:T(8,128)S(1)}, f32[19,8,128]{2,1,0:T(8,128)S(1)}, u32[]{:S(2)}, u32[]{:S(2)}) collective-permute-start(f32[19,8,128]{2,1,0:T(8,128)S(1)} %collective-permute-done.refs_1_), channel_id=1, source_target_pairs={{0,2},{1,3},{2,0},{3,1},{4,6},{5,7},{6,4},{7,5},{8,10},{9,11},{10,... | collective-permute-start | bytes 233480 | tf_op jit(solution)/shard_map/ppermute | solution.py:189
  11.0 0.6 %collective-permute-start.5 = (f32[19,8,128]{2,1,0:T(8,128)S(1)}, f32[19,8,128]{2,1,0:T(8,128)S(1)}, u32[]{:S(2)}, u32[]{:S(2)}) collective-permute-start(f32[19,8,128]{2,1,0:T(8,128)S(1)} %collective-permute-done.refs_1_), channel_id=1, source_target_pairs={{0,5},{1,4},{2,7},{3,6},{4,1},{5,0},{6,3},{7,2},{8,13},{9,12},{10,... | collective-permute-start | bytes 233480 | tf_op jit(solution)/shard_map/ppermute | solution.py:189
  11.6 0.2 %collective-permute-done.1.refs_2_ = f32[19,8,128]{2,1,0:T(8,128)S(1)} collective-permute-done((f32[19,8,128]{2,1,0:T(8,128)S(1)}, f32[19,8,128]{2,1,0:T(8,128)S(1)}, u32[]{:S(2)}, u32[]{:S(2)}) %collective-permute-start.1) | collective-permute-done | bytes 77856 | tf_op jit(solution)/shard_map/ppermute | solution.py:189
  11.8 1.3 %collective-permute-start.3 = (f32[76,8,128]{2,1,0:T(8,128)S(1)}, f32[76,8,128]{2,1,0:T(8,128)S(1)}, u32[]{:S(2)}, u32[]{:S(2)}) collective-permute-start(f32[76,8,128]{2,1,0:T(8,128)S(1)} %join.2.refs_0_), channel_id=1, source_target_pairs={{0,1},{1,0},{2,3},{3,2},{4,5},{5,4},{6,7},{7,6},{8,9},{9,8},{10,11... | collective-permute-start | bytes 933896 | tf_op jit(solution)/shard_map/ppermute | solution.py:189
  13.2 2.9 %collective-permute-done.4.refs_0_ = f32[19,8,128]{2,1,0:T(8,128)S(1)} collective-permute-done((f32[19,8,128]{2,1,0:T(8,128)S(1)}, f32[19,8,128]{2,1,0:T(8,128)S(1)}, u32[]{:S(2)}, u32[]{:S(2)}) %collective-permute-start.4) | collective-permute-done | bytes 77856 | tf_op jit(solution)/shard_map/ppermute | solution.py:189
  16.0 0.0 collective-permute-done.7.refs_3_
  16.0 0.1 collective-permute-done.6.refs_2_
  16.2 0.1 collective-permute-done.5.refs_1_
  16.3 0.2 collective-permute-start.8
  16.5 0.0 collective-permute-done.3.refs_1_
  16.5 1.5 %collective-permute-done.8.refs_3_ = f32[76,8,128]{2,1,0:T(8,128)S(1)} collective-permute-done((f32[76,8,128]{2,1,0:T(8,128)S(1)}, f32[76,8,128]{2,1,0:T(8,128)S(1)}, u32[]{:S(2)}, u32[]{:S(2)}) %collective-permute-start.8) | collective-permute-done | bytes 311328 | tf_op jit(solution)/shard_map/ppermute | solution.py:189
  18.0 2.8 %group_smacof.1 = (f32[16,24]{1,0:T(8,128)}, f32[1,3]{1,0:T(1,128)}) custom-call(f32[76,8,128]{2,1,0:T(8,128)S(1)} %join.2.refs_0_, f32[76,8,128]{2,1,0:T(8,128)S(1)} %collective-permute-done.3.refs_1_, f32[76,8,128]{2,1,0:T(8,128)S(1)} %join.3.refs_2_, f32[76,8,128]{2,1,0:T(8,128)S(1)} %collective-permute-done.8.refs_3_), custom_call_target="tpu_custom_call" | custom-call | tf_op jit(solution)/shard_map/group_smacof/pallas_call | solution.py:231
  (2 shorter events, 0.0 us)
Async XLA Ops:
  1.5 7.2 %collective-permute-start.2 = (f32[19,8,128]{2,1,0:T(8,128)S(1)}, f32[19,8,128]{2,1,0:T(8,128)S(1)}, u32[]{:S(2)}, u32[]{:S(2)}) collective-permute-start(f32[19,8,128]{2,1,0:T(8,128)S(1)} %pack.1.refs_0_), channel_id=1, source_target_pairs={{0,2},{1,3},{2,0},{3,1},{4,6},{5,7},{6,4},{7,5},{8,10},{9,11},{10,... | collective-permute-start | bytes 233480 | tf_op jit(solution)/shard_map/ppermute | solution.py:189
  4.5 5.9 %collective-permute-start = (f32[19,8,128]{2,1,0:T(8,128)S(1)}, f32[19,8,128]{2,1,0:T(8,128)S(1)}, u32[]{:S(2)}, u32[]{:S(2)}) collective-permute-start(f32[19,8,128]{2,1,0:T(8,128)S(1)} %pack.1.refs_0_), channel_id=1, source_target_pairs={{0,8},{1,9},{2,10},{3,11},{4,12},{5,13},{6,14},{7,15},{8,0},{9,1},... | collective-permute-start | bytes 233480 | tf_op jit(solution)/shard_map/ppermute | solution.py:189
  7.1 4.7 %collective-permute-start.1 = (f32[19,8,128]{2,1,0:T(8,128)S(1)}, f32[19,8,128]{2,1,0:T(8,128)S(1)}, u32[]{:S(2)}, u32[]{:S(2)}) collective-permute-start(f32[19,8,128]{2,1,0:T(8,128)S(1)} %pack.1.refs_0_), channel_id=1, source_target_pairs={{0,4},{1,5},{2,6},{3,7},{4,0},{5,1},{6,2},{7,3},{8,12},{9,13},{10,... | collective-permute-start | bytes 233480 | tf_op jit(solution)/shard_map/ppermute | solution.py:189
  8.7 7.3 %collective-permute-start.4 = (f32[19,8,128]{2,1,0:T(8,128)S(1)}, f32[19,8,128]{2,1,0:T(8,128)S(1)}, u32[]{:S(2)}, u32[]{:S(2)}) collective-permute-start(f32[19,8,128]{2,1,0:T(8,128)S(1)} %pack.1.refs_0_), channel_id=1, source_target_pairs={{0,15},{1,14},{2,13},{3,12},{4,11},{5,10},{6,9},{7,8},{8,7},{9,6},... | collective-permute-start | bytes 233480 | tf_op jit(solution)/shard_map/ppermute | solution.py:189
  8.7 7.3 %collective-permute-start.7 = (f32[19,8,128]{2,1,0:T(8,128)S(1)}, f32[19,8,128]{2,1,0:T(8,128)S(1)}, u32[]{:S(2)}, u32[]{:S(2)}) collective-permute-start(f32[19,8,128]{2,1,0:T(8,128)S(1)} %collective-permute-done.2.refs_3_), channel_id=1, source_target_pairs={{0,4},{1,5},{2,6},{3,7},{4,0},{5,1},{6,2},{7,3},{8,12},{9,13},{10,... | collective-permute-start | bytes 233480 | tf_op jit(solution)/shard_map/ppermute | solution.py:189
  10.5 5.7 %collective-permute-start.6 = (f32[19,8,128]{2,1,0:T(8,128)S(1)}, f32[19,8,128]{2,1,0:T(8,128)S(1)}, u32[]{:S(2)}, u32[]{:S(2)}) collective-permute-start(f32[19,8,128]{2,1,0:T(8,128)S(1)} %collective-permute-done.refs_1_), channel_id=1, source_target_pairs={{0,2},{1,3},{2,0},{3,1},{4,6},{5,7},{6,4},{7,5},{8,10},{9,11},{10,... | collective-permute-start | bytes 233480 | tf_op jit(solution)/shard_map/ppermute | solution.py:189
  11.0 5.3 %collective-permute-start.5 = (f32[19,8,128]{2,1,0:T(8,128)S(1)}, f32[19,8,128]{2,1,0:T(8,128)S(1)}, u32[]{:S(2)}, u32[]{:S(2)}) collective-permute-start(f32[19,8,128]{2,1,0:T(8,128)S(1)} %collective-permute-done.refs_1_), channel_id=1, source_target_pairs={{0,5},{1,4},{2,7},{3,6},{4,1},{5,0},{6,3},{7,2},{8,13},{9,12},{10,... | collective-permute-start | bytes 233480 | tf_op jit(solution)/shard_map/ppermute | solution.py:189
  11.8 4.6 %collective-permute-start.3 = (f32[76,8,128]{2,1,0:T(8,128)S(1)}, f32[76,8,128]{2,1,0:T(8,128)S(1)}, u32[]{:S(2)}, u32[]{:S(2)}) collective-permute-start(f32[76,8,128]{2,1,0:T(8,128)S(1)} %join.2.refs_0_), channel_id=1, source_target_pairs={{0,1},{1,0},{2,3},{3,2},{4,5},{5,4},{6,7},{7,6},{8,9},{9,8},{10,11... | collective-permute-start | bytes 933896 | tf_op jit(solution)/shard_map/ppermute | solution.py:189
  16.3 1.7 %collective-permute-start.8 = (f32[76,8,128]{2,1,0:T(8,128)S(1)}, f32[76,8,128]{2,1,0:T(8,128)S(1)}, u32[]{:S(2)}, u32[]{:S(2)}) collective-permute-start(f32[76,8,128]{2,1,0:T(8,128)S(1)} %join.3.refs_2_), channel_id=1, source_target_pairs={{0,1},{1,0},{2,3},{3,2},{4,5},{5,4},{6,7},{7,6},{8,9},{9,8},{10,11... | collective-permute-start | bytes 933896 | tf_op jit(solution)/shard_map/ppermute | solution.py:189

commit v28 on v27

--- a/solution.py
+++ b/solution.py
@@ -208,7 +208,7 @@
     held = {0: packed}
     for offset in (far, side, near, far | near | side | 1):
         held[offset] = swap(packed, offset)
-    for source, step in ((far, near | 1), (far, side), (side, near)):
+    for source, step in ((far, near | 1), (far, side | 1), (side, near)):
         held[source | step] = swap(held[source], step)
     early = [0, far, near, side]
     late = [offset for offset in held if offset not in early]

time: 21 us -> 20.8 us (level)
  waiting for transfers between devices: 6.14 us -> 5.69 us
  starting transfers between devices: 10.2 us -> 10.6 us
    ppermute x9, waiting for transfers between devices: 6.14 us -> 5.69 us  [swap(): lax.ppermute(value, 'wide', [(i, i ^ offset) for i in range(devices)])]
    ppermute x9, starting transfers between devices: 10.2 us -> 10.6 us  [swap(): lax.ppermute(value, 'wide', [(i, i ^ offset) for i in range(devices)])]
  transfers between devices with their start and end apart: 9 -> 9, of which waited for: 6 -> 4; matrix products, arithmetic and copies ran while one was open for 0% -> 0% of each run, Pallas kernels for 0% -> 0%
where the time goes in v28:
time: 20.8 us; the launch traced here: 20.6 us
  starting transfers between devices  10.6 us (51%)
  waiting for transfers between devices  5.69 us (27%)
  Pallas kernels  3.74 us (18%)
  between operations  0.66 us (3%)
    ppermute x9, starting transfers between devices, swap(): lax.ppermute(value, 'wide', [(i, i ^ offset) for i in range(devices)])  10.6 us
    ppermute x9, waiting for transfers between devices, swap(): lax.ppermute(value, 'wide', [(i, i ^ offset) for i in range(devices)])  5.69 us
    pallas_call x1, Pallas kernels, small_body(): pl.pallas_call(functools.partial(group_kernel, offsets, per_dev), out_sha...  2.81 us
    pallas_call x1, Pallas kernels, small_body(): pl.pallas_call(pack_kernel, out_shape=f32((tiles, SUBLANES, LANES)), in_s...  0.89 us
  transfers between devices with their start and end apart: 9, of which 4 were waited for; matrix products, arithmetic and copies ran while one was open for 0% of the time, Pallas kernels for 0%

profile of v28, /device:TPU:0, one launch (start us, length us, event | category | flops | bytes accessed | tf_op | source)
XLA Modules:
  0.0 20.6 jit_solution(8019591599632156965)
XLA Ops:
  0.6 0.9 %pack.1.refs_0_ = f32[19,8,128]{2,1,0:T(8,128)S(1)} custom-call(f32[24,384]{1,0:T(8,128)} %bitcast.7, s32[24,384]{1,0:T(8,128)} %bitcast.8, f32[16,24]{1,0:T(8,128)} %bitcast.9), custom_call_target="tpu_custom_call" | custom-call | tf_op jit(solution)/shard_map/pack/pallas_call | solution.py:193
  1.5 3.0 %collective-permute-start.2 = (f32[19,8,128]{2,1,0:T(8,128)S(1)}, f32[19,8,128]{2,1,0:T(8,128)S(1)}, u32[]{:S(2)}, u32[]{:S(2)}) collective-permute-start(f32[19,8,128]{2,1,0:T(8,128)S(1)} %pack.1.refs_0_), channel_id=1, source_target_pairs={{0,2},{1,3},{2,0},{3,1},{4,6},{5,7},{6,4},{7,5},{8,10},{9,11},{10,... | collective-permute-start | bytes 233480 | tf_op jit(solution)/shard_map/ppermute | solution.py:189
  4.5 2.6 %collective-permute-start = (f32[19,8,128]{2,1,0:T(8,128)S(1)}, f32[19,8,128]{2,1,0:T(8,128)S(1)}, u32[]{:S(2)}, u32[]{:S(2)}) collective-permute-start(f32[19,8,128]{2,1,0:T(8,128)S(1)} %pack.1.refs_0_), channel_id=1, source_target_pairs={{0,8},{1,9},{2,10},{3,11},{4,12},{5,13},{6,14},{7,15},{8,0},{9,1},... | collective-permute-start | bytes 233480 | tf_op jit(solution)/shard_map/ppermute | solution.py:189
  7.1 1.6 %collective-permute-start.1 = (f32[19,8,128]{2,1,0:T(8,128)S(1)}, f32[19,8,128]{2,1,0:T(8,128)S(1)}, u32[]{:S(2)}, u32[]{:S(2)}) collective-permute-start(f32[19,8,128]{2,1,0:T(8,128)S(1)} %pack.1.refs_0_), channel_id=1, source_target_pairs={{0,4},{1,5},{2,6},{3,7},{4,0},{5,1},{6,2},{7,3},{8,12},{9,13},{10,... | collective-permute-start | bytes 233480 | tf_op jit(solution)/shard_map/ppermute | solution.py:189
  8.7 0.0 collective-permute-start.4
  8.7 0.0 collective-permute-done.2.refs_3_
  8.7 0.5 %collective-permute-start.7 = (f32[19,8,128]{2,1,0:T(8,128)S(1)}, f32[19,8,128]{2,1,0:T(8,128)S(1)}, u32[]{:S(2)}, u32[]{:S(2)}) collective-permute-start(f32[19,8,128]{2,1,0:T(8,128)S(1)} %collective-permute-done.2.refs_3_), channel_id=1, source_target_pairs={{0,4},{1,5},{2,6},{3,7},{4,0},{5,1},{6,2},{7,3},{8,12},{9,13},{10,... | collective-permute-start | bytes 233480 | tf_op jit(solution)/shard_map/ppermute | solution.py:189
  9.2 1.3 %collective-permute-done.refs_1_ = f32[19,8,128]{2,1,0:T(8,128)S(1)} collective-permute-done((f32[19,8,128]{2,1,0:T(8,128)S(1)}, f32[19,8,128]{2,1,0:T(8,128)S(1)}, u32[]{:S(2)}, u32[]{:S(2)}) %collective-permute-start) | collective-permute-done | bytes 77856 | tf_op jit(solution)/shard_map/ppermute | solution.py:189
  10.5 0.0 collective-permute-start.6
  10.5 1.6 %collective-permute-start.5 = (f32[19,8,128]{2,1,0:T(8,128)S(1)}, f32[19,8,128]{2,1,0:T(8,128)S(1)}, u32[]{:S(2)}, u32[]{:S(2)}) collective-permute-start(f32[19,8,128]{2,1,0:T(8,128)S(1)} %collective-permute-done.refs_1_), channel_id=1, source_target_pairs={{0,5},{1,4},{2,7},{3,6},{4,1},{5,0},{6,3},{7,2},{8,13},{9,12},{10,... | collective-permute-start | bytes 233480 | tf_op jit(solution)/shard_map/ppermute | solution.py:189
  12.1 0.0 collective-permute-done.1.refs_2_
  12.1 1.1 %collective-permute-start.3 = (f32[76,8,128]{2,1,0:T(8,128)S(1)}, f32[76,8,128]{2,1,0:T(8,128)S(1)}, u32[]{:S(2)}, u32[]{:S(2)}) collective-permute-start(f32[76,8,128]{2,1,0:T(8,128)S(1)} %join.2.refs_0_), channel_id=1, source_target_pairs={{0,1},{1,0},{2,3},{3,2},{4,5},{5,4},{6,7},{7,6},{8,9},{9,8},{10,11... | collective-permute-start | bytes 933896 | tf_op jit(solution)/shard_map/ppermute | solution.py:189
  13.2 2.9 %collective-permute-done.4.refs_0_ = f32[19,8,128]{2,1,0:T(8,128)S(1)} collective-permute-done((f32[19,8,128]{2,1,0:T(8,128)S(1)}, f32[19,8,128]{2,1,0:T(8,128)S(1)}, u32[]{:S(2)}, u32[]{:S(2)}) %collective-permute-start.4) | collective-permute-done | bytes 77856 | tf_op jit(solution)/shard_map/ppermute | solution.py:189
  16.0 0.0 collective-permute-done.7.refs_3_
  16.0 0.0 collective-permute-done.6.refs_2_
  16.0 0.1 collective-permute-done.5.refs_1_
  16.2 0.3 %collective-permute-start.8 = (f32[76,8,128]{2,1,0:T(8,128)S(1)}, f32[76,8,128]{2,1,0:T(8,128)S(1)}, u32[]{:S(2)}, u32[]{:S(2)}) collective-permute-start(f32[76,8,128]{2,1,0:T(8,128)S(1)} %join.3.refs_2_), channel_id=1, source_target_pairs={{0,1},{1,0},{2,3},{3,2},{4,5},{5,4},{6,7},{7,6},{8,9},{9,8},{10,11... | collective-permute-start | bytes 933896 | tf_op jit(solution)/shard_map/ppermute | solution.py:189
  16.4 0.0 collective-permute-done.3.refs_1_
  16.4 1.4 %collective-permute-done.8.refs_3_ = f32[76,8,128]{2,1,0:T(8,128)S(1)} collective-permute-done((f32[76,8,128]{2,1,0:T(8,128)S(1)}, f32[76,8,128]{2,1,0:T(8,128)S(1)}, u32[]{:S(2)}, u32[]{:S(2)}) %collective-permute-start.8) | collective-permute-done | bytes 311328 | tf_op jit(solution)/shard_map/ppermute | solution.py:189
  17.8 2.8 %group_smacof.1 = (f32[16,24]{1,0:T(8,128)}, f32[1,3]{1,0:T(1,128)}) custom-call(f32[76,8,128]{2,1,0:T(8,128)S(1)} %join.2.refs_0_, f32[76,8,128]{2,1,0:T(8,128)S(1)} %collective-permute-done.3.refs_1_, f32[76,8,128]{2,1,0:T(8,128)S(1)} %join.3.refs_2_, f32[76,8,128]{2,1,0:T(8,128)S(1)} %collective-permute-done.8.refs_3_), custom_call_target="tpu_custom_call" | custom-call | tf_op jit(solution)/shard_map/group_smacof/pallas_call | solution.py:231
  (2 shorter events, 0.0 us)
Async XLA Ops:
  1.5 7.2 %collective-permute-start.2 = (f32[19,8,128]{2,1,0:T(8,128)S(1)}, f32[19,8,128]{2,1,0:T(8,128)S(1)}, u32[]{:S(2)}, u32[]{:S(2)}) collective-permute-start(f32[19,8,128]{2,1,0:T(8,128)S(1)} %pack.1.refs_0_), channel_id=1, source_target_pairs={{0,2},{1,3},{2,0},{3,1},{4,6},{5,7},{6,4},{7,5},{8,10},{9,11},{10,... | collective-permute-start | bytes 233480 | tf_op jit(solution)/shard_map/ppermute | solution.py:189
  4.5 5.9 %collective-permute-start = (f32[19,8,128]{2,1,0:T(8,128)S(1)}, f32[19,8,128]{2,1,0:T(8,128)S(1)}, u32[]{:S(2)}, u32[]{:S(2)}) collective-permute-start(f32[19,8,128]{2,1,0:T(8,128)S(1)} %pack.1.refs_0_), channel_id=1, source_target_pairs={{0,8},{1,9},{2,10},{3,11},{4,12},{5,13},{6,14},{7,15},{8,0},{9,1},... | collective-permute-start | bytes 233480 | tf_op jit(solution)/shard_map/ppermute | solution.py:189
  7.1 4.9 %collective-permute-start.1 = (f32[19,8,128]{2,1,0:T(8,128)S(1)}, f32[19,8,128]{2,1,0:T(8,128)S(1)}, u32[]{:S(2)}, u32[]{:S(2)}) collective-permute-start(f32[19,8,128]{2,1,0:T(8,128)S(1)} %pack.1.refs_0_), channel_id=1, source_target_pairs={{0,4},{1,5},{2,6},{3,7},{4,0},{5,1},{6,2},{7,3},{8,12},{9,13},{10,... | collective-permute-start | bytes 233480 | tf_op jit(solution)/shard_map/ppermute | solution.py:189
  8.7 7.3 %collective-permute-start.4 = (f32[19,8,128]{2,1,0:T(8,128)S(1)}, f32[19,8,128]{2,1,0:T(8,128)S(1)}, u32[]{:S(2)}, u32[]{:S(2)}) collective-permute-start(f32[19,8,128]{2,1,0:T(8,128)S(1)} %pack.1.refs_0_), channel_id=1, source_target_pairs={{0,15},{1,14},{2,13},{3,12},{4,11},{5,10},{6,9},{7,8},{8,7},{9,6},... | collective-permute-start | bytes 233480 | tf_op jit(solution)/shard_map/ppermute | solution.py:189
  8.7 7.3 %collective-permute-start.7 = (f32[19,8,128]{2,1,0:T(8,128)S(1)}, f32[19,8,128]{2,1,0:T(8,128)S(1)}, u32[]{:S(2)}, u32[]{:S(2)}) collective-permute-start(f32[19,8,128]{2,1,0:T(8,128)S(1)} %collective-permute-done.2.refs_3_), channel_id=1, source_target_pairs={{0,4},{1,5},{2,6},{3,7},{4,0},{5,1},{6,2},{7,3},{8,12},{9,13},{10,... | collective-permute-start | bytes 233480 | tf_op jit(solution)/shard_map/ppermute | solution.py:189
  10.5 5.6 %collective-permute-start.6 = (f32[19,8,128]{2,1,0:T(8,128)S(1)}, f32[19,8,128]{2,1,0:T(8,128)S(1)}, u32[]{:S(2)}, u32[]{:S(2)}) collective-permute-start(f32[19,8,128]{2,1,0:T(8,128)S(1)} %collective-permute-done.refs_1_), channel_id=1, source_target_pairs={{0,3},{1,2},{2,1},{3,0},{4,7},{5,6},{6,5},{7,4},{8,11},{9,10},{10,... | collective-permute-start | bytes 233480 | tf_op jit(solution)/shard_map/ppermute | solution.py:189
  10.5 5.6 %collective-permute-start.5 = (f32[19,8,128]{2,1,0:T(8,128)S(1)}, f32[19,8,128]{2,1,0:T(8,128)S(1)}, u32[]{:S(2)}, u32[]{:S(2)}) collective-permute-start(f32[19,8,128]{2,1,0:T(8,128)S(1)} %collective-permute-done.refs_1_), channel_id=1, source_target_pairs={{0,5},{1,4},{2,7},{3,6},{4,1},{5,0},{6,3},{7,2},{8,13},{9,12},{10,... | collective-permute-start | bytes 233480 | tf_op jit(solution)/shard_map/ppermute | solution.py:189
  12.1 4.3 %collective-permute-start.3 = (f32[76,8,128]{2,1,0:T(8,128)S(1)}, f32[76,8,128]{2,1,0:T(8,128)S(1)}, u32[]{:S(2)}, u32[]{:S(2)}) collective-permute-start(f32[76,8,128]{2,1,0:T(8,128)S(1)} %join.2.refs_0_), channel_id=1, source_target_pairs={{0,1},{1,0},{2,3},{3,2},{4,5},{5,4},{6,7},{7,6},{8,9},{9,8},{10,11... | collective-permute-start | bytes 933896 | tf_op jit(solution)/shard_map/ppermute | solution.py:189
  16.2 1.7 %collective-permute-start.8 = (f32[76,8,128]{2,1,0:T(8,128)S(1)}, f32[76,8,128]{2,1,0:T(8,128)S(1)}, u32[]{:S(2)}, u32[]{:S(2)}) collective-permute-start(f32[76,8,128]{2,1,0:T(8,128)S(1)} %join.3.refs_2_), channel_id=1, source_target_pairs={{0,1},{1,0},{2,3},{3,2},{4,5},{5,4},{6,7},{7,6},{8,9},{9,8},{10,11... | collective-permute-start | bytes 933896 | tf_op jit(solution)/shard_map/ppermute | solution.py:189
